TPU v7x, 512 devices: a whole 4x8x8 slice. The times are simulated.
512 devices in a mesh: gx: 8 (over y_lo, core), gy: 8 (over z), gz: 8 (over y_hi, x).
Axes of the slice: x: 4, y: 8 (y_hi: 2, y_lo: 4; y = y_hi * 4 + y_lo), z: 8, core: 2. Of those that a mesh axis runs over, the one named last changes fastest.
Arguments:
- tokens: bfloat16 [1024, 8192], P('gx', ('gz', 'gy')), may hold values from -6 to 6
- gate_weight: bfloat16 [14336, 8192], P(('gy', 'gx'), 'gz'), may hold values from -0.0625 to 0.0625
- up_weight: bfloat16 [14336, 8192], P(('gy', 'gx'), 'gz'), may hold values from -0.0625 to 0.0625
- down_weight: bfloat16 [14336, 8192], P(('gy', 'gx'), 'gz'), may hold values from -0.046875 to 0.046875
- reward_head: bfloat16 [8192], P(('gz', 'gy')), may hold values from -0.0625 to 0.0625
- lm_grad: float32 [1024, 8192], P('gx', ('gz', 'gy')), may hold values from -6 to 6
- pair_index: int32 [4, 2], replicated, may hold values from 0 to 7, as said below
Outputs:
- grad_tokens: float32 [1024, 8192], P('gx', ('gz', 'gy'))
- grad_gate: float32 [14336, 8192], P(('gy', 'gx'), 'gz')
- grad_up: float32 [14336, 8192], P(('gy', 'gx'), 'gz')
- grad_down: float32 [14336, 8192], P(('gy', 'gx'), 'gz')
- rewards: float32 [8], replicated
Inputs may be any that keep to these rules, and one draw needn't show every extreme that they name: Every sequence number of 0 to 7 stands exactly once in pair_index.
All inputs are finite; a program needn't handle non-finite values.
Results may differ from a plain program's by a relative error of at most 0.008.
Values may be sent and summed in bfloat16 or wider, within the bound.
No kernel may reach another device: no remote copies, remote signals or barrier semaphores. Data moves between devices by JAX's collectives and lax.ppermute only.
A program may use at most 64 MiB of HBM per device.

v0:
```python
import jax
import jax.numpy as jnp
from jax import lax
from jax.sharding import PartitionSpec as P

SEQ_LEN = 128


reward_weight = 64.0


def feature_blocks(shard):
    return lax.all_gather(shard, "gy", axis=1, tiled=True)


def output_sums(partial_value):
    return lax.psum_scatter(partial_value, "gy", scatter_dimension=1, tiled=True)


def right_product(left, right):
    return lax.dot_general(
        left, right, (((1,), (1,)), ((), ())), preferred_element_type=jnp.float32
    )


def body(tokens, gate_weight, up_weight, down_weight, reward_head, lm_grad, pair_index):
    row_count = tokens.shape[0]
    tok_block = feature_blocks(tokens)
    gate_full, up_full, down_full = (
        lax.all_gather(gate_weight, "gx", axis=0, tiled=True),
        lax.all_gather(up_weight, "gx", axis=0, tiled=True),
        lax.all_gather(down_weight, "gx", axis=0, tiled=True),
    )
    gate_part = right_product(tok_block, gate_full)
    up_part = right_product(tok_block, up_full)
    gate_sum, up_sum = (
        lax.psum_scatter(gate_part, "gz", scatter_dimension=1, tiled=True),
        lax.psum_scatter(up_part, "gz", scatter_dimension=1, tiled=True),
    )
    gate_sigmoid = jax.nn.sigmoid(gate_sum)
    silu_gate = gate_sum * gate_sigmoid
    hidden = (silu_gate * up_sum).astype(jnp.bfloat16)
    hidden_block = lax.all_gather(hidden, "gz", axis=1, tiled=True)
    ffn_out = output_sums(jnp.dot(hidden_block, down_full, preferred_element_type=jnp.float32))
    block_out = tokens.astype(jnp.float32) + ffn_out
    seq_dev = row_count // SEQ_LEN
    seq_total = seq_dev * lax.axis_size("gx")
    head_vec = reward_head.astype(jnp.float32)
    last_rows = block_out.reshape(seq_dev, SEQ_LEN, -1)[:, SEQ_LEN - 1, :]
    own_terms = jnp.sum(last_rows * head_vec[None, :], axis=1)
    offset = lax.axis_index("gx") * seq_dev
    spread = lax.dynamic_update_slice(jnp.zeros((seq_total,), jnp.float32), own_terms, (offset,))
    rewards = lax.psum(spread, ("gx", "gy", "gz"))
    sequence = jnp.arange(seq_total, dtype=jnp.int32)
    chosen_hot = (pair_index[:, 0:1] == sequence[None, :]).astype(jnp.float32)
    rejected_hot = (pair_index[:, 1:2] == sequence[None, :]).astype(jnp.float32)
    margin = jnp.sum(chosen_hot * rewards[None, :], axis=1) - jnp.sum(
        rejected_hot * rewards[None, :], axis=1
    )
    pair_weight = jax.nn.sigmoid(-margin)
    pair_coefs = jnp.sum((rejected_hot - chosen_hot) * pair_weight[:, None], axis=0)
    own_coefs = lax.dynamic_slice(pair_coefs, (offset,), (seq_dev,))
    head_term = reward_weight * own_coefs[:, None] * head_vec[None, :]
    grad_out = (
        lm_grad.reshape(seq_dev, SEQ_LEN, -1)
        .at[:, SEQ_LEN - 1, :]
        .add(head_term)
        .reshape(row_count, -1)
    )
    grad_low = grad_out.astype(jnp.bfloat16)
    grad_block = feature_blocks(grad_low)
    hidden_part = right_product(grad_block, down_full)
    hidden_grad = lax.psum_scatter(hidden_part, "gz", scatter_dimension=1, tiled=True)
    up_grad = (hidden_grad * silu_gate).astype(jnp.bfloat16)
    gate_grad = (
        hidden_grad * up_sum * gate_sigmoid * (1.0 + gate_sum * (1.0 - gate_sigmoid))
    ).astype(jnp.bfloat16)
    gate_grad_block, up_grad_block = (
        lax.all_gather(gate_grad, "gz", axis=1, tiled=True),
        lax.all_gather(up_grad, "gz", axis=1, tiled=True),
    )
    token_part = jnp.dot(gate_grad_block, gate_full, preferred_element_type=jnp.float32) + jnp.dot(
        up_grad_block, up_full, preferred_element_type=jnp.float32
    )
    grad_tokens = grad_out + output_sums(token_part)
    hidden_cols, gate_cols, up_cols = (
        lax.all_to_all(hidden_block, "gx", split_axis=1, concat_axis=0, tiled=True),
        lax.all_to_all(gate_grad_block, "gx", split_axis=1, concat_axis=0, tiled=True),
        lax.all_to_all(up_grad_block, "gx", split_axis=1, concat_axis=0, tiled=True),
    )
    tok_piece = lax.all_gather(tok_block, "gx", axis=0, tiled=True)
    grad_piece = lax.all_gather(grad_block, "gx", axis=0, tiled=True)
    gate_total = jnp.einsum("tf,td->fd", gate_cols, tok_piece, preferred_element_type=jnp.float32)
    up_total = jnp.einsum("tf,td->fd", up_cols, tok_piece, preferred_element_type=jnp.float32)
    down_total = jnp.einsum(
        "tf,td->fd", hidden_cols, grad_piece, preferred_element_type=jnp.float32
    )
    loss_scale = 1.0 / jnp.sqrt(jnp.float32(row_count * lax.axis_size("gx")))
    return (
        grad_tokens,
        gate_total * loss_scale,
        up_total * loss_scale,
        down_total * loss_scale,
        rewards,
    )


def solution(mesh):
    placed = (
        P("gx", ("gz", "gy")),
        P(("gy", "gx"), "gz"),
        P(("gy", "gx"), "gz"),
        P(("gy", "gx"), "gz"),
        P(("gz", "gy")),
        P("gx", ("gz", "gy")),
        P(),
    )
    return jax.shard_map(
        body,
        mesh=mesh,
        in_specs=placed,
        out_specs=(
            P("gx", ("gz", "gy")),
            P(("gy", "gx"), "gz"),
            P(("gy", "gx"), "gz"),
            P(("gy", "gx"), "gz"),
            P(),
        ),
        check_vma=False,
    )
```

profile of v0, /device:TPU:1, one launch (start us, length us, event | category | flops | bytes accessed | tf_op | source)
XLA Modules:
  0.0 804.8 jit_solution(16231011762949512689)
XLA Ops:
  7.2 0.0 all-gather.6.cloned.1.call-start
  7.2 0.8 copy.39
  8.1 0.0 all-gather.6.cloned.1.call-update
  8.1 0.0 all-gather.8.cloned.1.call-start
  8.1 0.7 all-gather.8.cloned.1.call-update
  8.8 0.0 reduce-scatter.6.cloned.1.call-start
  8.9 24.8 %all_gather.30 = bf16[128,1024]{1,0:T(8,128)(2,1)S(1)} all-gather(bf16[128,128]{1,0:T(8,128)(2,1)} %param.9), channel_id=1, replica_groups=mesh['gx'=8,'gy'=8,'gz'=8] {'gy'}, dimensions={1}, use_global_device_ids=true | all-gather | bytes 294912 | tf_op jit(solution)/shard_map/all_gather | solution.py:13
  33.7 32.2 %all-gather.6.cloned.1.call-done = bf16[1792,1024]{1,0:T(8,128)(2,1)} async-done(((bf16[224,1024]{1,0:T(8,128)(2,1)}), bf16[1792,1024]{1,0:T(8,128)(2,1)}) %all-gather.6.cloned.1.call-update) | async-done | bytes 3670032 | tf_op jit(solution)/shard_map/all_gather | solution.py:30
  65.9 4.1 fusion.9
  70.0 0.0 reduce-scatter.6.cloned.1.call-update
  70.0 0.0 reduce-scatter.8.cloned.1.call-start
  70.0 49.0 %all-gather.8.cloned.1.call-done = bf16[1792,1024]{1,0:T(8,128)(2,1)} async-done(((bf16[224,1024]{1,0:T(8,128)(2,1)}), bf16[1792,1024]{1,0:T(8,128)(2,1)}) %all-gather.8.cloned.1.call-update) | async-done | bytes 3670032 | tf_op jit(solution)/shard_map/all_gather | solution.py:31
  119.0 4.1 fusion.10
  123.1 0.0 copy-done.2
  123.1 0.0 reduce-scatter.8.cloned.1.call-update
  123.1 0.0 all-gather.10.cloned.1.call-start
  123.2 0.5 all-gather.10.cloned.1.call-update
  123.7 0.0 reduce-scatter.10.cloned.1.call-start
  123.7 90.2 %reduce-scatter.6.cloned.1.call-done = f32[128,224]{0,1:T(8,128)} async-done(((f32[128,1792]{0,1:T(8,128)}), f32[128,224]{0,1:T(8,128)}) %reduce-scatter.6.cloned.1.call-update) | async-done | bytes 114704 | tf_op jit(solution)/shard_map/reduce_scatter | solution.py:37
  213.9 92.1 %reduce-scatter.8.cloned.1.call-done = f32[128,224]{0,1:T(8,128)} async-done(((f32[128,1792]{0,1:T(8,128)}), f32[128,224]{0,1:T(8,128)}) %reduce-scatter.8.cloned.1.call-update) | async-done | bytes 114704 | tf_op jit(solution)/shard_map/reduce_scatter | solution.py:38
  306.0 1.0 multiply_convert_fusion.2
  307.0 41.7 %all_gather.33 = bf16[128,1792]{0,1:T(8,128)(2,1)} all-gather(bf16[128,224]{0,1:T(8,128)(2,1)S(1)} %multiply_convert_fusion.2), channel_id=1, replica_groups=mesh['gx'=8,'gy'=8,'gz'=8] {'gz'}, dimensions={1}, use_global_device_ids=true | all-gather | bytes 516096 | tf_op jit(solution)/shard_map/all_gather | solution.py:43
  348.7 13.5 %all-gather.10.cloned.1.call-done = bf16[1792,1024]{1,0:T(8,128)(2,1)} async-done(((bf16[224,1024]{1,0:T(8,128)(2,1)}), bf16[1792,1024]{1,0:T(8,128)(2,1)}) %all-gather.10.cloned.1.call-update) | async-done | bytes 3670032 | tf_op jit(solution)/shard_map/all_gather | solution.py:32
  362.2 3.7 fusion.11
  365.9 0.0 reduce-scatter.10.cloned.1.call-update
  365.9 0.0 reduce-scatter.12.cloned.1.call-start
  366.0 0.0 copy-done.7
  366.0 36.7 %reduce-scatter.10.cloned.1.call-done = f32[128,128]{1,0:T(8,128)} async-done(((f32[128,1024]{1,0:T(8,128)}), f32[128,128]{1,0:T(8,128)}) %reduce-scatter.10.cloned.1.call-update) | async-done | bytes 65552 | tf_op jit(solution)/shard_map/reduce_scatter | solution.py:17
  402.7 0.0 copy-done.6
  402.7 0.8 add_bitcast_fusion
  403.5 0.6 fusion.8
  404.1 0.8 dynamic_update_slice.3
  404.9 100.9 %psum.7 = f32[8]{0:T(128)S(1)} all-reduce(f32[8]{0:T(128)S(1)} %dynamic_update_slice.3), channel_id=1, replica_groups=mesh['gx'=8,'gy'=8,'gz'=8] {'gx','gy','gz'}, use_global_device_ids=true, to_apply=%region_4.0 | all-reduce | flops 8 | bytes 64 | tf_op jit(solution)/shard_map/psum | solution.py:53
  505.7 0.2 select_reduce_fusion
  506.0 0.1 multiply_reduce_fusion
  506.1 0.6 dynamic_slice.3
  507.4 18.0 %all_gather.35 = bf16[128,1024]{1,0:T(8,128)(2,1)S(1)} all-gather(bf16[128,128]{1,0:T(8,128)(2,1)S(1)} %convert_element_type.29), channel_id=1, replica_groups=mesh['gx'=8,'gy'=8,'gz'=8] {'gy'}, dimensions={1}, use_global_device_ids=true | all-gather | bytes 294912 | tf_op jit(solution)/shard_map/all_gather | solution.py:13
  525.4 4.2 fusion.12
  529.6 0.0 reduce-scatter.12.cloned.1.call-update
  529.6 0.0 all-gather.12.cloned.1.call-start
  529.7 0.7 all-gather.12.cloned.1.call-update
  530.4 0.0 reduce-scatter.14.cloned.1.call-start
  530.4 88.5 %reduce-scatter.12.cloned.1.call-done = f32[128,224]{0,1:T(8,128)} async-done(((f32[128,1792]{0,1:T(8,128)}), f32[128,224]{0,1:T(8,128)}) %reduce-scatter.12.cloned.1.call-update) | async-done | bytes 114704 | tf_op jit(solution)/shard_map/reduce_scatter | solution.py:73
  619.0 0.0 copy-done.5
  619.0 1.1 multiply_convert_fusion
  620.1 39.6 %all_gather.36 = bf16[128,1792]{0,1:T(8,128)(2,1)S(1)} all-gather(bf16[128,224]{0,1:T(8,128)(2,1)S(1)} %get-tuple-element.20), channel_id=1, replica_groups=mesh['gx'=8,'gy'=8,'gz'=8] {'gz'}, dimensions={1}, use_global_device_ids=true | all-gather | bytes 516096 | tf_op jit(solution)/shard_map/all_gather | solution.py:79
  659.7 0.0 copy-done.8
  659.7 38.5 %all_gather.37 = bf16[128,1792]{0,1:T(8,128)(2,1)S(1)} all-gather(bf16[128,224]{0,1:T(8,128)(2,1)S(1)} %get-tuple-element.19), channel_id=1, replica_groups=mesh['gx'=8,'gy'=8,'gz'=8] {'gz'}, dimensions={1}, use_global_device_ids=true | all-gather | bytes 516096 | tf_op jit(solution)/shard_map/all_gather | solution.py:80
  698.2 2.7 fusion.13
  700.9 0.0 copy-done
  700.9 1.5 convolution_add_fusion
  702.4 0.0 reduce-scatter.14.cloned.1.call-update
  702.4 0.0 all-gather.14.cloned.1.call-start
  702.5 0.5 all-gather.14.cloned.1.call-update
  703.0 30.6 %all_to_all.57 = bf16[128,8,224]{0,2,1:T(8,128)(2,1)S(1)} all-to-all(bf16[128,8,224]{0,2,1:T(8,128)(2,1)S(1)} %bitcast.59), channel_id=1, replica_groups=mesh['gx'=8,'gy'=8,'gz'=8] {'gx'}, dimensions={1} | all-to-all | bytes 917504 | tf_op jit(solution)/shard_map/all_to_all | solution.py:89
  733.6 16.5 %all_to_all.58 = bf16[128,8,224]{0,2,1:T(8,128)(2,1)S(1)} all-to-all(bf16[128,8,224]{0,2,1:T(8,128)(2,1)S(1)} %bitcast.58), channel_id=1, replica_groups=mesh['gx'=8,'gy'=8,'gz'=8] {'gx'}, dimensions={1} | all-to-all | bytes 917504 | tf_op jit(solution)/shard_map/all_to_all | solution.py:88
  750.1 4.2 all-to-all-start.2
  754.3 3.3 convolution_multiply_fusion.1
  757.6 0.0 copy-done.1
  757.6 1.6 convolution_multiply_fusion.2
  759.2 1.5 add.55
  760.7 6.7 all-to-all-done.2
  767.4 27.4 %all-gather.14.cloned.1.call-done = bf16[1024,1024]{1,0:T(8,128)(2,1)} async-done(((bf16[128,1024]{1,0:T(8,128)(2,1)}), bf16[1024,1024]{1,0:T(8,128)(2,1)}) %all-gather.14.cloned.1.call-update) | async-done | bytes 2097168 | tf_op jit(solution)/shard_map/all_gather | solution.py:92
  794.8 3.2 convolution_multiply_fusion
  (21 shorter events, 0.1 us)
Async XLA Ops:
  7.2 58.7 %all-gather.6.cloned.1.call-start = ((), (), s32[]{:S(2)}) async-start(), calls=%async_computation.8 | async-start | bytes 4128768 | tf_op jit(solution)/shard_map/all_gather | solution.py:30
  8.1 110.9 %all-gather.8.cloned.1.call-start = ((), (), s32[]{:S(2)}) async-start(), calls=%async_computation.10 | async-start | bytes 4128768 | tf_op jit(solution)/shard_map/all_gather | solution.py:31
  8.8 205.1 %reduce-scatter.6.cloned.1.call-start = ((), (), s32[]{:S(2)}) async-start(), calls=%async_computation.9 | async-start | bytes 1032192 | tf_op jit(solution)/shard_map/reduce_scatter | solution.py:37
  33.7 89.4 %copy-start.2 = (bf16[128,1024]{1,0:T(8,128)(2,1)}, bf16[128,1024]{1,0:T(8,128)(2,1)S(1)}, u32[]{:S(2)}) copy-start(bf16[128,1024]{1,0:T(8,128)(2,1)S(1)} %all_gather.30) | copy-start | bytes 786436
  70.0 236.0 %reduce-scatter.8.cloned.1.call-start = ((), (), s32[]{:S(2)}) async-start(), calls=%async_computation.11 | async-start | bytes 1032192 | tf_op jit(solution)/shard_map/reduce_scatter | solution.py:38
  123.1 242.9 %copy-start.7 = (s32[4,2]{0,1:T(2,128)S(1)}, s32[4,2]{0,1:T(2,128)}, u32[]{:S(2)}) copy-start(s32[4,2]{0,1:T(2,128)} %param.15) | copy-start | bytes 100
  123.1 279.6 %copy-start.6 = (bf16[128,128]{1,0:T(8,128)(2,1)S(1)}, bf16[128,128]{1,0:T(8,128)(2,1)}, u32[]{:S(2)}) copy-start(bf16[128,128]{1,0:T(8,128)(2,1)} %param.9) | copy-start | bytes 98308
  123.1 280.4 %copy-start.9 = (bf16[128]{0:T(256)(128)(2,1)S(1)}, bf16[128]{0:T(256)(128)(2,1)}, u32[]{:S(2)}) copy-start(bf16[128]{0:T(256)(128)(2,1)} %param.13) | copy-start | bytes 772
  123.1 239.1 %all-gather.10.cloned.1.call-start = ((), (), s32[]{:S(2)}) async-start(), calls=%async_computation.12 | async-start | bytes 4128768 | tf_op jit(solution)/shard_map/all_gather | solution.py:32
  123.7 279.0 %reduce-scatter.10.cloned.1.call-start = ((), (), s32[]{:S(2)}) async-start(), calls=%async_computation.13 | async-start | bytes 589824 | tf_op jit(solution)/shard_map/reduce_scatter | solution.py:17
  365.9 253.1 %copy-start.4 = (f32[128,224]{0,1:T(8,128)S(1)}, f32[128,224]{0,1:T(8,128)}, u32[]{:S(2)}) copy-start(f32[128,224]{0,1:T(8,128)} %reduce-scatter.6.cloned.1.call-done) | copy-start | bytes 344068
  365.9 253.1 %copy-start.5 = (f32[128,224]{0,1:T(8,128)S(1)}, f32[128,224]{0,1:T(8,128)}, u32[]{:S(2)}) copy-start(f32[128,224]{0,1:T(8,128)} %reduce-scatter.8.cloned.1.call-done) | copy-start | bytes 344068
  365.9 253.0 %reduce-scatter.12.cloned.1.call-start = ((), (), s32[]{:S(2)}) async-start(), calls=%async_computation.14 | async-start | bytes 1032192 | tf_op jit(solution)/shard_map/reduce_scatter | solution.py:73
  505.7 154.0 %copy-start.8 = (f32[8]{0:T(128)}, f32[8]{0:T(128)S(1)}, u32[]{:S(2)}) copy-start(f32[8]{0:T(128)S(1)} %psum.7) | copy-start | bytes 100
  525.4 172.8 %copy-start.3 = (bf16[128,1024]{1,0:T(8,128)(2,1)}, bf16[128,1024]{1,0:T(8,128)(2,1)S(1)}, u32[]{:S(2)}) copy-start(bf16[128,1024]{1,0:T(8,128)(2,1)S(1)} %all_gather.35) | copy-start | bytes 786436
  529.6 224.7 %all-gather.12.cloned.1.call-start = ((), (), s32[]{:S(2)}) async-start(), calls=%async_computation.16 | async-start | bytes 2359296 | tf_op jit(solution)/shard_map/all_gather | solution.py:91
  530.4 228.8 %reduce-scatter.14.cloned.1.call-start = ((), (), s32[]{:S(2)}) async-start(), calls=%async_computation.15 | async-start | bytes 589824 | tf_op jit(solution)/shard_map/reduce_scatter | solution.py:17
  619.0 82.0 %copy-start = (bf16[1792,1024]{1,0:T(8,128)(2,1)S(1)}, bf16[1792,1024]{1,0:T(8,128)(2,1)}, u32[]{:S(2)}) copy-start(bf16[1792,1024]{1,0:T(8,128)(2,1)} %all-gather.8.cloned.1.call-done) | copy-start | bytes 11010052
  702.4 92.3 %all-gather.14.cloned.1.call-start = ((), (), s32[]{:S(2)}) async-start(), calls=%async_computation.17 | async-start | bytes 2359296 | tf_op jit(solution)/shard_map/all_gather | solution.py:92
  750.1 17.3 %all-to-all-start.2 = ((bf16[128,8,224]{0,2,1:T(8,128)(2,1)}), bf16[128,8,224]{0,2,1:T(8,128)(2,1)S(1)}, u32[]{:S(2)}, u32[]{:S(2)}) async-start(bf16[128,8,224]{0,2,1:T(8,128)(2,1)} %bitcast.11), calls=%async_computation.7 | async-start | bytes 917504 | tf_op jit(solution)/shard_map/all_to_all | solution.py:87
  754.3 3.3 copy-start.1
Sparse Core Ops, SparseCore 0:
  10.1 55.7 all-gather.5
  68.0 50.9 all-gather.7
  124.1 89.7 reduce-scatter.5
  218.9 87.0 reduce-scatter.7
  307.9 54.2 all-gather.9
  366.0 36.5 reduce-scatter.9
  529.7 89.1 reduce-scatter.11
  621.8 40.5 all-gather.11
  702.5 46.8 reduce-scatter.13
  751.4 43.3 all-gather.13
where the time goes:
time: 806 us; the launch traced here: 805 us
  waiting for transfers between devices  439 us (54%)
  blocking collectives  311 us (39%)
  matrix products  28.2 us (3%)
  between operations  14.9 us (2%)
    psum x1, blocking collectives, body(): rewards = lax.psum(spread, ('gx', 'gy', 'gz'))  101 us
    reduce_scatter x1, waiting for transfers between devices, body(): lax.psum_scatter(up_part, 'gz', scatter_dimension=1, tiled=True)  92.1 us
    reduce_scatter x1, waiting for transfers between devices, body(): lax.psum_scatter(gate_part, 'gz', scatter_dimension=1, tiled=True)  90.2 us
    reduce_scatter x1, waiting for transfers between devices, body(): lax.psum_scatter(hidden_part, 'gz', scatter_dimension=1, tiled=True)  88.5 us
    all_gather x1, waiting for transfers between devices, body(): lax.all_gather(up_weight, 'gx', axis=0, tiled=True)  49 us
    all_gather x2, blocking collectives, feature_blocks(): return lax.all_gather(shard, 'gy', axis=1, tiled=True)  42.9 us
    all_gather x1, blocking collectives, body(): hidden_block = lax.all_gather(hidden, 'gz', axis=1, tiled=True)  41.7 us
    all_gather x1, blocking collectives, body(): lax.all_gather(gate_grad, 'gz', axis=1, tiled=True)  39.6 us
  transfers between devices with their start and end apart: 11, of which 9 were waited for; matrix products, arithmetic and copies ran while one was open for 3% of the time, Pallas kernels for 0%

commit v1 on v0

v1 whole, which is shorter than its diff:
```python
import jax
import jax.numpy as jnp
from jax import lax
from jax.sharding import Mesh, PartitionSpec as P

SEQ_LEN = 128
reward_weight = 64.0
EVERY = ("yl", "co", "gy", "yh", "xx")
PLANE = ("yl", "gy")
GZ = ("yh", "xx")
SWAP = [(0, 1), (1, 0)]
f32, bf16 = jnp.float32, jnp.bfloat16


def exchange(pieces, axes):
    return lax.all_to_all(pieces, axes, 0, 0)


def to_all(value, axes, count):
    return exchange(jnp.broadcast_to(value[None], (count,) + value.shape), axes)


def dot(left, right, left_dim, right_dim):
    return lax.dot_general(
        left, right, (((left_dim,), (right_dim,)), ((), ())), preferred_element_type=f32
    )


def body(tokens, gate_weight, up_weight, down_weight, reward_head, lm_grad, pair_index):
    n_yl, n_gy = lax.axis_size("yl"), lax.axis_size("gy")
    n_plane, n_gz = n_yl * n_gy, lax.axis_size(GZ)
    n_all = n_plane * n_gz * lax.axis_size("co")
    rows, cols = tokens.shape
    units, width = gate_weight.shape
    my_seq = lax.axis_index(("yl", "co"))
    core = lax.axis_index("co")

    def chip_block(weight):
        return jnp.concatenate([weight, lax.ppermute(weight, "co", SWAP)], axis=0)

    gate_w, up_w, down_w = chip_block(gate_weight), chip_block(up_weight), chip_block(down_weight)

    head_rows = jnp.pad(reward_head[None, :], ((0, 7), (0, 0)))
    block = jnp.concatenate([tokens, lm_grad.astype(bf16), head_rows], axis=0)
    got = to_all(block, PLANE, n_plane).reshape(n_yl, n_gy, 2 * rows + 8, cols)

    def spread(part):
        return part.transpose(0, 2, 1, 3).reshape(n_yl * rows, width)

    tok_half = spread(got[:, :, :rows])
    low_half = spread(got[:, :, rows : 2 * rows])
    head_vec = got[0, :, 2 * rows].reshape(1, width)
    half = n_yl * rows

    low_head = jnp.concatenate([low_half, jnp.pad(head_vec, ((0, 127), (0, 0)))], axis=0)
    gate_part = dot(gate_w, tok_half, 1, 1).astype(bf16)
    up_part = dot(up_w, tok_half, 1, 1).astype(bf16)
    back_part = dot(down_w, low_head, 1, 1)
    v_part = back_part[:, half : half + 1]
    v_hi = v_part.astype(bf16)
    v_mid = (v_part - v_hi.astype(f32)).astype(bf16)
    v_cols = jnp.pad(jnp.concatenate([v_hi, v_mid], axis=1), ((0, 0), (0, 126)))
    parts = jnp.concatenate([gate_part, up_part, back_part[:, :half].astype(bf16), v_cols], axis=1)
    own = 2 * units // n_gz
    sums = jnp.sum(exchange(parts.reshape(n_gz, own, 3 * half + 128), GZ).astype(f32), axis=0)
    gate_sum, up_sum, hidden_grad = (sums[:, i * half : (i + 1) * half] for i in range(3))
    head_down = sums[:, 3 * half : 3 * half + 1] + sums[:, 3 * half + 1 : 3 * half + 2]

    gate_sigmoid = jax.nn.sigmoid(gate_sum)
    silu_gate = gate_sum * gate_sigmoid
    hidden = (silu_gate * up_sum).astype(bf16)

    last_hidden = hidden.reshape(own, n_yl, rows)[:, :, rows - 1].astype(f32)
    seq_terms = jnp.sum(last_hidden * head_down, axis=0)
    own_term = jnp.sum(tokens[rows - 1].astype(f32) * reward_head.astype(f32))
    sequence = jnp.arange(2 * n_yl, dtype=jnp.int32)
    terms = jnp.where(sequence % 2 == core, jnp.repeat(seq_terms, 2), 0.0)
    terms = terms + jnp.where(sequence == my_seq, own_term, 0.0)
    term_row = jnp.pad(terms, (0, 128 - terms.shape[0]))[None, :]
    rewards = jnp.sum(to_all(term_row, EVERY, n_all), axis=(0, 1))[: 2 * n_yl]

    chosen_hot = (pair_index[:, 0:1] == sequence[None, :]).astype(f32)
    rejected_hot = (pair_index[:, 1:2] == sequence[None, :]).astype(f32)
    margin = jnp.sum((chosen_hot - rejected_hot) * rewards[None, :], axis=1)
    pair_weight = jax.nn.sigmoid(-margin)
    pair_coefs = jnp.sum((rejected_hot - chosen_hot) * pair_weight[:, None], axis=0)
    scaled = reward_weight * pair_coefs
    core_coefs = jnp.sum(
        jnp.where(sequence[:, None] == 2 * jnp.arange(n_yl)[None, :] + core, scaled[:, None], 0.0), axis=0
    )
    sib_coefs = jnp.sum(
        jnp.where(sequence[:, None] == 2 * jnp.arange(n_yl)[None, :] + 1 - core, scaled[:, None], 0.0), axis=0
    )
    my_coef = jnp.sum(jnp.where(sequence == my_seq, scaled, 0.0))

    def last_only(coefs):
        spot = jnp.arange(half)
        return jnp.where(spot % rows == rows - 1, jnp.repeat(coefs, rows), 0.0)

    hidden_grad = hidden_grad + head_down * last_only(core_coefs)[None, :]
    up_grad = (hidden_grad * silu_gate).astype(bf16)
    gate_grad = (
        hidden_grad * up_sum * gate_sigmoid * (1.0 + gate_sum * (1.0 - gate_sigmoid))
    ).astype(bf16)

    mine = jnp.concatenate([gate_grad, up_grad, hidden], axis=0)
    everyone = to_all(mine, GZ, n_gz)
    gate_g, up_g, hid = (
        everyone[:, i * own : (i + 1) * own].reshape(2 * units, half) for i in range(3)
    )

    token_part = dot(gate_g, gate_w, 0, 0) + dot(up_g, up_w, 0, 0)
    token_part = token_part.astype(bf16).reshape(n_yl, rows, n_gy, cols).transpose(0, 2, 1, 3)
    token_sum = jnp.sum(
        exchange(token_part.reshape(n_plane, rows, cols), PLANE).astype(f32), axis=0
    )
    head_own = reward_head.astype(f32)[None, :]
    row = jnp.arange(rows)[:, None]
    grad_out = lm_grad + jnp.where(row == rows - 1, my_coef * head_own, 0.0)
    grad_tokens = grad_out + token_sum

    loss_scale = 1.0 / jnp.sqrt(f32(rows * 2 * n_yl))
    head_full = head_vec.astype(f32)

    def cotangent(low, coefs):
        return (low.astype(f32) + last_only(coefs)[:, None] * head_full).astype(bf16)

    tok_sib = lax.ppermute(tok_half, "co", SWAP)
    low_sib = lax.ppermute(low_half, "co", SWAP)

    def weight_grad(full, own_right, sib_right):
        from_sib = lax.ppermute(full[units:], "co", SWAP)
        return (dot(full[:units], own_right, 1, 0) + dot(from_sib, sib_right, 1, 0)) * loss_scale

    grad_gate = weight_grad(gate_g, tok_half, tok_sib)
    grad_up = weight_grad(up_g, tok_half, tok_sib)
    grad_down = weight_grad(hid, cotangent(low_half, core_coefs), cotangent(low_sib, sib_coefs))
    return grad_tokens, grad_gate, grad_up, grad_down, rewards


def solution(mesh):
    fine = Mesh(mesh.devices.reshape(4, 2, 8, 2, 4), EVERY)
    gx, gz = ("yl", "co"), GZ
    weight = P(("gy",) + gx, gz)
    act = P(gx, gz + ("gy",))
    return jax.shard_map(
        body,
        mesh=fine,
        in_specs=(act, weight, weight, weight, P(gz + ("gy",)), act, P()),
        out_specs=(act, weight, weight, weight, P()),
        check_vma=False,
    )
```

time: 806 us -> 257 us (0.32)
  waiting for transfers between devices: 439 us -> 116 us
  blocking collectives: 311 us -> 0 us
  starting transfers between devices: 4.56 us -> 86.5 us
  local copies, waits for them, and re-layouts: 2.27 us -> 19.5 us
  between operations: 14.9 us -> 1.11 us
  matrix products: 28.2 us -> 16.8 us
  other arithmetic: 5.37 us -> 13.6 us
    reduce_scatter x5 -> x0, waiting for transfers between devices: 307 us -> none  [the longest x1 92.1 us: body(): lax.psum_scatter(up_part, 'gz', scatter_dimension=1, tiled=True)]
    all_gather x5 -> x0, blocking collectives: 163 us -> none  [the longest x2 42.9 us: feature_blocks(): return lax.all_gather(shard, 'gy', axis=1, tiled=True)]
    all_gather x5 -> x0, waiting for transfers between devices: 122 us -> none  [the longest x1 49 us: body(): lax.all_gather(up_weight, 'gx', axis=0, tiled=True)]
    all_to_all x1 -> x5, waiting for transfers between devices: 6.74 us -> 116 us  [exchange(): return lax.all_to_all(pieces, axes, 0, 0)]
    psum x1 -> x0, blocking collectives: 101 us -> none  [body(): rewards = lax.psum(spread, ('gx', 'gy', 'gz'))]
    all_to_all x1 -> x5, starting transfers between devices: 4.16 us -> 67.1 us  [exchange(): return lax.all_to_all(pieces, axes, 0, 0)]
    all_to_all x2 -> x0, blocking collectives: 47.1 us -> none  [the longest x1 30.6 us: body(): lax.all_to_all(up_grad_block, 'gx', split_axis=1, concat_axis=0, tiled=True)]
    ppermute x0 -> x8, starting transfers between devices: none -> 19.4 us  [the longest x3 7.74 us: weight_grad(): from_sib = lax.ppermute(full[units:], 'co', SWAP)]
  transfers between devices with their start and end apart: 11 -> 13, of which waited for: 9 -> 5; matrix products, arithmetic and copies ran while one was open for 3% -> 10% of each run, Pallas kernels for 0% -> 0%
where the time goes in v1:
time: 257 us; the launch traced here: 253 us
  waiting for transfers between devices  116 us (45%)
  starting transfers between devices  86.5 us (34%)
  local copies, waits for them, and re-layouts  19.5 us (8%)
  matrix products  16.8 us (7%)
  other arithmetic  13.6 us (5%)
    all_to_all x5, waiting for transfers between devices, exchange(): return lax.all_to_all(pieces, axes, 0, 0)  116 us
    all_to_all x5, starting transfers between devices, exchange(): return lax.all_to_all(pieces, axes, 0, 0)  67.1 us
    dot_general x11, matrix products, dot(): lax.dot_general(left, right, (((left_dim,), (right_dim,)), ((), ())), pre...  16.8 us
    ppermute x3, starting transfers between devices, weight_grad(): from_sib = lax.ppermute(full[units:], 'co', SWAP)  7.74 us
    ppermute x3, starting transfers between devices, chip_block(): return jnp.concatenate([weight, lax.ppermute(weight, 'co', SWAP)], axis=0)  7.2 us
    unnamed x30, local copies, waits for them, and re-layouts  6 us
  transfers between devices with their start and end apart: 13, of which 5 were waited for; matrix products, arithmetic and copies ran while one was open for 10% of the time, Pallas kernels for 0%

profile of v1, /device:TPU:1, one launch (start us, length us, event | category | flops | bytes accessed | tf_op | source)
XLA Modules:
  0.0 253.2 jit_solution(3648016153265025083)
XLA Ops:
  0.6 0.8 convert_element_type.102
  1.5 0.8 fusion.24
  2.3 1.6 broadcast_in_dim.102
  3.9 14.3 %all-to-all-start = ((bf16[32,264,128]{2,1,0:T(8,128)(2,1)}), bf16[32,264,128]{2,1,0:T(8,128)(2,1)S(1)}, u32[]{:S(2)}, u32[]{:S(2)}) async-start(bf16[32,264,128]{2,1,0:T(8,128)(2,1)} %broadcast_in_dim.102), calls=%async_computation | async-start | bytes 4325376 | tf_op jit(solution)/shard_map/all_to_all | solution.py:16
  18.2 2.9 %collective-permute-start.1 = (bf16[224,1024]{1,0:T(8,128)(2,1)}, bf16[224,1024]{1,0:T(8,128)(2,1)S(1)}, u32[]{:S(2)}, u32[]{:S(2)}) collective-permute-start(bf16[224,1024]{1,0:T(8,128)(2,1)} %param.9), channel_id=1, source_target_pairs={{0,64},{64,0},{1,65},{65,1},{2,66},{66,2},{3,67},{67,3},{4,68},{68... | collective-permute-start | bytes 1376264 | tf_op jit(solution)/shard_map/ppermute | solution.py:39
  21.1 1.9 collective-permute-start
  23.0 2.4 collective-permute-start.2
  25.4 1.1 constant_dynamic-update-slice_fusion.3
  26.5 1.1 constant_dynamic-update-slice_fusion.1
  27.6 0.9 copy-done.5
  28.5 45.6 %all-to-all-done = bf16[32,264,128]{2,1,0:T(8,128)(2,1)S(1)} async-done(((bf16[32,264,128]{2,1,0:T(8,128)(2,1)}), bf16[32,264,128]{2,1,0:T(8,128)(2,1)S(1)}, u32[]{:S(2)}, u32[]{:S(2)}) %all-to-all-start) | async-done | bytes 2162720 | tf_op jit(solution)/shard_map/all_to_all | solution.py:16
  74.1 1.1 slice_bitcast_fusion.1
  75.3 0.7 copy.44
  75.9 0.3 copy.67
  76.3 2.5 fusion.8
  78.7 0.8 slice.170
  79.7 0.2 copy.47
  79.9 1.9 copy.43
  81.8 1.9 convolution_convert_fusion
  83.8 0.7 convolution_convert_fusion.1
  84.5 0.3 copy-done.6
  84.8 1.2 fusion.2
  86.0 13.0 %all-to-all-start.1 = ((bf16[8,56,1664]{2,1,0:T(8,128)(2,1)}), bf16[8,56,1664]{2,1,0:T(8,128)(2,1)}, u32[]{:S(2)}, u32[]{:S(2)}) async-start(bf16[8,56,1664]{2,1,0:T(8,128)(2,1)} %bitcast.85), calls=%async_computation.1 | async-start | bytes 2981888 | tf_op jit(solution)/shard_map/all_to_all | solution.py:16
  99.1 1.3 fusion.42
  100.4 29.7 %all-to-all-done.1 = bf16[8,56,1664]{2,1,0:T(8,128)(2,1)} async-done(((bf16[8,56,1664]{2,1,0:T(8,128)(2,1)}), bf16[8,56,1664]{2,1,0:T(8,128)(2,1)}, u32[]{:S(2)}, u32[]{:S(2)}) %all-to-all-start.1) | async-done | bytes 1490976 | tf_op jit(solution)/shard_map/all_to_all | solution.py:16
  130.0 1.6 convert_reduce_fusion
  131.7 0.7 copy-done.1
  132.4 0.2 fusion.25
  133.1 0.7 fusion.40
  133.8 0.8 broadcast_in_dim.106
  134.6 21.9 %all-to-all-start.2 = ((f32[512,1,128]{2,1,0:T(1,128)}), f32[512,1,128]{2,1,0:T(1,128)S(1)}, u32[]{:S(2)}, u32[]{:S(2)}) async-start(f32[512,1,128]{2,1,0:T(1,128)} %broadcast_in_dim.106), calls=%async_computation.2 | async-start | bytes 524288 | tf_op jit(solution)/shard_map/all_to_all | solution.py:16
  156.5 0.5 add_subtract_fusion
  157.1 16.4 %all-to-all-done.2 = f32[512,1,128]{2,1,0:T(1,128)S(1)} async-done(((f32[512,1,128]{2,1,0:T(1,128)}), f32[512,1,128]{2,1,0:T(1,128)S(1)}, u32[]{:S(2)}, u32[]{:S(2)}) %all-to-all-start.2) | async-done | bytes 262176 | tf_op jit(solution)/shard_map/all_to_all | solution.py:16
  173.6 0.2 fusion.29
  173.9 0.7 fusion.41
  174.6 0.9 select_reduce_fusion
  175.5 1.1 multiply_convert_fusion.1
  176.6 1.2 broadcast_in_dim.113
  177.8 4.3 %all-to-all-start.3 = ((bf16[8,168,512]{2,1,0:T(8,128)(2,1)}), bf16[8,168,512]{2,1,0:T(8,128)(2,1)}, u32[]{:S(2)}, u32[]{:S(2)}) async-start(bf16[8,168,512]{2,1,0:T(8,128)(2,1)} %broadcast_in_dim.113), calls=%async_computation.3 | async-start | bytes 2752512 | tf_op jit(solution)/shard_map/all_to_all | solution.py:16
  182.1 2.6 %collective-permute-start.7 = (bf16[512,1024]{1,0:T(8,128)(2,1)}, bf16[512,1024]{1,0:T(8,128)(2,1)}, u32[]{:S(2)}, u32[]{:S(2)}) collective-permute-start(bf16[512,1024]{1,0:T(8,128)(2,1)} %bitcast.93), channel_id=1, source_target_pairs={{0,64},{64,0},{1,65},{65,1},{2,66},{66,2},{3,67},{67,3},{4,68},{68... | collective-permute-start | bytes 3145736 | tf_op jit(solution)/shard_map/ppermute | solution.py:129
  184.7 1.3 copy.68
  186.0 1.9 collective-permute-start.4
  188.1 1.4 add_convert_fusion.1
  189.5 18.5 %all-to-all-done.3 = bf16[8,168,512]{2,1,0:T(8,128)(2,1)} async-done(((bf16[8,168,512]{2,1,0:T(8,128)(2,1)}), bf16[8,168,512]{2,1,0:T(8,128)(2,1)}, u32[]{:S(2)}, u32[]{:S(2)}) %all-to-all-start.3) | async-done | bytes 1376288 | tf_op jit(solution)/shard_map/all_to_all | solution.py:16
  207.9 1.2 fusion.50
  209.2 2.0 fusion.52
  211.2 0.7 fusion.3
  211.9 0.3 copy.55
  212.2 1.2 copy.50
  213.4 13.6 %all-to-all-start.4 = ((bf16[32,128,128]{2,1,0:T(8,128)(2,1)}), bf16[32,128,128]{2,1,0:T(8,128)(2,1)S(1)}, u32[]{:S(2)}, u32[]{:S(2)}) async-start(bf16[32,128,128]{2,1,0:T(8,128)(2,1)} %bitcast.86), calls=%async_computation.4 | async-start | bytes 2097152 | tf_op jit(solution)/shard_map/all_to_all | solution.py:16
  227.0 0.7 convert_multiply_fusion.2
  227.7 0.7 copy.51
  228.3 1.6 fusion.49
  229.9 3.4 %collective-permute-start.6 = (bf16[224,512]{1,0:T(8,128)(2,1)S(1)}, bf16[224,512]{1,0:T(8,128)(2,1)S(1)}, u32[]{:S(2)}, u32[]{:S(2)}) collective-permute-start(bf16[224,512]{1,0:T(8,128)(2,1)S(1)} %bitcast.98), channel_id=1, source_target_pairs={{0,64},{64,0},{1,65},{65,1},{2,66},{66,2},{3,67},{67,3},{4,68},{68... | collective-permute-start | bytes 688136 | tf_op jit(solution)/shard_map/ppermute | solution.py:132
  233.3 1.9 collective-permute-start.5
  235.3 2.4 collective-permute-start.3
  237.7 0.4 fusion.47
  238.1 0.4 fusion.48
  238.5 0.4 fusion.13
  238.9 2.6 %fusion.5 = f32[224,1024]{1,0:T(8,128)} fusion(f32[224,1024]{1,0:T(8,128)S(1)} %fusion.47, bf16[224,512]{1,0:T(8,128)(2,1)S(1)} %collective-permute-done.5, bf16[512,1024]{1,0:T(8,128)(2,1)} %collective-permute-done.4), kind=kOutput, calls=%fused_computation.14 | convolution fusion | flops 235339776 | bytes 3112960 | tf_op jit(solution)/shard_map/dot_general | solution.py:24
  241.5 2.6 %fusion.6 = f32[224,1024]{1,0:T(8,128)} fusion(f32[224,1024]{1,0:T(8,128)S(1)} %fusion.48, bf16[224,512]{1,0:T(8,128)(2,1)S(1)} %collective-permute-done.3, bf16[512,1024]{1,0:T(8,128)(2,1)} %collective-permute-done.4), kind=kOutput, calls=%fused_computation.16 | convolution fusion | flops 235339776 | bytes 3112960 | tf_op jit(solution)/shard_map/dot_general | solution.py:24
  244.1 2.7 %fusion.4 = f32[224,1024]{1,0:T(8,128)} fusion(f32[224,1024]{1,0:T(8,128)S(1)} %fusion.13, bf16[224,512]{1,0:T(8,128)(2,1)S(1)} %collective-permute-done.6, bf16[512,1024]{1,0:T(8,128)(2,1)} %collective-permute-done.7, f32[1024]{0:T(1024)S(1)} %bitcast.102, f32[512]{0:T(512)S(1)} %bitcast_select_fusion), kind=kOutput, calls=%fused_computation.12 | convolution fusion | flops 237436928 | bytes 3119104 | tf_op jit(solution)/shard_map/dot_general | solution.py:24
  246.8 5.6 %all-to-all-done.4 = bf16[32,128,128]{2,1,0:T(8,128)(2,1)S(1)} async-done(((bf16[32,128,128]{2,1,0:T(8,128)(2,1)}), bf16[32,128,128]{2,1,0:T(8,128)(2,1)S(1)}, u32[]{:S(2)}, u32[]{:S(2)}) %all-to-all-start.4) | async-done | bytes 1048608 | tf_op jit(solution)/shard_map/all_to_all | solution.py:16
  252.5 0.7 add_add_fusion
  (54 shorter events, 1.4 us)
Async XLA Ops:
  3.9 70.2 %all-to-all-start = ((bf16[32,264,128]{2,1,0:T(8,128)(2,1)}), bf16[32,264,128]{2,1,0:T(8,128)(2,1)S(1)}, u32[]{:S(2)}, u32[]{:S(2)}) async-start(bf16[32,264,128]{2,1,0:T(8,128)(2,1)} %broadcast_in_dim.102), calls=%async_computation | async-start | bytes 4325376 | tf_op jit(solution)/shard_map/all_to_all | solution.py:16
  18.2 9.3 %collective-permute-start.1 = (bf16[224,1024]{1,0:T(8,128)(2,1)}, bf16[224,1024]{1,0:T(8,128)(2,1)S(1)}, u32[]{:S(2)}, u32[]{:S(2)}) collective-permute-start(bf16[224,1024]{1,0:T(8,128)(2,1)} %param.9), channel_id=1, source_target_pairs={{0,64},{64,0},{1,65},{65,1},{2,66},{66,2},{3,67},{67,3},{4,68},{68... | collective-permute-start | bytes 1376264 | tf_op jit(solution)/shard_map/ppermute | solution.py:39
  21.1 6.5 %collective-permute-start = (bf16[224,1024]{1,0:T(8,128)(2,1)}, bf16[224,1024]{1,0:T(8,128)(2,1)S(1)}, u32[]{:S(2)}, u32[]{:S(2)}) collective-permute-start(bf16[224,1024]{1,0:T(8,128)(2,1)} %param.8), channel_id=1, source_target_pairs={{0,64},{64,0},{1,65},{65,1},{2,66},{66,2},{3,67},{67,3},{4,68},{68... | collective-permute-start | bytes 1376264 | tf_op jit(solution)/shard_map/ppermute | solution.py:39
  23.0 53.3 %collective-permute-start.2 = (bf16[224,1024]{1,0:T(8,128)(2,1)}, bf16[224,1024]{1,0:T(8,128)(2,1)}, u32[]{:S(2)}, u32[]{:S(2)}) collective-permute-start(bf16[224,1024]{1,0:T(8,128)(2,1)} %param.10), channel_id=1, source_target_pairs={{0,64},{64,0},{1,65},{65,1},{2,66},{66,2},{3,67},{67,3},{4,68},{68... | collective-permute-start | bytes 1376264 | tf_op jit(solution)/shard_map/ppermute | solution.py:39
  27.6 0.9 copy-start.5
  28.5 46.7 %copy-start.2 = (bf16[448,1024]{1,0:T(8,128)(2,1)}, bf16[448,1024]{1,0:T(8,128)(2,1)S(1)}, u32[]{:S(2)}) copy-start(bf16[448,1024]{1,0:T(8,128)(2,1)S(1)} %constant_dynamic-update-slice_fusion) | copy-start | bytes 2752516
  76.2 2.5 copy-start.7
  81.8 2.0 copy-start.3
  83.8 1.0 copy-start.6
  86.0 13.0 %copy-start.11 = (bf16[128]{0:T(256)(128)(2,1)S(1)}, bf16[128]{0:T(256)(128)(2,1)}, u32[]{:S(2)}) copy-start(bf16[128]{0:T(256)(128)(2,1)} %param.11) | copy-start | bytes 772
  86.0 44.0 %all-to-all-start.1 = ((bf16[8,56,1664]{2,1,0:T(8,128)(2,1)}), bf16[8,56,1664]{2,1,0:T(8,128)(2,1)}, u32[]{:S(2)}, u32[]{:S(2)}) async-start(bf16[8,56,1664]{2,1,0:T(8,128)(2,1)} %bitcast.85), calls=%async_computation.1 | async-start | bytes 2981888 | tf_op jit(solution)/shard_map/all_to_all | solution.py:16
  99.1 58.0 %copy-start.10 = (s32[4,2]{0,1:T(2,128)S(1)}, s32[4,2]{0,1:T(2,128)}, u32[]{:S(2)}) copy-start(s32[4,2]{0,1:T(2,128)} %param.13) | copy-start | bytes 100
  131.7 0.7 copy-start.1
  134.6 38.9 %all-to-all-start.2 = ((f32[512,1,128]{2,1,0:T(1,128)}), f32[512,1,128]{2,1,0:T(1,128)S(1)}, u32[]{:S(2)}, u32[]{:S(2)}) async-start(f32[512,1,128]{2,1,0:T(1,128)} %broadcast_in_dim.106), calls=%async_computation.2 | async-start | bytes 524288 | tf_op jit(solution)/shard_map/all_to_all | solution.py:16
  173.6 4.2 %copy-start.9 = (f32[128]{0:T(128)}, f32[128]{0:T(128)S(1)}, u32[]{:S(2)}) copy-start(f32[128]{0:T(128)S(1)} %reduce_sum.93) | copy-start | bytes 1540
  177.8 30.1 %all-to-all-start.3 = ((bf16[8,168,512]{2,1,0:T(8,128)(2,1)}), bf16[8,168,512]{2,1,0:T(8,128)(2,1)}, u32[]{:S(2)}, u32[]{:S(2)}) async-start(bf16[8,168,512]{2,1,0:T(8,128)(2,1)} %broadcast_in_dim.113), calls=%async_computation.3 | async-start | bytes 2752512 | tf_op jit(solution)/shard_map/all_to_all | solution.py:16
  182.1 62.0 %collective-permute-start.7 = (bf16[512,1024]{1,0:T(8,128)(2,1)}, bf16[512,1024]{1,0:T(8,128)(2,1)}, u32[]{:S(2)}, u32[]{:S(2)}) collective-permute-start(bf16[512,1024]{1,0:T(8,128)(2,1)} %bitcast.93), channel_id=1, source_target_pairs={{0,64},{64,0},{1,65},{65,1},{2,66},{66,2},{3,67},{67,3},{4,68},{68... | collective-permute-start | bytes 3145736 | tf_op jit(solution)/shard_map/ppermute | solution.py:129
  186.0 52.9 %collective-permute-start.4 = (bf16[512,1024]{1,0:T(8,128)(2,1)}, bf16[512,1024]{1,0:T(8,128)(2,1)}, u32[]{:S(2)}, u32[]{:S(2)}) collective-permute-start(bf16[512,1024]{1,0:T(8,128)(2,1)} %bitcast.75), channel_id=1, source_target_pairs={{0,64},{64,0},{1,65},{65,1},{2,66},{66,2},{3,67},{67,3},{4,68},{68... | collective-permute-start | bytes 3145736 | tf_op jit(solution)/shard_map/ppermute | solution.py:128
  209.2 2.0 copy-start.4
  212.2 15.5 %copy-start = (bf16[4,128,8,128]{3,1,2,0:T(8,128)(2,1)S(1)}, bf16[4,128,8,128]{3,1,2,0:T(8,128)(2,1)}, u32[]{:S(2)}) copy-start(bf16[4,128,8,128]{3,1,2,0:T(8,128)(2,1)} %add_convert_fusion.1) | copy-start | bytes 3145732
  213.4 38.9 %all-to-all-start.4 = ((bf16[32,128,128]{2,1,0:T(8,128)(2,1)}), bf16[32,128,128]{2,1,0:T(8,128)(2,1)S(1)}, u32[]{:S(2)}, u32[]{:S(2)}) async-start(bf16[32,128,128]{2,1,0:T(8,128)(2,1)} %bitcast.86), calls=%async_computation.4 | async-start | bytes 2097152 | tf_op jit(solution)/shard_map/all_to_all | solution.py:16
  229.9 14.1 %collective-permute-start.6 = (bf16[224,512]{1,0:T(8,128)(2,1)S(1)}, bf16[224,512]{1,0:T(8,128)(2,1)S(1)}, u32[]{:S(2)}, u32[]{:S(2)}) collective-permute-start(bf16[224,512]{1,0:T(8,128)(2,1)S(1)} %bitcast.98), channel_id=1, source_target_pairs={{0,64},{64,0},{1,65},{65,1},{2,66},{66,2},{3,67},{67,3},{4,68},{68... | collective-permute-start | bytes 688136 | tf_op jit(solution)/shard_map/ppermute | solution.py:132
  233.3 5.6 %collective-permute-start.5 = (bf16[224,512]{1,0:T(8,128)(2,1)S(1)}, bf16[224,512]{1,0:T(8,128)(2,1)S(1)}, u32[]{:S(2)}, u32[]{:S(2)}) collective-permute-start(bf16[224,512]{1,0:T(8,128)(2,1)S(1)} %bitcast.100), channel_id=1, source_target_pairs={{0,64},{64,0},{1,65},{65,1},{2,66},{66,2},{3,67},{67,3},{4,68},{68... | collective-permute-start | bytes 688136 | tf_op jit(solution)/shard_map/ppermute | solution.py:132
  235.3 6.2 %collective-permute-start.3 = (bf16[224,512]{1,0:T(8,128)(2,1)S(1)}, bf16[224,512]{1,0:T(8,128)(2,1)S(1)}, u32[]{:S(2)}, u32[]{:S(2)}) collective-permute-start(bf16[224,512]{1,0:T(8,128)(2,1)S(1)} %bitcast.99), channel_id=1, source_target_pairs={{0,64},{64,0},{1,65},{65,1},{2,66},{66,2},{3,67},{67,3},{4,68},{68... | collective-permute-start | bytes 688136 | tf_op jit(solution)/shard_map/ppermute | solution.py:132
  244.1 8.4 %copy-start.8 = (f32[128,128]{1,0:T(8,128)S(1)}, f32[128,128]{1,0:T(8,128)}, u32[]{:S(2)}) copy-start(f32[128,128]{1,0:T(8,128)} %param.12) | copy-start | bytes 196612

commit v2 on v1

v2 whole, which is shorter than its diff:
```python
import jax
import jax.numpy as jnp
from jax import lax
from jax.sharding import Mesh, PartitionSpec as P

SEQ_LEN = 128
reward_weight = 64.0
FINE = ("yl", "co", "gy", "yh", "xx")
PLANE = ("yl", "gy")
GZ = ("yh", "xx")
SWAP = [(0, 1), (1, 0)]
f32, bf16 = jnp.float32, jnp.bfloat16


def exchange(pieces, axes):
    return lax.all_to_all(pieces, axes, 0, 0)


def to_all(value, axes, count):
    return exchange(jnp.broadcast_to(value[None], (count,) + value.shape), axes)


def dot(left, right, left_dim, right_dim):
    return lax.dot_general(
        left, right, (((left_dim,), (right_dim,)), ((), ())), preferred_element_type=f32
    )


def pieces(value):
    high = lax.reduce_precision(value, 8, 7)
    middle = lax.reduce_precision(value - high, 8, 7)
    return jnp.stack([high, middle, value - high - middle]).astype(bf16)


def body(tokens, gate_weight, up_weight, down_weight, reward_head, lm_grad, pair_index):
    n_yl, n_gy = lax.axis_size("yl"), lax.axis_size("gy")
    n_plane, n_gz = n_yl * n_gy, lax.axis_size(GZ)
    rows, cols = tokens.shape
    units, width = gate_weight.shape
    my_seq = lax.axis_index(("yl", "co"))
    core = lax.axis_index("co")

    def chip_block(weight):
        return jnp.concatenate([weight, lax.ppermute(weight, "co", SWAP)], axis=0)

    gate_w, up_w, down_w = chip_block(gate_weight), chip_block(up_weight), chip_block(down_weight)

    head_rows = jnp.broadcast_to(reward_head[None, :], (16, cols))
    block = jnp.concatenate([tokens, lm_grad.astype(bf16), head_rows], axis=0)
    block = to_all(block, "yl", n_yl)
    up, down = [block], [block]
    for step in range(n_gy // 2):
        up.append(lax.ppermute(up[-1], "gy", [(k, (k + 1) % n_gy) for k in range(n_gy)]))
        if step < n_gy // 2 - 1:
            down.append(lax.ppermute(down[-1], "gy", [(k, (k - 1) % n_gy) for k in range(n_gy)]))
    got = jnp.roll(jnp.stack(down + up[:0:-1]), lax.axis_index("gy"), axis=0)

    def spread(part):
        return part.transpose(1, 2, 0, 3).reshape(n_yl * rows, width)

    tok_half = spread(got[:, :, :rows])
    low_half = spread(got[:, :, rows : 2 * rows])
    head_vec = got[:, 0, 2 * rows].reshape(1, width)
    half = n_yl * rows

    low_head = jnp.concatenate([low_half, jnp.pad(head_vec, ((0, 127), (0, 0)))], axis=0)
    gate_part = dot(gate_w, tok_half, 1, 1).astype(bf16)
    up_part = dot(up_w, tok_half, 1, 1).astype(bf16)
    back_part = dot(down_w, low_head, 1, 1)
    v_part = back_part[:, half : half + 1]
    v_high = lax.reduce_precision(v_part, 8, 7)
    v_cols = jnp.concatenate([v_high, v_part - v_high], axis=1).astype(bf16)
    v_cols = jnp.pad(v_cols, ((0, 0), (0, 126)))
    parts = jnp.concatenate([gate_part, up_part, back_part[:, :half].astype(bf16), v_cols], axis=1)
    own = 2 * units // n_gz
    sums = jnp.sum(exchange(parts.reshape(n_gz, own, 3 * half + 128), GZ).astype(f32), axis=0)
    gate_sum, up_sum, hidden_grad = (sums[:, i * half : (i + 1) * half] for i in range(3))
    head_down = sums[:, 3 * half : 3 * half + 1] + sums[:, 3 * half + 1 : 3 * half + 2]

    gate_sigmoid = jax.nn.sigmoid(gate_sum)
    silu_gate = gate_sum * gate_sigmoid
    hidden = (silu_gate * up_sum).astype(bf16)

    gate_slope = up_sum * gate_sigmoid * (1.0 + gate_sum * (1.0 - gate_sigmoid))
    up_grad = (hidden_grad * silu_gate).astype(bf16)
    gate_grad = (hidden_grad * gate_slope).astype(bf16)

    def last_cols(value):
        return value.reshape(own, n_yl, rows)[:, :, rows - 1].astype(f32)

    gate_unit = (head_down * last_cols(gate_slope)).astype(bf16).T
    up_unit = (head_down * last_cols(silu_gate)).astype(bf16).T
    own_term = jnp.sum(tokens[rows - 1].astype(f32) * reward_head.astype(f32))
    terms = jnp.sum(last_cols(hidden) * head_down, axis=0)
    terms = terms + jnp.where(jnp.arange(n_yl) == lax.axis_index("yl"), own_term, 0.0)
    unit_rows = jnp.concatenate(
        [jnp.pad(gate_unit, ((0, 0), (0, 128 - own))), jnp.pad(up_unit, ((0, 0), (0, half - 128 - own)))], axis=1
    )
    term_rows = jnp.pad(pieces(terms).reshape(1, -1), ((0, 7 - n_yl), (0, half - 3 * n_yl)))
    mine = jnp.concatenate([gate_grad, up_grad, hidden, unit_rows, term_rows], axis=0)
    everyone = to_all(mine, GZ, n_gz)
    gate_g, up_g, hid = (
        everyone[:, i * own : (i + 1) * own].reshape(2 * units, half) for i in range(3)
    )
    units_at = everyone[:, 3 * own : 3 * own + n_yl].transpose(1, 0, 2)
    gate_u, up_u = (
        units_at[:, :, i * 128 : i * 128 + own].reshape(n_yl, 2 * units) for i in range(2)
    )
    core_terms = jnp.sum(
        everyone[:, 3 * own + n_yl, : 3 * n_yl].astype(f32).reshape(n_gz * 3, n_yl), axis=0
    )
    pair_terms = jnp.stack([core_terms, lax.ppermute(core_terms, "co", SWAP)])

    token_part = dot(gate_g, gate_w, 0, 0) + dot(up_g, up_w, 0, 0)
    token_part = token_part.astype(bf16).reshape(n_yl, rows, n_gy, cols).transpose(0, 2, 1, 3)
    unit_part = (dot(gate_u, gate_w, 1, 0) + dot(up_u, up_w, 1, 0)).astype(bf16)
    term_row = jnp.pad(pieces(pair_terms).reshape(1, 1, -1), ((0, 0), (0, 0), (0, cols - 6 * n_yl)))
    extra = jnp.concatenate(
        [unit_part.reshape(n_plane, 1, cols), jnp.broadcast_to(term_row, (n_plane, 1, cols))], axis=1
    )
    sent = jnp.concatenate(
        [token_part.reshape(n_plane, rows, cols), jnp.pad(extra, ((0, 0), (0, 6), (0, 0)))], axis=1
    )
    token_sum = jnp.sum(exchange(sent, PLANE).astype(f32), axis=0)

    both = jnp.sum(token_sum[rows + 1, : 6 * n_yl].reshape(3, 2, n_yl), axis=0)
    sequence = jnp.arange(2 * n_yl, dtype=jnp.int32)
    rewards = jnp.where(sequence % 2 == core, jnp.repeat(both[0], 2), jnp.repeat(both[1], 2))
    chosen_hot = (pair_index[:, 0:1] == sequence[None, :]).astype(f32)
    rejected_hot = (pair_index[:, 1:2] == sequence[None, :]).astype(f32)
    margin = jnp.sum((chosen_hot - rejected_hot) * rewards[None, :], axis=1)
    pair_weight = jax.nn.sigmoid(-margin)
    scaled = reward_weight * jnp.sum((rejected_hot - chosen_hot) * pair_weight[:, None], axis=0)
    by_core = scaled.reshape(n_yl, 2)
    core_coefs = jnp.where(core == 0, by_core[:, 0], by_core[:, 1])
    sib_coefs = jnp.where(core == 0, by_core[:, 1], by_core[:, 0])
    coefs = jnp.concatenate([core_coefs, sib_coefs])
    my_coef = jnp.sum(jnp.where(sequence == my_seq, scaled, 0.0))

    row = jnp.arange(rows)[:, None]
    head_term = my_coef * (reward_head.astype(f32) + token_sum[rows])
    grad_tokens = lm_grad + token_sum[:rows] + jnp.where(row == rows - 1, head_term[None, :], 0.0)

    loss_scale = 1.0 / jnp.sqrt(f32(rows * 2 * n_yl))
    tok_sib = lax.ppermute(tok_half, "co", SWAP)
    low_sib = lax.ppermute(low_half, "co", SWAP)
    unit_swap = lax.ppermute(jnp.concatenate([gate_u[:, units:], up_u[:, units:]], axis=0), "co", SWAP)
    gate_u8 = jnp.concatenate([gate_u[:, :units], unit_swap[:n_yl]], axis=0)
    up_u8 = jnp.concatenate([up_u[:, :units], unit_swap[n_yl:]], axis=0)

    def last_rows(value):
        return value.reshape(n_yl, rows, width)[:, rows - 1]

    last_tok = jnp.concatenate([last_rows(tok_half), last_rows(tok_sib)], axis=0).astype(f32)
    last_tok = (last_tok * coefs[:, None]).astype(bf16)
    head_term8 = (coefs[:, None] * head_vec.astype(f32)).astype(bf16)

    def weight_grad(full, own_right, sib_right, last_left, last_right):
        from_sib = lax.ppermute(full[units:], "co", SWAP)
        total = lax.optimization_barrier(
            (dot(full[:units], own_right, 1, 0) + dot(from_sib, sib_right, 1, 0)) * loss_scale
        )
        if last_left is None:
            ends = [v.reshape(units, n_yl, rows)[:, :, rows - 1] for v in (full[:units], from_sib)]
            last_left = jnp.concatenate(ends, axis=1).T
        return total + dot(last_left, last_right, 0, 0) * loss_scale

    grad_gate = weight_grad(gate_g, tok_half, tok_sib, gate_u8, last_tok)
    grad_up = weight_grad(up_g, tok_half, tok_sib, up_u8, last_tok)
    grad_down = weight_grad(hid, low_half, low_sib, None, head_term8)
    return grad_tokens, grad_gate, grad_up, grad_down, rewards


def solution(mesh):
    fine = Mesh(mesh.devices.reshape(4, 2, 8, 2, 4), FINE)
    gx, gz = ("yl", "co"), GZ
    weight = P(("gy",) + gx, gz)
    act = P(gx, gz + ("gy",))
    return jax.shard_map(
        body,
        mesh=fine,
        in_specs=(act, weight, weight, weight, P(gz + ("gy",)), act, P()),
        out_specs=(act, weight, weight, weight, P()),
        check_vma=False,
    )
```

time: 257 us -> 239 us (0.930)
  waiting for transfers between devices: 116 us -> 61.4 us
  blocking collectives: 0 us -> 11.8 us
  starting transfers between devices: 86.5 us -> 96.4 us
  matrix products: 16.8 us -> 23.9 us
  local copies, waits for them, and re-layouts: 19.5 us -> 24.7 us
  other arithmetic: 13.6 us -> 17.7 us
    all_to_all x5 -> x3, waiting for transfers between devices: 116 us -> 36.3 us  [exchange(): return lax.all_to_all(pieces, axes, 0, 0)]
    ppermute x0 -> x9, starting transfers between devices: none -> 52.7 us  [the longest x1 21.7 us: body(): pair_terms = jnp.stack([core_terms, lax.ppermute(core_terms, 'co', SWAP)])]
    all_to_all x5 -> x3, starting transfers between devices: 67.1 us -> 15.5 us  [exchange(): return lax.all_to_all(pieces, axes, 0, 0)]
    ppermute x0 -> x9, waiting for transfers between devices: none -> 25 us  [the longest x4 25 us: body(): lax.ppermute(up[-1], 'gy', [(k, (k + 1) % n_gy) for k in range(n_gy)])]
    all_to_all x0 -> x1, blocking collectives: none -> 11.8 us  [exchange(): return lax.all_to_all(pieces, axes, 0, 0)]
    ppermute x1, starting transfers between devices: 1.91 us -> 10.7 us  [body(): tok_sib = lax.ppermute(tok_half, 'co', SWAP)]
    dot_general x11 -> x16, matrix products: 16.8 us -> 23.9 us  [dot(): lax.dot_general(left, right, (((left_dim,), (right_dim,)), ((), ())), pre...]
    slice x1 -> x18, local copies, waits for them, and re-layouts: 0.1 us -> 5.35 us  [the longest x1 1.77 us: body(): tok_half = spread(got[:, :, :rows])]
  transfers between devices with their start and end apart: 13 -> 20, of which waited for: 5 -> 5; matrix products, arithmetic and copies ran while one was open for 10% -> 16% of each run, Pallas kernels for 0% -> 0%
where the time goes in v2:
time: 239 us; the launch traced here: 238 us
  starting transfers between devices  96.4 us (40%)
  waiting for transfers between devices  61.4 us (26%)
  local copies, waits for them, and re-layouts  24.7 us (10%)
  matrix products  23.9 us (10%)
  other arithmetic  17.7 us (7%)
  blocking collectives  11.8 us (5%)
    all_to_all x3, waiting for transfers between devices, exchange(): return lax.all_to_all(pieces, axes, 0, 0)  36.3 us
    ppermute x4, waiting for transfers between devices, body(): lax.ppermute(up[-1], 'gy', [(k, (k + 1) % n_gy) for k in range(n_gy)])  25 us
    dot_general x16, matrix products, dot(): lax.dot_general(left, right, (((left_dim,), (right_dim,)), ((), ())), pre...  23.9 us
    ppermute x1, starting transfers between devices, body(): pair_terms = jnp.stack([core_terms, lax.ppermute(core_terms, 'co', SWAP)])  21.7 us
    ppermute x3, starting transfers between devices, body(): lax.ppermute(down[-1], 'gy', [(k, (k - 1) % n_gy) for k in range(n_gy)])  20.9 us
    all_to_all x3, starting transfers between devices, exchange(): return lax.all_to_all(pieces, axes, 0, 0)  15.5 us
    all_to_all x1, blocking collectives, exchange(): return lax.all_to_all(pieces, axes, 0, 0)  11.8 us
    ppermute x1, starting transfers between devices, body(): tok_sib = lax.ppermute(tok_half, 'co', SWAP)  10.7 us
  transfers between devices with their start and end apart: 20, of which 5 were waited for; matrix products, arithmetic and copies ran while one was open for 16% of the time, Pallas kernels for 0%

profile of v2, /device:TPU:1, one launch (start us, length us, event | category | flops | bytes accessed | tf_op | source)
XLA Modules:
  0.0 237.6 jit_solution(11586307114050026069)
XLA Ops:
  0.6 0.9 convert_element_type.123
  2.2 0.8 pad_maximum_fusion.1
  3.0 11.8 %all_to_all.20 = bf16[4,272,128]{2,1,0:T(8,128)(2,1)S(1)} all-to-all(bf16[4,272,128]{2,1,0:T(8,128)(2,1)S(1)} %broadcast_in_dim.72), channel_id=1, replica_groups=mesh['yl'=4,'co'=2,'gy'=8,'yh'=2,'xx'=4] {'yl'}, dimensions={0} | all-to-all | bytes 557056 | tf_op jit(solution)/shard_map/all_to_all | solution.py:16
  15.0 11.5 %collective-permute-start.1 = (bf16[4,272,128]{1,2,0:T(8,128)(2,1)S(1)}, bf16[4,272,128]{1,2,0:T(8,128)(2,1)S(1)}, u32[]{:S(2)}, u32[]{:S(2)}) collective-permute-start(bf16[4,272,128]{1,2,0:T(8,128)(2,1)S(1)} %copy.120), channel_id=1, source_target_pairs={{0,56},{8,0},{16,8},{24,16},{32,24},{40,32},{48,40},{56,48},{1,57}... | collective-permute-start | bytes 835592 | tf_op jit(solution)/shard_map/ppermute | solution.py:55
  26.5 1.9 collective-permute-start.4
  28.5 5.0 %collective-permute-start.9 = (bf16[224,1024]{1,0:T(8,128)(2,1)}, bf16[224,1024]{1,0:T(8,128)(2,1)}, u32[]{:S(2)}, u32[]{:S(2)}) collective-permute-start(bf16[224,1024]{1,0:T(8,128)(2,1)} %param.10), channel_id=1, source_target_pairs={{0,64},{64,0},{1,65},{65,1},{2,66},{66,2},{3,67},{67,3},{4,68},{68... | collective-permute-start | bytes 1376264 | tf_op jit(solution)/shard_map/ppermute | solution.py:44
  33.4 1.9 collective-permute-start.8
  35.4 2.4 %collective-permute-start = (bf16[224,1024]{1,0:T(8,128)(2,1)}, bf16[224,1024]{1,0:T(8,128)(2,1)}, u32[]{:S(2)}, u32[]{:S(2)}) collective-permute-start(bf16[224,1024]{1,0:T(8,128)(2,1)} %param.8), channel_id=1, source_target_pairs={{0,64},{64,0},{1,65},{65,1},{2,66},{66,2},{3,67},{67,3},{4,68},{68... | collective-permute-start | bytes 1376264 | tf_op jit(solution)/shard_map/ppermute | solution.py:44
  37.8 1.1 constant_dynamic-update-slice_fusion.3
  38.9 4.9 %collective-permute-start.2 = (bf16[4,272,128]{1,2,0:T(8,128)(2,1)S(1)}, bf16[4,272,128]{1,2,0:T(8,128)(2,1)S(1)}, u32[]{:S(2)}, u32[]{:S(2)}) collective-permute-start(bf16[4,272,128]{1,2,0:T(8,128)(2,1)S(1)} %collective-permute-done.1), channel_id=1, source_target_pairs={{0,56},{8,0},{16,8},{24,16},{32,24},{40,32},{48,40},{56,48},{1,57}... | collective-permute-start | bytes 835592 | tf_op jit(solution)/shard_map/ppermute | solution.py:55
  43.8 1.9 collective-permute-start.5
  45.8 1.1 constant_dynamic-update-slice_fusion.2
  46.8 10.5 %collective-permute-done.5 = bf16[4,272,128]{1,2,0:T(8,128)(2,1)S(1)} collective-permute-done((bf16[4,272,128]{1,2,0:T(8,128)(2,1)S(1)}, bf16[4,272,128]{1,2,0:T(8,128)(2,1)S(1)}, u32[]{:S(2)}, u32[]{:S(2)}) %collective-permute-start.5) | collective-permute-done | bytes 278560 | tf_op jit(solution)/shard_map/ppermute | solution.py:53
  57.3 1.9 collective-permute-start.6
  59.2 1.1 constant_dynamic-update-slice_fusion
  60.3 4.6 %collective-permute-start.3 = (bf16[4,272,128]{1,2,0:T(8,128)(2,1)S(1)}, bf16[4,272,128]{1,2,0:T(8,128)(2,1)S(1)}, u32[]{:S(2)}, u32[]{:S(2)}) collective-permute-start(bf16[4,272,128]{1,2,0:T(8,128)(2,1)S(1)} %collective-permute-done.2), channel_id=1, source_target_pairs={{0,56},{8,0},{16,8},{24,16},{32,24},{40,32},{48,40},{56,48},{1,57}... | collective-permute-start | bytes 835592 | tf_op jit(solution)/shard_map/ppermute | solution.py:55
  65.0 4.9 %collective-permute-done.6 = bf16[4,272,128]{1,2,0:T(8,128)(2,1)S(1)} collective-permute-done((bf16[4,272,128]{1,2,0:T(8,128)(2,1)S(1)}, bf16[4,272,128]{1,2,0:T(8,128)(2,1)S(1)}, u32[]{:S(2)}, u32[]{:S(2)}) %collective-permute-start.6) | collective-permute-done | bytes 278560 | tf_op jit(solution)/shard_map/ppermute | solution.py:53
  69.9 1.9 collective-permute-start.7
  72.0 9.6 %collective-permute-done.7 = bf16[4,272,128]{1,2,0:T(8,128)(2,1)S(1)} collective-permute-done((bf16[4,272,128]{1,2,0:T(8,128)(2,1)S(1)}, bf16[4,272,128]{1,2,0:T(8,128)(2,1)S(1)}, u32[]{:S(2)}, u32[]{:S(2)}) %collective-permute-start.7) | collective-permute-done | bytes 278560 | tf_op jit(solution)/shard_map/ppermute | solution.py:53
  82.6 1.8 constant_dynamic-slice_fusion
  84.4 1.1 copy-done.11
  85.4 1.7 copy.134
  87.5 2.3 fusion.11
  90.6 1.0 copy.147
  91.6 0.8 copy.152
  95.1 1.2 fusion.2
  96.3 7.2 %all-to-all-start.1 = ((bf16[8,56,1664]{2,1,0:T(8,128)(2,1)}), bf16[8,56,1664]{2,1,0:T(8,128)(2,1)}, u32[]{:S(2)}, u32[]{:S(2)}) async-start(bf16[8,56,1664]{2,1,0:T(8,128)(2,1)} %bitcast.160), calls=%async_computation.1 | async-start | bytes 2981888 | tf_op jit(solution)/shard_map/all_to_all | solution.py:16
  103.5 1.3 fusion.58
  104.8 27.0 %all-to-all-done.1 = bf16[8,56,1664]{2,1,0:T(8,128)(2,1)} async-done(((bf16[8,56,1664]{2,1,0:T(8,128)(2,1)}), bf16[8,56,1664]{2,1,0:T(8,128)(2,1)}, u32[]{:S(2)}, u32[]{:S(2)}) %all-to-all-start.1) | async-done | bytes 1490976 | tf_op jit(solution)/shard_map/all_to_all | solution.py:16
  131.8 1.6 convert_reduce_fusion
  135.5 1.2 broadcast_in_dim.75
  136.7 4.1 %all-to-all-start.2 = ((bf16[8,176,512]{2,1,0:T(8,128)(2,1)}), bf16[8,176,512]{2,1,0:T(8,128)(2,1)S(1)}, u32[]{:S(2)}, u32[]{:S(2)}) async-start(bf16[8,176,512]{2,1,0:T(8,128)(2,1)} %broadcast_in_dim.75), calls=%async_computation.2 | async-start | bytes 2883584 | tf_op jit(solution)/shard_map/all_to_all | solution.py:16
  140.8 1.3 copy.167
  142.1 10.7 %collective-permute-start.12 = (bf16[512,1024]{1,0:T(8,128)(2,1)}, bf16[512,1024]{1,0:T(8,128)(2,1)}, u32[]{:S(2)}, u32[]{:S(2)}) collective-permute-start(bf16[512,1024]{1,0:T(8,128)(2,1)} %bitcast.148), channel_id=1, source_target_pairs={{0,64},{64,0},{1,65},{65,1},{2,66},{66,2},{3,67},{67,3},{4,68},{68... | collective-permute-start | bytes 3145736 | tf_op jit(solution)/shard_map/ppermute | solution.py:145
  154.0 1.9 collective-permute-start.16
  155.9 1.7 convert_reduce_fusion.2
  157.6 0.7 slice_reduce_fusion
  158.4 0.9 slice.241
  159.5 1.4 fusion.76
  162.1 21.7 %collective-permute-start.10 = (f32[4]{0:T(128)}, f32[4]{0:T(128)}, u32[]{:S(2)}, u32[]{:S(2)}) collective-permute-start(f32[4]{0:T(128)} %reduce_sum.87), channel_id=1, source_target_pairs={{0,64},{64,0},{1,65},{65,1},{2,66},{66,2},{3,67},{67,3},{4,68},{68... | collective-permute-start | bytes 56 | tf_op jit(solution)/shard_map/ppermute | solution.py:112
  184.0 1.4 fusion.16
  187.2 0.7 fusion.3
  188.5 1.1 fusion.69
  190.4 0.8 fusion.24
  191.2 1.1 pad_maximum_fusion
  192.3 4.2 %all-to-all-start.3 = ((bf16[32,136,128]{2,1,0:T(8,128)(2,1)}), bf16[32,136,128]{2,1,0:T(8,128)(2,1)S(1)}, u32[]{:S(2)}, u32[]{:S(2)}) async-start(bf16[32,136,128]{2,1,0:T(8,128)(2,1)} %pad_maximum_fusion), calls=%async_computation.3 | async-start | bytes 2228224 | tf_op jit(solution)/shard_map/all_to_all | solution.py:16
  196.6 1.9 collective-permute-start.11
  198.5 2.4 %collective-permute-start.13 = (bf16[8,224]{1,0:T(8,128)(2,1)S(1)}, bf16[8,224]{1,0:T(8,128)(2,1)S(1)}, u32[]{:S(2)}, u32[]{:S(2)}) collective-permute-start(bf16[8,224]{1,0:T(8,128)(2,1)S(1)} %pad_maximum_fusion.2), channel_id=1, source_target_pairs={{0,64},{64,0},{1,65},{65,1},{2,66},{66,2},{3,67},{67,3},{4,68},{68... | collective-permute-start | bytes 10760 | tf_op jit(solution)/shard_map/ppermute | solution.py:147
  201.0 1.9 collective-permute-start.14
  202.9 2.3 fusion.67
  205.2 2.3 fusion.66
  207.4 1.3 fusion.65
  208.8 2.4 %collective-permute-start.15 = (bf16[224,512]{1,0:T(8,128)(2,1)}, bf16[224,512]{1,0:T(8,128)(2,1)S(1)}, u32[]{:S(2)}, u32[]{:S(2)}) collective-permute-start(bf16[224,512]{1,0:T(8,128)(2,1)} %bitcast.170), channel_id=1, source_target_pairs={{0,64},{64,0},{1,65},{65,1},{2,66},{66,2},{3,67},{67,3},{4,68},{68... | collective-permute-start | bytes 688136 | tf_op jit(solution)/shard_map/ppermute | solution.py:159
  211.7 1.8 fusion.9
  213.5 2.0 fusion.7
  215.5 2.6 %fusion.5 = f32[224,1024]{1,0:T(8,128)} fusion(f32[224,1024]{1,0:T(8,128)S(1)} %copy-done.8, bf16[224,512]{1,0:T(8,128)(2,1)S(1)} %collective-permute-done.15, bf16[512,1024]{1,0:T(8,128)(2,1)} %collective-permute-done.16), kind=kOutput, calls=%fused_computation.12 | convolution fusion | flops 235339776 | bytes 3112960 | tf_op jit(solution)/shard_map/dot_general | solution.py:24
  218.5 9.3 %all-to-all-done.3 = bf16[32,136,128]{2,1,0:T(8,128)(2,1)S(1)} async-done(((bf16[32,136,128]{2,1,0:T(8,128)(2,1)}), bf16[32,136,128]{2,1,0:T(8,128)(2,1)S(1)}, u32[]{:S(2)}, u32[]{:S(2)}) %all-to-all-start.3) | async-done | bytes 1114144 | tf_op jit(solution)/shard_map/all_to_all | solution.py:16
  228.5 0.9 fusion.46
  229.3 0.8 fusion.44
  230.7 1.3 fusion.57
  232.1 1.4 fusion.25
  233.8 1.3 fusion.8
  235.0 1.3 fusion.6
  236.3 1.3 fusion.4
  (160 shorter events, 16.0 us)
Async XLA Ops:
  0.6 38.2 %copy-start.13 = (bf16[224,1024]{1,0:T(8,128)(2,1)S(1)}, bf16[224,1024]{1,0:T(8,128)(2,1)}, u32[]{:S(2)}) copy-start(bf16[224,1024]{1,0:T(8,128)(2,1)} %param.8) | copy-start | bytes 1376260
  15.0 23.9 %collective-permute-start.1 = (bf16[4,272,128]{1,2,0:T(8,128)(2,1)S(1)}, bf16[4,272,128]{1,2,0:T(8,128)(2,1)S(1)}, u32[]{:S(2)}, u32[]{:S(2)}) collective-permute-start(bf16[4,272,128]{1,2,0:T(8,128)(2,1)S(1)} %copy.120), channel_id=1, source_target_pairs={{0,56},{8,0},{16,8},{24,16},{32,24},{40,32},{48,40},{56,48},{1,57}... | collective-permute-start | bytes 835592 | tf_op jit(solution)/shard_map/ppermute | solution.py:55
  26.5 17.2 %collective-permute-start.4 = (bf16[4,272,128]{1,2,0:T(8,128)(2,1)S(1)}, bf16[4,272,128]{1,2,0:T(8,128)(2,1)S(1)}, u32[]{:S(2)}, u32[]{:S(2)}) collective-permute-start(bf16[4,272,128]{1,2,0:T(8,128)(2,1)S(1)} %copy.120), channel_id=1, source_target_pairs={{0,8},{8,16},{16,24},{24,32},{32,40},{40,48},{48,56},{56,0},{1,9},... | collective-permute-start | bytes 835592 | tf_op jit(solution)/shard_map/ppermute | solution.py:53
  28.5 59.0 %collective-permute-start.9 = (bf16[224,1024]{1,0:T(8,128)(2,1)}, bf16[224,1024]{1,0:T(8,128)(2,1)}, u32[]{:S(2)}, u32[]{:S(2)}) collective-permute-start(bf16[224,1024]{1,0:T(8,128)(2,1)} %param.10), channel_id=1, source_target_pairs={{0,64},{64,0},{1,65},{65,1},{2,66},{66,2},{3,67},{67,3},{4,68},{68... | collective-permute-start | bytes 1376264 | tf_op jit(solution)/shard_map/ppermute | solution.py:44
  33.4 12.3 %collective-permute-start.8 = (bf16[224,1024]{1,0:T(8,128)(2,1)}, bf16[224,1024]{1,0:T(8,128)(2,1)}, u32[]{:S(2)}, u32[]{:S(2)}) collective-permute-start(bf16[224,1024]{1,0:T(8,128)(2,1)} %param.9), channel_id=1, source_target_pairs={{0,64},{64,0},{1,65},{65,1},{2,66},{66,2},{3,67},{67,3},{4,68},{68... | collective-permute-start | bytes 1376264 | tf_op jit(solution)/shard_map/ppermute | solution.py:44
  35.4 23.9 %collective-permute-start = (bf16[224,1024]{1,0:T(8,128)(2,1)}, bf16[224,1024]{1,0:T(8,128)(2,1)}, u32[]{:S(2)}, u32[]{:S(2)}) collective-permute-start(bf16[224,1024]{1,0:T(8,128)(2,1)} %param.8), channel_id=1, source_target_pairs={{0,64},{64,0},{1,65},{65,1},{2,66},{66,2},{3,67},{67,3},{4,68},{68... | collective-permute-start | bytes 1376264 | tf_op jit(solution)/shard_map/ppermute | solution.py:44
  38.9 21.4 %collective-permute-start.2 = (bf16[4,272,128]{1,2,0:T(8,128)(2,1)S(1)}, bf16[4,272,128]{1,2,0:T(8,128)(2,1)S(1)}, u32[]{:S(2)}, u32[]{:S(2)}) collective-permute-start(bf16[4,272,128]{1,2,0:T(8,128)(2,1)S(1)} %collective-permute-done.1), channel_id=1, source_target_pairs={{0,56},{8,0},{16,8},{24,16},{32,24},{40,32},{48,40},{56,48},{1,57}... | collective-permute-start | bytes 835592 | tf_op jit(solution)/shard_map/ppermute | solution.py:55
  43.8 13.5 %collective-permute-start.5 = (bf16[4,272,128]{1,2,0:T(8,128)(2,1)S(1)}, bf16[4,272,128]{1,2,0:T(8,128)(2,1)S(1)}, u32[]{:S(2)}, u32[]{:S(2)}) collective-permute-start(bf16[4,272,128]{1,2,0:T(8,128)(2,1)S(1)} %collective-permute-done.4), channel_id=1, source_target_pairs={{0,8},{8,16},{16,24},{24,32},{32,40},{40,48},{48,56},{56,0},{1,9},... | collective-permute-start | bytes 835592 | tf_op jit(solution)/shard_map/ppermute | solution.py:53
  46.8 46.4 %copy-start.2 = (bf16[448,1024]{1,0:T(8,128)(2,1)}, bf16[448,1024]{1,0:T(8,128)(2,1)S(1)}, u32[]{:S(2)}) copy-start(bf16[448,1024]{1,0:T(8,128)(2,1)S(1)} %constant_dynamic-update-slice_fusion.2) | copy-start | bytes 2752516
  57.3 12.6 %collective-permute-start.6 = (bf16[4,272,128]{1,2,0:T(8,128)(2,1)S(1)}, bf16[4,272,128]{1,2,0:T(8,128)(2,1)S(1)}, u32[]{:S(2)}, u32[]{:S(2)}) collective-permute-start(bf16[4,272,128]{1,2,0:T(8,128)(2,1)S(1)} %collective-permute-done.5), channel_id=1, source_target_pairs={{0,8},{8,16},{16,24},{24,32},{32,40},{40,48},{48,56},{56,0},{1,9},... | collective-permute-start | bytes 835592 | tf_op jit(solution)/shard_map/ppermute | solution.py:53
  60.3 21.6 %copy-start.4 = (bf16[448,1024]{1,0:T(8,128)(2,1)}, bf16[448,1024]{1,0:T(8,128)(2,1)S(1)}, u32[]{:S(2)}) copy-start(bf16[448,1024]{1,0:T(8,128)(2,1)S(1)} %constant_dynamic-update-slice_fusion) | copy-start | bytes 2752516
  60.3 11.6 %collective-permute-start.3 = (bf16[4,272,128]{1,2,0:T(8,128)(2,1)S(1)}, bf16[4,272,128]{1,2,0:T(8,128)(2,1)S(1)}, u32[]{:S(2)}, u32[]{:S(2)}) collective-permute-start(bf16[4,272,128]{1,2,0:T(8,128)(2,1)S(1)} %collective-permute-done.2), channel_id=1, source_target_pairs={{0,56},{8,0},{16,8},{24,16},{32,24},{40,32},{48,40},{56,48},{1,57}... | collective-permute-start | bytes 835592 | tf_op jit(solution)/shard_map/ppermute | solution.py:55
  69.9 11.7 %collective-permute-start.7 = (bf16[4,272,128]{1,2,0:T(8,128)(2,1)S(1)}, bf16[4,272,128]{1,2,0:T(8,128)(2,1)S(1)}, u32[]{:S(2)}, u32[]{:S(2)}) collective-permute-start(bf16[4,272,128]{1,2,0:T(8,128)(2,1)S(1)} %collective-permute-done.6), channel_id=1, source_target_pairs={{0,8},{8,16},{16,24},{24,32},{32,40},{40,48},{48,56},{56,0},{1,9},... | collective-permute-start | bytes 835592 | tf_op jit(solution)/shard_map/ppermute | solution.py:53
  82.4 3.0 %copy-start.11 = (bf16[16,4,272,128]{2,3,0,1:T(8,128)(2,1)}, bf16[16,4,272,128]{2,3,0,1:T(8,128)(2,1)S(1)}, u32[]{:S(2)}) copy-start(bf16[16,4,272,128]{2,3,0,1:T(8,128)(2,1)S(1)} %bitcast_dynamic-update-slice_fusion.11) | copy-start | bytes 13369348
  85.4 2.0 copy-start.24
  87.2 2.6 %copy-start = (bf16[4,128,8,128]{3,2,1,0:T(8,128)(2,1)}, bf16[4,128,8,128]{3,2,1,0:T(8,128)(2,1)S(1)}, u32[]{:S(2)}) copy-start(bf16[4,128,8,128]{3,2,1,0:T(8,128)(2,1)S(1)} %copy.134) | copy-start | bytes 3145732
  87.5 2.3 copy-start.12
  93.2 1.2 copy-start.5
  93.2 1.8 copy-start.14
  95.0 8.5 %copy-start.21 = (bf16[128]{0:T(256)(128)(2,1)S(1)}, bf16[128]{0:T(256)(128)(2,1)}, u32[]{:S(2)}) copy-start(bf16[128]{0:T(256)(128)(2,1)} %param.11) | copy-start | bytes 772
  96.3 35.5 %all-to-all-start.1 = ((bf16[8,56,1664]{2,1,0:T(8,128)(2,1)}), bf16[8,56,1664]{2,1,0:T(8,128)(2,1)}, u32[]{:S(2)}, u32[]{:S(2)}) async-start(bf16[8,56,1664]{2,1,0:T(8,128)(2,1)} %bitcast.160), calls=%async_computation.1 | async-start | bytes 2981888 | tf_op jit(solution)/shard_map/all_to_all | solution.py:16
  135.5 17.9 %copy-start.23 = (s32[4,2]{0,1:T(2,128)S(1)}, s32[4,2]{0,1:T(2,128)}, u32[]{:S(2)}) copy-start(s32[4,2]{0,1:T(2,128)} %param.13) | copy-start | bytes 100
  136.7 22.6 %all-to-all-start.2 = ((bf16[8,176,512]{2,1,0:T(8,128)(2,1)}), bf16[8,176,512]{2,1,0:T(8,128)(2,1)S(1)}, u32[]{:S(2)}, u32[]{:S(2)}) async-start(bf16[8,176,512]{2,1,0:T(8,128)(2,1)} %broadcast_in_dim.75), calls=%async_computation.2 | async-start | bytes 2883584 | tf_op jit(solution)/shard_map/all_to_all | solution.py:16
  142.1 16.3 %collective-permute-start.12 = (bf16[512,1024]{1,0:T(8,128)(2,1)}, bf16[512,1024]{1,0:T(8,128)(2,1)}, u32[]{:S(2)}, u32[]{:S(2)}) collective-permute-start(bf16[512,1024]{1,0:T(8,128)(2,1)} %bitcast.148), channel_id=1, source_target_pairs={{0,64},{64,0},{1,65},{65,1},{2,66},{66,2},{3,67},{67,3},{4,68},{68... | collective-permute-start | bytes 3145736 | tf_op jit(solution)/shard_map/ppermute | solution.py:145
  154.0 61.5 %collective-permute-start.16 = (bf16[512,1024]{1,0:T(8,128)(2,1)}, bf16[512,1024]{1,0:T(8,128)(2,1)}, u32[]{:S(2)}, u32[]{:S(2)}) collective-permute-start(bf16[512,1024]{1,0:T(8,128)(2,1)} %bitcast.167), channel_id=1, source_target_pairs={{0,64},{64,0},{1,65},{65,1},{2,66},{66,2},{3,67},{67,3},{4,68},{68... | collective-permute-start | bytes 3145736 | tf_op jit(solution)/shard_map/ppermute | solution.py:146
  158.3 27.8 %copy-start.3 = (bf16[448,1024]{1,0:T(8,128)(2,1)S(1)}, bf16[448,1024]{1,0:T(8,128)(2,1)}, u32[]{:S(2)}) copy-start(bf16[448,1024]{1,0:T(8,128)(2,1)} %copy-done.2) | copy-start | bytes 2752516
  162.1 27.4 %collective-permute-start.10 = (f32[4]{0:T(128)}, f32[4]{0:T(128)}, u32[]{:S(2)}, u32[]{:S(2)}) collective-permute-start(f32[4]{0:T(128)} %reduce_sum.87), channel_id=1, source_target_pairs={{0,64},{64,0},{1,65},{65,1},{2,66},{66,2},{3,67},{67,3},{4,68},{68... | collective-permute-start | bytes 56 | tf_op jit(solution)/shard_map/ppermute | solution.py:112
  184.0 2.9 %copy-start.16 = (bf16[4,448]{1,0:T(4,128)(2,1)}, bf16[4,448]{1,0:T(4,128)(2,1)S(1)}, u32[]{:S(2)}) copy-start(bf16[4,448]{1,0:T(4,128)(2,1)S(1)} %reshape.314) | copy-start | bytes 10756
  186.0 1.2 copy-start.6
  189.6 6.9 %copy-start.17 = (bf16[4,448]{1,0:T(4,128)(2,1)S(1)}, bf16[4,448]{1,0:T(4,128)(2,1)}, u32[]{:S(2)}) copy-start(bf16[4,448]{1,0:T(4,128)(2,1)} %copy-done.16) | copy-start | bytes 10756
  189.6 8.9 %copy-start.19 = (bf16[4,224]{1,0:T(4,128)(2,1)S(1)}, bf16[4,224]{1,0:T(4,128)(2,1)}, u32[]{:S(2)}) copy-start(bf16[4,224]{1,0:T(4,128)(2,1)} %get-tuple-element.29) | copy-start | bytes 5380
  192.3 15.2 %copy-start.1 = (bf16[4,128,8,128]{3,2,1,0:T(8,128)(2,1)S(1)}, bf16[4,128,8,128]{3,2,1,0:T(8,128)(2,1)}, u32[]{:S(2)}) copy-start(bf16[4,128,8,128]{3,2,1,0:T(8,128)(2,1)} %copy-done) | copy-start | bytes 3145732
  192.3 15.2 %copy-start.10 = (bf16[4,56,512]{2,1,0:T(8,128)(2,1)S(1)}, bf16[4,56,512]{2,1,0:T(8,128)(2,1)}, u32[]{:S(2)}) copy-start(bf16[4,56,512]{2,1,0:T(8,128)(2,1)} %get-tuple-element.14) | copy-start | bytes 688132
  192.3 35.6 %all-to-all-start.3 = ((bf16[32,136,128]{2,1,0:T(8,128)(2,1)}), bf16[32,136,128]{2,1,0:T(8,128)(2,1)S(1)}, u32[]{:S(2)}, u32[]{:S(2)}) async-start(bf16[32,136,128]{2,1,0:T(8,128)(2,1)} %pad_maximum_fusion), calls=%async_computation.3 | async-start | bytes 2228224 | tf_op jit(solution)/shard_map/all_to_all | solution.py:16
  196.6 15.0 %collective-permute-start.11 = (bf16[224,512]{1,0:T(8,128)(2,1)}, bf16[224,512]{1,0:T(8,128)(2,1)}, u32[]{:S(2)}, u32[]{:S(2)}) collective-permute-start(bf16[224,512]{1,0:T(8,128)(2,1)} %bitcast.172), channel_id=1, source_target_pairs={{0,64},{64,0},{1,65},{65,1},{2,66},{66,2},{3,67},{67,3},{4,68},{68... | collective-permute-start | bytes 688136 | tf_op jit(solution)/shard_map/ppermute | solution.py:159
  198.5 13.1 %collective-permute-start.13 = (bf16[8,224]{1,0:T(8,128)(2,1)S(1)}, bf16[8,224]{1,0:T(8,128)(2,1)S(1)}, u32[]{:S(2)}, u32[]{:S(2)}) collective-permute-start(bf16[8,224]{1,0:T(8,128)(2,1)S(1)} %pad_maximum_fusion.2), channel_id=1, source_target_pairs={{0,64},{64,0},{1,65},{65,1},{2,66},{66,2},{3,67},{67,3},{4,68},{68... | collective-permute-start | bytes 10760 | tf_op jit(solution)/shard_map/ppermute | solution.py:147
  201.0 12.5 %collective-permute-start.14 = (bf16[224,512]{1,0:T(8,128)(2,1)}, bf16[224,512]{1,0:T(8,128)(2,1)}, u32[]{:S(2)}, u32[]{:S(2)}) collective-permute-start(bf16[224,512]{1,0:T(8,128)(2,1)} %bitcast.171), channel_id=1, source_target_pairs={{0,64},{64,0},{1,65},{65,1},{2,66},{66,2},{3,67},{67,3},{4,68},{68... | collective-permute-start | bytes 688136 | tf_op jit(solution)/shard_map/ppermute | solution.py:159
  207.4 4.2 %copy-start.9 = (f32[224,1024]{1,0:T(8,128)S(1)}, f32[224,1024]{1,0:T(8,128)}, u32[]{:S(2)}) copy-start(f32[224,1024]{1,0:T(8,128)} %fusion.67) | copy-start | bytes 2752516
  208.8 6.7 %collective-permute-start.15 = (bf16[224,512]{1,0:T(8,128)(2,1)}, bf16[224,512]{1,0:T(8,128)(2,1)S(1)}, u32[]{:S(2)}, u32[]{:S(2)}) collective-permute-start(bf16[224,512]{1,0:T(8,128)(2,1)} %bitcast.170), channel_id=1, source_target_pairs={{0,64},{64,0},{1,65},{65,1},{2,66},{66,2},{3,67},{67,3},{4,68},{68... | collective-permute-start | bytes 688136 | tf_op jit(solution)/shard_map/ppermute | solution.py:159
  211.6 3.9 %copy-start.8 = (f32[224,1024]{1,0:T(8,128)S(1)}, f32[224,1024]{1,0:T(8,128)}, u32[]{:S(2)}) copy-start(f32[224,1024]{1,0:T(8,128)} %fusion.65) | copy-start | bytes 2752516
  215.5 16.6 %copy-start.15 = (f32[128,128]{1,0:T(8,128)S(1)}, f32[128,128]{1,0:T(8,128)}, u32[]{:S(2)}) copy-start(f32[128,128]{1,0:T(8,128)} %param.12) | copy-start | bytes 196612
  218.1 17.0 %copy-start.20 = (bf16[4,224]{1,0:T(4,128)(2,1)S(1)}, bf16[4,224]{1,0:T(4,128)(2,1)}, u32[]{:S(2)}) copy-start(bf16[4,224]{1,0:T(4,128)(2,1)} %get-tuple-element.28) | copy-start | bytes 5380
  218.2 18.1 %copy-start.18 = (f32[8,128]{1,0:T(8,128)S(1)}, f32[8,128]{1,0:T(8,128)}, u32[]{:S(2)}) copy-start(f32[8,128]{1,0:T(8,128)} %convert_reduce_fusion.2) | copy-start | bytes 12292
  228.0 8.3 %copy-start.7 = (f32[224,1024]{1,0:T(8,128)S(1)}, f32[224,1024]{1,0:T(8,128)}, u32[]{:S(2)}) copy-start(f32[224,1024]{1,0:T(8,128)} %fusion.5) | copy-start | bytes 2752516
  228.5 9.1 %copy-start.22 = (f32[8]{0:T(128)}, f32[8]{0:T(128)S(1)}, u32[]{:S(2)}) copy-start(f32[8]{0:T(128)S(1)} %compare_select_fusion) | copy-start | bytes 100

commit v3 on v2

--- a/solution.py
+++ b/solution.py
@@ -1,6 +1,8 @@
 import jax
 import jax.numpy as jnp
 from jax import lax
+from jax.experimental import pallas as pl
+from jax.experimental.pallas import tpu as pltpu
 from jax.sharding import Mesh, PartitionSpec as P
 
 SEQ_LEN = 128
@@ -32,6 +34,31 @@
     return jnp.stack([high, middle, value - high - middle]).astype(bf16)
 
 
+def first_products(tok_got, low_got, *refs):
+    weights, (parts, tok, low, head, wide_head) = refs[:6], refs[6:]
+    n_gy, n_yl, rows, cols = low_got.shape
+    units, half = weights[0].shape[0], n_yl * rows
+    for z in range(n_gy):
+        at = slice(z * cols, (z + 1) * cols)
+        for y in range(n_yl):
+            tok[y * rows : (y + 1) * rows, at] = tok_got[y * n_gy + z, :rows]
+            low[y * rows : (y + 1) * rows, at] = low_got[z, y]
+        head[:, at] = tok_got[z, rows:]
+        for r in range(0, 128, 16):
+            wide_head[r : r + 16, at] = tok_got[z, rows:]
+    for c in range(2):
+        here = slice(c * units, (c + 1) * units)
+        gate_w, up_w, down_w = (weights[2 * i + c][...] for i in range(3))
+        parts[here, :half] = dot(gate_w, tok[...], 1, 1).astype(bf16)
+        parts[here, half : 2 * half] = dot(up_w, tok[...], 1, 1).astype(bf16)
+        parts[here, 2 * half : 3 * half] = dot(down_w, low[...], 1, 1).astype(bf16)
+        v = dot(down_w, wide_head[...], 1, 1)
+        high = v.astype(bf16).astype(f32)
+        lane = lax.broadcasted_iota(jnp.int32, v.shape, 1)
+        v = jnp.where(lane == 0, high, jnp.where(lane == 1, v - high, 0.0))
+        parts[here, 3 * half :] = v.astype(bf16)
+
+
 def body(tokens, gate_weight, up_weight, down_weight, reward_head, lm_grad, pair_index):
     n_yl, n_gy = lax.axis_size("yl"), lax.axis_size("gy")
     n_plane, n_gz = n_yl * n_gy, lax.axis_size(GZ)
@@ -41,37 +68,39 @@
     core = lax.axis_index("co")
 
     def chip_block(weight):
-        return jnp.concatenate([weight, lax.ppermute(weight, "co", SWAP)], axis=0)
-
-    gate_w, up_w, down_w = chip_block(gate_weight), chip_block(up_weight), chip_block(down_weight)
+        return weight, lax.ppermute(weight, "co", SWAP)
+
+    gate_ws, up_ws, down_ws = chip_block(gate_weight), chip_block(up_weight), chip_block(down_weight)
+    gate_w, up_w = jnp.concatenate(gate_ws, axis=0), jnp.concatenate(up_ws, axis=0)
 
     head_rows = jnp.broadcast_to(reward_head[None, :], (16, cols))
-    block = jnp.concatenate([tokens, lm_grad.astype(bf16), head_rows], axis=0)
-    block = to_all(block, "yl", n_yl)
-    up, down = [block], [block]
-    for step in range(n_gy // 2):
-        up.append(lax.ppermute(up[-1], "gy", [(k, (k + 1) % n_gy) for k in range(n_gy)]))
-        if step < n_gy // 2 - 1:
-            down.append(lax.ppermute(down[-1], "gy", [(k, (k - 1) % n_gy) for k in range(n_gy)]))
-    got = jnp.roll(jnp.stack(down + up[:0:-1]), lax.axis_index("gy"), axis=0)
-
-    def spread(part):
-        return part.transpose(1, 2, 0, 3).reshape(n_yl * rows, width)
-
-    tok_half = spread(got[:, :, :rows])
-    low_half = spread(got[:, :, rows : 2 * rows])
-    head_vec = got[:, 0, 2 * rows].reshape(1, width)
+    low_got = to_all(lm_grad.astype(bf16), "yl", n_yl)
+    tok_block, low_got = lax.optimization_barrier(
+        (jnp.concatenate([tokens, head_rows], axis=0), low_got)
+    )
+    low_got = lax.all_gather(low_got, "gy")
+    tok_got = to_all(tok_block, PLANE, n_plane)
+
     half = n_yl * rows
-
-    low_head = jnp.concatenate([low_half, jnp.pad(head_vec, ((0, 127), (0, 0)))], axis=0)
-    gate_part = dot(gate_w, tok_half, 1, 1).astype(bf16)
-    up_part = dot(up_w, tok_half, 1, 1).astype(bf16)
-    back_part = dot(down_w, low_head, 1, 1)
-    v_part = back_part[:, half : half + 1]
-    v_high = lax.reduce_precision(v_part, 8, 7)
-    v_cols = jnp.concatenate([v_high, v_part - v_high], axis=1).astype(bf16)
-    v_cols = jnp.pad(v_cols, ((0, 0), (0, 126)))
-    parts = jnp.concatenate([gate_part, up_part, back_part[:, :half].astype(bf16), v_cols], axis=1)
+    whole = pl.BlockSpec(memory_space=pltpu.VMEM)
+    parts, tok_half, low_half, head_vec = pl.pallas_call(
+        first_products,
+        out_shape=(
+            jax.ShapeDtypeStruct((2 * units, 3 * half + 128), bf16),
+            jax.ShapeDtypeStruct((half, width), bf16),
+            jax.ShapeDtypeStruct((half, width), bf16),
+            jax.ShapeDtypeStruct((16, width), bf16),
+        ),
+        in_specs=[whole] * 8,
+        out_specs=(whole,) * 4,
+        scratch_shapes=[pltpu.VMEM((128, width), bf16)],
+        compiler_params=pltpu.CompilerParams(vmem_limit_bytes=40 * 2**20),
+        cost_estimate=pl.CostEstimate(
+            flops=2 * 2 * units * width * (3 * half + 128), bytes_accessed=12 * 2**20, transcendentals=0
+        ),
+        name="first_products",
+    )(tok_got, low_got, *gate_ws, *up_ws, *down_ws)
+    head_vec = head_vec[:1]
     own = 2 * units // n_gz
     sums = jnp.sum(exchange(parts.reshape(n_gz, own, 3 * half + 128), GZ).astype(f32), axis=0)
     gate_sum, up_sum, hidden_grad = (sums[:, i * half : (i + 1) * half] for i in range(3))

time: 239 us -> 249 us (1.042)
  waiting for transfers between devices: 61.4 us -> 82.5 us
  between operations: 1.6 us -> 14.7 us
  blocking collectives: 11.8 us -> 0 us
  other arithmetic: 17.7 us -> 10.3 us
  matrix products: 23.9 us -> 17.1 us
  starting transfers between devices: 96.4 us -> 92.1 us
  Pallas kernels: 0 us -> 3.32 us
  local copies, waits for them, and re-layouts: 24.7 us -> 27.2 us
    all_to_all x3 -> x5, starting transfers between devices: 15.5 us -> 66.3 us  [exchange(): return lax.all_to_all(pieces, axes, 0, 0)]
    all_gather x0 -> x1, waiting for transfers between devices: none -> 36.2 us  [body(): low_got = lax.all_gather(low_got, 'gy')]
    ppermute x10 -> x3, starting transfers between devices: 37.9 us -> 7.77 us  [chip_block(): return (weight, lax.ppermute(weight, 'co', SWAP))]
    ppermute x10 -> x3, waiting for transfers between devices: 25 us -> 0.08 us  [chip_block(): return (weight, lax.ppermute(weight, 'co', SWAP))]
    ppermute x1, starting transfers between devices: 21.7 us -> 3.47 us  [body(): pair_terms = jnp.stack([core_terms, lax.ppermute(core_terms, 'co', SWAP)])]
    all_to_all x1 -> x0, blocking collectives: 11.8 us -> none  [exchange(): return lax.all_to_all(pieces, axes, 0, 0)]
    all_to_all x3 -> x5, waiting for transfers between devices: 36.3 us -> 45.4 us  [exchange(): return lax.all_to_all(pieces, axes, 0, 0)]
    ppermute x1, starting transfers between devices: 10.7 us -> 3.77 us  [body(): tok_sib = lax.ppermute(tok_half, 'co', SWAP)]
  transfers between devices with their start and end apart: 20 -> 16, of which waited for: 5 -> 6; matrix products, arithmetic and copies ran while one was open for 16% -> 12% of each run, Pallas kernels for 0% -> 0%
where the time goes in v3:
time: 249 us; the launch traced here: 247 us
  starting transfers between devices  92.1 us (37%)
  waiting for transfers between devices  82.5 us (33%)
  local copies, waits for them, and re-layouts  27.2 us (11%)
  matrix products  17.1 us (7%)
  between operations  14.7 us (6%)
  other arithmetic  10.3 us (4%)
  Pallas kernels  3.32 us (1%)
    all_to_all x5, starting transfers between devices, exchange(): return lax.all_to_all(pieces, axes, 0, 0)  66.3 us
    all_to_all x5, waiting for transfers between devices, exchange(): return lax.all_to_all(pieces, axes, 0, 0)  45.4 us
    all_gather x1, waiting for transfers between devices, body(): low_got = lax.all_gather(low_got, 'gy')  36.2 us
    dot_general x13, matrix products, dot(): lax.dot_general(left, right, (((left_dim,), (right_dim,)), ((), ())), pre...  17.1 us
    unnamed x70, local copies, waits for them, and re-layouts  11.8 us
    ppermute x3, starting transfers between devices, chip_block(): return (weight, lax.ppermute(weight, 'co', SWAP))  7.77 us
    ppermute x3, starting transfers between devices, weight_grad(): from_sib = lax.ppermute(full[units:], 'co', SWAP)  6.42 us
  transfers between devices with their start and end apart: 16, of which 6 were waited for; matrix products, arithmetic and copies ran while one was open for 12% of the time, Pallas kernels for 0%

profile of v3, /device:TPU:1, one launch (start us, length us, event | category | flops | bytes accessed | tf_op | source)
XLA Modules:
  0.0 247.0 jit_solution(77153088596531973)
XLA Ops:
  7.2 0.8 convert_element_type.101
  8.0 0.7 broadcast_in_dim.78
  8.7 5.4 %all-to-all-start = ((bf16[4,128,128]{2,1,0:T(8,128)(2,1)}), bf16[4,128,128]{2,1,0:T(8,128)(2,1)S(1)}, u32[]{:S(2)}, u32[]{:S(2)}) async-start(bf16[4,128,128]{2,1,0:T(8,128)(2,1)} %broadcast_in_dim.78), calls=%async_computation | async-start | bytes 262144 | tf_op jit(solution)/shard_map/all_to_all | solution.py:18
  14.8 0.8 pad_maximum_fusion.1
  15.5 3.4 %all-to-all-done = bf16[4,128,128]{2,1,0:T(8,128)(2,1)S(1)} async-done(((bf16[4,128,128]{2,1,0:T(8,128)(2,1)}), bf16[4,128,128]{2,1,0:T(8,128)(2,1)S(1)}, u32[]{:S(2)}, u32[]{:S(2)}) %all-to-all-start) | async-done | bytes 131104 | tf_op jit(solution)/shard_map/all_to_all | solution.py:18
  18.9 1.2 broadcast_in_dim.79
  20.1 12.5 %all-to-all-start.1 = ((bf16[32,144,128]{2,1,0:T(8,128)(2,1)}), bf16[32,144,128]{2,1,0:T(8,128)(2,1)S(1)}, u32[]{:S(2)}, u32[]{:S(2)}) async-start(bf16[32,144,128]{2,1,0:T(8,128)(2,1)} %broadcast_in_dim.79), calls=%async_computation.1 | async-start | bytes 2359296 | tf_op jit(solution)/shard_map/all_to_all | solution.py:18
  32.6 0.7 all-gather.3.cloned.1.call-update
  33.3 3.4 %collective-permute-start = (bf16[224,1024]{1,0:T(8,128)(2,1)S(1)}, bf16[224,1024]{1,0:T(8,128)(2,1)S(1)}, u32[]{:S(2)}, u32[]{:S(2)}) collective-permute-start(bf16[224,1024]{1,0:T(8,128)(2,1)S(1)} %copy-done.3), channel_id=1, source_target_pairs={{0,64},{64,0},{1,65},{65,1},{2,66},{66,2},{3,67},{67,3},{4,68},{68... | collective-permute-start | bytes 1376264 | tf_op jit(solution)/shard_map/ppermute | solution.py:71
  36.7 1.9 collective-permute-start.1
  38.7 2.4 collective-permute-start.2
  41.1 0.8 copy-done.6
  41.9 0.8 copy-done.9
  42.7 0.8 copy-done.14
  43.5 36.2 %all-gather.3.cloned.1.call-done = bf16[32,128,128]{2,1,0:T(8,128)(2,1)} async-done(((bf16[4,128,128]{2,1,0:T(8,128)(2,1)}), bf16[32,128,128]{2,1,0:T(8,128)(2,1)}) %all-gather.3.cloned.1.call-update) | async-done | bytes 1048592 | tf_op jit(solution)/shard_map/all_gather | solution.py:81
  79.7 1.0 copy-done.1
  80.7 1.0 copy-done.4
  81.7 1.0 copy-done.7
  82.7 1.0 copy-done.10
  83.8 1.2 copy-done.12
  85.0 1.0 copy-done.13
  86.0 1.0 copy-done.15
  87.0 3.3 %first_products.1 = (bf16[448,1664]{1,0:T(8,128)(2,1)}, bf16[512,1024]{1,0:T(8,128)(2,1)S(1)}, bf16[512,1024]{1,0:T(8,128)(2,1)S(1)}, bf16[16,1024]{1,0:T(8,128)(2,1)S(1)}) custom-call(bf16[32,144,128]{2,1,0:T(8,128)(2,1)S(1)} %all-to-all-done.1.tok_got, bf16[8,4,128,128]{3,2,1,0:T(8,128)(2,1)S(1)} %bitcast.92, bf16[224,1024]{1,0:T(8,128)(2,1)S(1)} %copy-done.4, ...), custom_call_target="tpu_custom_call" | custom-call | flops 1526726656 | bytes 12582912 | tf_op jit(solution)/shard_map/first_products/pallas_call | solution.py:86
  90.3 8.5 %all-to-all-start.2 = ((bf16[8,56,1664]{2,1,0:T(8,128)(2,1)}), bf16[8,56,1664]{2,1,0:T(8,128)(2,1)}, u32[]{:S(2)}, u32[]{:S(2)}) async-start(bf16[8,56,1664]{2,1,0:T(8,128)(2,1)} %bitcast.1), calls=%async_computation.2 | async-start | bytes 2981888 | tf_op jit(solution)/shard_map/all_to_all | solution.py:18
  98.8 1.3 fusion.44
  100.1 17.2 %all-to-all-done.2 = bf16[8,56,1664]{2,1,0:T(8,128)(2,1)} async-done(((bf16[8,56,1664]{2,1,0:T(8,128)(2,1)}), bf16[8,56,1664]{2,1,0:T(8,128)(2,1)}, u32[]{:S(2)}, u32[]{:S(2)}) %all-to-all-start.2) | async-done | bytes 1490976 | tf_op jit(solution)/shard_map/all_to_all | solution.py:18
  117.4 1.6 convert_reduce_fusion
  120.2 0.7 reduce-precision_convert_fusion.3
  121.0 1.2 broadcast_in_dim.82
  122.3 8.4 %all-to-all-start.3 = ((bf16[8,176,512]{2,1,0:T(8,128)(2,1)}), bf16[8,176,512]{2,1,0:T(8,128)(2,1)}, u32[]{:S(2)}, u32[]{:S(2)}) async-start(bf16[8,176,512]{2,1,0:T(8,128)(2,1)} %broadcast_in_dim.82), calls=%async_computation.3 | async-start | bytes 2883584 | tf_op jit(solution)/shard_map/all_to_all | solution.py:18
  130.7 3.8 %collective-permute-start.5 = (bf16[512,1024]{1,0:T(8,128)(2,1)S(1)}, bf16[512,1024]{1,0:T(8,128)(2,1)S(1)}, u32[]{:S(2)}, u32[]{:S(2)}) collective-permute-start(bf16[512,1024]{1,0:T(8,128)(2,1)S(1)} %get-tuple-element.14), channel_id=1, source_target_pairs={{0,64},{64,0},{1,65},{65,1},{2,66},{66,2},{3,67},{67,3},{4,68},{68... | collective-permute-start | bytes 3145736 | tf_op jit(solution)/shard_map/ppermute | solution.py:174
  134.8 1.9 collective-permute-start.9
  136.7 1.0 copy-done.20
  137.7 14.6 %all-to-all-done.3 = bf16[8,176,512]{2,1,0:T(8,128)(2,1)} async-done(((bf16[8,176,512]{2,1,0:T(8,128)(2,1)}), bf16[8,176,512]{2,1,0:T(8,128)(2,1)}, u32[]{:S(2)}, u32[]{:S(2)}) %all-to-all-start.3) | async-done | bytes 1441824 | tf_op jit(solution)/shard_map/all_to_all | solution.py:18
  152.3 0.7 fusion.19
  153.1 3.5 %collective-permute-start.3 = (f32[4]{0:T(128)S(1)}, f32[4]{0:T(128)S(1)}, u32[]{:S(2)}, u32[]{:S(2)}) collective-permute-start(f32[4]{0:T(128)S(1)} %reduce_sum.87), channel_id=1, source_target_pairs={{0,64},{64,0},{1,65},{65,1},{2,66},{66,2},{3,67},{67,3},{4,68},{68... | collective-permute-start | bytes 56 | tf_op jit(solution)/shard_map/ppermute | solution.py:141
  156.6 0.9 slice_bitcast_fusion
  157.7 1.4 fusion.56
  159.3 1.5 fusion.7
  160.8 1.2 fusion.50
  162.0 0.7 fusion.55
  163.2 0.7 fusion
  164.5 2.4 fusion.49
  166.9 1.9 collective-permute-start.4
  168.9 2.4 collective-permute-start.6
  171.5 1.1 pad_maximum_fusion
  172.6 31.5 %all-to-all-start.4 = ((bf16[32,136,128]{2,1,0:T(8,128)(2,1)}), bf16[32,136,128]{2,1,0:T(8,128)(2,1)S(1)}, u32[]{:S(2)}, u32[]{:S(2)}) async-start(bf16[32,136,128]{2,1,0:T(8,128)(2,1)} %pad_maximum_fusion), calls=%async_computation.4 | async-start | bytes 2228224 | tf_op jit(solution)/shard_map/all_to_all | solution.py:18
  204.1 2.2 collective-permute-start.7
  206.3 2.3 collective-permute-start.8
  208.7 0.8 reshape.308
  209.4 1.8 slice.229
  211.3 1.1 copy.56
  212.4 1.8 fusion.57
  214.3 1.3 fusion.6
  215.6 1.4 fusion.58
  217.0 1.3 fusion.4
  218.3 1.8 fusion.59
  220.1 1.3 fusion.2
  221.4 1.1 reshape.309
  222.9 10.3 %all-to-all-done.4 = bf16[32,136,128]{2,1,0:T(8,128)(2,1)S(1)} async-done(((bf16[32,136,128]{2,1,0:T(8,128)(2,1)}), bf16[32,136,128]{2,1,0:T(8,128)(2,1)S(1)}, u32[]{:S(2)}, u32[]{:S(2)}) %all-to-all-start.4) | async-done | bytes 1114144 | tf_op jit(solution)/shard_map/all_to_all | solution.py:18
  235.4 0.7 fusion.12
  236.4 1.3 fusion.5
  237.7 1.3 fusion.3
  238.9 1.3 fusion.1
  (134 shorter events, 6.9 us)
Async XLA Ops:
  8.7 10.2 %all-to-all-start = ((bf16[4,128,128]{2,1,0:T(8,128)(2,1)}), bf16[4,128,128]{2,1,0:T(8,128)(2,1)S(1)}, u32[]{:S(2)}, u32[]{:S(2)}) async-start(bf16[4,128,128]{2,1,0:T(8,128)(2,1)} %broadcast_in_dim.78), calls=%async_computation | async-start | bytes 262144 | tf_op jit(solution)/shard_map/all_to_all | solution.py:18
  18.9 1.2 copy-start.27
  20.1 13.2 %copy-start.3 = (bf16[224,1024]{1,0:T(8,128)(2,1)S(1)}, bf16[224,1024]{1,0:T(8,128)(2,1)}, u32[]{:S(2)}) copy-start(bf16[224,1024]{1,0:T(8,128)(2,1)} %refs_0_.1) | copy-start | bytes 1376260
  20.1 16.7 %copy-start = (bf16[224,1024]{1,0:T(8,128)(2,1)S(1)}, bf16[224,1024]{1,0:T(8,128)(2,1)}, u32[]{:S(2)}) copy-start(bf16[224,1024]{1,0:T(8,128)(2,1)} %refs_2_.1) | copy-start | bytes 1376260
  20.1 59.6 %all-to-all-start.1 = ((bf16[32,144,128]{2,1,0:T(8,128)(2,1)}), bf16[32,144,128]{2,1,0:T(8,128)(2,1)S(1)}, u32[]{:S(2)}, u32[]{:S(2)}) async-start(bf16[32,144,128]{2,1,0:T(8,128)(2,1)} %broadcast_in_dim.79), calls=%async_computation.1 | async-start | bytes 2359296 | tf_op jit(solution)/shard_map/all_to_all | solution.py:18
  32.5 47.2 %all-gather.3.cloned.1.call-start = ((), (), s32[]{:S(2)}) async-start(), calls=%async_computation.5 | async-start | bytes 1179648 | tf_op jit(solution)/shard_map/all_gather | solution.py:81
  33.3 7.8 %collective-permute-start = (bf16[224,1024]{1,0:T(8,128)(2,1)S(1)}, bf16[224,1024]{1,0:T(8,128)(2,1)S(1)}, u32[]{:S(2)}, u32[]{:S(2)}) collective-permute-start(bf16[224,1024]{1,0:T(8,128)(2,1)S(1)} %copy-done.3), channel_id=1, source_target_pairs={{0,64},{64,0},{1,65},{65,1},{2,66},{66,2},{3,67},{67,3},{4,68},{68... | collective-permute-start | bytes 1376264 | tf_op jit(solution)/shard_map/ppermute | solution.py:71
  36.7 5.1 %collective-permute-start.1 = (bf16[224,1024]{1,0:T(8,128)(2,1)S(1)}, bf16[224,1024]{1,0:T(8,128)(2,1)S(1)}, u32[]{:S(2)}, u32[]{:S(2)}) collective-permute-start(bf16[224,1024]{1,0:T(8,128)(2,1)S(1)} %copy-done), channel_id=1, source_target_pairs={{0,64},{64,0},{1,65},{65,1},{2,66},{66,2},{3,67},{67,3},{4,68},{68... | collective-permute-start | bytes 1376264 | tf_op jit(solution)/shard_map/ppermute | solution.py:71
  38.7 4.0 %collective-permute-start.2 = (bf16[224,1024]{1,0:T(8,128)(2,1)}, bf16[224,1024]{1,0:T(8,128)(2,1)S(1)}, u32[]{:S(2)}, u32[]{:S(2)}) collective-permute-start(bf16[224,1024]{1,0:T(8,128)(2,1)} %refs_4_.1), channel_id=1, source_target_pairs={{0,64},{64,0},{1,65},{65,1},{2,66},{66,2},{3,67},{67,3},{4,68},{68... | collective-permute-start | bytes 1376264 | tf_op jit(solution)/shard_map/ppermute | solution.py:71
  41.1 0.8 copy-start.6
  41.9 0.8 copy-start.9
  42.7 0.8 copy-start.14
  79.7 1.0 copy-start.1
  80.7 1.0 copy-start.4
  81.7 1.0 copy-start.7
  82.7 1.0 copy-start.10
  83.8 1.2 copy-start.12
  85.0 1.0 copy-start.13
  86.0 1.0 copy-start.15
  90.3 8.5 %copy-start.29 = (bf16[128]{0:T(256)(128)(2,1)S(1)}, bf16[128]{0:T(256)(128)(2,1)}, u32[]{:S(2)}) copy-start(bf16[128]{0:T(256)(128)(2,1)} %param.11) | copy-start | bytes 772
  90.3 27.0 %all-to-all-start.2 = ((bf16[8,56,1664]{2,1,0:T(8,128)(2,1)}), bf16[8,56,1664]{2,1,0:T(8,128)(2,1)}, u32[]{:S(2)}, u32[]{:S(2)}) async-start(bf16[8,56,1664]{2,1,0:T(8,128)(2,1)} %bitcast.1), calls=%async_computation.2 | async-start | bytes 2981888 | tf_op jit(solution)/shard_map/all_to_all | solution.py:18
  122.3 12.2 %copy-start.2 = (bf16[224,1024]{1,0:T(8,128)(2,1)S(1)}, bf16[224,1024]{1,0:T(8,128)(2,1)}, u32[]{:S(2)}) copy-start(bf16[224,1024]{1,0:T(8,128)(2,1)} %refs_2_.1) | copy-start | bytes 1376260
  122.3 12.3 %copy-start.5 = (bf16[224,1024]{1,0:T(8,128)(2,1)S(1)}, bf16[224,1024]{1,0:T(8,128)(2,1)}, u32[]{:S(2)}) copy-start(bf16[224,1024]{1,0:T(8,128)(2,1)} %refs_0_.1) | copy-start | bytes 1376260
  122.3 30.0 %all-to-all-start.3 = ((bf16[8,176,512]{2,1,0:T(8,128)(2,1)}), bf16[8,176,512]{2,1,0:T(8,128)(2,1)}, u32[]{:S(2)}, u32[]{:S(2)}) async-start(bf16[8,176,512]{2,1,0:T(8,128)(2,1)} %broadcast_in_dim.82), calls=%async_computation.3 | async-start | bytes 2883584 | tf_op jit(solution)/shard_map/all_to_all | solution.py:18
  130.7 3.9 %copy-start.31 = (s32[4,2]{0,1:T(2,128)S(1)}, s32[4,2]{0,1:T(2,128)}, u32[]{:S(2)}) copy-start(s32[4,2]{0,1:T(2,128)} %param.13) | copy-start | bytes 100
  130.7 4.0 %copy-start.8 = (bf16[224,1024]{1,0:T(8,128)(2,1)S(1)}, bf16[224,1024]{1,0:T(8,128)(2,1)}, u32[]{:S(2)}) copy-start(bf16[224,1024]{1,0:T(8,128)(2,1)} %copy-done.6) | copy-start | bytes 1376260
  130.7 3.9 %copy-start.11 = (bf16[224,1024]{1,0:T(8,128)(2,1)S(1)}, bf16[224,1024]{1,0:T(8,128)(2,1)}, u32[]{:S(2)}) copy-start(bf16[224,1024]{1,0:T(8,128)(2,1)} %copy-done.9) | copy-start | bytes 1376260
  130.7 6.0 %collective-permute-start.5 = (bf16[512,1024]{1,0:T(8,128)(2,1)S(1)}, bf16[512,1024]{1,0:T(8,128)(2,1)S(1)}, u32[]{:S(2)}, u32[]{:S(2)}) collective-permute-start(bf16[512,1024]{1,0:T(8,128)(2,1)S(1)} %get-tuple-element.14), channel_id=1, source_target_pairs={{0,64},{64,0},{1,65},{65,1},{2,66},{66,2},{3,67},{67,3},{4,68},{68... | collective-permute-start | bytes 3145736 | tf_op jit(solution)/shard_map/ppermute | solution.py:174
  134.7 2.1 copy-start.16
  134.7 2.0 copy-start.18
  134.8 83.6 %collective-permute-start.9 = (bf16[512,1024]{1,0:T(8,128)(2,1)S(1)}, bf16[512,1024]{1,0:T(8,128)(2,1)}, u32[]{:S(2)}, u32[]{:S(2)}) collective-permute-start(bf16[512,1024]{1,0:T(8,128)(2,1)S(1)} %get-tuple-element.15), channel_id=1, source_target_pairs={{0,64},{64,0},{1,65},{65,1},{2,66},{66,2},{3,67},{67,3},{4,68},{68... | collective-permute-start | bytes 3145736 | tf_op jit(solution)/shard_map/ppermute | solution.py:175
  136.7 1.0 copy-start.20
  153.1 18.1 %collective-permute-start.3 = (f32[4]{0:T(128)S(1)}, f32[4]{0:T(128)S(1)}, u32[]{:S(2)}, u32[]{:S(2)}) collective-permute-start(f32[4]{0:T(128)S(1)} %reduce_sum.87), channel_id=1, source_target_pairs={{0,64},{64,0},{1,65},{65,1},{2,66},{66,2},{3,67},{67,3},{4,68},{68... | collective-permute-start | bytes 56 | tf_op jit(solution)/shard_map/ppermute | solution.py:141
  159.1 2.9 %copy-start.17 = (bf16[448,1024]{1,0:T(8,128)(2,1)S(1)}, bf16[448,1024]{1,0:T(8,128)(2,1)}, u32[]{:S(2)}) copy-start(bf16[448,1024]{1,0:T(8,128)(2,1)} %copy-done.16) | copy-start | bytes 2752516
  162.0 1.2 copy-start.19
  166.9 45.5 %collective-permute-start.4 = (bf16[224,512]{1,0:T(8,128)(2,1)}, bf16[224,512]{1,0:T(8,128)(2,1)}, u32[]{:S(2)}, u32[]{:S(2)}) collective-permute-start(bf16[224,512]{1,0:T(8,128)(2,1)} %bitcast.23), channel_id=1, source_target_pairs={{0,64},{64,0},{1,65},{65,1},{2,66},{66,2},{3,67},{67,3},{4,68},{68... | collective-permute-start | bytes 688136 | tf_op jit(solution)/shard_map/ppermute | solution.py:188
  168.9 43.5 %collective-permute-start.6 = (bf16[8,224]{1,0:T(8,128)(2,1)S(1)}, bf16[8,224]{1,0:T(8,128)(2,1)S(1)}, u32[]{:S(2)}, u32[]{:S(2)}) collective-permute-start(bf16[8,224]{1,0:T(8,128)(2,1)S(1)} %pad_maximum_fusion.2), channel_id=1, source_target_pairs={{0,64},{64,0},{1,65},{65,1},{2,66},{66,2},{3,67},{67,3},{4,68},{68... | collective-permute-start | bytes 10760 | tf_op jit(solution)/shard_map/ppermute | solution.py:176
  172.6 60.5 %all-to-all-start.4 = ((bf16[32,136,128]{2,1,0:T(8,128)(2,1)}), bf16[32,136,128]{2,1,0:T(8,128)(2,1)S(1)}, u32[]{:S(2)}, u32[]{:S(2)}) async-start(bf16[32,136,128]{2,1,0:T(8,128)(2,1)} %pad_maximum_fusion), calls=%async_computation.4 | async-start | bytes 2228224 | tf_op jit(solution)/shard_map/all_to_all | solution.py:18
  204.1 11.5 %collective-permute-start.7 = (bf16[224,512]{1,0:T(8,128)(2,1)}, bf16[224,512]{1,0:T(8,128)(2,1)}, u32[]{:S(2)}, u32[]{:S(2)}) collective-permute-start(bf16[224,512]{1,0:T(8,128)(2,1)} %bitcast.102), channel_id=1, source_target_pairs={{0,64},{64,0},{1,65},{65,1},{2,66},{66,2},{3,67},{67,3},{4,68},{68... | collective-permute-start | bytes 688136 | tf_op jit(solution)/shard_map/ppermute | solution.py:188
  206.3 12.0 %collective-permute-start.8 = (bf16[224,512]{1,0:T(8,128)(2,1)}, bf16[224,512]{1,0:T(8,128)(2,1)}, u32[]{:S(2)}, u32[]{:S(2)}) collective-permute-start(bf16[224,512]{1,0:T(8,128)(2,1)} %bitcast.101), channel_id=1, source_target_pairs={{0,64},{64,0},{1,65},{65,1},{2,66},{66,2},{3,67},{67,3},{4,68},{68... | collective-permute-start | bytes 688136 | tf_op jit(solution)/shard_map/ppermute | solution.py:188
  212.4 1.8 copy-start.26
  214.2 1.4 copy-start.21
  215.6 1.4 copy-start.25
  221.4 14.0 %copy-start.28 = (f32[128,128]{1,0:T(8,128)S(1)}, f32[128,128]{1,0:T(8,128)}, u32[]{:S(2)}) copy-start(f32[128,128]{1,0:T(8,128)} %param.12) | copy-start | bytes 196612
  221.4 15.0 %copy-start.22 = (f32[224,1024]{1,0:T(8,128)S(1)}, f32[224,1024]{1,0:T(8,128)}, u32[]{:S(2)}) copy-start(f32[224,1024]{1,0:T(8,128)} %fusion.6) | copy-start | bytes 2752516
  222.9 14.8 %copy-start.23 = (f32[224,1024]{1,0:T(8,128)S(1)}, f32[224,1024]{1,0:T(8,128)}, u32[]{:S(2)}) copy-start(f32[224,1024]{1,0:T(8,128)} %fusion.4) | copy-start | bytes 2752516
  233.7 5.2 %copy-start.30 = (f32[8]{0:T(128)}, f32[8]{0:T(128)S(1)}, u32[]{:S(2)}) copy-start(f32[8]{0:T(128)S(1)} %compare_select_fusion) | copy-start | bytes 100
  236.4 2.5 %copy-start.24 = (f32[224,1024]{1,0:T(8,128)S(1)}, f32[224,1024]{1,0:T(8,128)}, u32[]{:S(2)}) copy-start(f32[224,1024]{1,0:T(8,128)} %fusion.2) | copy-start | bytes 2752516
Sparse Core Ops, SparseCore 0:
  35.4 44.1 all-gather.2

commit v4 on v3

--- a/solution.py
+++ b/solution.py
@@ -34,29 +34,57 @@
     return jnp.stack([high, middle, value - high - middle]).astype(bf16)
 
 
-def first_products(tok_got, low_got, *refs):
-    weights, (parts, tok, low, head, wide_head) = refs[:6], refs[6:]
-    n_gy, n_yl, rows, cols = low_got.shape
-    units, half = weights[0].shape[0], n_yl * rows
+def load(sources, held, sems):
+    copies = [pltpu.make_async_copy(src, held.at[i], sems.at[i]) for i, src in enumerate(sources)]
+    for copy in copies:
+        copy.start()
+    return copies
+
+
+def token_products(tok_got, *refs):
+    weights, (parts, tok, head, held, wide_head, sems) = refs[:6], refs[6:]
+    copies = load(weights, held, sems)
+    width, cols = tok.shape[1], tok_got.shape[2]
+    n_gy = width // cols
+    n_yl = tok_got.shape[0] // n_gy
+    rows = tok.shape[0] // n_yl
+    units, half = weights[0].shape[0], tok.shape[0]
     for z in range(n_gy):
         at = slice(z * cols, (z + 1) * cols)
         for y in range(n_yl):
             tok[y * rows : (y + 1) * rows, at] = tok_got[y * n_gy + z, :rows]
-            low[y * rows : (y + 1) * rows, at] = low_got[z, y]
         head[:, at] = tok_got[z, rows:]
         for r in range(0, 128, 16):
             wide_head[r : r + 16, at] = tok_got[z, rows:]
-    for c in range(2):
-        here = slice(c * units, (c + 1) * units)
-        gate_w, up_w, down_w = (weights[2 * i + c][...] for i in range(3))
-        parts[here, :half] = dot(gate_w, tok[...], 1, 1).astype(bf16)
-        parts[here, half : 2 * half] = dot(up_w, tok[...], 1, 1).astype(bf16)
-        parts[here, 2 * half : 3 * half] = dot(down_w, low[...], 1, 1).astype(bf16)
-        v = dot(down_w, wide_head[...], 1, 1)
-        high = v.astype(bf16).astype(f32)
-        lane = lax.broadcasted_iota(jnp.int32, v.shape, 1)
-        v = jnp.where(lane == 0, high, jnp.where(lane == 1, v - high, 0.0))
-        parts[here, 3 * half :] = v.astype(bf16)
+    for i in range(6):
+        copies[i].wait()
+        here = slice(i % 2 * units, (i % 2 + 1) * units)
+        if i < 4:
+            at = slice(i // 2 * half, (i // 2 + 1) * half)
+            parts[here, at] = dot(held[i], tok[...], 1, 1).astype(bf16)
+        else:
+            v = dot(held[i], wide_head[...], 1, 1)
+            high = v.astype(bf16).astype(f32)
+            lane = lax.broadcasted_iota(jnp.int32, v.shape, 1)
+            v = jnp.where(lane == 0, high, jnp.where(lane == 1, v - high, 0.0))
+            parts[here, 2 * half :] = v.astype(bf16)
+
+
+def cotangent_products(at_yl, low_got, *refs):
+    weights, (parts, low, held, low_held, sems) = refs[:2], refs[2:]
+    copies = load(weights, held, sems)
+    arrival = pltpu.make_async_copy(low_got, low_held, sems.at[2])
+    arrival.start()
+    arrival.wait()
+    n_gy, n_yl, rows, cols = low_held.shape
+    units = weights[0].shape[0]
+    for shift in range(n_yl):
+        first = pl.multiple_of(lax.rem(at_yl[0] + (n_yl - shift), n_yl) * rows, rows)
+        for z in range(n_gy):
+            low[pl.ds(first, rows), z * cols : (z + 1) * cols] = low_held[z, shift]
+    for i in range(2):
+        copies[i].wait()
+        parts[i * units : (i + 1) * units, :] = dot(held[i], low[...], 1, 1).astype(bf16)
 
 
 def body(tokens, gate_weight, up_weight, down_weight, reward_head, lm_grad, pair_index):
@@ -73,46 +101,69 @@
     gate_ws, up_ws, down_ws = chip_block(gate_weight), chip_block(up_weight), chip_block(down_weight)
     gate_w, up_w = jnp.concatenate(gate_ws, axis=0), jnp.concatenate(up_ws, axis=0)
 
+    low = lm_grad.astype(bf16)
+    low_rows = [low]
+    for shift in range(1, n_yl):
+        low_rows.append(lax.ppermute(low, "yl", [(k, (k + shift) % n_yl) for k in range(n_yl)]))
+    low_got = lax.all_gather(jnp.stack(low_rows), "gy")
     head_rows = jnp.broadcast_to(reward_head[None, :], (16, cols))
-    low_got = to_all(lm_grad.astype(bf16), "yl", n_yl)
-    tok_block, low_got = lax.optimization_barrier(
-        (jnp.concatenate([tokens, head_rows], axis=0), low_got)
-    )
-    low_got = lax.all_gather(low_got, "gy")
-    tok_got = to_all(tok_block, PLANE, n_plane)
-
-    half = n_yl * rows
-    whole = pl.BlockSpec(memory_space=pltpu.VMEM)
-    parts, tok_half, low_half, head_vec = pl.pallas_call(
-        first_products,
+    tok_got = to_all(jnp.concatenate([tokens, head_rows], axis=0), PLANE, n_plane)
+
+    half, own = n_yl * rows, 2 * units // n_gz
+    whole, apart = pl.BlockSpec(memory_space=pltpu.VMEM), pl.BlockSpec(memory_space=pl.ANY)
+    grant = pltpu.CompilerParams(vmem_limit_bytes=40 * 2**20)
+    parts, tok_half, head_vec = pl.pallas_call(
+        token_products,
         out_shape=(
-            jax.ShapeDtypeStruct((2 * units, 3 * half + 128), bf16),
-            jax.ShapeDtypeStruct((half, width), bf16),
+            jax.ShapeDtypeStruct((2 * units, 2 * half + 128), bf16),
             jax.ShapeDtypeStruct((half, width), bf16),
             jax.ShapeDtypeStruct((16, width), bf16),
         ),
-        in_specs=[whole] * 8,
-        out_specs=(whole,) * 4,
-        scratch_shapes=[pltpu.VMEM((128, width), bf16)],
-        compiler_params=pltpu.CompilerParams(vmem_limit_bytes=40 * 2**20),
+        in_specs=[whole] + [apart] * 6,
+        out_specs=(whole,) * 3,
+        scratch_shapes=[
+            pltpu.VMEM((6, units, width), bf16),
+            pltpu.VMEM((128, width), bf16),
+            pltpu.SemaphoreType.DMA((6,)),
+        ],
+        compiler_params=grant,
         cost_estimate=pl.CostEstimate(
-            flops=2 * 2 * units * width * (3 * half + 128), bytes_accessed=12 * 2**20, transcendentals=0
-        ),
-        name="first_products",
-    )(tok_got, low_got, *gate_ws, *up_ws, *down_ws)
+            flops=4 * units * width * (2 * half + 128), bytes_accessed=8 * 2**20, transcendentals=0
+        ),
+        name="token_products",
+    )(tok_got, *gate_ws, *up_ws, *down_ws)
     head_vec = head_vec[:1]
-    own = 2 * units // n_gz
-    sums = jnp.sum(exchange(parts.reshape(n_gz, own, 3 * half + 128), GZ).astype(f32), axis=0)
-    gate_sum, up_sum, hidden_grad = (sums[:, i * half : (i + 1) * half] for i in range(3))
-    head_down = sums[:, 3 * half : 3 * half + 1] + sums[:, 3 * half + 1 : 3 * half + 2]
-
+    first = exchange(parts.reshape(n_gz, own, 2 * half + 128), GZ)
+
+    back_parts, low_half = pl.pallas_call(
+        cotangent_products,
+        out_shape=(
+            jax.ShapeDtypeStruct((2 * units, half), bf16),
+            jax.ShapeDtypeStruct((half, width), bf16),
+        ),
+        in_specs=[pl.BlockSpec(memory_space=pltpu.SMEM)] + [apart] * 3,
+        out_specs=(whole,) * 2,
+        scratch_shapes=[
+            pltpu.VMEM((2, units, width), bf16),
+            pltpu.VMEM((n_gy, n_yl, rows, cols), bf16),
+            pltpu.SemaphoreType.DMA((3,)),
+        ],
+        compiler_params=grant,
+        cost_estimate=pl.CostEstimate(
+            flops=4 * units * width * half, bytes_accessed=5 * 2**20, transcendentals=0
+        ),
+        name="cotangent_products",
+    )(lax.axis_index("yl").astype(jnp.int32)[None], low_got, *down_ws)
+    first, back_parts = lax.optimization_barrier((first, back_parts))
+    second = exchange(back_parts.reshape(n_gz, own, half), GZ)
+
+    sums = jnp.sum(first.astype(f32), axis=0)
+    gate_sum, up_sum = sums[:, :half], sums[:, half : 2 * half]
+    head_down = sums[:, 2 * half : 2 * half + 1] + sums[:, 2 * half + 1 : 2 * half + 2]
     gate_sigmoid = jax.nn.sigmoid(gate_sum)
     silu_gate = gate_sum * gate_sigmoid
     hidden = (silu_gate * up_sum).astype(bf16)
-
     gate_slope = up_sum * gate_sigmoid * (1.0 + gate_sum * (1.0 - gate_sigmoid))
-    up_grad = (hidden_grad * silu_gate).astype(bf16)
-    gate_grad = (hidden_grad * gate_slope).astype(bf16)
 
     def last_cols(value):
         return value.reshape(own, n_yl, rows)[:, :, rows - 1].astype(f32)
@@ -126,7 +177,13 @@
         [jnp.pad(gate_unit, ((0, 0), (0, 128 - own))), jnp.pad(up_unit, ((0, 0), (0, half - 128 - own)))], axis=1
     )
     term_rows = jnp.pad(pieces(terms).reshape(1, -1), ((0, 7 - n_yl), (0, half - 3 * n_yl)))
-    mine = jnp.concatenate([gate_grad, up_grad, hidden, unit_rows, term_rows], axis=0)
+    silu_gate, gate_slope, early, second = lax.optimization_barrier(
+        (silu_gate, gate_slope, jnp.concatenate([hidden, unit_rows, term_rows], axis=0), second)
+    )
+    hidden_grad = jnp.sum(second.astype(f32), axis=0)
+    up_grad = (hidden_grad * silu_gate).astype(bf16)
+    gate_grad = (hidden_grad * gate_slope).astype(bf16)
+    mine = jnp.concatenate([gate_grad, up_grad, early], axis=0)
     everyone = to_all(mine, GZ, n_gz)
     gate_g, up_g, hid = (
         everyone[:, i * own : (i + 1) * own].reshape(2 * units, half) for i in range(3)
@@ -149,6 +206,9 @@
     )
     sent = jnp.concatenate(
         [token_part.reshape(n_plane, rows, cols), jnp.pad(extra, ((0, 0), (0, 6), (0, 0)))], axis=1
+    )
+    sent, gate_g, up_g, hid, gate_u, up_u = lax.optimization_barrier(
+        (sent, gate_g, up_g, hid, gate_u, up_u)
     )
     token_sum = jnp.sum(exchange(sent, PLANE).astype(f32), axis=0)
 

time: 249 us -> 232 us (0.932)
  waiting for transfers between devices: 82.5 us -> 37.1 us
  starting transfers between devices: 92.1 us -> 115 us
  Pallas kernels: 3.32 us -> 7.05 us
  local copies, waits for them, and re-layouts: 27.2 us -> 29.8 us
    all_to_all x5, waiting for transfers between devices: 45.4 us -> 10.8 us  [exchange(): return lax.all_to_all(pieces, axes, 0, 0)]
    all_to_all x5, starting transfers between devices: 66.3 us -> 41.4 us  [exchange(): return lax.all_to_all(pieces, axes, 0, 0)]
    ppermute x1, starting transfers between devices: 3.47 us -> 25 us  [body(): pair_terms = jnp.stack([core_terms, lax.ppermute(core_terms, 'co', SWAP)])]
    ppermute x0 -> x3, starting transfers between devices: none -> 20.7 us  [body(): lax.ppermute(low, 'yl', [(k, (k + shift) % n_yl) for k in range(n_yl)])]
    all_gather x1, waiting for transfers between devices: 36.2 us -> 20.8 us  [body(): low_got = lax.all_gather(jnp.stack(low_rows), 'gy')]
    ppermute x1, starting transfers between devices: 3.77 us -> 9.38 us  [body(): tok_sib = lax.ppermute(tok_half, 'co', SWAP)]
    ppermute x0 -> x3, waiting for transfers between devices: none -> 5.46 us  [body(): lax.ppermute(low, 'yl', [(k, (k + shift) % n_yl) for k in range(n_yl)])]
    pallas_call x1 -> x2, Pallas kernels: 3.32 us -> 7.05 us  [the longest x1 4.49 us: body(): pl.pallas_call(token_products, out_shape=(jax.ShapeDtypeStruct((2 * units...]
  transfers between devices with their start and end apart: 16 -> 19, of which waited for: 6 -> 5; matrix products, arithmetic and copies ran while one was open for 12% -> 16% of each run, Pallas kernels for 0% -> 3%
where the time goes in v4:
time: 232 us; the launch traced here: 230 us
  starting transfers between devices  115 us (50%)
  waiting for transfers between devices  37.1 us (16%)
  local copies, waits for them, and re-layouts  29.8 us (13%)
  matrix products  16.8 us (7%)
  between operations  14.8 us (6%)
  other arithmetic  9.88 us (4%)
  Pallas kernels  7.05 us (3%)
    all_to_all x5, starting transfers between devices, exchange(): return lax.all_to_all(pieces, axes, 0, 0)  41.4 us
    ppermute x1, starting transfers between devices, body(): pair_terms = jnp.stack([core_terms, lax.ppermute(core_terms, 'co', SWAP)])  25 us
    all_gather x1, waiting for transfers between devices, body(): low_got = lax.all_gather(jnp.stack(low_rows), 'gy')  20.8 us
    ppermute x3, starting transfers between devices, body(): lax.ppermute(low, 'yl', [(k, (k + shift) % n_yl) for k in range(n_yl)])  20.7 us
    dot_general x13, matrix products, dot(): lax.dot_general(left, right, (((left_dim,), (right_dim,)), ((), ())), pre...  16.8 us
    all_to_all x5, waiting for transfers between devices, exchange(): return lax.all_to_all(pieces, axes, 0, 0)  10.8 us
    unnamed x73, local copies, waits for them, and re-layouts  10.4 us
    ppermute x1, starting transfers between devices, body(): tok_sib = lax.ppermute(tok_half, 'co', SWAP)  9.38 us
  transfers between devices with their start and end apart: 19, of which 5 were waited for; matrix products, arithmetic and copies ran while one was open for 16% of the time, Pallas kernels for 3%

profile of v4, /device:TPU:1, one launch (start us, length us, event | category | flops | bytes accessed | tf_op | source)
XLA Modules:
  0.0 229.9 jit_solution(5467719743846493275)
XLA Ops:
  7.2 0.7 broadcast_in_dim.74
  7.8 0.8 pad_maximum_fusion.3
  8.6 1.2 broadcast_in_dim.75
  9.8 14.4 %all-to-all-start = ((bf16[32,144,128]{2,1,0:T(8,128)(2,1)}), bf16[32,144,128]{2,1,0:T(8,128)(2,1)S(1)}, u32[]{:S(2)}, u32[]{:S(2)}) async-start(bf16[32,144,128]{2,1,0:T(8,128)(2,1)} %broadcast_in_dim.75), calls=%async_computation | async-start | bytes 2359296 | tf_op jit(solution)/shard_map/all_to_all | solution.py:18
  24.3 2.9 %collective-permute-start = (bf16[224,1024]{1,0:T(8,128)(2,1)S(1)}, bf16[224,1024]{1,0:T(8,128)(2,1)S(1)}, u32[]{:S(2)}, u32[]{:S(2)}) collective-permute-start(bf16[224,1024]{1,0:T(8,128)(2,1)S(1)} %copy-done.1), channel_id=1, source_target_pairs={{0,64},{64,0},{1,65},{65,1},{2,66},{66,2},{3,67},{67,3},{4,68},{68... | collective-permute-start | bytes 1376264 | tf_op jit(solution)/shard_map/ppermute | solution.py:99
  27.2 1.9 collective-permute-start.1
  29.1 2.4 %collective-permute-start.2 = (bf16[224,1024]{1,0:T(8,128)(2,1)}, bf16[224,1024]{1,0:T(8,128)(2,1)}, u32[]{:S(2)}, u32[]{:S(2)}) collective-permute-start(bf16[224,1024]{1,0:T(8,128)(2,1)} %refs_0_.3), channel_id=1, source_target_pairs={{0,64},{64,0},{1,65},{65,1},{2,66},{66,2},{3,67},{67,3},{4,68},{68... | collective-permute-start | bytes 1376264 | tf_op jit(solution)/shard_map/ppermute | solution.py:99
  31.5 5.3 %collective-permute-start.5 = (bf16[128,128]{1,0:T(8,128)(2,1)S(1)}, bf16[128,128]{1,0:T(8,128)(2,1)S(1)}, u32[]{:S(2)}, u32[]{:S(2)}) collective-permute-start(bf16[128,128]{1,0:T(8,128)(2,1)S(1)} %convert_element_type.104), channel_id=1, source_target_pairs={{0,384},{128,0},{256,128},{384,256},{1,385},{129,1},{257,129},{385... | collective-permute-start | bytes 98312 | tf_op jit(solution)/shard_map/ppermute | solution.py:107
  36.8 1.9 collective-permute-start.4
  38.7 4.5 %collective-permute-done.5 = bf16[128,128]{1,0:T(8,128)(2,1)S(1)} collective-permute-done((bf16[128,128]{1,0:T(8,128)(2,1)S(1)}, bf16[128,128]{1,0:T(8,128)(2,1)S(1)}, u32[]{:S(2)}, u32[]{:S(2)}) %collective-permute-start.5) | collective-permute-done | bytes 32800 | tf_op jit(solution)/shard_map/ppermute | solution.py:107
  43.2 13.5 %collective-permute-start.3 = (bf16[128,128]{1,0:T(8,128)(2,1)S(1)}, bf16[128,128]{1,0:T(8,128)(2,1)S(1)}, u32[]{:S(2)}, u32[]{:S(2)}) collective-permute-start(bf16[128,128]{1,0:T(8,128)(2,1)S(1)} %convert_element_type.104), channel_id=1, source_target_pairs={{0,128},{128,256},{256,384},{384,0},{1,129},{129,257},{257,385},{3... | collective-permute-start | bytes 98312 | tf_op jit(solution)/shard_map/ppermute | solution.py:107
  56.7 1.0 collective-permute-done.3
  57.7 0.7 pad_maximum_fusion.2
  58.4 0.8 copy-done.2
  59.2 0.8 copy-done.5
  60.0 1.0 copy-done.3
  61.0 1.0 copy-done.6
  62.0 1.0 copy-done.8
  63.0 4.5 %token_products.1 = (bf16[448,1152]{1,0:T(8,128)(2,1)S(1)}, bf16[512,1024]{1,0:T(8,128)(2,1)S(1)}, bf16[16,1024]{1,0:T(8,128)(2,1)S(1)}) custom-call(bf16[32,144,128]{2,1,0:T(8,128)(2,1)S(1)} %all-to-all-done.tok_got, bf16[224,1024]{1,0:T(8,128)(2,1)S(1)} %copy-done.1, bf16[224,1024]{1,0:T(8,128)(2,1)S(1)} %copy-done.3, bf16[224,1024]{1,0:T(8,128)(2,1)S(1)} %copy-done, ...), custom_call_target="tpu_custom_call" | custom-call | flops 1056964608 | bytes 8388608 | tf_op jit(solution)/shard_map/token_products/pallas_call | solution.py:115
  67.6 1.0 copy-done.11
  68.5 6.7 %all-to-all-start.1 = ((bf16[8,56,1152]{2,1,0:T(8,128)(2,1)}), bf16[8,56,1152]{2,1,0:T(8,128)(2,1)S(1)}, u32[]{:S(2)}, u32[]{:S(2)}) async-start(bf16[8,56,1152]{2,1,0:T(8,128)(2,1)} %bitcast.92), calls=%async_computation.1 | async-start | bytes 2064384 | tf_op jit(solution)/shard_map/all_to_all | solution.py:18
  75.2 1.3 fusion.54
  76.5 20.8 %all-gather.3.cloned.1.call-done = bf16[32,128,128]{2,1,0:T(8,128)(2,1)} async-done(((bf16[4,128,128]{2,1,0:T(8,128)(2,1)}), bf16[32,128,128]{2,1,0:T(8,128)(2,1)}) %all-gather.3.cloned.1.call-update) | async-done | bytes 1048592 | tf_op jit(solution)/shard_map/all_gather | solution.py:108
  97.4 1.2 copy-done.10
  98.6 2.6 %cotangent_products.1 = (bf16[448,512]{1,0:T(8,128)(2,1)}, bf16[512,1024]{1,0:T(8,128)(2,1)}) custom-call(s32[1]{0:T(128)} %bitcast.1.at_yl, bf16[8,4,128,128]{3,2,1,0:T(8,128)(2,1)S(1)} %bitcast.91, bf16[224,1024]{1,0:T(8,128)(2,1)S(1)} %copy-done.9, bf16[224,1024]{1,0:T(8,128)(2,1)} %collective-permute-done.2.refs_5_.refs_1_), custom_call_target="tpu_custom_call" | custom-call | flops 469762048 | bytes 5242880 | tf_op jit(solution)/shard_map/cotangent_products/pallas_call | solution.py:138
  102.4 8.8 %all-to-all-start.2 = ((bf16[8,56,512]{2,1,0:T(8,128)(2,1)}), bf16[8,56,512]{2,1,0:T(8,128)(2,1)S(1)}, u32[]{:S(2)}, u32[]{:S(2)}) async-start(bf16[8,56,512]{2,1,0:T(8,128)(2,1)} %bitcast.14), calls=%async_computation.2 | async-start | bytes 917504 | tf_op jit(solution)/shard_map/all_to_all | solution.py:18
  112.1 10.1 %all-to-all-done.2 = bf16[8,56,512]{2,1,0:T(8,128)(2,1)S(1)} async-done(((bf16[8,56,512]{2,1,0:T(8,128)(2,1)}), bf16[8,56,512]{2,1,0:T(8,128)(2,1)S(1)}, u32[]{:S(2)}, u32[]{:S(2)}) %all-to-all-start.2) | async-done | bytes 458784 | tf_op jit(solution)/shard_map/all_to_all | solution.py:18
  122.4 1.3 broadcast_in_dim.79
  123.6 4.3 %all-to-all-start.3 = ((bf16[8,176,512]{2,1,0:T(8,128)(2,1)}), bf16[8,176,512]{2,1,0:T(8,128)(2,1)}, u32[]{:S(2)}, u32[]{:S(2)}) async-start(bf16[8,176,512]{2,1,0:T(8,128)(2,1)} %broadcast_in_dim.79), calls=%async_computation.3 | async-start | bytes 2883584 | tf_op jit(solution)/shard_map/all_to_all | solution.py:18
  128.0 9.4 %collective-permute-start.8 = (bf16[512,1024]{1,0:T(8,128)(2,1)S(1)}, bf16[512,1024]{1,0:T(8,128)(2,1)S(1)}, u32[]{:S(2)}, u32[]{:S(2)}) collective-permute-start(bf16[512,1024]{1,0:T(8,128)(2,1)S(1)} %get-tuple-element.32), channel_id=1, source_target_pairs={{0,64},{64,0},{1,65},{65,1},{2,66},{66,2},{3,67},{67,3},{4,68},{68... | collective-permute-start | bytes 3145736 | tf_op jit(solution)/shard_map/ppermute | solution.py:234
  138.7 1.9 collective-permute-start.12
  141.3 0.9 copy-done.16
  142.3 0.7 all-to-all-done.3
  143.0 0.7 fusion.29
  143.8 25.0 %collective-permute-start.6 = (f32[4]{0:T(128)S(1)}, f32[4]{0:T(128)S(1)}, u32[]{:S(2)}, u32[]{:S(2)}) collective-permute-start(f32[4]{0:T(128)S(1)} %reduce_sum.97), channel_id=1, source_target_pairs={{0,64},{64,0},{1,65},{65,1},{2,66},{66,2},{3,67},{67,3},{4,68},{68... | collective-permute-start | bytes 56 | tf_op jit(solution)/shard_map/ppermute | solution.py:198
  168.8 0.9 slice_bitcast_fusion
  169.9 1.4 fusion.67
  171.3 1.4 fusion.7
  172.8 2.2 fusion.60
  175.0 0.7 fusion.66
  176.5 0.7 fusion
  178.0 1.1 pad_maximum_fusion
  179.1 7.1 %all-to-all-start.4 = ((bf16[32,136,128]{2,1,0:T(8,128)(2,1)}), bf16[32,136,128]{2,1,0:T(8,128)(2,1)S(1)}, u32[]{:S(2)}, u32[]{:S(2)}) async-start(bf16[32,136,128]{2,1,0:T(8,128)(2,1)} %pad_maximum_fusion), calls=%async_computation.4 | async-start | bytes 2228224 | tf_op jit(solution)/shard_map/all_to_all | solution.py:18
  186.3 1.7 slice.149
  188.0 2.2 collective-permute-start.7
  190.3 2.1 collective-permute-start.9
  192.4 1.6 slice.159
  194.1 2.2 collective-permute-start.10
  196.3 1.9 fusion.61
  198.1 2.3 collective-permute-start.11
  200.4 1.7 reshape.307
  202.1 1.8 slice.188
  203.9 1.1 copy.86
  205.1 1.4 fusion.68
  206.5 1.3 fusion.6
  207.8 1.4 fusion.69
  209.7 1.7 fusion.70
  211.4 2.5 %fusion.2 = f32[224,1024]{1,0:T(8,128)} fusion(f32[224,1024]{1,0:T(8,128)S(1)} %fusion.70, bf16[512,1024]{1,0:T(8,128)(2,1)} %get-tuple-element.37, bf16[448,512]{1,0:T(8,128)(2,1)S(1)} %bitcast.103), kind=kOutput, calls=%fused_computation.7 | convolution fusion | flops 235339776 | bytes 3112960 | tf_op jit(solution)/shard_map/dot_general | solution.py:26
  214.0 0.7 reshape.308
  214.7 1.1 slice.189
  218.3 0.7 fusion.25
  219.3 1.3 fusion.5
  220.6 1.3 fusion.3
  221.8 1.3 fusion.1
  (146 shorter events, 9.2 us)
Async XLA Ops:
  9.8 14.5 %copy-start.1 = (bf16[224,1024]{1,0:T(8,128)(2,1)S(1)}, bf16[224,1024]{1,0:T(8,128)(2,1)}, u32[]{:S(2)}) copy-start(bf16[224,1024]{1,0:T(8,128)(2,1)} %refs_0_.2) | copy-start | bytes 1376260
  9.8 17.4 %copy-start = (bf16[224,1024]{1,0:T(8,128)(2,1)S(1)}, bf16[224,1024]{1,0:T(8,128)(2,1)}, u32[]{:S(2)}) copy-start(bf16[224,1024]{1,0:T(8,128)(2,1)} %refs_2_.1) | copy-start | bytes 1376260
  9.8 21.7 %copy-start.25 = (f32[128,128]{1,0:T(8,128)S(1)}, f32[128,128]{1,0:T(8,128)}, u32[]{:S(2)}) copy-start(f32[128,128]{1,0:T(8,128)} %param.12) | copy-start | bytes 196612
  9.8 50.2 %all-to-all-start = ((bf16[32,144,128]{2,1,0:T(8,128)(2,1)}), bf16[32,144,128]{2,1,0:T(8,128)(2,1)S(1)}, u32[]{:S(2)}, u32[]{:S(2)}) async-start(bf16[32,144,128]{2,1,0:T(8,128)(2,1)} %broadcast_in_dim.75), calls=%async_computation | async-start | bytes 2359296 | tf_op jit(solution)/shard_map/all_to_all | solution.py:18
  24.2 73.1 %all-gather.3.cloned.1.call-start = ((), (), s32[]{:S(2)}) async-start(), calls=%async_computation.5 | async-start | bytes 1179648 | tf_op jit(solution)/shard_map/all_gather | solution.py:108
  24.3 34.2 %collective-permute-start = (bf16[224,1024]{1,0:T(8,128)(2,1)S(1)}, bf16[224,1024]{1,0:T(8,128)(2,1)S(1)}, u32[]{:S(2)}, u32[]{:S(2)}) collective-permute-start(bf16[224,1024]{1,0:T(8,128)(2,1)S(1)} %copy-done.1), channel_id=1, source_target_pairs={{0,64},{64,0},{1,65},{65,1},{2,66},{66,2},{3,67},{67,3},{4,68},{68... | collective-permute-start | bytes 1376264 | tf_op jit(solution)/shard_map/ppermute | solution.py:99
  27.2 32.1 %collective-permute-start.1 = (bf16[224,1024]{1,0:T(8,128)(2,1)S(1)}, bf16[224,1024]{1,0:T(8,128)(2,1)S(1)}, u32[]{:S(2)}, u32[]{:S(2)}) collective-permute-start(bf16[224,1024]{1,0:T(8,128)(2,1)S(1)} %copy-done), channel_id=1, source_target_pairs={{0,64},{64,0},{1,65},{65,1},{2,66},{66,2},{3,67},{67,3},{4,68},{68... | collective-permute-start | bytes 1376264 | tf_op jit(solution)/shard_map/ppermute | solution.py:99
  29.1 30.9 %collective-permute-start.2 = (bf16[224,1024]{1,0:T(8,128)(2,1)}, bf16[224,1024]{1,0:T(8,128)(2,1)}, u32[]{:S(2)}, u32[]{:S(2)}) collective-permute-start(bf16[224,1024]{1,0:T(8,128)(2,1)} %refs_0_.3), channel_id=1, source_target_pairs={{0,64},{64,0},{1,65},{65,1},{2,66},{66,2},{3,67},{67,3},{4,68},{68... | collective-permute-start | bytes 1376264 | tf_op jit(solution)/shard_map/ppermute | solution.py:99
  31.5 11.7 %collective-permute-start.5 = (bf16[128,128]{1,0:T(8,128)(2,1)S(1)}, bf16[128,128]{1,0:T(8,128)(2,1)S(1)}, u32[]{:S(2)}, u32[]{:S(2)}) collective-permute-start(bf16[128,128]{1,0:T(8,128)(2,1)S(1)} %convert_element_type.104), channel_id=1, source_target_pairs={{0,384},{128,0},{256,128},{384,256},{1,385},{129,1},{257,129},{385... | collective-permute-start | bytes 98312 | tf_op jit(solution)/shard_map/ppermute | solution.py:107
  36.8 19.9 %collective-permute-start.4 = (bf16[128,128]{1,0:T(8,128)(2,1)S(1)}, bf16[128,128]{1,0:T(8,128)(2,1)S(1)}, u32[]{:S(2)}, u32[]{:S(2)}) collective-permute-start(bf16[128,128]{1,0:T(8,128)(2,1)S(1)} %convert_element_type.104), channel_id=1, source_target_pairs={{0,256},{128,384},{256,0},{384,128},{1,257},{129,385},{257,1},{385... | collective-permute-start | bytes 98312 | tf_op jit(solution)/shard_map/ppermute | solution.py:107
  43.2 14.5 %collective-permute-start.3 = (bf16[128,128]{1,0:T(8,128)(2,1)S(1)}, bf16[128,128]{1,0:T(8,128)(2,1)S(1)}, u32[]{:S(2)}, u32[]{:S(2)}) collective-permute-start(bf16[128,128]{1,0:T(8,128)(2,1)S(1)} %convert_element_type.104), channel_id=1, source_target_pairs={{0,128},{128,256},{256,384},{384,0},{1,129},{129,257},{257,385},{3... | collective-permute-start | bytes 98312 | tf_op jit(solution)/shard_map/ppermute | solution.py:107
  58.4 0.8 copy-start.2
  59.2 0.8 copy-start.5
  60.0 1.0 copy-start.3
  61.0 1.0 copy-start.6
  62.0 1.0 copy-start.8
  67.5 1.0 copy-start.11
  68.5 28.8 %copy-start.9 = (bf16[224,1024]{1,0:T(8,128)(2,1)S(1)}, bf16[224,1024]{1,0:T(8,128)(2,1)}, u32[]{:S(2)}) copy-start(bf16[224,1024]{1,0:T(8,128)(2,1)} %refs_0_.3) | copy-start | bytes 1376260
  68.5 32.6 %all-to-all-start.1 = ((bf16[8,56,1152]{2,1,0:T(8,128)(2,1)}), bf16[8,56,1152]{2,1,0:T(8,128)(2,1)S(1)}, u32[]{:S(2)}, u32[]{:S(2)}) async-start(bf16[8,56,1152]{2,1,0:T(8,128)(2,1)} %bitcast.92), calls=%async_computation.1 | async-start | bytes 2064384 | tf_op jit(solution)/shard_map/all_to_all | solution.py:18
  97.4 1.2 copy-start.10
  102.4 19.9 %all-to-all-start.2 = ((bf16[8,56,512]{2,1,0:T(8,128)(2,1)}), bf16[8,56,512]{2,1,0:T(8,128)(2,1)S(1)}, u32[]{:S(2)}, u32[]{:S(2)}) async-start(bf16[8,56,512]{2,1,0:T(8,128)(2,1)} %bitcast.14), calls=%async_computation.2 | async-start | bytes 917504 | tf_op jit(solution)/shard_map/all_to_all | solution.py:18
  123.6 19.3 %all-to-all-start.3 = ((bf16[8,176,512]{2,1,0:T(8,128)(2,1)}), bf16[8,176,512]{2,1,0:T(8,128)(2,1)}, u32[]{:S(2)}, u32[]{:S(2)}) async-start(bf16[8,176,512]{2,1,0:T(8,128)(2,1)} %broadcast_in_dim.79), calls=%async_computation.3 | async-start | bytes 2883584 | tf_op jit(solution)/shard_map/all_to_all | solution.py:18
  127.9 10.1 %copy-start.31 = (s32[4,2]{0,1:T(2,128)S(1)}, s32[4,2]{0,1:T(2,128)}, u32[]{:S(2)}) copy-start(s32[4,2]{0,1:T(2,128)} %param.13) | copy-start | bytes 100
  127.9 10.7 %copy-start.7 = (bf16[224,1024]{1,0:T(8,128)(2,1)S(1)}, bf16[224,1024]{1,0:T(8,128)(2,1)}, u32[]{:S(2)}) copy-start(bf16[224,1024]{1,0:T(8,128)(2,1)} %copy-done.5) | copy-start | bytes 1376260
  128.0 10.7 %copy-start.4 = (bf16[224,1024]{1,0:T(8,128)(2,1)S(1)}, bf16[224,1024]{1,0:T(8,128)(2,1)}, u32[]{:S(2)}) copy-start(bf16[224,1024]{1,0:T(8,128)(2,1)} %copy-done.2) | copy-start | bytes 1376260
  128.0 13.3 %collective-permute-start.8 = (bf16[512,1024]{1,0:T(8,128)(2,1)S(1)}, bf16[512,1024]{1,0:T(8,128)(2,1)S(1)}, u32[]{:S(2)}, u32[]{:S(2)}) collective-permute-start(bf16[512,1024]{1,0:T(8,128)(2,1)S(1)} %get-tuple-element.32), channel_id=1, source_target_pairs={{0,64},{64,0},{1,65},{65,1},{2,66},{66,2},{3,67},{67,3},{4,68},{68... | collective-permute-start | bytes 3145736 | tf_op jit(solution)/shard_map/ppermute | solution.py:234
  138.7 2.6 %copy-start.12 = (bf16[448,1024]{1,0:T(8,128)(2,1)}, bf16[448,1024]{1,0:T(8,128)(2,1)S(1)}, u32[]{:S(2)}) copy-start(bf16[448,1024]{1,0:T(8,128)(2,1)S(1)} %constant_dynamic-update-slice_fusion.2) | copy-start | bytes 2752516
  138.7 2.6 %copy-start.14 = (bf16[448,1024]{1,0:T(8,128)(2,1)}, bf16[448,1024]{1,0:T(8,128)(2,1)S(1)}, u32[]{:S(2)}) copy-start(bf16[448,1024]{1,0:T(8,128)(2,1)S(1)} %constant_dynamic-update-slice_fusion) | copy-start | bytes 2752516
  138.7 71.0 %collective-permute-start.12 = (bf16[512,1024]{1,0:T(8,128)(2,1)}, bf16[512,1024]{1,0:T(8,128)(2,1)}, u32[]{:S(2)}, u32[]{:S(2)}) collective-permute-start(bf16[512,1024]{1,0:T(8,128)(2,1)} %get-tuple-element.37), channel_id=1, source_target_pairs={{0,64},{64,0},{1,65},{65,1},{2,66},{66,2},{3,67},{67,3},{4,68},{68... | collective-permute-start | bytes 3145736 | tf_op jit(solution)/shard_map/ppermute | solution.py:235
  141.3 1.0 copy-start.16
  143.8 34.0 %collective-permute-start.6 = (f32[4]{0:T(128)S(1)}, f32[4]{0:T(128)S(1)}, u32[]{:S(2)}, u32[]{:S(2)}) collective-permute-start(f32[4]{0:T(128)S(1)} %reduce_sum.97), channel_id=1, source_target_pairs={{0,64},{64,0},{1,65},{65,1},{2,66},{66,2},{3,67},{67,3},{4,68},{68... | collective-permute-start | bytes 56 | tf_op jit(solution)/shard_map/ppermute | solution.py:198
  172.7 2.3 copy-start.13
  175.0 0.8 copy-start.20
  175.0 0.9 copy-start.18
  175.0 1.5 copy-start.15
  179.1 36.9 %all-to-all-start.4 = ((bf16[32,136,128]{2,1,0:T(8,128)(2,1)}), bf16[32,136,128]{2,1,0:T(8,128)(2,1)S(1)}, u32[]{:S(2)}, u32[]{:S(2)}) async-start(bf16[32,136,128]{2,1,0:T(8,128)(2,1)} %pad_maximum_fusion), calls=%async_computation.4 | async-start | bytes 2228224 | tf_op jit(solution)/shard_map/all_to_all | solution.py:18
  186.3 18.8 %copy-start.17 = (bf16[512,1024]{1,0:T(8,128)(2,1)S(1)}, bf16[512,1024]{1,0:T(8,128)(2,1)}, u32[]{:S(2)}) copy-start(bf16[512,1024]{1,0:T(8,128)(2,1)} %copy-done.16) | copy-start | bytes 3145732
  188.0 17.1 %collective-permute-start.7 = (bf16[224,512]{1,0:T(8,128)(2,1)}, bf16[224,512]{1,0:T(8,128)(2,1)}, u32[]{:S(2)}, u32[]{:S(2)}) collective-permute-start(bf16[224,512]{1,0:T(8,128)(2,1)} %slice.149), channel_id=1, source_target_pairs={{0,64},{64,0},{1,65},{65,1},{2,66},{66,2},{3,67},{67,3},{4,68},{68... | collective-permute-start | bytes 688136 | tf_op jit(solution)/shard_map/ppermute | solution.py:248
  190.3 14.8 %collective-permute-start.9 = (bf16[8,224]{1,0:T(8,128)(2,1)S(1)}, bf16[8,224]{1,0:T(8,128)(2,1)S(1)}, u32[]{:S(2)}, u32[]{:S(2)}) collective-permute-start(bf16[8,224]{1,0:T(8,128)(2,1)S(1)} %pad_maximum_fusion.4), channel_id=1, source_target_pairs={{0,64},{64,0},{1,65},{65,1},{2,66},{66,2},{3,67},{67,3},{4,68},{68... | collective-permute-start | bytes 10760 | tf_op jit(solution)/shard_map/ppermute | solution.py:236
  194.1 13.8 %collective-permute-start.10 = (bf16[224,512]{1,0:T(8,128)(2,1)}, bf16[224,512]{1,0:T(8,128)(2,1)}, u32[]{:S(2)}, u32[]{:S(2)}) collective-permute-start(bf16[224,512]{1,0:T(8,128)(2,1)} %slice.159), channel_id=1, source_target_pairs={{0,64},{64,0},{1,65},{65,1},{2,66},{66,2},{3,67},{67,3},{4,68},{68... | collective-permute-start | bytes 688136 | tf_op jit(solution)/shard_map/ppermute | solution.py:248
  198.1 11.6 %collective-permute-start.11 = (bf16[224,512]{1,0:T(8,128)(2,1)}, bf16[224,512]{1,0:T(8,128)(2,1)S(1)}, u32[]{:S(2)}, u32[]{:S(2)}) collective-permute-start(bf16[224,512]{1,0:T(8,128)(2,1)} %get-tuple-element.47), channel_id=1, source_target_pairs={{0,64},{64,0},{1,65},{65,1},{2,66},{66,2},{3,67},{67,3},{4,68},{68... | collective-permute-start | bytes 688136 | tf_op jit(solution)/shard_map/ppermute | solution.py:248
  205.1 1.4 copy-start.19
  207.8 1.4 copy-start.21
  209.7 1.7 copy-start.24
  213.9 2.7 %copy-start.27 = (s32[4]{0:T(128)S(1)}, s32[4]{0:T(128)}, u32[]{:S(2)}) copy-start(s32[4]{0:T(128)} %get-tuple-element.61) | copy-start | bytes 52
  214.0 2.7 %copy-start.28 = (s32[4]{0:T(128)S(1)}, s32[4]{0:T(128)}, u32[]{:S(2)}) copy-start(s32[4]{0:T(128)} %get-tuple-element.62) | copy-start | bytes 52
  214.0 3.6 %copy-start.29 = (bf16[128]{0:T(256)(128)(2,1)S(1)}, bf16[128]{0:T(256)(128)(2,1)}, u32[]{:S(2)}) copy-start(bf16[128]{0:T(256)(128)(2,1)} %param.11) | copy-start | bytes 772
  214.0 4.4 %copy-start.32 = (pred[128]{0:T(512)(128)(4,1)S(1)}, pred[128]{0:T(512)(128)(4,1)}, u32[]{:S(2)}) copy-start(pred[128]{0:T(512)(128)(4,1)} %iota_compare_fusion.8) | copy-start | bytes 388
  214.0 5.3 %copy-start.22 = (f32[224,1024]{1,0:T(8,128)S(1)}, f32[224,1024]{1,0:T(8,128)}, u32[]{:S(2)}) copy-start(f32[224,1024]{1,0:T(8,128)} %fusion.6) | copy-start | bytes 2752516
  216.6 5.2 %copy-start.30 = (f32[8]{0:T(128)}, f32[8]{0:T(128)S(1)}, u32[]{:S(2)}) copy-start(f32[8]{0:T(128)S(1)} %compare_select_fusion) | copy-start | bytes 100
  219.3 2.5 %copy-start.23 = (f32[224,1024]{1,0:T(8,128)S(1)}, f32[224,1024]{1,0:T(8,128)}, u32[]{:S(2)}) copy-start(f32[224,1024]{1,0:T(8,128)} %fusion.2) | copy-start | bytes 2752516
  219.3 2.5 %copy-start.26 = (f32[1,1024]{1,0:T(1,128)S(1)}, f32[1,1024]{1,0:T(1,128)}, u32[]{:S(2)}) copy-start(f32[1,1024]{1,0:T(1,128)} %slice_convert_fusion.1) | copy-start | bytes 12292
Sparse Core Ops, SparseCore 0:
  58.5 38.7 all-gather.2

commit v5 on v4

--- a/solution.py
+++ b/solution.py
@@ -34,21 +34,12 @@
     return jnp.stack([high, middle, value - high - middle]).astype(bf16)
 
 
-def load(sources, held, sems):
-    copies = [pltpu.make_async_copy(src, held.at[i], sems.at[i]) for i, src in enumerate(sources)]
-    for copy in copies:
-        copy.start()
-    return copies
-
-
-def token_products(tok_got, *refs):
-    weights, (parts, tok, head, held, wide_head, sems) = refs[:6], refs[6:]
-    copies = load(weights, held, sems)
+def token_products(tok_got, gate_w, up_w, down_w, parts, tok, head, wide_head):
     width, cols = tok.shape[1], tok_got.shape[2]
     n_gy = width // cols
     n_yl = tok_got.shape[0] // n_gy
     rows = tok.shape[0] // n_yl
-    units, half = weights[0].shape[0], tok.shape[0]
+    chip_units, half = down_w.shape[0], tok.shape[0]
     for z in range(n_gy):
         at = slice(z * cols, (z + 1) * cols)
         for y in range(n_yl):
@@ -56,35 +47,52 @@
         head[:, at] = tok_got[z, rows:]
         for r in range(0, 128, 16):
             wide_head[r : r + 16, at] = tok_got[z, rows:]
-    for i in range(6):
-        copies[i].wait()
-        here = slice(i % 2 * units, (i % 2 + 1) * units)
-        if i < 4:
-            at = slice(i // 2 * half, (i // 2 + 1) * half)
-            parts[here, at] = dot(held[i], tok[...], 1, 1).astype(bf16)
-        else:
-            v = dot(held[i], wide_head[...], 1, 1)
-            high = v.astype(bf16).astype(f32)
-            lane = lax.broadcasted_iota(jnp.int32, v.shape, 1)
-            v = jnp.where(lane == 0, high, jnp.where(lane == 1, v - high, 0.0))
-            parts[here, 2 * half :] = v.astype(bf16)
-
-
-def cotangent_products(at_yl, low_got, *refs):
-    weights, (parts, low, held, low_held, sems) = refs[:2], refs[2:]
-    copies = load(weights, held, sems)
-    arrival = pltpu.make_async_copy(low_got, low_held, sems.at[2])
-    arrival.start()
-    arrival.wait()
-    n_gy, n_yl, rows, cols = low_held.shape
-    units = weights[0].shape[0]
-    for shift in range(n_yl):
-        first = pl.multiple_of(lax.rem(at_yl[0] + (n_yl - shift), n_yl) * rows, rows)
+    parts[:, :half] = dot(gate_w[:chip_units], tok[...], 1, 1).astype(bf16)
+    parts[:, half : 2 * half] = dot(up_w[:chip_units], tok[...], 1, 1).astype(bf16)
+    v = dot(down_w[...], wide_head[...], 1, 1)
+    high = v.astype(bf16).astype(f32)
+    lane = lax.broadcasted_iota(jnp.int32, v.shape, 1)
+    v = jnp.where(lane == 0, high, jnp.where(lane == 1, v - high, 0.0))
+    parts[:, 2 * half :] = v.astype(bf16)
+
+
+def cotangent_products(low_got, down_w, parts, low):
+    n_gy, n_yl, rows, cols = low_got.shape
+    for y in range(n_yl):
         for z in range(n_gy):
-            low[pl.ds(first, rows), z * cols : (z + 1) * cols] = low_held[z, shift]
+            low[y * rows : (y + 1) * rows, z * cols : (z + 1) * cols] = low_got[z, y]
+    parts[...] = dot(down_w[...], low[...], 1, 1).astype(bf16)
+
+
+def token_gradients(everyone, gate_w, up_w, sent, full):
+    width = gate_w.shape[1]
+    n_gz, n_rows, half = everyone.shape
+    own = (n_rows - 8) // 3
+    n_plane, piece_rows, cols = sent.shape
+    n_gy, rows = width // cols, piece_rows - 16
+    unit = jnp.zeros((8, half), f32)
+    for j in range(n_gz):
+        block = everyone[j].astype(f32)
+        for i in range(2):
+            full[i, j * own : (j + 1) * own] = block[i * own : (i + 1) * own]
+        unit += block[3 * own :]
     for i in range(2):
-        copies[i].wait()
-        parts[i * units : (i + 1) * units, :] = dot(held[i], low[...], 1, 1).astype(bf16)
+        full[i, n_gz * own :] = jnp.zeros((full.shape[1] - n_gz * own, half), f32)
+    unit = unit.astype(bf16)
+    gate_t, up_t = (full[i].T.astype(bf16) for i in range(2))
+    step = 2 * cols
+    for c in range(0, width, step):
+        part = dot(gate_t, gate_w[:, c : c + step], 1, 0) + dot(up_t, up_w[:, c : c + step], 1, 0)
+        units_here = (
+            dot(unit, gate_w[:, c : c + step], 1, 0)[:4] + dot(unit, up_w[:, c : c + step], 1, 0)[4:]
+        )
+        for z in range(c // cols, (c + step) // cols):
+            at = slice(z * cols - c, (z + 1) * cols - c)
+            for y in range(n_plane // n_gy):
+                piece = y * n_gy + z
+                sent[piece, :rows] = part[y * rows : (y + 1) * rows, at].astype(bf16)
+                row = lax.broadcasted_iota(jnp.int32, (16, cols), 0)
+                sent[piece, rows:] = jnp.where(row == 0, units_here[y : y + 1, at], 0.0).astype(bf16)
 
 
 def body(tokens, gate_weight, up_weight, down_weight, reward_head, lm_grad, pair_index):
@@ -95,22 +103,23 @@
     my_seq = lax.axis_index(("yl", "co"))
     core = lax.axis_index("co")
 
-    def chip_block(weight):
-        return weight, lax.ppermute(weight, "co", SWAP)
-
-    gate_ws, up_ws, down_ws = chip_block(gate_weight), chip_block(up_weight), chip_block(down_weight)
-    gate_w, up_w = jnp.concatenate(gate_ws, axis=0), jnp.concatenate(up_ws, axis=0)
-
-    low = lm_grad.astype(bf16)
-    low_rows = [low]
-    for shift in range(1, n_yl):
-        low_rows.append(lax.ppermute(low, "yl", [(k, (k + shift) % n_yl) for k in range(n_yl)]))
-    low_got = lax.all_gather(jnp.stack(low_rows), "gy")
+    def chip_block(weight, padding):
+        parts = [weight, lax.ppermute(weight, "co", SWAP), jnp.zeros((padding, width), bf16)]
+        return jnp.concatenate(parts, axis=0)
+
+    padding = -2 * units % 128
+    gate_w, up_w = chip_block(gate_weight, padding), chip_block(up_weight, padding)
+    down_w = chip_block(down_weight, 0)
+
+    low_got = to_all(lm_grad.astype(bf16), "yl", n_yl)
     head_rows = jnp.broadcast_to(reward_head[None, :], (16, cols))
-    tok_got = to_all(jnp.concatenate([tokens, head_rows], axis=0), PLANE, n_plane)
+    tok_block = jnp.concatenate([tokens, head_rows], axis=0)
+    low_got, tok_block = lax.optimization_barrier((low_got, tok_block))
+    low_got = lax.all_gather(low_got, "gy")
+    tok_got = to_all(tok_block, PLANE, n_plane)
 
     half, own = n_yl * rows, 2 * units // n_gz
-    whole, apart = pl.BlockSpec(memory_space=pltpu.VMEM), pl.BlockSpec(memory_space=pl.ANY)
+    whole = pl.BlockSpec(memory_space=pltpu.VMEM)
     grant = pltpu.CompilerParams(vmem_limit_bytes=40 * 2**20)
     parts, tok_half, head_vec = pl.pallas_call(
         token_products,
@@ -119,19 +128,15 @@
             jax.ShapeDtypeStruct((half, width), bf16),
             jax.ShapeDtypeStruct((16, width), bf16),
         ),
-        in_specs=[whole] + [apart] * 6,
+        in_specs=[whole] * 4,
         out_specs=(whole,) * 3,
-        scratch_shapes=[
-            pltpu.VMEM((6, units, width), bf16),
-            pltpu.VMEM((128, width), bf16),
-            pltpu.SemaphoreType.DMA((6,)),
-        ],
+        scratch_shapes=[pltpu.VMEM((128, width), bf16)],
         compiler_params=grant,
         cost_estimate=pl.CostEstimate(
             flops=4 * units * width * (2 * half + 128), bytes_accessed=8 * 2**20, transcendentals=0
         ),
         name="token_products",
-    )(tok_got, *gate_ws, *up_ws, *down_ws)
+    )(tok_got, gate_w, up_w, down_w)
     head_vec = head_vec[:1]
     first = exchange(parts.reshape(n_gz, own, 2 * half + 128), GZ)
 
@@ -141,19 +146,14 @@
             jax.ShapeDtypeStruct((2 * units, half), bf16),
             jax.ShapeDtypeStruct((half, width), bf16),
         ),
-        in_specs=[pl.BlockSpec(memory_space=pltpu.SMEM)] + [apart] * 3,
+        in_specs=[whole] * 2,
         out_specs=(whole,) * 2,
-        scratch_shapes=[
-            pltpu.VMEM((2, units, width), bf16),
-            pltpu.VMEM((n_gy, n_yl, rows, cols), bf16),
-            pltpu.SemaphoreType.DMA((3,)),
-        ],
         compiler_params=grant,
         cost_estimate=pl.CostEstimate(
             flops=4 * units * width * half, bytes_accessed=5 * 2**20, transcendentals=0
         ),
         name="cotangent_products",
-    )(lax.axis_index("yl").astype(jnp.int32)[None], low_got, *down_ws)
+    )(low_got, down_w)
     first, back_parts = lax.optimization_barrier((first, back_parts))
     second = exchange(back_parts.reshape(n_gz, own, half), GZ)
 
@@ -173,43 +173,47 @@
     own_term = jnp.sum(tokens[rows - 1].astype(f32) * reward_head.astype(f32))
     terms = jnp.sum(last_cols(hidden) * head_down, axis=0)
     terms = terms + jnp.where(jnp.arange(n_yl) == lax.axis_index("yl"), own_term, 0.0)
-    unit_rows = jnp.concatenate(
-        [jnp.pad(gate_unit, ((0, 0), (0, 128 - own))), jnp.pad(up_unit, ((0, 0), (0, half - 128 - own)))], axis=1
-    )
-    term_rows = jnp.pad(pieces(terms).reshape(1, -1), ((0, 7 - n_yl), (0, half - 3 * n_yl)))
+    unit_rows = lax.dynamic_update_slice(
+        jnp.zeros((2 * n_yl, half), bf16),
+        jnp.concatenate([gate_unit, up_unit], axis=0),
+        (0, lax.axis_index(GZ) * own),
+    )
+    term_rows = pieces(terms).reshape(1, -1)
+    unit_rows = lax.dynamic_update_slice(unit_rows, term_rows, (0, 2 * units))
     silu_gate, gate_slope, early, second = lax.optimization_barrier(
-        (silu_gate, gate_slope, jnp.concatenate([hidden, unit_rows, term_rows], axis=0), second)
+        (silu_gate, gate_slope, jnp.concatenate([hidden, unit_rows], axis=0), second)
     )
     hidden_grad = jnp.sum(second.astype(f32), axis=0)
     up_grad = (hidden_grad * silu_gate).astype(bf16)
     gate_grad = (hidden_grad * gate_slope).astype(bf16)
     mine = jnp.concatenate([gate_grad, up_grad, early], axis=0)
     everyone = to_all(mine, GZ, n_gz)
+    core_terms = jnp.sum(
+        everyone[:, 3 * own, 2 * units : 2 * units + 3 * n_yl].astype(f32).reshape(n_gz * 3, n_yl), axis=0
+    )
+    pair_terms = jnp.stack([core_terms, lax.ppermute(core_terms, "co", SWAP)])
+    sent = pl.pallas_call(
+        token_gradients,
+        out_shape=jax.ShapeDtypeStruct((n_plane, rows + 16, cols), bf16),
+        in_specs=[whole] * 3,
+        out_specs=whole,
+        scratch_shapes=[pltpu.VMEM((2, 2 * units + padding, half), f32)],
+        compiler_params=grant,
+        cost_estimate=pl.CostEstimate(
+            flops=8 * units * width * half, bytes_accessed=5 * 2**20, transcendentals=0
+        ),
+        name="token_gradients",
+    )(everyone, gate_w, up_w)
+    term_row = pieces(pair_terms).reshape(1, 1, 6 * n_yl)
+    sent = lax.dynamic_update_slice(
+        sent, jnp.broadcast_to(term_row, (n_plane, 1, 6 * n_yl)), (0, rows + 1, 0)
+    )
+    sent, everyone = lax.optimization_barrier((sent, everyone))
     gate_g, up_g, hid = (
         everyone[:, i * own : (i + 1) * own].reshape(2 * units, half) for i in range(3)
     )
-    units_at = everyone[:, 3 * own : 3 * own + n_yl].transpose(1, 0, 2)
-    gate_u, up_u = (
-        units_at[:, :, i * 128 : i * 128 + own].reshape(n_yl, 2 * units) for i in range(2)
-    )
-    core_terms = jnp.sum(
-        everyone[:, 3 * own + n_yl, : 3 * n_yl].astype(f32).reshape(n_gz * 3, n_yl), axis=0
-    )
-    pair_terms = jnp.stack([core_terms, lax.ppermute(core_terms, "co", SWAP)])
-
-    token_part = dot(gate_g, gate_w, 0, 0) + dot(up_g, up_w, 0, 0)
-    token_part = token_part.astype(bf16).reshape(n_yl, rows, n_gy, cols).transpose(0, 2, 1, 3)
-    unit_part = (dot(gate_u, gate_w, 1, 0) + dot(up_u, up_w, 1, 0)).astype(bf16)
-    term_row = jnp.pad(pieces(pair_terms).reshape(1, 1, -1), ((0, 0), (0, 0), (0, cols - 6 * n_yl)))
-    extra = jnp.concatenate(
-        [unit_part.reshape(n_plane, 1, cols), jnp.broadcast_to(term_row, (n_plane, 1, cols))], axis=1
-    )
-    sent = jnp.concatenate(
-        [token_part.reshape(n_plane, rows, cols), jnp.pad(extra, ((0, 0), (0, 6), (0, 0)))], axis=1
-    )
-    sent, gate_g, up_g, hid, gate_u, up_u = lax.optimization_barrier(
-        (sent, gate_g, up_g, hid, gate_u, up_u)
-    )
+    units_at = jnp.sum(everyone[:, 3 * own :, : 2 * units].astype(f32), axis=0).astype(bf16)
+    gate_u, up_u = units_at[:n_yl], units_at[n_yl:]
     token_sum = jnp.sum(exchange(sent, PLANE).astype(f32), axis=0)
 
     both = jnp.sum(token_sum[rows + 1, : 6 * n_yl].reshape(3, 2, n_yl), axis=0)

time: 232 us -> 225 us (0.970)
  waiting for transfers between devices: 37.1 us -> 53.4 us
  local copies, waits for them, and re-layouts: 29.8 us -> 18.9 us
  starting transfers between devices: 115 us -> 106 us
  matrix products: 16.8 us -> 10 us
  other arithmetic: 9.88 us -> 14.9 us
    all_to_all x5 -> x6, waiting for transfers between devices: 10.8 us -> 46.8 us  [exchange(): return lax.all_to_all(pieces, axes, 0, 0)]
    ppermute x6 -> x3, starting transfers between devices: 27.9 us -> 7.9 us  [chip_block(): lax.ppermute(weight, 'co', SWAP)]
    all_to_all x5 -> x6, starting transfers between devices: 41.4 us -> 58.1 us  [exchange(): return lax.all_to_all(pieces, axes, 0, 0)]
    all_gather x1, waiting for transfers between devices: 20.8 us -> 5.19 us  [body(): low_got = lax.all_gather(low_got, 'gy')]
    ppermute x1, starting transfers between devices: 25 us -> 14.3 us  [body(): pair_terms = jnp.stack([core_terms, lax.ppermute(core_terms, 'co', SWAP)])]
    dot_general x13 -> x9, matrix products: 16.8 us -> 10 us  [dot(): lax.dot_general(left, right, (((left_dim,), (right_dim,)), ((), ())), pre...]
    slice x6 -> x0, local copies, waits for them, and re-layouts: 5.62 us -> none  [the longest x2 3.37 us: weight_grad(): from_sib = lax.ppermute(full[units:], 'co', SWAP)]
    ppermute x1, starting transfers between devices: 9.38 us -> 14.8 us  [body(): tok_sib = lax.ppermute(tok_half, 'co', SWAP)]
  transfers between devices with their start and end apart: 19 -> 17, of which waited for: 5 -> 7; matrix products, arithmetic and copies ran while one was open for 16% -> 10% of each run, Pallas kernels for 3% -> 3%
where the time goes in v5:
time: 225 us; the launch traced here: 224 us
  starting transfers between devices  106 us (47%)
  waiting for transfers between devices  53.4 us (24%)
  local copies, waits for them, and re-layouts  18.9 us (8%)
  other arithmetic  14.9 us (7%)
  between operations  14.7 us (7%)
  matrix products  10 us (4%)
  Pallas kernels  5.73 us (3%)
    all_to_all x6, starting transfers between devices, exchange(): return lax.all_to_all(pieces, axes, 0, 0)  58.1 us
    all_to_all x6, waiting for transfers between devices, exchange(): return lax.all_to_all(pieces, axes, 0, 0)  46.8 us
    ppermute x1, starting transfers between devices, body(): tok_sib = lax.ppermute(tok_half, 'co', SWAP)  14.8 us
    ppermute x1, starting transfers between devices, body(): pair_terms = jnp.stack([core_terms, lax.ppermute(core_terms, 'co', SWAP)])  14.3 us
    dot_general x9, matrix products, dot(): lax.dot_general(left, right, (((left_dim,), (right_dim,)), ((), ())), pre...  10 us
    ppermute x3, starting transfers between devices, chip_block(): lax.ppermute(weight, 'co', SWAP)  7.9 us
    ppermute x3, starting transfers between devices, weight_grad(): from_sib = lax.ppermute(full[units:], 'co', SWAP)  6.69 us
    unnamed x59, local copies, waits for them, and re-layouts  6.45 us
  transfers between devices with their start and end apart: 17, of which 7 were waited for; matrix products, arithmetic and copies ran while one was open for 10% of the time, Pallas kernels for 3%

profile of v5, /device:TPU:1, one launch (start us, length us, event | category | flops | bytes accessed | tf_op | source)
XLA Modules:
  0.0 223.5 jit_solution(1881370186432423075)
XLA Ops:
  7.2 0.8 convert_element_type.87
  8.0 0.7 broadcast_in_dim.48
  8.7 5.4 %all-to-all-start = ((bf16[4,128,128]{2,1,0:T(8,128)(2,1)}), bf16[4,128,128]{2,1,0:T(8,128)(2,1)S(1)}, u32[]{:S(2)}, u32[]{:S(2)}) async-start(bf16[4,128,128]{2,1,0:T(8,128)(2,1)} %broadcast_in_dim.48), calls=%async_computation | async-start | bytes 262144 | tf_op jit(solution)/shard_map/all_to_all | solution.py:18
  14.1 0.7 broadcast_in_dim.49
  14.8 0.8 pad_maximum_fusion.2
  15.5 3.4 %all-to-all-done = bf16[4,128,128]{2,1,0:T(8,128)(2,1)S(1)} async-done(((bf16[4,128,128]{2,1,0:T(8,128)(2,1)}), bf16[4,128,128]{2,1,0:T(8,128)(2,1)S(1)}, u32[]{:S(2)}, u32[]{:S(2)}) %all-to-all-start) | async-done | bytes 131104 | tf_op jit(solution)/shard_map/all_to_all | solution.py:18
  18.9 1.2 broadcast_in_dim.80
  20.1 12.6 %all-to-all-start.1 = ((bf16[32,144,128]{2,1,0:T(8,128)(2,1)}), bf16[32,144,128]{2,1,0:T(8,128)(2,1)}, u32[]{:S(2)}, u32[]{:S(2)}) async-start(bf16[32,144,128]{2,1,0:T(8,128)(2,1)} %broadcast_in_dim.80), calls=%async_computation.1 | async-start | bytes 2359296 | tf_op jit(solution)/shard_map/all_to_all | solution.py:18
  32.7 3.6 %collective-permute-start.2 = (bf16[224,1024]{1,0:T(8,128)(2,1)S(1)}, bf16[224,1024]{1,0:T(8,128)(2,1)S(1)}, u32[]{:S(2)}, u32[]{:S(2)}) collective-permute-start(bf16[224,1024]{1,0:T(8,128)(2,1)S(1)} %copy-done.13), channel_id=1, source_target_pairs={{0,64},{64,0},{1,65},{65,1},{2,66},{66,2},{3,67},{67,3},{4,68},{68... | collective-permute-start | bytes 1376264 | tf_op jit(solution)/shard_map/ppermute | solution.py:107
  36.3 1.9 collective-permute-start.1
  38.2 2.4 %collective-permute-start = (bf16[224,1024]{1,0:T(8,128)(2,1)S(1)}, bf16[224,1024]{1,0:T(8,128)(2,1)}, u32[]{:S(2)}, u32[]{:S(2)}) collective-permute-start(bf16[224,1024]{1,0:T(8,128)(2,1)S(1)} %copy-done.16), channel_id=1, source_target_pairs={{0,64},{64,0},{1,65},{65,1},{2,66},{66,2},{3,67},{67,3},{4,68},{68... | collective-permute-start | bytes 1376264 | tf_op jit(solution)/shard_map/ppermute | solution.py:107
  40.9 1.3 collective-permute-done
  42.2 1.7 maximum_maximum_fusion.1
  43.9 17.1 %all-to-all-done.1.tok_got = bf16[32,144,128]{2,1,0:T(8,128)(2,1)} async-done(((bf16[32,144,128]{2,1,0:T(8,128)(2,1)}), bf16[32,144,128]{2,1,0:T(8,128)(2,1)}, u32[]{:S(2)}, u32[]{:S(2)}) %all-to-all-start.1) | async-done | bytes 1179680 | tf_op jit(solution)/shard_map/all_to_all | solution.py:18
  61.0 2.7 %token_products.1 = (bf16[448,1152]{1,0:T(8,128)(2,1)S(1)}, bf16[512,1024]{1,0:T(8,128)(2,1)S(1)}, bf16[16,1024]{1,0:T(8,128)(2,1)S(1)}) custom-call(bf16[32,144,128]{2,1,0:T(8,128)(2,1)} %all-to-all-done.1.tok_got, bf16[512,1024]{1,0:T(8,128)(2,1)S(1)} %get-tuple-element.62.gate_w, bf16[512,1024]{1,0:T(8,128)(2,1)S(1)} %get-tuple-element.61.up_w, ...), custom_call_target="tpu_custom_call" | custom-call | flops 1056964608 | bytes 8388608 | tf_op jit(solution)/shard_map/token_products/pallas_call | solution.py:124
  63.7 1.0 copy-done.1
  64.7 1.0 copy-done.6
  65.7 0.6 copy-done.7
  66.3 7.9 %all-to-all-start.2 = ((bf16[8,56,1152]{2,1,0:T(8,128)(2,1)}), bf16[8,56,1152]{2,1,0:T(8,128)(2,1)}, u32[]{:S(2)}, u32[]{:S(2)}) async-start(bf16[8,56,1152]{2,1,0:T(8,128)(2,1)} %bitcast.73), calls=%async_computation.2 | async-start | bytes 2064384 | tf_op jit(solution)/shard_map/all_to_all | solution.py:18
  74.2 1.3 fusion.36
  75.5 5.2 %all-gather.3.cloned.1.call-done = bf16[32,128,128]{2,1,0:T(8,128)(2,1)} async-done(((bf16[4,128,128]{2,1,0:T(8,128)(2,1)}), bf16[32,128,128]{2,1,0:T(8,128)(2,1)}) %all-gather.3.cloned.1.call-update) | async-done | bytes 1048592 | tf_op jit(solution)/shard_map/all_gather | solution.py:118
  80.7 1.2 copy-done.5
  81.9 1.5 cotangent_products.1
  83.4 1.0 copy-done.3
  84.4 3.1 %all-to-all-done.2 = bf16[8,56,1152]{2,1,0:T(8,128)(2,1)} async-done(((bf16[8,56,1152]{2,1,0:T(8,128)(2,1)}), bf16[8,56,1152]{2,1,0:T(8,128)(2,1)}, u32[]{:S(2)}, u32[]{:S(2)}) %all-to-all-start.2) | async-done | bytes 1032224 | tf_op jit(solution)/shard_map/all_to_all | solution.py:18
  87.6 1.4 convert_reduce_fusion.1
  90.0 6.8 %all-to-all-start.3 = ((bf16[8,56,512]{2,1,0:T(8,128)(2,1)}), bf16[8,56,512]{2,1,0:T(8,128)(2,1)S(1)}, u32[]{:S(2)}, u32[]{:S(2)}) async-start(bf16[8,56,512]{2,1,0:T(8,128)(2,1)} %bitcast.9), calls=%async_computation.3 | async-start | bytes 917504 | tf_op jit(solution)/shard_map/all_to_all | solution.py:18
  96.9 0.7 reduce-precision_convert_fusion.3
  98.2 9.4 %all-to-all-done.3 = bf16[8,56,512]{2,1,0:T(8,128)(2,1)S(1)} async-done(((bf16[8,56,512]{2,1,0:T(8,128)(2,1)}), bf16[8,56,512]{2,1,0:T(8,128)(2,1)S(1)}, u32[]{:S(2)}, u32[]{:S(2)}) %all-to-all-start.3) | async-done | bytes 458784 | tf_op jit(solution)/shard_map/all_to_all | solution.py:18
  107.7 1.2 broadcast_in_dim.84
  108.9 6.7 %all-to-all-start.4 = ((bf16[8,176,512]{2,1,0:T(8,128)(2,1)}), bf16[8,176,512]{2,1,0:T(8,128)(2,1)S(1)}, u32[]{:S(2)}, u32[]{:S(2)}) async-start(bf16[8,176,512]{2,1,0:T(8,128)(2,1)} %broadcast_in_dim.84), calls=%async_computation.4 | async-start | bytes 2883584 | tf_op jit(solution)/shard_map/all_to_all | solution.py:18
  115.6 14.8 %collective-permute-start.5 = (bf16[512,1024]{1,0:T(8,128)(2,1)}, bf16[512,1024]{1,0:T(8,128)(2,1)}, u32[]{:S(2)}, u32[]{:S(2)}) collective-permute-start(bf16[512,1024]{1,0:T(8,128)(2,1)} %copy-done.1), channel_id=1, source_target_pairs={{0,64},{64,0},{1,65},{65,1},{2,66},{66,2},{3,67},{67,3},{4,68},{68... | collective-permute-start | bytes 3145736 | tf_op jit(solution)/shard_map/ppermute | solution.py:238
  130.4 0.6 iota_compare_fusion.2
  131.0 0.6 slice_bitcast_fusion.4
  131.6 1.9 collective-permute-start.9
  133.5 0.9 slice.194
  134.4 1.3 slice_convert_fusion.1
  135.7 0.9 slice.195
  136.6 0.7 fusion.11
  137.3 1.4 reshape.285
  138.6 1.2 reduce_sum.109
  139.9 14.3 %collective-permute-start.3 = (f32[4]{0:T(128)}, f32[4]{0:T(128)S(1)}, u32[]{:S(2)}, u32[]{:S(2)}) collective-permute-start(f32[4]{0:T(128)} %reduce_sum.109), channel_id=1, source_target_pairs={{0,64},{64,0},{1,65},{65,1},{2,66},{66,2},{3,67},{67,3},{4,68},{68... | collective-permute-start | bytes 56 | tf_op jit(solution)/shard_map/ppermute | solution.py:194
  154.2 1.5 token_gradients.1
  155.7 1.0 copy-done
  156.9 1.7 dynamic_update_slice.11
  158.6 18.7 %all-to-all-start.5 = ((bf16[32,144,128]{2,1,0:T(8,128)(2,1)}), bf16[32,144,128]{2,1,0:T(8,128)(2,1)}, u32[]{:S(2)}, u32[]{:S(2)}) async-start(bf16[32,144,128]{2,1,0:T(8,128)(2,1)} %dynamic_update_slice.11), calls=%async_computation.5 | async-start | bytes 2359296 | tf_op jit(solution)/shard_map/all_to_all | solution.py:18
  177.3 1.0 fusion.41
  178.3 2.2 collective-permute-start.4
  180.6 2.1 collective-permute-start.6
  182.7 2.2 collective-permute-start.7
  184.9 2.3 %collective-permute-start.8 = (bf16[224,512]{1,0:T(8,128)(2,1)}, bf16[224,512]{1,0:T(8,128)(2,1)S(1)}, u32[]{:S(2)}, u32[]{:S(2)}) collective-permute-start(bf16[224,512]{1,0:T(8,128)(2,1)} %bitcast.26), channel_id=1, source_target_pairs={{0,64},{64,0},{1,65},{65,1},{2,66},{66,2},{3,67},{67,3},{4,68},{68... | collective-permute-start | bytes 688136 | tf_op jit(solution)/shard_map/ppermute | solution.py:252
  187.7 1.6 fusion.44
  189.4 0.4 fusion.5
  189.8 1.7 fusion.45
  191.5 0.4 fusion.3
  191.9 1.7 fusion.46
  194.6 13.8 %all-to-all-done.5 = bf16[32,144,128]{2,1,0:T(8,128)(2,1)} async-done(((bf16[32,144,128]{2,1,0:T(8,128)(2,1)}), bf16[32,144,128]{2,1,0:T(8,128)(2,1)}, u32[]{:S(2)}, u32[]{:S(2)}) %all-to-all-start.5) | async-done | bytes 1179680 | tf_op jit(solution)/shard_map/all_to_all | solution.py:18
  208.3 1.4 convert_reduce_fusion
  210.6 0.6 broadcast_multiply_fusion
  211.2 0.6 fusion.35
  211.9 0.7 fusion.7
  212.9 1.3 fusion.4
  214.2 1.3 fusion.2
  215.4 1.3 fusion
  (118 shorter events, 4.7 us)
Async XLA Ops:
  8.7 10.2 %all-to-all-start = ((bf16[4,128,128]{2,1,0:T(8,128)(2,1)}), bf16[4,128,128]{2,1,0:T(8,128)(2,1)S(1)}, u32[]{:S(2)}, u32[]{:S(2)}) async-start(bf16[4,128,128]{2,1,0:T(8,128)(2,1)} %broadcast_in_dim.48), calls=%async_computation | async-start | bytes 262144 | tf_op jit(solution)/shard_map/all_to_all | solution.py:18
  18.9 1.2 copy-start.12
  20.0 12.7 %copy-start.13 = (bf16[224,1024]{1,0:T(8,128)(2,1)S(1)}, bf16[224,1024]{1,0:T(8,128)(2,1)}, u32[]{:S(2)}) copy-start(bf16[224,1024]{1,0:T(8,128)(2,1)} %param.10) | copy-start | bytes 1376260
  20.0 16.2 %copy-start.14 = (bf16[224,1024]{1,0:T(8,128)(2,1)S(1)}, bf16[224,1024]{1,0:T(8,128)(2,1)}, u32[]{:S(2)}) copy-start(bf16[224,1024]{1,0:T(8,128)(2,1)} %param.9) | copy-start | bytes 1376260
  20.0 18.2 %copy-start.16 = (bf16[224,1024]{1,0:T(8,128)(2,1)S(1)}, bf16[224,1024]{1,0:T(8,128)(2,1)}, u32[]{:S(2)}) copy-start(bf16[224,1024]{1,0:T(8,128)(2,1)} %param.8) | copy-start | bytes 1376260
  20.1 41.0 %all-to-all-start.1 = ((bf16[32,144,128]{2,1,0:T(8,128)(2,1)}), bf16[32,144,128]{2,1,0:T(8,128)(2,1)}, u32[]{:S(2)}, u32[]{:S(2)}) async-start(bf16[32,144,128]{2,1,0:T(8,128)(2,1)} %broadcast_in_dim.80), calls=%async_computation.1 | async-start | bytes 2359296 | tf_op jit(solution)/shard_map/all_to_all | solution.py:18
  32.6 9.6 %copy-start.15 = (bf16[224,1024]{1,0:T(8,128)(2,1)S(1)}, bf16[224,1024]{1,0:T(8,128)(2,1)}, u32[]{:S(2)}) copy-start(bf16[224,1024]{1,0:T(8,128)(2,1)} %param.9) | copy-start | bytes 1376260
  32.7 48.1 %all-gather.3.cloned.1.call-start = ((), (), s32[]{:S(2)}) async-start(), calls=%async_computation.6 | async-start | bytes 1179648 | tf_op jit(solution)/shard_map/all_gather | solution.py:118
  32.7 8.1 %collective-permute-start.2 = (bf16[224,1024]{1,0:T(8,128)(2,1)S(1)}, bf16[224,1024]{1,0:T(8,128)(2,1)S(1)}, u32[]{:S(2)}, u32[]{:S(2)}) collective-permute-start(bf16[224,1024]{1,0:T(8,128)(2,1)S(1)} %copy-done.13), channel_id=1, source_target_pairs={{0,64},{64,0},{1,65},{65,1},{2,66},{66,2},{3,67},{67,3},{4,68},{68... | collective-permute-start | bytes 1376264 | tf_op jit(solution)/shard_map/ppermute | solution.py:107
  36.3 4.6 %collective-permute-start.1 = (bf16[224,1024]{1,0:T(8,128)(2,1)S(1)}, bf16[224,1024]{1,0:T(8,128)(2,1)}, u32[]{:S(2)}, u32[]{:S(2)}) collective-permute-start(bf16[224,1024]{1,0:T(8,128)(2,1)S(1)} %copy-done.14), channel_id=1, source_target_pairs={{0,64},{64,0},{1,65},{65,1},{2,66},{66,2},{3,67},{67,3},{4,68},{68... | collective-permute-start | bytes 1376264 | tf_op jit(solution)/shard_map/ppermute | solution.py:107
  38.2 4.0 %collective-permute-start = (bf16[224,1024]{1,0:T(8,128)(2,1)S(1)}, bf16[224,1024]{1,0:T(8,128)(2,1)}, u32[]{:S(2)}, u32[]{:S(2)}) collective-permute-start(bf16[224,1024]{1,0:T(8,128)(2,1)S(1)} %copy-done.16), channel_id=1, source_target_pairs={{0,64},{64,0},{1,65},{65,1},{2,66},{66,2},{3,67},{67,3},{4,68},{68... | collective-permute-start | bytes 1376264 | tf_op jit(solution)/shard_map/ppermute | solution.py:107
  63.7 1.0 copy-start.1
  64.7 1.0 copy-start.6
  65.7 0.6 copy-start.7
  66.3 7.9 %copy-start.21 = (bf16[128]{0:T(256)(128)(2,1)S(1)}, bf16[128]{0:T(256)(128)(2,1)}, u32[]{:S(2)}) copy-start(bf16[128]{0:T(256)(128)(2,1)} %param.11) | copy-start | bytes 772
  66.3 21.3 %all-to-all-start.2 = ((bf16[8,56,1152]{2,1,0:T(8,128)(2,1)}), bf16[8,56,1152]{2,1,0:T(8,128)(2,1)}, u32[]{:S(2)}, u32[]{:S(2)}) async-start(bf16[8,56,1152]{2,1,0:T(8,128)(2,1)} %bitcast.73), calls=%async_computation.2 | async-start | bytes 2064384 | tf_op jit(solution)/shard_map/all_to_all | solution.py:18
  80.7 1.2 copy-start.5
  83.4 1.0 copy-start.3
  90.0 17.6 %all-to-all-start.3 = ((bf16[8,56,512]{2,1,0:T(8,128)(2,1)}), bf16[8,56,512]{2,1,0:T(8,128)(2,1)S(1)}, u32[]{:S(2)}, u32[]{:S(2)}) async-start(bf16[8,56,512]{2,1,0:T(8,128)(2,1)} %bitcast.9), calls=%async_computation.3 | async-start | bytes 917504 | tf_op jit(solution)/shard_map/all_to_all | solution.py:18
  108.9 22.1 %copy-start.25 = (s32[4,2]{0,1:T(2,128)S(1)}, s32[4,2]{0,1:T(2,128)}, u32[]{:S(2)}) copy-start(s32[4,2]{0,1:T(2,128)} %param.13) | copy-start | bytes 100
  108.9 27.6 %all-to-all-start.4 = ((bf16[8,176,512]{2,1,0:T(8,128)(2,1)}), bf16[8,176,512]{2,1,0:T(8,128)(2,1)S(1)}, u32[]{:S(2)}, u32[]{:S(2)}) async-start(bf16[8,176,512]{2,1,0:T(8,128)(2,1)} %broadcast_in_dim.84), calls=%async_computation.4 | async-start | bytes 2883584 | tf_op jit(solution)/shard_map/all_to_all | solution.py:18
  115.6 20.1 %collective-permute-start.5 = (bf16[512,1024]{1,0:T(8,128)(2,1)}, bf16[512,1024]{1,0:T(8,128)(2,1)}, u32[]{:S(2)}, u32[]{:S(2)}) collective-permute-start(bf16[512,1024]{1,0:T(8,128)(2,1)} %copy-done.1), channel_id=1, source_target_pairs={{0,64},{64,0},{1,65},{65,1},{2,66},{66,2},{3,67},{67,3},{4,68},{68... | collective-permute-start | bytes 3145736 | tf_op jit(solution)/shard_map/ppermute | solution.py:238
  131.6 60.3 %collective-permute-start.9 = (bf16[512,1024]{1,0:T(8,128)(2,1)}, bf16[512,1024]{1,0:T(8,128)(2,1)}, u32[]{:S(2)}, u32[]{:S(2)}) collective-permute-start(bf16[512,1024]{1,0:T(8,128)(2,1)} %copy-done.3), channel_id=1, source_target_pairs={{0,64},{64,0},{1,65},{65,1},{2,66},{66,2},{3,67},{67,3},{4,68},{68... | collective-permute-start | bytes 3145736 | tf_op jit(solution)/shard_map/ppermute | solution.py:239
  139.9 16.9 %copy-start.24 = (f32[4]{0:T(128)S(1)}, f32[4]{0:T(128)}, u32[]{:S(2)}) copy-start(f32[4]{0:T(128)} %reduce_sum.109) | copy-start | bytes 52
  139.9 16.9 %collective-permute-start.3 = (f32[4]{0:T(128)}, f32[4]{0:T(128)S(1)}, u32[]{:S(2)}, u32[]{:S(2)}) collective-permute-start(f32[4]{0:T(128)} %reduce_sum.109), channel_id=1, source_target_pairs={{0,64},{64,0},{1,65},{65,1},{2,66},{66,2},{3,67},{67,3},{4,68},{68... | collective-permute-start | bytes 56 | tf_op jit(solution)/shard_map/ppermute | solution.py:194
  155.7 1.0 copy-start
  158.6 49.8 %all-to-all-start.5 = ((bf16[32,144,128]{2,1,0:T(8,128)(2,1)}), bf16[32,144,128]{2,1,0:T(8,128)(2,1)}, u32[]{:S(2)}, u32[]{:S(2)}) async-start(bf16[32,144,128]{2,1,0:T(8,128)(2,1)} %dynamic_update_slice.11), calls=%async_computation.5 | async-start | bytes 2359296 | tf_op jit(solution)/shard_map/all_to_all | solution.py:18
  178.3 9.0 %copy-start.8 = (bf16[4,56,512]{2,1,0:T(8,128)(2,1)}, bf16[4,56,512]{2,1,0:T(8,128)(2,1)S(1)}, u32[]{:S(2)}) copy-start(bf16[4,56,512]{2,1,0:T(8,128)(2,1)S(1)} %get-tuple-element.39) | copy-start | bytes 688132
  178.3 9.4 %collective-permute-start.4 = (bf16[224,512]{1,0:T(8,128)(2,1)S(1)}, bf16[224,512]{1,0:T(8,128)(2,1)S(1)}, u32[]{:S(2)}, u32[]{:S(2)}) collective-permute-start(bf16[224,512]{1,0:T(8,128)(2,1)S(1)} %bitcast.77), channel_id=1, source_target_pairs={{0,64},{64,0},{1,65},{65,1},{2,66},{66,2},{3,67},{67,3},{4,68},{68... | collective-permute-start | bytes 688136 | tf_op jit(solution)/shard_map/ppermute | solution.py:252
  180.6 7.1 %collective-permute-start.6 = (bf16[8,224]{1,0:T(8,128)(2,1)S(1)}, bf16[8,224]{1,0:T(8,128)(2,1)S(1)}, u32[]{:S(2)}, u32[]{:S(2)}) collective-permute-start(bf16[8,224]{1,0:T(8,128)(2,1)S(1)} %concatenate.76), channel_id=1, source_target_pairs={{0,64},{64,0},{1,65},{65,1},{2,66},{66,2},{3,67},{67,3},{4,68},{68... | collective-permute-start | bytes 10760 | tf_op jit(solution)/shard_map/ppermute | solution.py:240
  182.7 7.1 %collective-permute-start.7 = (bf16[224,512]{1,0:T(8,128)(2,1)}, bf16[224,512]{1,0:T(8,128)(2,1)S(1)}, u32[]{:S(2)}, u32[]{:S(2)}) collective-permute-start(bf16[224,512]{1,0:T(8,128)(2,1)} %bitcast.24), channel_id=1, source_target_pairs={{0,64},{64,0},{1,65},{65,1},{2,66},{66,2},{3,67},{67,3},{4,68},{68... | collective-permute-start | bytes 688136 | tf_op jit(solution)/shard_map/ppermute | solution.py:252
  184.9 7.0 %collective-permute-start.8 = (bf16[224,512]{1,0:T(8,128)(2,1)}, bf16[224,512]{1,0:T(8,128)(2,1)S(1)}, u32[]{:S(2)}, u32[]{:S(2)}) collective-permute-start(bf16[224,512]{1,0:T(8,128)(2,1)} %bitcast.26), channel_id=1, source_target_pairs={{0,64},{64,0},{1,65},{65,1},{2,66},{66,2},{3,67},{67,3},{4,68},{68... | collective-permute-start | bytes 688136 | tf_op jit(solution)/shard_map/ppermute | solution.py:252
  187.3 2.0 copy-start.2
  187.3 2.0 copy-start.11
  189.8 1.7 copy-start.10
  191.9 1.8 copy-start.4
  191.9 1.8 copy-start.9
  194.1 16.1 %copy-start.19 = (s32[4]{0:T(128)S(1)}, s32[4]{0:T(128)}, u32[]{:S(2)}) copy-start(s32[4]{0:T(128)} %get-tuple-element.54) | copy-start | bytes 52
  194.1 16.1 %copy-start.20 = (s32[4]{0:T(128)S(1)}, s32[4]{0:T(128)}, u32[]{:S(2)}) copy-start(s32[4]{0:T(128)} %get-tuple-element.55) | copy-start | bytes 52
  194.1 17.0 %copy-start.22 = (bf16[128]{0:T(256)(128)(2,1)S(1)}, bf16[128]{0:T(256)(128)(2,1)}, u32[]{:S(2)}) copy-start(bf16[128]{0:T(256)(128)(2,1)} %param.11) | copy-start | bytes 772
  194.1 17.8 %copy-start.17 = (f32[128,128]{1,0:T(8,128)S(1)}, f32[128,128]{1,0:T(8,128)}, u32[]{:S(2)}) copy-start(f32[128,128]{1,0:T(8,128)} %param.12) | copy-start | bytes 196612
  194.2 17.8 %copy-start.26 = (pred[128]{0:T(512)(128)(4,1)S(1)}, pred[128]{0:T(512)(128)(4,1)}, u32[]{:S(2)}) copy-start(pred[128]{0:T(512)(128)(4,1)} %iota_compare_fusion.2) | copy-start | bytes 388
  210.2 5.2 %copy-start.23 = (f32[8]{0:T(128)}, f32[8]{0:T(128)S(1)}, u32[]{:S(2)}) copy-start(f32[8]{0:T(128)S(1)} %compare_select_fusion) | copy-start | bytes 100
  212.9 2.5 %copy-start.18 = (f32[1,1024]{1,0:T(1,128)S(1)}, f32[1,1024]{1,0:T(1,128)}, u32[]{:S(2)}) copy-start(f32[1,1024]{1,0:T(1,128)} %slice_convert_fusion.1) | copy-start | bytes 12292
Sparse Core Ops, SparseCore 0:
  40.9 39.7 all-gather.2

commit v6 on v5

--- a/solution.py
+++ b/solution.py
@@ -34,34 +34,69 @@
     return jnp.stack([high, middle, value - high - middle]).astype(bf16)
 
 
-def token_products(tok_got, gate_w, up_w, down_w, parts, tok, head, wide_head):
-    width, cols = tok.shape[1], tok_got.shape[2]
+def first_products(got, gate_w, up_w, down_w, parts, tok, low, head, wide_head):
+    width, cols = tok.shape[1], got.shape[2]
     n_gy = width // cols
-    n_yl = tok_got.shape[0] // n_gy
-    rows = tok.shape[0] // n_yl
-    chip_units, half = down_w.shape[0], tok.shape[0]
+    n_yl = got.shape[0] // n_gy
+    half = tok.shape[0]
+    rows = half // n_yl
+    chip_units = down_w.shape[0]
     for z in range(n_gy):
         at = slice(z * cols, (z + 1) * cols)
         for y in range(n_yl):
-            tok[y * rows : (y + 1) * rows, at] = tok_got[y * n_gy + z, :rows]
-        head[:, at] = tok_got[z, rows:]
+            tok[y * rows : (y + 1) * rows, at] = got[y * n_gy + z, :rows]
+            low[y * rows : (y + 1) * rows, at] = got[y * n_gy + z, rows : 2 * rows]
+        head[:, at] = got[z, 2 * rows :]
         for r in range(0, 128, 16):
-            wide_head[r : r + 16, at] = tok_got[z, rows:]
+            wide_head[r : r + 16, at] = got[z, 2 * rows :]
     parts[:, :half] = dot(gate_w[:chip_units], tok[...], 1, 1).astype(bf16)
     parts[:, half : 2 * half] = dot(up_w[:chip_units], tok[...], 1, 1).astype(bf16)
+    parts[:, 2 * half : 3 * half] = dot(down_w[...], low[...], 1, 1).astype(bf16)
     v = dot(down_w[...], wide_head[...], 1, 1)
     high = v.astype(bf16).astype(f32)
     lane = lax.broadcasted_iota(jnp.int32, v.shape, 1)
     v = jnp.where(lane == 0, high, jnp.where(lane == 1, v - high, 0.0))
-    parts[:, 2 * half :] = v.astype(bf16)
-
-
-def cotangent_products(low_got, down_w, parts, low):
-    n_gy, n_yl, rows, cols = low_got.shape
-    for y in range(n_yl):
-        for z in range(n_gy):
-            low[y * rows : (y + 1) * rows, z * cols : (z + 1) * cols] = low_got[z, y]
-    parts[...] = dot(down_w[...], low[...], 1, 1).astype(bf16)
+    parts[:, 3 * half :] = v.astype(bf16)
+
+
+def hidden_units(place, got, own_terms, sent):
+    n_gz, own, lanes = got.shape
+    half = sent.shape[2]
+    n_seq = half // SEQ_LEN
+    sums = got[0].astype(f32)
+    for j in range(1, n_gz):
+        sums += got[j].astype(f32)
+    gate_sum, up_sum, hidden_grad = (sums[:, i * half : (i + 1) * half] for i in range(3))
+    head_down = sums[:, 3 * half : 3 * half + 1] + sums[:, 3 * half + 1 : 3 * half + 2]
+    gate_sigmoid = jax.nn.sigmoid(gate_sum)
+    silu_gate = gate_sum * gate_sigmoid
+    hidden = (silu_gate * up_sum).astype(bf16).astype(f32)
+    gate_slope = up_sum * gate_sigmoid * (1.0 + gate_sum * (1.0 - gate_sigmoid))
+
+    row = lax.broadcasted_iota(jnp.int32, (8, half), 0)
+    lane = lax.broadcasted_iota(jnp.int32, (8, half), 1)
+    blank = jnp.zeros((128 - own, half), f32)
+
+    def picked(value, first):
+        pick = (lane == (row - first) * SEQ_LEN + SEQ_LEN - 1) & (row >= first) & (row < first + n_seq)
+        value = jnp.concatenate([value * head_down, blank], axis=0).astype(bf16)
+        return dot(jnp.where(pick, 1.0, 0.0).astype(bf16), value, 1, 1)
+
+    unit = picked(gate_slope, 0) + picked(silu_gate, n_seq)
+    unit = jnp.concatenate([unit, jnp.zeros((8, half - 128), f32)], axis=1)
+    unit = pltpu.roll(unit, place[0], 1)
+
+    terms = jnp.sum(hidden * head_down, axis=0, keepdims=True) + own_terms[...]
+    for s in range(n_seq):
+        rest = jnp.sum(jnp.where(lane[:1] == s * SEQ_LEN + SEQ_LEN - 1, terms, 0.0), axis=1, keepdims=True)
+        for i in range(3):
+            piece = rest.astype(bf16).astype(f32)
+            unit += jnp.where((row == 0) & (lane == n_gz * own + i * n_seq + s), piece, 0.0)
+            rest = rest - piece
+    mine = jnp.concatenate([hidden_grad * gate_slope, hidden_grad * silu_gate, hidden, unit], axis=0)
+    mine = mine.astype(bf16)
+    for j in range(n_gz):
+        sent[j] = mine
 
 
 def token_gradients(everyone, gate_w, up_w, sent, full):
@@ -111,83 +146,47 @@
     gate_w, up_w = chip_block(gate_weight, padding), chip_block(up_weight, padding)
     down_w = chip_block(down_weight, 0)
 
-    low_got = to_all(lm_grad.astype(bf16), "yl", n_yl)
     head_rows = jnp.broadcast_to(reward_head[None, :], (16, cols))
-    tok_block = jnp.concatenate([tokens, head_rows], axis=0)
-    low_got, tok_block = lax.optimization_barrier((low_got, tok_block))
-    low_got = lax.all_gather(low_got, "gy")
-    tok_got = to_all(tok_block, PLANE, n_plane)
+    got = to_all(jnp.concatenate([tokens, lm_grad.astype(bf16), head_rows], axis=0), PLANE, n_plane)
 
     half, own = n_yl * rows, 2 * units // n_gz
     whole = pl.BlockSpec(memory_space=pltpu.VMEM)
     grant = pltpu.CompilerParams(vmem_limit_bytes=40 * 2**20)
-    parts, tok_half, head_vec = pl.pallas_call(
-        token_products,
+    parts, tok_half, low_half, head_vec = pl.pallas_call(
+        first_products,
         out_shape=(
-            jax.ShapeDtypeStruct((2 * units, 2 * half + 128), bf16),
+            jax.ShapeDtypeStruct((2 * units, 3 * half + 128), bf16),
+            jax.ShapeDtypeStruct((half, width), bf16),
             jax.ShapeDtypeStruct((half, width), bf16),
             jax.ShapeDtypeStruct((16, width), bf16),
         ),
         in_specs=[whole] * 4,
-        out_specs=(whole,) * 3,
+        out_specs=(whole,) * 4,
         scratch_shapes=[pltpu.VMEM((128, width), bf16)],
         compiler_params=grant,
         cost_estimate=pl.CostEstimate(
-            flops=4 * units * width * (2 * half + 128), bytes_accessed=8 * 2**20, transcendentals=0
-        ),
-        name="token_products",
-    )(tok_got, gate_w, up_w, down_w)
+            flops=4 * units * width * (3 * half + 128), bytes_accessed=12 * 2**20, transcendentals=0
+        ),
+        name="first_products",
+    )(got, gate_w, up_w, down_w)
     head_vec = head_vec[:1]
-    first = exchange(parts.reshape(n_gz, own, 2 * half + 128), GZ)
-
-    back_parts, low_half = pl.pallas_call(
-        cotangent_products,
-        out_shape=(
-            jax.ShapeDtypeStruct((2 * units, half), bf16),
-            jax.ShapeDtypeStruct((half, width), bf16),
-        ),
-        in_specs=[whole] * 2,
-        out_specs=(whole,) * 2,
+    sums_got = exchange(parts.reshape(n_gz, own, 3 * half + 128), GZ)
+
+    own_term = jnp.sum(tokens[rows - 1].astype(f32) * reward_head.astype(f32))
+    spot = lax.axis_index("yl") * rows + rows - 1
+    own_terms = jnp.where(jnp.arange(half)[None, :] == spot, own_term, 0.0)
+    to_send = pl.pallas_call(
+        hidden_units,
+        out_shape=jax.ShapeDtypeStruct((n_gz, 3 * own + 8, half), bf16),
+        in_specs=[pl.BlockSpec(memory_space=pltpu.SMEM), whole, whole],
+        out_specs=whole,
         compiler_params=grant,
         cost_estimate=pl.CostEstimate(
-            flops=4 * units * width * half, bytes_accessed=5 * 2**20, transcendentals=0
-        ),
-        name="cotangent_products",
-    )(low_got, down_w)
-    first, back_parts = lax.optimization_barrier((first, back_parts))
-    second = exchange(back_parts.reshape(n_gz, own, half), GZ)
-
-    sums = jnp.sum(first.astype(f32), axis=0)
-    gate_sum, up_sum = sums[:, :half], sums[:, half : 2 * half]
-    head_down = sums[:, 2 * half : 2 * half + 1] + sums[:, 2 * half + 1 : 2 * half + 2]
-    gate_sigmoid = jax.nn.sigmoid(gate_sum)
-    silu_gate = gate_sum * gate_sigmoid
-    hidden = (silu_gate * up_sum).astype(bf16)
-    gate_slope = up_sum * gate_sigmoid * (1.0 + gate_sum * (1.0 - gate_sigmoid))
-
-    def last_cols(value):
-        return value.reshape(own, n_yl, rows)[:, :, rows - 1].astype(f32)
-
-    gate_unit = (head_down * last_cols(gate_slope)).astype(bf16).T
-    up_unit = (head_down * last_cols(silu_gate)).astype(bf16).T
-    own_term = jnp.sum(tokens[rows - 1].astype(f32) * reward_head.astype(f32))
-    terms = jnp.sum(last_cols(hidden) * head_down, axis=0)
-    terms = terms + jnp.where(jnp.arange(n_yl) == lax.axis_index("yl"), own_term, 0.0)
-    unit_rows = lax.dynamic_update_slice(
-        jnp.zeros((2 * n_yl, half), bf16),
-        jnp.concatenate([gate_unit, up_unit], axis=0),
-        (0, lax.axis_index(GZ) * own),
-    )
-    term_rows = pieces(terms).reshape(1, -1)
-    unit_rows = lax.dynamic_update_slice(unit_rows, term_rows, (0, 2 * units))
-    silu_gate, gate_slope, early, second = lax.optimization_barrier(
-        (silu_gate, gate_slope, jnp.concatenate([hidden, unit_rows], axis=0), second)
-    )
-    hidden_grad = jnp.sum(second.astype(f32), axis=0)
-    up_grad = (hidden_grad * silu_gate).astype(bf16)
-    gate_grad = (hidden_grad * gate_slope).astype(bf16)
-    mine = jnp.concatenate([gate_grad, up_grad, early], axis=0)
-    everyone = to_all(mine, GZ, n_gz)
+            flops=40 * own * half, bytes_accessed=4 * 2**20, transcendentals=own * half
+        ),
+        name="hidden_units",
+    )((lax.axis_index(GZ) * own).astype(jnp.int32)[None], sums_got, own_terms)
+    everyone = exchange(to_send, GZ)
     core_terms = jnp.sum(
         everyone[:, 3 * own, 2 * units : 2 * units + 3 * n_yl].astype(f32).reshape(n_gz * 3, n_yl), axis=0
     )

time: 225 us -> 239 us (1.062); the launches traced: 224 us -> 234 us
  waiting for transfers between devices: 53.4 us -> 105 us
  starting transfers between devices: 106 us -> 76.8 us
  between operations: 14.7 us -> 1.08 us
  matrix products: 10 us -> 12.9 us
    all_to_all x6 -> x4, waiting for transfers between devices: 46.8 us -> 105 us  [exchange(): return lax.all_to_all(pieces, axes, 0, 0)]
    ppermute x1, starting transfers between devices: 14.8 us -> 2.74 us  [body(): tok_sib = lax.ppermute(tok_half, 'co', SWAP)]
    ppermute x1, starting transfers between devices: 14.3 us -> 3.79 us  [body(): pair_terms = jnp.stack([core_terms, lax.ppermute(core_terms, 'co', SWAP)])]
    all_to_all x6 -> x4, starting transfers between devices: 58.1 us -> 52 us  [exchange(): return lax.all_to_all(pieces, axes, 0, 0)]
    all_gather x1 -> x0, waiting for transfers between devices: 5.19 us -> none  [body(): low_got = lax.all_gather(low_got, 'gy')]
    unnamed x59 -> x50, local copies, waits for them, and re-layouts: 6.45 us -> 9.68 us
    dot_general x9, matrix products: 10 us -> 12.9 us  [dot(): lax.dot_general(left, right, (((left_dim,), (right_dim,)), ((), ())), pre...]
  transfers between devices with their start and end apart: 17 -> 14, of which waited for: 7 -> 5; matrix products, arithmetic and copies ran while one was open for 10% -> 8% of each run, Pallas kernels for 3% -> 1%
where the time goes in v6:
time: 239 us; the launch traced here: 234 us
  waiting for transfers between devices  105 us (44%)
  starting transfers between devices  76.8 us (32%)
  local copies, waits for them, and re-layouts  18.7 us (8%)
  other arithmetic  13.1 us (5%)
  matrix products  12.9 us (5%)
  Pallas kernels  6.21 us (3%)
    all_to_all x4, waiting for transfers between devices, exchange(): return lax.all_to_all(pieces, axes, 0, 0)  105 us
    all_to_all x4, starting transfers between devices, exchange(): return lax.all_to_all(pieces, axes, 0, 0)  52 us
    dot_general x9, matrix products, dot(): lax.dot_general(left, right, (((left_dim,), (right_dim,)), ((), ())), pre...  12.9 us
    unnamed x50, local copies, waits for them, and re-layouts  9.68 us
    ppermute x3, starting transfers between devices, chip_block(): lax.ppermute(weight, 'co', SWAP)  7.33 us
    ppermute x3, starting transfers between devices, weight_grad(): from_sib = lax.ppermute(full[units:], 'co', SWAP)  6.25 us
  transfers between devices with their start and end apart: 14, of which 5 were waited for; matrix products, arithmetic and copies ran while one was open for 8% of the time, Pallas kernels for 1%

profile of v6, /device:TPU:1, one launch (start us, length us, event | category | flops | bytes accessed | tf_op | source)
XLA Modules:
  0.0 234.1 jit_solution(15898103944922110019)
XLA Ops:
  0.6 0.8 convert_element_type.49
  1.5 0.7 broadcast_in_dim.68
  2.1 0.8 pad_maximum_fusion.1
  2.9 1.7 broadcast_in_dim.69
  4.6 14.4 %all-to-all-start = ((bf16[32,272,128]{2,1,0:T(8,128)(2,1)}), bf16[32,272,128]{2,1,0:T(8,128)(2,1)S(1)}, u32[]{:S(2)}, u32[]{:S(2)}) async-start(bf16[32,272,128]{2,1,0:T(8,128)(2,1)} %broadcast_in_dim.69), calls=%async_computation | async-start | bytes 4456448 | tf_op jit(solution)/shard_map/all_to_all | solution.py:18
  19.0 3.0 %collective-permute-start.2 = (bf16[224,1024]{1,0:T(8,128)(2,1)S(1)}, bf16[224,1024]{1,0:T(8,128)(2,1)S(1)}, u32[]{:S(2)}, u32[]{:S(2)}) collective-permute-start(bf16[224,1024]{1,0:T(8,128)(2,1)S(1)} %copy-done.16), channel_id=1, source_target_pairs={{0,64},{64,0},{1,65},{65,1},{2,66},{66,2},{3,67},{67,3},{4,68},{68... | collective-permute-start | bytes 1376264 | tf_op jit(solution)/shard_map/ppermute | solution.py:142
  22.1 1.9 collective-permute-start
  24.0 2.4 %collective-permute-start.1 = (bf16[224,1024]{1,0:T(8,128)(2,1)}, bf16[224,1024]{1,0:T(8,128)(2,1)S(1)}, u32[]{:S(2)}, u32[]{:S(2)}) collective-permute-start(bf16[224,1024]{1,0:T(8,128)(2,1)} %param.9), channel_id=1, source_target_pairs={{0,64},{64,0},{1,65},{65,1},{2,66},{66,2},{3,67},{67,3},{4,68},{68... | collective-permute-start | bytes 1376264 | tf_op jit(solution)/shard_map/ppermute | solution.py:142
  26.5 1.0 pad_maximum_fusion.down_w
  27.5 0.6 collective-permute-done.1
  28.0 1.3 maximum_maximum_fusion.1
  29.4 47.3 %all-to-all-done.got = bf16[32,272,128]{2,1,0:T(8,128)(2,1)S(1)} async-done(((bf16[32,272,128]{2,1,0:T(8,128)(2,1)}), bf16[32,272,128]{2,1,0:T(8,128)(2,1)S(1)}, u32[]{:S(2)}, u32[]{:S(2)}) %all-to-all-start) | async-done | bytes 2228256 | tf_op jit(solution)/shard_map/all_to_all | solution.py:18
  76.7 1.4 copy-done.4
  78.1 1.2 copy-done.2
  79.3 1.6 copy-done.5
  81.0 1.2 copy-done.9
  82.1 1.9 first_products.1
  84.1 1.1 copy-done.6
  85.2 0.3 copy-done.7
  85.5 14.7 %all-to-all-start.1 = ((bf16[8,56,1664]{2,1,0:T(8,128)(2,1)}), bf16[8,56,1664]{2,1,0:T(8,128)(2,1)S(1)}, u32[]{:S(2)}, u32[]{:S(2)}) async-start(bf16[8,56,1664]{2,1,0:T(8,128)(2,1)} %bitcast.49), calls=%async_computation.1 | async-start | bytes 2981888 | tf_op jit(solution)/shard_map/all_to_all | solution.py:18
  100.2 1.3 fusion.27
  101.5 0.6 compare_select_fusion.own_terms
  102.2 29.3 %all-to-all-done.1.got = bf16[8,56,1664]{2,1,0:T(8,128)(2,1)S(1)} async-done(((bf16[8,56,1664]{2,1,0:T(8,128)(2,1)}), bf16[8,56,1664]{2,1,0:T(8,128)(2,1)S(1)}, u32[]{:S(2)}, u32[]{:S(2)}) %all-to-all-start.1) | async-done | bytes 1490976 | tf_op jit(solution)/shard_map/all_to_all | solution.py:18
  131.5 1.7 hidden_units.1
  133.2 9.3 %all-to-all-start.2 = ((bf16[8,176,512]{2,1,0:T(8,128)(2,1)}), bf16[8,176,512]{2,1,0:T(8,128)(2,1)S(1)}, u32[]{:S(2)}, u32[]{:S(2)}) async-start(bf16[8,176,512]{2,1,0:T(8,128)(2,1)} %hidden_units.1), calls=%async_computation.2 | async-start | bytes 2883584 | tf_op jit(solution)/shard_map/all_to_all | solution.py:18
  142.5 2.7 %collective-permute-start.5 = (bf16[512,1024]{1,0:T(8,128)(2,1)S(1)}, bf16[512,1024]{1,0:T(8,128)(2,1)}, u32[]{:S(2)}, u32[]{:S(2)}) collective-permute-start(bf16[512,1024]{1,0:T(8,128)(2,1)S(1)} %get-tuple-element.14), channel_id=1, source_target_pairs={{0,64},{64,0},{1,65},{65,1},{2,66},{66,2},{3,67},{67,3},{4,68},{68... | collective-permute-start | bytes 3145736 | tf_op jit(solution)/shard_map/ppermute | solution.py:237
  145.3 0.5 iota_compare_fusion.2
  145.8 0.6 slice_bitcast_fusion.4
  146.4 1.9 collective-permute-start.9
  148.3 0.9 slice.160
  149.2 17.9 %all-to-all-done.2.everyone = bf16[8,176,512]{2,1,0:T(8,128)(2,1)S(1)} async-done(((bf16[8,176,512]{2,1,0:T(8,128)(2,1)}), bf16[8,176,512]{2,1,0:T(8,128)(2,1)S(1)}, u32[]{:S(2)}, u32[]{:S(2)}) %all-to-all-start.2) | async-done | bytes 1441824 | tf_op jit(solution)/shard_map/all_to_all | solution.py:18
  167.3 3.8 %collective-permute-start.3 = (f32[4]{0:T(128)S(1)}, f32[4]{0:T(128)S(1)}, u32[]{:S(2)}, u32[]{:S(2)}) collective-permute-start(f32[4]{0:T(128)S(1)} %reduce_sum.76), channel_id=1, source_target_pairs={{0,64},{64,0},{1,65},{65,1},{2,66},{66,2},{3,67},{67,3},{4,68},{68... | collective-permute-start | bytes 56 | tf_op jit(solution)/shard_map/ppermute | solution.py:193
  171.1 1.2 copy-done.1
  172.4 1.2 copy-done.3
  173.6 2.6 %token_gradients.1 = bf16[32,144,128]{2,1,0:T(8,128)(2,1)} custom-call(bf16[8,176,512]{2,1,0:T(8,128)(2,1)S(1)} %all-to-all-done.2.everyone, bf16[512,1024]{1,0:T(8,128)(2,1)S(1)} %copy-done.3, bf16[512,1024]{1,0:T(8,128)(2,1)S(1)} %copy-done.1), custom_call_target="tpu_custom_call" | custom-call | flops 939524096 | bytes 5242880 | tf_op jit(solution)/shard_map/token_gradients/pallas_call | solution.py:194
  176.3 1.7 dynamic_update_slice.3
  178.0 1.0 fusion.31
  179.0 1.9 collective-permute-start.8
  180.9 13.6 %all-to-all-start.3 = ((bf16[32,144,128]{2,1,0:T(8,128)(2,1)}), bf16[32,144,128]{2,1,0:T(8,128)(2,1)}, u32[]{:S(2)}, u32[]{:S(2)}) async-start(bf16[32,144,128]{2,1,0:T(8,128)(2,1)} %dynamic_update_slice.3), calls=%async_computation.3 | async-start | bytes 2359296 | tf_op jit(solution)/shard_map/all_to_all | solution.py:18
  194.6 2.8 %collective-permute-start.6 = (bf16[8,224]{1,0:T(8,128)(2,1)S(1)}, bf16[8,224]{1,0:T(8,128)(2,1)S(1)}, u32[]{:S(2)}, u32[]{:S(2)}) collective-permute-start(bf16[8,224]{1,0:T(8,128)(2,1)S(1)} %concatenate.64), channel_id=1, source_target_pairs={{0,64},{64,0},{1,65},{65,1},{2,66},{66,2},{3,67},{67,3},{4,68},{68... | collective-permute-start | bytes 10760 | tf_op jit(solution)/shard_map/ppermute | solution.py:239
  197.4 0.6 fusion.32
  198.1 0.2 slice.163
  198.2 0.2 copy.27
  198.4 1.9 collective-permute-start.7
  200.3 2.4 %collective-permute-start.4 = (bf16[224,512]{1,0:T(8,128)(2,1)}, bf16[224,512]{1,0:T(8,128)(2,1)}, u32[]{:S(2)}, u32[]{:S(2)}) collective-permute-start(bf16[224,512]{1,0:T(8,128)(2,1)} %bitcast.11), channel_id=1, source_target_pairs={{0,64},{64,0},{1,65},{65,1},{2,66},{66,2},{3,67},{67,3},{4,68},{68... | collective-permute-start | bytes 688136 | tf_op jit(solution)/shard_map/ppermute | solution.py:251
  202.8 0.6 fusion.33
  203.4 1.7 fusion.36
  205.1 1.4 fusion.1
  206.6 0.2 slice.164
  207.0 1.8 fusion.35
  208.8 0.4 fusion.3
  209.2 1.8 fusion.34
  211.0 1.3 fusion.5
  212.4 10.2 %all-to-all-done.3 = bf16[32,144,128]{2,1,0:T(8,128)(2,1)} async-done(((bf16[32,144,128]{2,1,0:T(8,128)(2,1)}), bf16[32,144,128]{2,1,0:T(8,128)(2,1)}, u32[]{:S(2)}, u32[]{:S(2)}) %all-to-all-start.3) | async-done | bytes 1179680 | tf_op jit(solution)/shard_map/all_to_all | solution.py:18
  222.5 1.4 convert_reduce_fusion
  224.4 0.9 fusion.22
  225.3 0.8 fusion.20
  226.1 0.6 broadcast_multiply_fusion
  226.8 1.3 fusion.26
  228.1 0.2 select_reduce_fusion.1
  228.4 1.3 fusion.6
  229.7 1.9 fusion.2
  231.6 1.3 fusion.4
  232.9 1.3 fusion
  (78 shorter events, 1.5 us)
Async XLA Ops:
  4.6 14.4 %copy-start.16 = (bf16[224,1024]{1,0:T(8,128)(2,1)S(1)}, bf16[224,1024]{1,0:T(8,128)(2,1)}, u32[]{:S(2)}) copy-start(bf16[224,1024]{1,0:T(8,128)(2,1)} %param.10) | copy-start | bytes 1376260
  4.6 72.1 %all-to-all-start = ((bf16[32,272,128]{2,1,0:T(8,128)(2,1)}), bf16[32,272,128]{2,1,0:T(8,128)(2,1)S(1)}, u32[]{:S(2)}, u32[]{:S(2)}) async-start(bf16[32,272,128]{2,1,0:T(8,128)(2,1)} %broadcast_in_dim.69), calls=%async_computation | async-start | bytes 4456448 | tf_op jit(solution)/shard_map/all_to_all | solution.py:18
  19.0 9.0 %copy-start.17 = (bf16[224,1024]{1,0:T(8,128)(2,1)S(1)}, bf16[224,1024]{1,0:T(8,128)(2,1)}, u32[]{:S(2)}) copy-start(bf16[224,1024]{1,0:T(8,128)(2,1)} %param.9) | copy-start | bytes 1376260
  19.0 9.0 %copy-start.18 = (bf16[224,1024]{1,0:T(8,128)(2,1)S(1)}, bf16[224,1024]{1,0:T(8,128)(2,1)}, u32[]{:S(2)}) copy-start(bf16[224,1024]{1,0:T(8,128)(2,1)} %param.8) | copy-start | bytes 1376260
  19.0 7.4 %collective-permute-start.2 = (bf16[224,1024]{1,0:T(8,128)(2,1)S(1)}, bf16[224,1024]{1,0:T(8,128)(2,1)S(1)}, u32[]{:S(2)}, u32[]{:S(2)}) collective-permute-start(bf16[224,1024]{1,0:T(8,128)(2,1)S(1)} %copy-done.16), channel_id=1, source_target_pairs={{0,64},{64,0},{1,65},{65,1},{2,66},{66,2},{3,67},{67,3},{4,68},{68... | collective-permute-start | bytes 1376264 | tf_op jit(solution)/shard_map/ppermute | solution.py:142
  22.1 5.4 %collective-permute-start = (bf16[224,1024]{1,0:T(8,128)(2,1)}, bf16[224,1024]{1,0:T(8,128)(2,1)S(1)}, u32[]{:S(2)}, u32[]{:S(2)}) collective-permute-start(bf16[224,1024]{1,0:T(8,128)(2,1)} %param.8), channel_id=1, source_target_pairs={{0,64},{64,0},{1,65},{65,1},{2,66},{66,2},{3,67},{67,3},{4,68},{68... | collective-permute-start | bytes 1376264 | tf_op jit(solution)/shard_map/ppermute | solution.py:142
  24.0 4.0 %collective-permute-start.1 = (bf16[224,1024]{1,0:T(8,128)(2,1)}, bf16[224,1024]{1,0:T(8,128)(2,1)S(1)}, u32[]{:S(2)}, u32[]{:S(2)}) collective-permute-start(bf16[224,1024]{1,0:T(8,128)(2,1)} %param.9), channel_id=1, source_target_pairs={{0,64},{64,0},{1,65},{65,1},{2,66},{66,2},{3,67},{67,3},{4,68},{68... | collective-permute-start | bytes 1376264 | tf_op jit(solution)/shard_map/ppermute | solution.py:142
  29.4 54.7 %copy-start = (bf16[512,1024]{1,0:T(8,128)(2,1)}, bf16[512,1024]{1,0:T(8,128)(2,1)S(1)}, u32[]{:S(2)}) copy-start(bf16[512,1024]{1,0:T(8,128)(2,1)S(1)} %get-tuple-element.36.up_w) | copy-start | bytes 3145732
  76.7 1.4 copy-start.4
  78.1 1.2 copy-start.2
  79.3 1.6 copy-start.5
  81.0 1.2 copy-start.9
  84.1 1.2 copy-start.6
  84.1 1.4 copy-start.7
  84.1 16.1 %copy-start.21 = (bf16[128]{0:T(256)(128)(2,1)S(1)}, bf16[128]{0:T(256)(128)(2,1)}, u32[]{:S(2)}) copy-start(bf16[128]{0:T(256)(128)(2,1)} %param.11) | copy-start | bytes 772
  85.5 46.0 %all-to-all-start.1 = ((bf16[8,56,1664]{2,1,0:T(8,128)(2,1)}), bf16[8,56,1664]{2,1,0:T(8,128)(2,1)S(1)}, u32[]{:S(2)}, u32[]{:S(2)}) async-start(bf16[8,56,1664]{2,1,0:T(8,128)(2,1)} %bitcast.49), calls=%async_computation.1 | async-start | bytes 2981888 | tf_op jit(solution)/shard_map/all_to_all | solution.py:18
  133.2 12.5 %copy-start.23 = (s32[4,2]{0,1:T(2,128)S(1)}, s32[4,2]{0,1:T(2,128)}, u32[]{:S(2)}) copy-start(s32[4,2]{0,1:T(2,128)} %param.13) | copy-start | bytes 100
  133.2 33.9 %all-to-all-start.2 = ((bf16[8,176,512]{2,1,0:T(8,128)(2,1)}), bf16[8,176,512]{2,1,0:T(8,128)(2,1)S(1)}, u32[]{:S(2)}, u32[]{:S(2)}) async-start(bf16[8,176,512]{2,1,0:T(8,128)(2,1)} %hidden_units.1), calls=%async_computation.2 | async-start | bytes 2883584 | tf_op jit(solution)/shard_map/all_to_all | solution.py:18
  142.5 5.8 %collective-permute-start.5 = (bf16[512,1024]{1,0:T(8,128)(2,1)S(1)}, bf16[512,1024]{1,0:T(8,128)(2,1)}, u32[]{:S(2)}, u32[]{:S(2)}) collective-permute-start(bf16[512,1024]{1,0:T(8,128)(2,1)S(1)} %get-tuple-element.14), channel_id=1, source_target_pairs={{0,64},{64,0},{1,65},{65,1},{2,66},{66,2},{3,67},{67,3},{4,68},{68... | collective-permute-start | bytes 3145736 | tf_op jit(solution)/shard_map/ppermute | solution.py:237
  146.4 57.0 %collective-permute-start.9 = (bf16[512,1024]{1,0:T(8,128)(2,1)}, bf16[512,1024]{1,0:T(8,128)(2,1)}, u32[]{:S(2)}, u32[]{:S(2)}) collective-permute-start(bf16[512,1024]{1,0:T(8,128)(2,1)} %copy-done.7), channel_id=1, source_target_pairs={{0,64},{64,0},{1,65},{65,1},{2,66},{66,2},{3,67},{67,3},{4,68},{68... | collective-permute-start | bytes 3145736 | tf_op jit(solution)/shard_map/ppermute | solution.py:238
  167.3 8.8 %collective-permute-start.3 = (f32[4]{0:T(128)S(1)}, f32[4]{0:T(128)S(1)}, u32[]{:S(2)}, u32[]{:S(2)}) collective-permute-start(f32[4]{0:T(128)S(1)} %reduce_sum.76), channel_id=1, source_target_pairs={{0,64},{64,0},{1,65},{65,1},{2,66},{66,2},{3,67},{67,3},{4,68},{68... | collective-permute-start | bytes 56 | tf_op jit(solution)/shard_map/ppermute | solution.py:193
  171.1 1.2 copy-start.1
  172.4 1.2 copy-start.3
  179.0 26.1 %copy-start.11 = (bf16[4,56,512]{2,1,0:T(8,128)(2,1)}, bf16[4,56,512]{2,1,0:T(8,128)(2,1)S(1)}, u32[]{:S(2)}) copy-start(bf16[4,56,512]{2,1,0:T(8,128)(2,1)S(1)} %get-tuple-element.19) | copy-start | bytes 688132
  179.0 24.4 %collective-permute-start.8 = (bf16[224,512]{1,0:T(8,128)(2,1)S(1)}, bf16[224,512]{1,0:T(8,128)(2,1)S(1)}, u32[]{:S(2)}, u32[]{:S(2)}) collective-permute-start(bf16[224,512]{1,0:T(8,128)(2,1)S(1)} %bitcast.53), channel_id=1, source_target_pairs={{0,64},{64,0},{1,65},{65,1},{2,66},{66,2},{3,67},{67,3},{4,68},{68... | collective-permute-start | bytes 688136 | tf_op jit(solution)/shard_map/ppermute | solution.py:251
  180.9 41.6 %all-to-all-start.3 = ((bf16[32,144,128]{2,1,0:T(8,128)(2,1)}), bf16[32,144,128]{2,1,0:T(8,128)(2,1)}, u32[]{:S(2)}, u32[]{:S(2)}) async-start(bf16[32,144,128]{2,1,0:T(8,128)(2,1)} %dynamic_update_slice.3), calls=%async_computation.3 | async-start | bytes 2359296 | tf_op jit(solution)/shard_map/all_to_all | solution.py:18
  194.5 10.6 %copy-start.8 = (bf16[512,1024]{1,0:T(8,128)(2,1)S(1)}, bf16[512,1024]{1,0:T(8,128)(2,1)}, u32[]{:S(2)}) copy-start(bf16[512,1024]{1,0:T(8,128)(2,1)} %copy-done.7) | copy-start | bytes 3145732
  194.6 8.2 %collective-permute-start.6 = (bf16[8,224]{1,0:T(8,128)(2,1)S(1)}, bf16[8,224]{1,0:T(8,128)(2,1)S(1)}, u32[]{:S(2)}, u32[]{:S(2)}) collective-permute-start(bf16[8,224]{1,0:T(8,128)(2,1)S(1)} %concatenate.64), channel_id=1, source_target_pairs={{0,64},{64,0},{1,65},{65,1},{2,66},{66,2},{3,67},{67,3},{4,68},{68... | collective-permute-start | bytes 10760 | tf_op jit(solution)/shard_map/ppermute | solution.py:239
  198.4 8.6 %collective-permute-start.7 = (bf16[224,512]{1,0:T(8,128)(2,1)}, bf16[224,512]{1,0:T(8,128)(2,1)}, u32[]{:S(2)}, u32[]{:S(2)}) collective-permute-start(bf16[224,512]{1,0:T(8,128)(2,1)} %bitcast.17), channel_id=1, source_target_pairs={{0,64},{64,0},{1,65},{65,1},{2,66},{66,2},{3,67},{67,3},{4,68},{68... | collective-permute-start | bytes 688136 | tf_op jit(solution)/shard_map/ppermute | solution.py:251
  200.3 8.9 %collective-permute-start.4 = (bf16[224,512]{1,0:T(8,128)(2,1)}, bf16[224,512]{1,0:T(8,128)(2,1)}, u32[]{:S(2)}, u32[]{:S(2)}) collective-permute-start(bf16[224,512]{1,0:T(8,128)(2,1)} %bitcast.11), channel_id=1, source_target_pairs={{0,64},{64,0},{1,65},{65,1},{2,66},{66,2},{3,67},{67,3},{4,68},{68... | collective-permute-start | bytes 688136 | tf_op jit(solution)/shard_map/ppermute | solution.py:251
  203.4 1.7 copy-start.12
  205.1 1.4 copy-start.13
  206.6 2.2 copy-start.15
  209.2 1.8 copy-start.14
  211.0 17.4 %copy-start.19 = (f32[128,128]{1,0:T(8,128)S(1)}, f32[128,128]{1,0:T(8,128)}, u32[]{:S(2)}) copy-start(f32[128,128]{1,0:T(8,128)} %param.12) | copy-start | bytes 196612
  212.4 19.3 %copy-start.10 = (f32[224,1024]{1,0:T(8,128)S(1)}, f32[224,1024]{1,0:T(8,128)}, u32[]{:S(2)}) copy-start(f32[224,1024]{1,0:T(8,128)} %fusion.5) | copy-start | bytes 2752516
  212.4 19.3 %copy-start.20 = (bf16[4,224]{1,0:T(4,128)(2,1)S(1)}, bf16[4,224]{1,0:T(4,128)(2,1)}, u32[]{:S(2)}) copy-start(bf16[4,224]{1,0:T(4,128)(2,1)} %get-tuple-element.28) | copy-start | bytes 5380
  224.4 8.4 %copy-start.22 = (f32[8]{0:T(128)}, f32[8]{0:T(128)S(1)}, u32[]{:S(2)}) copy-start(f32[8]{0:T(128)S(1)} %compare_select_fusion.1) | copy-start | bytes 100

commit v7 on v5

--- a/solution.py
+++ b/solution.py
@@ -1,3 +1,5 @@
+import functools
+
 import jax
 import jax.numpy as jnp
 from jax import lax
@@ -62,6 +64,58 @@
         for z in range(n_gy):
             low[y * rows : (y + 1) * rows, z * cols : (z + 1) * cols] = low_got[z, y]
     parts[...] = dot(down_w[...], low[...], 1, 1).astype(bf16)
+
+
+def split_sums(in_two, place, got, keep, give, total):
+    own = keep.shape[0]
+    sums = got[0].astype(f32)
+    for j in range(1, got.shape[0]):
+        sums += got[j].astype(f32)
+    total[...] = sums
+    keep[...] = total[pl.ds(pl.multiple_of(place[0] * own, 8), own), :]
+    away = total[pl.ds(pl.multiple_of((1 - place[0]) * own, 8), own), :]
+    give[...] = away.astype(bf16)
+    if in_two:
+        ends = away[:, -128:]
+        lost = pltpu.roll(ends - ends.astype(bf16).astype(f32), 1, 1)
+        lane = lax.broadcasted_iota(jnp.int32, ends.shape, 1)
+        give[:, -128:] = jnp.where(lane == 1, ends + lost, ends).astype(bf16)
+
+
+def hidden_units(chip_units, place, keep, got, back_keep, back_got, own_terms, mine):
+    own, half = back_keep.shape
+    n_seq = half // SEQ_LEN
+    sums = keep[...] + got[...].astype(f32)
+    hidden_grad = back_keep[...] + back_got[...].astype(f32)
+    gate_sum, up_sum = sums[:, :half], sums[:, half : 2 * half]
+    head_down = sums[:, 2 * half : 2 * half + 1] + sums[:, 2 * half + 1 : 2 * half + 2]
+    gate_sigmoid = jax.nn.sigmoid(gate_sum)
+    silu_gate = gate_sum * gate_sigmoid
+    hidden = (silu_gate * up_sum).astype(bf16).astype(f32)
+    gate_slope = up_sum * gate_sigmoid * (1.0 + gate_sum * (1.0 - gate_sigmoid))
+
+    row = lax.broadcasted_iota(jnp.int32, (8, half), 0)
+    lane = lax.broadcasted_iota(jnp.int32, (8, half), 1)
+    blank = jnp.zeros((128 - own, half), f32)
+
+    def picked(value, first):
+        pick = (lane == (row - first) * SEQ_LEN + SEQ_LEN - 1) & (row >= first) & (row < first + n_seq)
+        value = jnp.concatenate([value * head_down, blank], axis=0).astype(bf16)
+        return dot(jnp.where(pick, 1.0, 0.0).astype(bf16), value, 1, 1)
+
+    unit = picked(gate_slope, 0) + picked(silu_gate, n_seq)
+    unit = jnp.concatenate([unit, jnp.zeros((8, half - 128), f32)], axis=1)
+    unit = pltpu.roll(unit, place[0], 1)
+
+    terms = jnp.sum(hidden * head_down, axis=0, keepdims=True) + own_terms[...]
+    for s in range(n_seq):
+        rest = jnp.sum(jnp.where(lane[:1] == s * SEQ_LEN + SEQ_LEN - 1, terms, 0.0), axis=1, keepdims=True)
+        for i in range(3):
+            piece = rest.astype(bf16).astype(f32)
+            unit += jnp.where((row == 0) & (lane == chip_units + i * n_seq + s), piece, 0.0)
+            rest = rest - piece
+    rows = jnp.concatenate([hidden_grad * gate_slope, hidden_grad * silu_gate, hidden, unit], axis=0)
+    mine[...] = rows.astype(bf16)
 
 
 def token_gradients(everyone, gate_w, up_w, sent, full):
@@ -138,7 +192,24 @@
         name="token_products",
     )(tok_got, gate_w, up_w, down_w)
     head_vec = head_vec[:1]
-    first = exchange(parts.reshape(n_gz, own, 2 * half + 128), GZ)
+    n_xx = lax.axis_size("xx")
+    first = exchange(parts.reshape(n_xx, 2 * own, 2 * half + 128), "xx")
+    y_half = lax.axis_index("yh").astype(jnp.int32)[None]
+    scalar = pl.BlockSpec(memory_space=pltpu.SMEM)
+
+    def halves(got, in_two):
+        lanes = got.shape[2]
+        keep, give = pl.pallas_call(
+            functools.partial(split_sums, in_two),
+            out_shape=(jax.ShapeDtypeStruct((own, lanes), f32), jax.ShapeDtypeStruct((own, lanes), bf16)),
+            in_specs=[scalar, whole],
+            out_specs=(whole,) * 2,
+            scratch_shapes=[pltpu.VMEM((2 * own, lanes), f32)],
+            compiler_params=grant,
+            cost_estimate=pl.CostEstimate(flops=8 * own * lanes, bytes_accessed=22 * own * lanes, transcendentals=0),
+            name="split_sums",
+        )(y_half, got)
+        return keep, lax.ppermute(give, "yh", SWAP)
 
     back_parts, low_half = pl.pallas_call(
         cotangent_products,
@@ -155,39 +226,28 @@
         name="cotangent_products",
     )(low_got, down_w)
     first, back_parts = lax.optimization_barrier((first, back_parts))
-    second = exchange(back_parts.reshape(n_gz, own, half), GZ)
-
-    sums = jnp.sum(first.astype(f32), axis=0)
-    gate_sum, up_sum = sums[:, :half], sums[:, half : 2 * half]
-    head_down = sums[:, 2 * half : 2 * half + 1] + sums[:, 2 * half + 1 : 2 * half + 2]
-    gate_sigmoid = jax.nn.sigmoid(gate_sum)
-    silu_gate = gate_sum * gate_sigmoid
-    hidden = (silu_gate * up_sum).astype(bf16)
-    gate_slope = up_sum * gate_sigmoid * (1.0 + gate_sum * (1.0 - gate_sigmoid))
-
-    def last_cols(value):
-        return value.reshape(own, n_yl, rows)[:, :, rows - 1].astype(f32)
-
-    gate_unit = (head_down * last_cols(gate_slope)).astype(bf16).T
-    up_unit = (head_down * last_cols(silu_gate)).astype(bf16).T
+    second = exchange(back_parts.reshape(n_xx, 2 * own, half), "xx")
+    sums, sums_got = halves(first, True)
+    back, back_got = halves(second, False)
+
     own_term = jnp.sum(tokens[rows - 1].astype(f32) * reward_head.astype(f32))
-    terms = jnp.sum(last_cols(hidden) * head_down, axis=0)
-    terms = terms + jnp.where(jnp.arange(n_yl) == lax.axis_index("yl"), own_term, 0.0)
-    unit_rows = lax.dynamic_update_slice(
-        jnp.zeros((2 * n_yl, half), bf16),
-        jnp.concatenate([gate_unit, up_unit], axis=0),
-        (0, lax.axis_index(GZ) * own),
-    )
-    term_rows = pieces(terms).reshape(1, -1)
-    unit_rows = lax.dynamic_update_slice(unit_rows, term_rows, (0, 2 * units))
-    silu_gate, gate_slope, early, second = lax.optimization_barrier(
-        (silu_gate, gate_slope, jnp.concatenate([hidden, unit_rows], axis=0), second)
-    )
-    hidden_grad = jnp.sum(second.astype(f32), axis=0)
-    up_grad = (hidden_grad * silu_gate).astype(bf16)
-    gate_grad = (hidden_grad * gate_slope).astype(bf16)
-    mine = jnp.concatenate([gate_grad, up_grad, early], axis=0)
-    everyone = to_all(mine, GZ, n_gz)
+    spot = lax.axis_index("yl") * rows + rows - 1
+    own_terms = jnp.where(jnp.arange(half)[None, :] == spot, own_term, 0.0)
+    place = (lax.axis_index(("xx", "yh")) * own).astype(jnp.int32)[None]
+    mine = pl.pallas_call(
+        functools.partial(hidden_units, 2 * units),
+        out_shape=jax.ShapeDtypeStruct((3 * own + 8, half), bf16),
+        in_specs=[scalar] + [whole] * 5,
+        out_specs=whole,
+        compiler_params=grant,
+        cost_estimate=pl.CostEstimate(
+            flops=40 * own * half, bytes_accessed=12 * own * half, transcendentals=own * half
+        ),
+        name="hidden_units",
+    )(place, sums, sums_got, back, back_got, own_terms)
+    other = lax.ppermute(mine, "yh", SWAP)
+    pair = jnp.stack([jnp.where(y_half == 0, mine, other), jnp.where(y_half == 0, other, mine)])
+    everyone = to_all(pair, "xx", n_xx).reshape(n_gz, 3 * own + 8, half)
     core_terms = jnp.sum(
         everyone[:, 3 * own, 2 * units : 2 * units + 3 * n_yl].astype(f32).reshape(n_gz * 3, n_yl), axis=0
     )

time: 225 us -> 205 us (0.911)
  starting transfers between devices: 106 us -> 95.9 us
  waiting for transfers between devices: 53.4 us -> 44 us
  other arithmetic: 14.9 us -> 9.74 us
  matrix products: 10 us -> 13.4 us
    all_to_all x6, starting transfers between devices: 58.1 us -> 38.2 us  [exchange(): return lax.all_to_all(pieces, axes, 0, 0)]
    all_to_all x6, waiting for transfers between devices: 46.8 us -> 27 us  [exchange(): return lax.all_to_all(pieces, axes, 0, 0)]
    ppermute x0 -> x3, starting transfers between devices: none -> 16.6 us  [the longest x2 10.6 us: halves(): return (keep, lax.ppermute(give, 'yh', SWAP))]
    ppermute x1, starting transfers between devices: 14.8 us -> 6.56 us  [body(): tok_sib = lax.ppermute(tok_half, 'co', SWAP)]
    ppermute x1, starting transfers between devices: 1.91 us -> 9.15 us  [body(): low_sib = lax.ppermute(low_half, 'co', SWAP)]
    ppermute x1, starting transfers between devices: 14.3 us -> 8.78 us  [body(): pair_terms = jnp.stack([core_terms, lax.ppermute(core_terms, 'co', SWAP)])]
    all_gather x1, waiting for transfers between devices: 5.19 us -> 9.84 us  [body(): low_got = lax.all_gather(low_got, 'gy')]
    ppermute x0 -> x3, waiting for transfers between devices: none -> 4.37 us  [the longest x2 4.37 us: halves(): return (keep, lax.ppermute(give, 'yh', SWAP))]
  transfers between devices with their start and end apart: 17 -> 20, of which waited for: 7 -> 7; matrix products, arithmetic and copies ran while one was open for 10% -> 13% of each run, Pallas kernels for 3% -> 4%
where the time goes in v7:
time: 205 us; the launch traced here: 203 us
  starting transfers between devices  95.9 us (47%)
  waiting for transfers between devices  44 us (21%)
  local copies, waits for them, and re-layouts  17.2 us (8%)
  between operations  14.7 us (7%)
  matrix products  13.4 us (7%)
  other arithmetic  9.74 us (5%)
  Pallas kernels  7.87 us (4%)
    all_to_all x6, starting transfers between devices, exchange(): return lax.all_to_all(pieces, axes, 0, 0)  38.2 us
    all_to_all x6, waiting for transfers between devices, exchange(): return lax.all_to_all(pieces, axes, 0, 0)  27 us
    dot_general x9, matrix products, dot(): lax.dot_general(left, right, (((left_dim,), (right_dim,)), ((), ())), pre...  13.4 us
    ppermute x2, starting transfers between devices, halves(): return (keep, lax.ppermute(give, 'yh', SWAP))  10.6 us
    all_gather x1, waiting for transfers between devices, body(): low_got = lax.all_gather(low_got, 'gy')  9.84 us
    ppermute x1, starting transfers between devices, body(): low_sib = lax.ppermute(low_half, 'co', SWAP)  9.15 us
    ppermute x1, starting transfers between devices, body(): pair_terms = jnp.stack([core_terms, lax.ppermute(core_terms, 'co', SWAP)])  8.78 us
    ppermute x3, starting transfers between devices, chip_block(): lax.ppermute(weight, 'co', SWAP)  7.76 us
  transfers between devices with their start and end apart: 20, of which 7 were waited for; matrix products, arithmetic and copies ran while one was open for 13% of the time, Pallas kernels for 4%

profile of v7, /device:TPU:1, one launch (start us, length us, event | category | flops | bytes accessed | tf_op | source)
XLA Modules:
  0.0 202.7 jit_solution(1358573614604470594)
XLA Ops:
  7.2 0.8 convert_element_type.49
  8.0 0.7 broadcast_in_dim.96
  8.7 5.4 %all-to-all-start = ((bf16[4,128,128]{2,1,0:T(8,128)(2,1)}), bf16[4,128,128]{2,1,0:T(8,128)(2,1)S(1)}, u32[]{:S(2)}, u32[]{:S(2)}) async-start(bf16[4,128,128]{2,1,0:T(8,128)(2,1)} %broadcast_in_dim.96), calls=%async_computation | async-start | bytes 262144 | tf_op jit(solution)/shard_map/all_to_all | solution.py:20
  14.1 0.7 broadcast_in_dim.97
  14.8 0.8 pad_maximum_fusion.1
  15.5 3.4 %all-to-all-done = bf16[4,128,128]{2,1,0:T(8,128)(2,1)S(1)} async-done(((bf16[4,128,128]{2,1,0:T(8,128)(2,1)}), bf16[4,128,128]{2,1,0:T(8,128)(2,1)S(1)}, u32[]{:S(2)}, u32[]{:S(2)}) %all-to-all-start) | async-done | bytes 131104 | tf_op jit(solution)/shard_map/all_to_all | solution.py:20
  18.9 1.2 broadcast_in_dim.98
  20.1 12.6 %all-to-all-start.1 = ((bf16[32,144,128]{2,1,0:T(8,128)(2,1)}), bf16[32,144,128]{2,1,0:T(8,128)(2,1)}, u32[]{:S(2)}, u32[]{:S(2)}) async-start(bf16[32,144,128]{2,1,0:T(8,128)(2,1)} %broadcast_in_dim.98), calls=%async_computation.1 | async-start | bytes 2359296 | tf_op jit(solution)/shard_map/all_to_all | solution.py:20
  32.7 0.7 all-gather.3.cloned.1.call-update
  33.4 3.4 %collective-permute-start.2 = (bf16[224,1024]{1,0:T(8,128)(2,1)S(1)}, bf16[224,1024]{1,0:T(8,128)(2,1)S(1)}, u32[]{:S(2)}, u32[]{:S(2)}) collective-permute-start(bf16[224,1024]{1,0:T(8,128)(2,1)S(1)} %copy-done.12), channel_id=1, source_target_pairs={{0,64},{64,0},{1,65},{65,1},{2,66},{66,2},{3,67},{67,3},{4,68},{68... | collective-permute-start | bytes 1376264 | tf_op jit(solution)/shard_map/ppermute | solution.py:161
  36.9 1.9 collective-permute-start.1
  38.8 2.4 %collective-permute-start = (bf16[224,1024]{1,0:T(8,128)(2,1)S(1)}, bf16[224,1024]{1,0:T(8,128)(2,1)S(1)}, u32[]{:S(2)}, u32[]{:S(2)}) collective-permute-start(bf16[224,1024]{1,0:T(8,128)(2,1)S(1)} %copy-done.15), channel_id=1, source_target_pairs={{0,64},{64,0},{1,65},{65,1},{2,66},{66,2},{3,67},{67,3},{4,68},{68... | collective-permute-start | bytes 1376264 | tf_op jit(solution)/shard_map/ppermute | solution.py:161
  41.4 1.2 collective-permute-done
  42.6 1.4 maximum_maximum_fusion.1
  44.0 17.0 %all-to-all-done.1.tok_got = bf16[32,144,128]{2,1,0:T(8,128)(2,1)} async-done(((bf16[32,144,128]{2,1,0:T(8,128)(2,1)}), bf16[32,144,128]{2,1,0:T(8,128)(2,1)}, u32[]{:S(2)}, u32[]{:S(2)}) %all-to-all-start.1) | async-done | bytes 1179680 | tf_op jit(solution)/shard_map/all_to_all | solution.py:20
  61.0 2.9 %token_products.1 = (bf16[448,1152]{1,0:T(8,128)(2,1)S(1)}, bf16[512,1024]{1,0:T(8,128)(2,1)}, bf16[16,1024]{1,0:T(8,128)(2,1)S(1)}) custom-call(bf16[32,144,128]{2,1,0:T(8,128)(2,1)} %all-to-all-done.1.tok_got, bf16[512,1024]{1,0:T(8,128)(2,1)S(1)} %get-tuple-element.57.gate_w, bf16[512,1024]{1,0:T(8,128)(2,1)S(1)} %get-tuple-element.56.up_w, ...), custom_call_target="tpu_custom_call" | custom-call | flops 1056964608 | bytes 8388608 | tf_op jit(solution)/shard_map/token_products/pallas_call | solution.py:178
  63.9 1.0 copy-done.4
  64.9 0.6 copy-done.5
  65.5 4.2 %all-to-all-start.2 = ((bf16[4,112,1152]{2,1,0:T(8,128)(2,1)}), bf16[4,112,1152]{2,1,0:T(8,128)(2,1)}, u32[]{:S(2)}, u32[]{:S(2)}) async-start(bf16[4,112,1152]{2,1,0:T(8,128)(2,1)} %bitcast.62), calls=%async_computation.2 | async-start | bytes 2064384 | tf_op jit(solution)/shard_map/all_to_all | solution.py:20
  69.7 9.8 %all-gather.3.cloned.1.call-done = bf16[32,128,128]{2,1,0:T(8,128)(2,1)} async-done(((bf16[4,128,128]{2,1,0:T(8,128)(2,1)}), bf16[32,128,128]{2,1,0:T(8,128)(2,1)}) %all-gather.3.cloned.1.call-update) | async-done | bytes 1048592 | tf_op jit(solution)/shard_map/all_gather | solution.py:172
  79.6 1.2 copy-done.3
  80.8 1.5 cotangent_products.1
  82.3 1.0 copy-done.1
  83.3 4.1 %all-to-all-start.3 = ((bf16[4,112,512]{2,1,0:T(8,128)(2,1)}), bf16[4,112,512]{2,1,0:T(8,128)(2,1)S(1)}, u32[]{:S(2)}, u32[]{:S(2)}) async-start(bf16[4,112,512]{2,1,0:T(8,128)(2,1)} %bitcast.5), calls=%async_computation.3 | async-start | bytes 917504 | tf_op jit(solution)/shard_map/all_to_all | solution.py:20
  87.4 1.5 split_sums.2
  88.9 6.8 %collective-permute-start.3 = (bf16[56,1152]{1,0:T(8,128)(2,1)S(1)}, bf16[56,1152]{1,0:T(8,128)(2,1)S(1)}, u32[]{:S(2)}, u32[]{:S(2)}) collective-permute-start(bf16[56,1152]{1,0:T(8,128)(2,1)S(1)} %get-tuple-element.26), channel_id=1, source_target_pairs={{0,4},{4,0},{1,5},{5,1},{2,6},{6,2},{3,7},{7,3},{8,12},{12,8},{9,1... | collective-permute-start | bytes 387080 | tf_op jit(solution)/shard_map/ppermute | solution.py:212
  95.7 1.3 fusion.27
  97.1 3.8 %collective-permute-start.4 = (bf16[56,512]{1,0:T(8,128)(2,1)S(1)}, bf16[56,512]{1,0:T(8,128)(2,1)S(1)}, u32[]{:S(2)}, u32[]{:S(2)}) collective-permute-start(bf16[56,512]{1,0:T(8,128)(2,1)S(1)} %get-tuple-element.29), channel_id=1, source_target_pairs={{0,4},{4,0},{1,5},{5,1},{2,6},{6,2},{3,7},{7,3},{8,12},{12,8},{9,1... | collective-permute-start | bytes 172040 | tf_op jit(solution)/shard_map/ppermute | solution.py:212
  100.9 0.7 compare_select_fusion.own_terms
  101.6 4.4 %collective-permute-done.4.back_got = bf16[56,512]{1,0:T(8,128)(2,1)S(1)} collective-permute-done((bf16[56,512]{1,0:T(8,128)(2,1)S(1)}, bf16[56,512]{1,0:T(8,128)(2,1)S(1)}, u32[]{:S(2)}, u32[]{:S(2)}) %collective-permute-start.4) | collective-permute-done | bytes 57376 | tf_op jit(solution)/shard_map/ppermute | solution.py:212
  106.3 6.0 %collective-permute-start.5 = (bf16[176,512]{1,0:T(8,128)(2,1)S(1)}, bf16[176,512]{1,0:T(8,128)(2,1)S(1)}, u32[]{:S(2)}, u32[]{:S(2)}) collective-permute-start(bf16[176,512]{1,0:T(8,128)(2,1)S(1)} %hidden_units.1), channel_id=1, source_target_pairs={{0,4},{4,0},{1,5},{5,1},{2,6},{6,2},{3,7},{7,3},{8,12},{12,8},{9,1... | collective-permute-start | bytes 540680 | tf_op jit(solution)/shard_map/ppermute | solution.py:248
  112.3 6.6 %collective-permute-start.8 = (bf16[512,1024]{1,0:T(8,128)(2,1)}, bf16[512,1024]{1,0:T(8,128)(2,1)}, u32[]{:S(2)}, u32[]{:S(2)}) collective-permute-start(bf16[512,1024]{1,0:T(8,128)(2,1)} %get-tuple-element.32), channel_id=1, source_target_pairs={{0,64},{64,0},{1,65},{65,1},{2,66},{66,2},{3,67},{67,3},{4,68},{68... | collective-permute-start | bytes 3145736 | tf_op jit(solution)/shard_map/ppermute | solution.py:298
  119.0 1.3 broadcast_in_dim.101
  120.3 3.7 %all-to-all-start.4 = ((bf16[4,2,176,512]{3,2,1,0:T(8,128)(2,1)}), bf16[4,2,176,512]{3,2,1,0:T(8,128)(2,1)S(1)}, u32[]{:S(2)}, u32[]{:S(2)}) async-start(bf16[4,2,176,512]{3,2,1,0:T(8,128)(2,1)} %broadcast_in_dim.101), calls=%async_computation.4 | async-start | bytes 2883584 | tf_op jit(solution)/shard_map/all_to_all | solution.py:20
  125.1 9.1 %collective-permute-start.12 = (bf16[512,1024]{1,0:T(8,128)(2,1)}, bf16[512,1024]{1,0:T(8,128)(2,1)}, u32[]{:S(2)}, u32[]{:S(2)}) collective-permute-start(bf16[512,1024]{1,0:T(8,128)(2,1)} %copy-done.1), channel_id=1, source_target_pairs={{0,64},{64,0},{1,65},{65,1},{2,66},{66,2},{3,67},{67,3},{4,68},{68... | collective-permute-start | bytes 3145736 | tf_op jit(solution)/shard_map/ppermute | solution.py:299
  134.3 0.9 slice.159
  135.1 1.3 slice_convert_fusion.1
  136.4 0.9 slice.160
  137.3 1.5 token_gradients.1
  138.9 1.0 copy-done
  140.1 8.8 %collective-permute-start.6 = (f32[4]{0:T(128)S(1)}, f32[4]{0:T(128)S(1)}, u32[]{:S(2)}, u32[]{:S(2)}) collective-permute-start(f32[4]{0:T(128)S(1)} %reduce_sum.76), channel_id=1, source_target_pairs={{0,64},{64,0},{1,65},{65,1},{2,66},{66,2},{3,67},{67,3},{4,68},{68... | collective-permute-start | bytes 56 | tf_op jit(solution)/shard_map/ppermute | solution.py:254
  148.9 0.8 collective-permute-done.6
  149.8 1.7 dynamic_update_slice.3
  151.5 8.1 %all-to-all-start.5 = ((bf16[32,144,128]{2,1,0:T(8,128)(2,1)}), bf16[32,144,128]{2,1,0:T(8,128)(2,1)S(1)}, u32[]{:S(2)}, u32[]{:S(2)}) async-start(bf16[32,144,128]{2,1,0:T(8,128)(2,1)} %dynamic_update_slice.3), calls=%async_computation.5 | async-start | bytes 2359296 | tf_op jit(solution)/shard_map/all_to_all | solution.py:20
  159.6 1.0 fusion.31
  160.6 2.5 %collective-permute-start.7 = (bf16[224,512]{1,0:T(8,128)(2,1)}, bf16[224,512]{1,0:T(8,128)(2,1)S(1)}, u32[]{:S(2)}, u32[]{:S(2)}) collective-permute-start(bf16[224,512]{1,0:T(8,128)(2,1)} %bitcast.18), channel_id=1, source_target_pairs={{0,64},{64,0},{1,65},{65,1},{2,66},{66,2},{3,67},{67,3},{4,68},{68... | collective-permute-start | bytes 688136 | tf_op jit(solution)/shard_map/ppermute | solution.py:312
  163.2 1.9 collective-permute-start.9
  165.2 0.6 fusion.32
  165.7 2.4 %collective-permute-start.10 = (bf16[224,512]{1,0:T(8,128)(2,1)}, bf16[224,512]{1,0:T(8,128)(2,1)S(1)}, u32[]{:S(2)}, u32[]{:S(2)}) collective-permute-start(bf16[224,512]{1,0:T(8,128)(2,1)} %bitcast.24), channel_id=1, source_target_pairs={{0,64},{64,0},{1,65},{65,1},{2,66},{66,2},{3,67},{67,3},{4,68},{68... | collective-permute-start | bytes 688136 | tf_op jit(solution)/shard_map/ppermute | solution.py:312
  168.1 2.1 %collective-permute-start.11 = (bf16[224,512]{1,0:T(8,128)(2,1)}, bf16[224,512]{1,0:T(8,128)(2,1)S(1)}, u32[]{:S(2)}, u32[]{:S(2)}) collective-permute-start(bf16[224,512]{1,0:T(8,128)(2,1)} %bitcast.26), channel_id=1, source_target_pairs={{0,64},{64,0},{1,65},{65,1},{2,66},{66,2},{3,67},{67,3},{4,68},{68... | collective-permute-start | bytes 688136 | tf_op jit(solution)/shard_map/ppermute | solution.py:312
  170.5 0.8 copy.31
  171.9 1.6 fusion.34
  173.5 1.6 fusion.5
  175.2 1.7 fusion.35
  176.9 1.6 fusion.3
  178.6 1.7 fusion.36
  180.3 1.3 fusion.1
  182.1 6.7 %all-to-all-done.5 = bf16[32,144,128]{2,1,0:T(8,128)(2,1)S(1)} async-done(((bf16[32,144,128]{2,1,0:T(8,128)(2,1)}), bf16[32,144,128]{2,1,0:T(8,128)(2,1)S(1)}, u32[]{:S(2)}, u32[]{:S(2)}) %all-to-all-start.5) | async-done | bytes 1179680 | tf_op jit(solution)/shard_map/all_to_all | solution.py:20
  189.7 0.6 broadcast_multiply_fusion
  190.3 0.6 fusion.26
  191.1 0.7 fusion.6
  192.1 1.3 fusion.4
  193.4 1.3 fusion.2
  194.6 1.3 fusion
  (111 shorter events, 4.9 us)
Async XLA Ops:
  8.7 10.2 %all-to-all-start = ((bf16[4,128,128]{2,1,0:T(8,128)(2,1)}), bf16[4,128,128]{2,1,0:T(8,128)(2,1)S(1)}, u32[]{:S(2)}, u32[]{:S(2)}) async-start(bf16[4,128,128]{2,1,0:T(8,128)(2,1)} %broadcast_in_dim.96), calls=%async_computation | async-start | bytes 262144 | tf_op jit(solution)/shard_map/all_to_all | solution.py:20
  18.9 1.2 copy-start.11
  20.0 13.4 %copy-start.12 = (bf16[224,1024]{1,0:T(8,128)(2,1)S(1)}, bf16[224,1024]{1,0:T(8,128)(2,1)}, u32[]{:S(2)}) copy-start(bf16[224,1024]{1,0:T(8,128)(2,1)} %param.10) | copy-start | bytes 1376260
  20.1 16.8 %copy-start.13 = (bf16[224,1024]{1,0:T(8,128)(2,1)S(1)}, bf16[224,1024]{1,0:T(8,128)(2,1)}, u32[]{:S(2)}) copy-start(bf16[224,1024]{1,0:T(8,128)(2,1)} %param.9) | copy-start | bytes 1376260
  20.1 18.7 %copy-start.15 = (bf16[224,1024]{1,0:T(8,128)(2,1)S(1)}, bf16[224,1024]{1,0:T(8,128)(2,1)}, u32[]{:S(2)}) copy-start(bf16[224,1024]{1,0:T(8,128)(2,1)} %param.8) | copy-start | bytes 1376260
  20.1 41.0 %all-to-all-start.1 = ((bf16[32,144,128]{2,1,0:T(8,128)(2,1)}), bf16[32,144,128]{2,1,0:T(8,128)(2,1)}, u32[]{:S(2)}, u32[]{:S(2)}) async-start(bf16[32,144,128]{2,1,0:T(8,128)(2,1)} %broadcast_in_dim.98), calls=%async_computation.1 | async-start | bytes 2359296 | tf_op jit(solution)/shard_map/all_to_all | solution.py:20
  32.6 10.0 %copy-start.14 = (bf16[224,1024]{1,0:T(8,128)(2,1)S(1)}, bf16[224,1024]{1,0:T(8,128)(2,1)}, u32[]{:S(2)}) copy-start(bf16[224,1024]{1,0:T(8,128)(2,1)} %param.9) | copy-start | bytes 1376260
  32.7 46.9 %all-gather.3.cloned.1.call-start = ((), (), s32[]{:S(2)}) async-start(), calls=%async_computation.6 | async-start | bytes 1179648 | tf_op jit(solution)/shard_map/all_gather | solution.py:172
  33.4 7.9 %collective-permute-start.2 = (bf16[224,1024]{1,0:T(8,128)(2,1)S(1)}, bf16[224,1024]{1,0:T(8,128)(2,1)S(1)}, u32[]{:S(2)}, u32[]{:S(2)}) collective-permute-start(bf16[224,1024]{1,0:T(8,128)(2,1)S(1)} %copy-done.12), channel_id=1, source_target_pairs={{0,64},{64,0},{1,65},{65,1},{2,66},{66,2},{3,67},{67,3},{4,68},{68... | collective-permute-start | bytes 1376264 | tf_op jit(solution)/shard_map/ppermute | solution.py:161
  36.9 4.5 %collective-permute-start.1 = (bf16[224,1024]{1,0:T(8,128)(2,1)S(1)}, bf16[224,1024]{1,0:T(8,128)(2,1)S(1)}, u32[]{:S(2)}, u32[]{:S(2)}) collective-permute-start(bf16[224,1024]{1,0:T(8,128)(2,1)S(1)} %copy-done.13), channel_id=1, source_target_pairs={{0,64},{64,0},{1,65},{65,1},{2,66},{66,2},{3,67},{67,3},{4,68},{68... | collective-permute-start | bytes 1376264 | tf_op jit(solution)/shard_map/ppermute | solution.py:161
  38.8 3.8 %collective-permute-start = (bf16[224,1024]{1,0:T(8,128)(2,1)S(1)}, bf16[224,1024]{1,0:T(8,128)(2,1)S(1)}, u32[]{:S(2)}, u32[]{:S(2)}) collective-permute-start(bf16[224,1024]{1,0:T(8,128)(2,1)S(1)} %copy-done.15), channel_id=1, source_target_pairs={{0,64},{64,0},{1,65},{65,1},{2,66},{66,2},{3,67},{67,3},{4,68},{68... | collective-permute-start | bytes 1376264 | tf_op jit(solution)/shard_map/ppermute | solution.py:161
  63.9 1.0 copy-start.4
  64.9 0.6 copy-start.5
  65.5 17.8 %all-to-all-start.2 = ((bf16[4,112,1152]{2,1,0:T(8,128)(2,1)}), bf16[4,112,1152]{2,1,0:T(8,128)(2,1)}, u32[]{:S(2)}, u32[]{:S(2)}) async-start(bf16[4,112,1152]{2,1,0:T(8,128)(2,1)} %bitcast.62), calls=%async_computation.2 | async-start | bytes 2064384 | tf_op jit(solution)/shard_map/all_to_all | solution.py:20
  79.6 1.2 copy-start.3
  82.3 1.0 copy-start.1
  83.3 12.4 %copy-start.25 = (bf16[128]{0:T(256)(128)(2,1)S(1)}, bf16[128]{0:T(256)(128)(2,1)}, u32[]{:S(2)}) copy-start(bf16[128]{0:T(256)(128)(2,1)} %param.11) | copy-start | bytes 772
  83.3 13.7 %all-to-all-start.3 = ((bf16[4,112,512]{2,1,0:T(8,128)(2,1)}), bf16[4,112,512]{2,1,0:T(8,128)(2,1)S(1)}, u32[]{:S(2)}, u32[]{:S(2)}) async-start(bf16[4,112,512]{2,1,0:T(8,128)(2,1)} %bitcast.5), calls=%async_computation.3 | async-start | bytes 917504 | tf_op jit(solution)/shard_map/all_to_all | solution.py:20
  88.9 12.7 %collective-permute-start.3 = (bf16[56,1152]{1,0:T(8,128)(2,1)S(1)}, bf16[56,1152]{1,0:T(8,128)(2,1)S(1)}, u32[]{:S(2)}, u32[]{:S(2)}) collective-permute-start(bf16[56,1152]{1,0:T(8,128)(2,1)S(1)} %get-tuple-element.26), channel_id=1, source_target_pairs={{0,4},{4,0},{1,5},{5,1},{2,6},{6,2},{3,7},{7,3},{8,12},{12,8},{9,1... | collective-permute-start | bytes 387080 | tf_op jit(solution)/shard_map/ppermute | solution.py:212
  97.1 8.8 %collective-permute-start.4 = (bf16[56,512]{1,0:T(8,128)(2,1)S(1)}, bf16[56,512]{1,0:T(8,128)(2,1)S(1)}, u32[]{:S(2)}, u32[]{:S(2)}) collective-permute-start(bf16[56,512]{1,0:T(8,128)(2,1)S(1)} %get-tuple-element.29), channel_id=1, source_target_pairs={{0,4},{4,0},{1,5},{5,1},{2,6},{6,2},{3,7},{7,3},{8,12},{12,8},{9,1... | collective-permute-start | bytes 172040 | tf_op jit(solution)/shard_map/ppermute | solution.py:212
  106.3 12.6 %collective-permute-start.5 = (bf16[176,512]{1,0:T(8,128)(2,1)S(1)}, bf16[176,512]{1,0:T(8,128)(2,1)S(1)}, u32[]{:S(2)}, u32[]{:S(2)}) collective-permute-start(bf16[176,512]{1,0:T(8,128)(2,1)S(1)} %hidden_units.1), channel_id=1, source_target_pairs={{0,4},{4,0},{1,5},{5,1},{2,6},{6,2},{3,7},{7,3},{8,12},{12,8},{9,1... | collective-permute-start | bytes 540680 | tf_op jit(solution)/shard_map/ppermute | solution.py:248
  112.3 24.1 %collective-permute-start.8 = (bf16[512,1024]{1,0:T(8,128)(2,1)}, bf16[512,1024]{1,0:T(8,128)(2,1)}, u32[]{:S(2)}, u32[]{:S(2)}) collective-permute-start(bf16[512,1024]{1,0:T(8,128)(2,1)} %get-tuple-element.32), channel_id=1, source_target_pairs={{0,64},{64,0},{1,65},{65,1},{2,66},{66,2},{3,67},{67,3},{4,68},{68... | collective-permute-start | bytes 3145736 | tf_op jit(solution)/shard_map/ppermute | solution.py:298
  120.3 4.3 %copy-start.28 = (s32[4,2]{0,1:T(2,128)S(1)}, s32[4,2]{0,1:T(2,128)}, u32[]{:S(2)}) copy-start(s32[4,2]{0,1:T(2,128)} %param.13) | copy-start | bytes 100
  120.3 17.1 %all-to-all-start.4 = ((bf16[4,2,176,512]{3,2,1,0:T(8,128)(2,1)}), bf16[4,2,176,512]{3,2,1,0:T(8,128)(2,1)S(1)}, u32[]{:S(2)}, u32[]{:S(2)}) async-start(bf16[4,2,176,512]{3,2,1,0:T(8,128)(2,1)} %broadcast_in_dim.101), calls=%async_computation.4 | async-start | bytes 2883584 | tf_op jit(solution)/shard_map/all_to_all | solution.py:20
  125.1 53.4 %collective-permute-start.12 = (bf16[512,1024]{1,0:T(8,128)(2,1)}, bf16[512,1024]{1,0:T(8,128)(2,1)}, u32[]{:S(2)}, u32[]{:S(2)}) collective-permute-start(bf16[512,1024]{1,0:T(8,128)(2,1)} %copy-done.1), channel_id=1, source_target_pairs={{0,64},{64,0},{1,65},{65,1},{2,66},{66,2},{3,67},{67,3},{4,68},{68... | collective-permute-start | bytes 3145736 | tf_op jit(solution)/shard_map/ppermute | solution.py:299
  138.9 1.0 copy-start
  140.1 9.6 %collective-permute-start.6 = (f32[4]{0:T(128)S(1)}, f32[4]{0:T(128)S(1)}, u32[]{:S(2)}, u32[]{:S(2)}) collective-permute-start(f32[4]{0:T(128)S(1)} %reduce_sum.76), channel_id=1, source_target_pairs={{0,64},{64,0},{1,65},{65,1},{2,66},{66,2},{3,67},{67,3},{4,68},{68... | collective-permute-start | bytes 56 | tf_op jit(solution)/shard_map/ppermute | solution.py:254
  151.5 37.3 %all-to-all-start.5 = ((bf16[32,144,128]{2,1,0:T(8,128)(2,1)}), bf16[32,144,128]{2,1,0:T(8,128)(2,1)S(1)}, u32[]{:S(2)}, u32[]{:S(2)}) async-start(bf16[32,144,128]{2,1,0:T(8,128)(2,1)} %dynamic_update_slice.3), calls=%async_computation.5 | async-start | bytes 2359296 | tf_op jit(solution)/shard_map/all_to_all | solution.py:20
  160.6 12.9 %copy-start.7 = (bf16[4,56,512]{2,1,0:T(8,128)(2,1)}, bf16[4,56,512]{2,1,0:T(8,128)(2,1)S(1)}, u32[]{:S(2)}) copy-start(bf16[4,56,512]{2,1,0:T(8,128)(2,1)S(1)} %get-tuple-element.37) | copy-start | bytes 688132
  160.6 11.2 %collective-permute-start.7 = (bf16[224,512]{1,0:T(8,128)(2,1)}, bf16[224,512]{1,0:T(8,128)(2,1)S(1)}, u32[]{:S(2)}, u32[]{:S(2)}) collective-permute-start(bf16[224,512]{1,0:T(8,128)(2,1)} %bitcast.18), channel_id=1, source_target_pairs={{0,64},{64,0},{1,65},{65,1},{2,66},{66,2},{3,67},{67,3},{4,68},{68... | collective-permute-start | bytes 688136 | tf_op jit(solution)/shard_map/ppermute | solution.py:312
  163.2 8.1 %collective-permute-start.9 = (bf16[8,224]{1,0:T(8,128)(2,1)S(1)}, bf16[8,224]{1,0:T(8,128)(2,1)S(1)}, u32[]{:S(2)}, u32[]{:S(2)}) collective-permute-start(bf16[8,224]{1,0:T(8,128)(2,1)S(1)} %concatenate.64), channel_id=1, source_target_pairs={{0,64},{64,0},{1,65},{65,1},{2,66},{66,2},{3,67},{67,3},{4,68},{68... | collective-permute-start | bytes 10760 | tf_op jit(solution)/shard_map/ppermute | solution.py:300
  165.7 9.4 %collective-permute-start.10 = (bf16[224,512]{1,0:T(8,128)(2,1)}, bf16[224,512]{1,0:T(8,128)(2,1)S(1)}, u32[]{:S(2)}, u32[]{:S(2)}) collective-permute-start(bf16[224,512]{1,0:T(8,128)(2,1)} %bitcast.24), channel_id=1, source_target_pairs={{0,64},{64,0},{1,65},{65,1},{2,66},{66,2},{3,67},{67,3},{4,68},{68... | collective-permute-start | bytes 688136 | tf_op jit(solution)/shard_map/ppermute | solution.py:312
  168.1 10.4 %collective-permute-start.11 = (bf16[224,512]{1,0:T(8,128)(2,1)}, bf16[224,512]{1,0:T(8,128)(2,1)S(1)}, u32[]{:S(2)}, u32[]{:S(2)}) collective-permute-start(bf16[224,512]{1,0:T(8,128)(2,1)} %bitcast.26), channel_id=1, source_target_pairs={{0,64},{64,0},{1,65},{65,1},{2,66},{66,2},{3,67},{67,3},{4,68},{68... | collective-permute-start | bytes 688136 | tf_op jit(solution)/shard_map/ppermute | solution.py:312
  170.3 3.2 %copy-start.10 = (bf16[4,56,512]{2,1,0:T(8,128)(2,1)S(1)}, bf16[4,56,512]{2,1,0:T(8,128)(2,1)}, u32[]{:S(2)}) copy-start(bf16[4,56,512]{2,1,0:T(8,128)(2,1)} %get-tuple-element.42) | copy-start | bytes 688132
  175.2 1.7 copy-start.9
  178.5 1.8 copy-start.2
  178.5 1.8 copy-start.8
  181.6 9.4 %copy-start.16 = (f32[128,128]{1,0:T(8,128)S(1)}, f32[128,128]{1,0:T(8,128)}, u32[]{:S(2)}) copy-start(f32[128,128]{1,0:T(8,128)} %param.12) | copy-start | bytes 196612
  181.9 7.5 %copy-start.23 = (s32[4]{0:T(128)S(1)}, s32[4]{0:T(128)}, u32[]{:S(2)}) copy-start(s32[4]{0:T(128)} %get-tuple-element.49) | copy-start | bytes 52
  181.9 7.5 %copy-start.24 = (s32[4]{0:T(128)S(1)}, s32[4]{0:T(128)}, u32[]{:S(2)}) copy-start(s32[4]{0:T(128)} %get-tuple-element.50) | copy-start | bytes 52
  181.9 8.4 %copy-start.26 = (bf16[128]{0:T(256)(128)(2,1)S(1)}, bf16[128]{0:T(256)(128)(2,1)}, u32[]{:S(2)}) copy-start(bf16[128]{0:T(256)(128)(2,1)} %param.11) | copy-start | bytes 772
  181.9 9.2 %copy-start.29 = (pred[128]{0:T(512)(128)(4,1)S(1)}, pred[128]{0:T(512)(128)(4,1)}, u32[]{:S(2)}) copy-start(pred[128]{0:T(512)(128)(4,1)} %iota_compare_fusion.2) | copy-start | bytes 388
  181.9 10.1 %copy-start.20 = (bf16[4,224]{1,0:T(4,128)(2,1)S(1)}, bf16[4,224]{1,0:T(4,128)(2,1)}, u32[]{:S(2)}) copy-start(bf16[4,224]{1,0:T(4,128)(2,1)} %get-tuple-element.46) | copy-start | bytes 5380
  181.9 10.1 %copy-start.22 = (bf16[4,224]{1,0:T(4,128)(2,1)S(1)}, bf16[4,224]{1,0:T(4,128)(2,1)}, u32[]{:S(2)}) copy-start(bf16[4,224]{1,0:T(4,128)(2,1)} %get-tuple-element.48) | copy-start | bytes 5380
  182.1 11.2 %copy-start.19 = (bf16[4,224]{1,0:T(4,128)(2,1)S(1)}, bf16[4,224]{1,0:T(4,128)(2,1)}, u32[]{:S(2)}) copy-start(bf16[4,224]{1,0:T(4,128)(2,1)} %get-tuple-element.45) | copy-start | bytes 5380
  182.1 11.2 %copy-start.21 = (bf16[4,224]{1,0:T(4,128)(2,1)S(1)}, bf16[4,224]{1,0:T(4,128)(2,1)}, u32[]{:S(2)}) copy-start(bf16[4,224]{1,0:T(4,128)(2,1)} %get-tuple-element.47) | copy-start | bytes 5380
  189.4 5.2 %copy-start.27 = (f32[8]{0:T(128)}, f32[8]{0:T(128)S(1)}, u32[]{:S(2)}) copy-start(f32[8]{0:T(128)S(1)} %compare_select_fusion.1) | copy-start | bytes 100
  192.1 2.5 %copy-start.6 = (f32[224,1024]{1,0:T(8,128)S(1)}, f32[224,1024]{1,0:T(8,128)}, u32[]{:S(2)}) copy-start(f32[224,1024]{1,0:T(8,128)} %fusion.1) | copy-start | bytes 2752516
  192.1 2.5 %copy-start.17 = (f32[1,1024]{1,0:T(1,128)S(1)}, f32[1,1024]{1,0:T(1,128)}, u32[]{:S(2)}) copy-start(f32[1,1024]{1,0:T(1,128)} %slice_convert_fusion.1) | copy-start | bytes 12292
  192.1 2.5 %copy-start.18 = (bf16[224,4,1]{0,1,2:T(4,128)(2,1)S(1)}, bf16[224,4,1]{0,1,2:T(4,128)(2,1)}, u32[]{:S(2)}) copy-start(bf16[224,4,1]{0,1,2:T(4,128)(2,1)} %copy.31) | copy-start | bytes 5380
Sparse Core Ops, SparseCore 0:
  36.2 43.3 all-gather.2

commit v8 on v7

v8 whole, which is shorter than its diff:
```python
import functools

import jax
import jax.numpy as jnp
from jax import lax
from jax.experimental import pallas as pl
from jax.experimental.pallas import tpu as pltpu
from jax.sharding import Mesh, PartitionSpec as P

SEQ_LEN = 128
reward_weight = 64.0
FINE = ("yl", "co", "gy", "yh", "xx")
PLANE = ("yl", "gy")
GZ = ("yh", "xx")
SWAP = [(0, 1), (1, 0)]
f32, bf16 = jnp.float32, jnp.bfloat16


def exchange(pieces, axes):
    return lax.all_to_all(pieces, axes, 0, 0)


def to_all(value, axes, count):
    return exchange(jnp.broadcast_to(value[None], (count,) + value.shape), axes)


def dot(left, right, left_dim, right_dim):
    return lax.dot_general(
        left, right, (((left_dim,), (right_dim,)), ((), ())), preferred_element_type=f32
    )


def token_products(tok_got, gate_w, up_w, parts, tok):
    n_plane, rows, cols = tok_got.shape
    half, width = tok.shape
    n_gy, n_yl = width // cols, half // rows
    chip_units = parts.shape[0]
    for y in range(n_yl):
        for z in range(n_gy):
            tok[y * rows : (y + 1) * rows, z * cols : (z + 1) * cols] = tok_got[y * n_gy + z]
    parts[:, :half] = dot(gate_w[:chip_units], tok[...], 1, 1).astype(bf16)
    parts[:, half:] = dot(up_w[:chip_units], tok[...], 1, 1).astype(bf16)


def cotangent_products(core, low_got, tok, tok_sib, gate_w, up_w, down_w, parts, low, head, wide):
    n_gy, _, cols = low_got.shape
    half, width = low.shape
    n_yl = half // SEQ_LEN
    chip_units = down_w.shape[0]
    for z in range(n_gy):
        at = slice(z * cols, (z + 1) * cols)
        low[:, at] = low_got[z, :half]
        head[:, at] = low_got[z, half:]
    ends = [
        [ref[(y + 1) * SEQ_LEN - 16 : (y + 1) * SEQ_LEN].astype(f32)[15:] for y in range(n_yl)]
        for ref in (tok, tok_sib)
    ]
    here, there = (jnp.concatenate(rows, axis=0) for rows in ends)
    ends = [jnp.where(core[0] == 0, here, there), jnp.where(core[0] == 0, there, here)]
    wide[:16] = head[...]
    wide[16:32] = jnp.concatenate(ends + [jnp.zeros((16 - 2 * n_yl, width), f32)], axis=0).astype(bf16)
    wide[32:] = jnp.zeros((96, width), bf16)
    parts[:, :half] = dot(down_w[...], low[...], 1, 1).astype(bf16)
    v = dot(down_w[...], wide[...], 1, 1)
    gate = dot(gate_w[:chip_units], wide[...], 1, 1)
    up = pltpu.roll(dot(up_w[:chip_units], wide[...], 1, 1), 16, 1)
    high = v.astype(bf16).astype(f32)
    lane = lax.broadcasted_iota(jnp.int32, v.shape, 1)
    more = jnp.where(lane == 0, high, jnp.where(lane == 1, v - high, 0.0))
    more = jnp.where((lane >= 16) & (lane < 32), gate, jnp.where((lane >= 32) & (lane < 48), up, more))
    parts[:, half:] = more.astype(bf16)


def split_sums(in_two, place, got, keep, give, total):
    own = keep.shape[0]
    sums = got[0].astype(f32)
    for j in range(1, got.shape[0]):
        sums += got[j].astype(f32)
    total[...] = sums
    keep[...] = total[pl.ds(pl.multiple_of(place[0] * own, 8), own), :]
    away = total[pl.ds(pl.multiple_of((1 - place[0]) * own, 8), own), :]
    give[...] = away.astype(bf16)
    if in_two:
        ends = away[:, -128:]
        lost = pltpu.roll(ends - ends.astype(bf16).astype(f32), 1, 1)
        lane = lax.broadcasted_iota(jnp.int32, ends.shape, 1)
        give[:, -128:] = jnp.where(lane == 1, ends + lost, ends).astype(bf16)


def hidden_units(chip_units, place, keep, got, back_keep, back_got, tok_terms, mine):
    own, half = keep.shape[0], keep.shape[1] // 2
    n_seq = half // SEQ_LEN
    sums = keep[...] + got[...].astype(f32)
    back = back_keep[...] + back_got[...].astype(f32)
    gate_sum, up_sum, hidden_grad = sums[:, :half], sums[:, half:], back[:, :half]
    more = back[:, half:]
    head_down = more[:, 0:1] + more[:, 1:2]
    gate_sigmoid = jax.nn.sigmoid(gate_sum)
    silu_gate = gate_sum * gate_sigmoid
    hidden = (silu_gate * up_sum).astype(bf16).astype(f32)
    gate_slope = up_sum * gate_sigmoid * (1.0 + gate_sum * (1.0 - gate_sigmoid))

    row = lax.broadcasted_iota(jnp.int32, (8, half), 0)
    lane = lax.broadcasted_iota(jnp.int32, (8, half), 1)
    blank = jnp.zeros((128 - own, half), f32)

    def picked(value, first):
        pick = (lane == (row - first) * SEQ_LEN + SEQ_LEN - 1) & (row >= first) & (row < first + n_seq)
        value = jnp.concatenate([value * head_down, blank], axis=0).astype(bf16)
        return dot(jnp.where(pick, 1.0, 0.0).astype(bf16), value, 1, 1)

    unit = picked(gate_slope, 0) + picked(silu_gate, n_seq)
    unit = jnp.concatenate([unit, jnp.zeros((8, half - 128), f32)], axis=1)
    unit = pltpu.roll(unit, place[0], 1)

    last_hidden = (more * jax.nn.sigmoid(more) * pltpu.roll(more, 128 - 16, 1)).astype(bf16).astype(f32)
    terms = jnp.sum(last_hidden * head_down, axis=0, keepdims=True) + tok_terms[...]
    for s in range(2 * n_seq):
        rest = jnp.sum(jnp.where(lane[:1, :128] == 16 + s, terms, 0.0), axis=1, keepdims=True)
        for i in range(3):
            piece = rest.astype(bf16).astype(f32)
            unit += jnp.where((row == 0) & (lane == chip_units + 2 * i * n_seq + s), piece, 0.0)
            rest = rest - piece
    rows = jnp.concatenate([hidden_grad * gate_slope, hidden_grad * silu_gate, hidden, unit], axis=0)
    mine[...] = rows.astype(bf16)


def token_gradients(everyone, gate_w, up_w, sent, full):
    width = gate_w.shape[1]
    n_gz, n_rows, half = everyone.shape
    own = (n_rows - 8) // 3
    n_plane, piece_rows, cols = sent.shape
    n_gy, rows = width // cols, piece_rows - 16
    unit = jnp.zeros((8, half), f32)
    for j in range(n_gz):
        block = everyone[j].astype(f32)
        for i in range(2):
            full[i, j * own : (j + 1) * own] = block[i * own : (i + 1) * own]
        unit += block[3 * own :]
    terms = unit + pltpu.roll(unit, half - 8, 1) + pltpu.roll(unit, half - 16, 1)
    terms = pltpu.roll(terms, half - n_gz * own, 1)[:, :cols]
    lane = lax.broadcasted_iota(jnp.int32, terms.shape, 1)
    high = terms.astype(bf16).astype(f32)
    middle = (terms - high).astype(bf16).astype(f32)
    terms = jnp.where(
        lane < 8,
        high,
        jnp.where(lane < 16, pltpu.roll(middle, 8, 1), pltpu.roll(terms - high - middle, 16, 1)),
    )
    terms = jnp.where(lane < 24, terms, 0.0)[:1]
    for i in range(2):
        full[i, n_gz * own :] = jnp.zeros((full.shape[1] - n_gz * own, half), f32)
    unit = unit.astype(bf16)
    gate_t, up_t = (full[i].T.astype(bf16) for i in range(2))
    step = 2 * cols
    for c in range(0, width, step):
        part = dot(gate_t, gate_w[:, c : c + step], 1, 0) + dot(up_t, up_w[:, c : c + step], 1, 0)
        units_here = (
            dot(unit, gate_w[:, c : c + step], 1, 0)[:4] + dot(unit, up_w[:, c : c + step], 1, 0)[4:]
        )
        for z in range(c // cols, (c + step) // cols):
            at = slice(z * cols - c, (z + 1) * cols - c)
            for y in range(n_plane // n_gy):
                piece = y * n_gy + z
                sent[piece, :rows] = part[y * rows : (y + 1) * rows, at].astype(bf16)
                row = lax.broadcasted_iota(jnp.int32, (16, cols), 0)
                extra = jnp.where(row == 0, units_here[y : y + 1, at], jnp.where(row == 1, terms, 0.0))
                sent[piece, rows:] = extra.astype(bf16)


def body(tokens, gate_weight, up_weight, down_weight, reward_head, lm_grad, pair_index):
    n_yl, n_gy = lax.axis_size("yl"), lax.axis_size("gy")
    n_plane, n_gz = n_yl * n_gy, lax.axis_size(GZ)
    rows, cols = tokens.shape
    units, width = gate_weight.shape
    my_seq = lax.axis_index(("yl", "co"))
    core = lax.axis_index("co")

    def core_order(here, there):
        return [jnp.where(core == 0, here, there), jnp.where(core == 0, there, here)]

    def chip_block(weight, padding):
        parts = core_order(weight, lax.ppermute(weight, "co", SWAP))
        return jnp.concatenate(parts + [jnp.zeros((padding, width), bf16)], axis=0)

    padding = -2 * units % 128
    gate_w, up_w = chip_block(gate_weight, padding), chip_block(up_weight, padding)
    down_w = chip_block(down_weight, 0)

    half = n_yl * rows
    low_got = to_all(lm_grad.astype(bf16), "yl", n_yl).reshape(half, cols)
    low_got, tok_block = lax.optimization_barrier((low_got, tokens))
    head_rows = jnp.broadcast_to(reward_head[None, :], (16, cols))
    low_got = lax.all_gather(jnp.concatenate([low_got, head_rows], axis=0), "gy")
    tok_got = to_all(tok_block, PLANE, n_plane)

    own = 2 * units // n_gz
    whole, scalar = pl.BlockSpec(memory_space=pltpu.VMEM), pl.BlockSpec(memory_space=pltpu.SMEM)
    grant = pltpu.CompilerParams(vmem_limit_bytes=40 * 2**20)
    parts, tok_half = pl.pallas_call(
        token_products,
        out_shape=(
            jax.ShapeDtypeStruct((2 * units, 2 * half), bf16),
            jax.ShapeDtypeStruct((half, width), bf16),
        ),
        in_specs=[whole] * 3,
        out_specs=(whole,) * 2,
        compiler_params=grant,
        cost_estimate=pl.CostEstimate(
            flops=8 * units * width * half, bytes_accessed=8 * 2**20, transcendentals=0
        ),
        name="token_products",
    )(tok_got, gate_w, up_w)
    tok_sib = lax.ppermute(tok_half, "co", SWAP)

    n_xx = lax.axis_size("xx")
    first = exchange(parts.reshape(n_xx, 2 * own, 2 * half), "xx")
    y_half = lax.axis_index("yh").astype(jnp.int32)[None]

    def halves(got, in_two):
        lanes = got.shape[2]
        keep, give = pl.pallas_call(
            functools.partial(split_sums, in_two),
            out_shape=(jax.ShapeDtypeStruct((own, lanes), f32), jax.ShapeDtypeStruct((own, lanes), bf16)),
            in_specs=[scalar, whole],
            out_specs=(whole,) * 2,
            scratch_shapes=[pltpu.VMEM((2 * own, lanes), f32)],
            compiler_params=grant,
            cost_estimate=pl.CostEstimate(flops=8 * own * lanes, bytes_accessed=22 * own * lanes, transcendentals=0),
            name="split_sums",
        )(y_half, got)
        return keep, lax.ppermute(give, "yh", SWAP)

    back_parts, low_half, head_vec = pl.pallas_call(
        cotangent_products,
        out_shape=(
            jax.ShapeDtypeStruct((2 * units, half + 128), bf16),
            jax.ShapeDtypeStruct((half, width), bf16),
            jax.ShapeDtypeStruct((16, width), bf16),
        ),
        in_specs=[scalar] + [whole] * 6,
        out_specs=(whole,) * 3,
        scratch_shapes=[pltpu.VMEM((128, width), bf16)],
        compiler_params=grant,
        cost_estimate=pl.CostEstimate(
            flops=4 * units * width * (half + 384), bytes_accessed=5 * 2**20, transcendentals=0
        ),
        name="cotangent_products",
    )(core.astype(jnp.int32)[None], low_got, tok_half, tok_sib, gate_w, up_w, down_w)
    head_vec = head_vec[:1]
    first, back_parts = lax.optimization_barrier((first, back_parts))
    second = exchange(back_parts.reshape(n_xx, 2 * own, half + 128), "xx")
    sums, sums_got = halves(first, False)
    back, back_got = halves(second, True)

    own_term = jnp.sum(tokens[rows - 1].astype(f32) * reward_head.astype(f32))
    sib_term = lax.ppermute(own_term[None], "co", SWAP)[0]
    spot = jnp.arange(128)[None, :] - 16 - lax.axis_index("yl")
    first_term, second_term = core_order(own_term, sib_term)
    tok_terms = jnp.where(spot == 0, first_term, jnp.where(spot == n_yl, second_term, 0.0))
    place = (lax.axis_index(("xx", "yh")) * own).astype(jnp.int32)[None]
    mine = pl.pallas_call(
        functools.partial(hidden_units, 2 * units),
        out_shape=jax.ShapeDtypeStruct((3 * own + 8, half), bf16),
        in_specs=[scalar] + [whole] * 5,
        out_specs=whole,
        compiler_params=grant,
        cost_estimate=pl.CostEstimate(
            flops=40 * own * half, bytes_accessed=12 * own * half, transcendentals=own * half
        ),
        name="hidden_units",
    )(place, sums, sums_got, back, back_got, tok_terms)
    other = lax.ppermute(mine, "yh", SWAP)
    pair = jnp.stack([jnp.where(y_half == 0, mine, other), jnp.where(y_half == 0, other, mine)])
    everyone = to_all(pair, "xx", n_xx).reshape(n_gz, 3 * own + 8, half)
    sent = pl.pallas_call(
        token_gradients,
        out_shape=jax.ShapeDtypeStruct((n_plane, rows + 16, cols), bf16),
        in_specs=[whole] * 3,
        out_specs=whole,
        scratch_shapes=[pltpu.VMEM((2, 2 * units + padding, half), f32)],
        compiler_params=grant,
        cost_estimate=pl.CostEstimate(
            flops=8 * units * width * half, bytes_accessed=5 * 2**20, transcendentals=0
        ),
        name="token_gradients",
    )(everyone, gate_w, up_w)
    sent, everyone = lax.optimization_barrier((sent, everyone))
    gate_g, up_g, hid = (
        everyone[:, i * own : (i + 1) * own].reshape(2 * units, half) for i in range(3)
    )
    units_at = jnp.sum(everyone[:, 3 * own :, : 2 * units].astype(f32), axis=0).astype(bf16)
    token_sum = jnp.sum(exchange(sent, PLANE).astype(f32), axis=0)

    both = jnp.sum(token_sum[rows + 1, : 6 * n_yl].reshape(3, 2, n_yl), axis=0)
    sequence = jnp.arange(2 * n_yl, dtype=jnp.int32)
    rewards = both.T.reshape(2 * n_yl)
    chosen_hot = (pair_index[:, 0:1] == sequence[None, :]).astype(f32)
    rejected_hot = (pair_index[:, 1:2] == sequence[None, :]).astype(f32)
    margin = jnp.sum((chosen_hot - rejected_hot) * rewards[None, :], axis=1)
    pair_weight = jax.nn.sigmoid(-margin)
    scaled = reward_weight * jnp.sum((rejected_hot - chosen_hot) * pair_weight[:, None], axis=0)
    by_core = scaled.reshape(n_yl, 2)
    core_coefs = jnp.where(core == 0, by_core[:, 0], by_core[:, 1])
    sib_coefs = jnp.where(core == 0, by_core[:, 1], by_core[:, 0])
    coefs = jnp.concatenate([core_coefs, sib_coefs])
    my_coef = jnp.sum(jnp.where(sequence == my_seq, scaled, 0.0))

    row = jnp.arange(rows)[:, None]
    head_term = my_coef * (reward_head.astype(f32) + token_sum[rows])
    grad_tokens = lm_grad + token_sum[:rows] + jnp.where(row == rows - 1, head_term[None, :], 0.0)

    loss_scale = 1.0 / jnp.sqrt(f32(rows * 2 * n_yl))
    low_sib = lax.ppermute(low_half, "co", SWAP)

    def core_parts(value, axis):
        return [
            lax.dynamic_slice_in_dim(value, which * units, units, axis) for which in (core, 1 - core)
        ]

    unit_here, unit_there = core_parts(units_at, 1)
    unit_swap = lax.ppermute(unit_there, "co", SWAP)
    gate_u8 = jnp.concatenate([unit_here[:n_yl], unit_swap[:n_yl]], axis=0)
    up_u8 = jnp.concatenate([unit_here[n_yl:], unit_swap[n_yl:]], axis=0)

    def last_rows(value):
        return value.reshape(n_yl, rows, width)[:, rows - 1]

    last_tok = jnp.concatenate([last_rows(tok_half), last_rows(tok_sib)], axis=0).astype(f32)
    last_tok = (last_tok * coefs[:, None]).astype(bf16)
    head_term8 = (coefs[:, None] * head_vec.astype(f32)).astype(bf16)

    def weight_grad(full, own_right, sib_right, last_left, last_right):
        here, there = core_parts(full, 0)
        from_sib = lax.ppermute(there, "co", SWAP)
        total = lax.optimization_barrier(
            (dot(here, own_right, 1, 0) + dot(from_sib, sib_right, 1, 0)) * loss_scale
        )
        if last_left is None:
            ends = [v.reshape(units, n_yl, rows)[:, :, rows - 1] for v in (here, from_sib)]
            last_left = jnp.concatenate(ends, axis=1).T
        return total + dot(last_left, last_right, 0, 0) * loss_scale

    grad_gate = weight_grad(gate_g, tok_half, tok_sib, gate_u8, last_tok)
    grad_up = weight_grad(up_g, tok_half, tok_sib, up_u8, last_tok)
    grad_down = weight_grad(hid, low_half, low_sib, None, head_term8)
    return grad_tokens, grad_gate, grad_up, grad_down, rewards


def solution(mesh):
    fine = Mesh(mesh.devices.reshape(4, 2, 8, 2, 4), FINE)
    gx, gz = ("yl", "co"), GZ
    weight = P(("gy",) + gx, gz)
    act = P(gx, gz + ("gy",))
    return jax.shard_map(
        body,
        mesh=fine,
        in_specs=(act, weight, weight, weight, P(gz + ("gy",)), act, P()),
        out_specs=(act, weight, weight, weight, P()),
        check_vma=False,
    )
```

time: 205 us -> 217 us (1.059)
  blocking collectives: 0 us -> 9.99 us
  starting transfers between devices: 95.9 us -> 89.9 us
  local copies, waits for them, and re-layouts: 17.2 us -> 22.7 us
  between operations: 14.7 us -> 17 us
    all_to_all x0 -> x1, blocking collectives: none -> 9.99 us  [exchange(): return lax.all_to_all(pieces, axes, 0, 0)]
    ppermute x1, waiting for transfers between devices: 0.01 us -> 8.79 us  [body(): other = lax.ppermute(mine, 'yh', SWAP)]
    all_to_all x6 -> x5, waiting for transfers between devices: 27 us -> 20.5 us  [exchange(): return lax.all_to_all(pieces, axes, 0, 0)]
    all_gather x1, waiting for transfers between devices: 9.84 us -> 3.51 us  [body(): lax.all_gather(jnp.concatenate([low_got, head_rows], axis=0), 'gy')]
    unnamed x63 -> x68, local copies, waits for them, and re-layouts: 5.88 us -> 11.1 us
    dynamic_slice x0 -> x4, local copies, waits for them, and re-layouts: none -> 4.1 us  [core_parts(): lax.dynamic_slice_in_dim(value, which * units, units, axis)]
    ppermute x1, starting transfers between devices: 6 us -> 1.92 us  [body(): other = lax.ppermute(mine, 'yh', SWAP)]
    all_to_all x6 -> x5, starting transfers between devices: 38.2 us -> 41.2 us  [exchange(): return lax.all_to_all(pieces, axes, 0, 0)]
  transfers between devices with their start and end apart: 20 -> 19, of which waited for: 7 -> 8; matrix products, arithmetic and copies ran while one was open for 13% -> 13% of each run, Pallas kernels for 4% -> 3%
where the time goes in v8:
time: 217 us; the launch traced here: 214 us
  starting transfers between devices  89.9 us (41%)
  waiting for transfers between devices  42.1 us (19%)
  local copies, waits for them, and re-layouts  22.7 us (10%)
  between operations  17 us (8%)
  matrix products  15.5 us (7%)
  other arithmetic  10.8 us (5%)
  blocking collectives  9.99 us (5%)
  Pallas kernels  6.17 us (3%)
    all_to_all x5, starting transfers between devices, exchange(): return lax.all_to_all(pieces, axes, 0, 0)  41.2 us
    all_to_all x5, waiting for transfers between devices, exchange(): return lax.all_to_all(pieces, axes, 0, 0)  20.5 us
    dot_general x9, matrix products, dot(): lax.dot_general(left, right, (((left_dim,), (right_dim,)), ((), ())), pre...  15.5 us
    unnamed x68, local copies, waits for them, and re-layouts  11.1 us
    all_to_all x1, blocking collectives, exchange(): return lax.all_to_all(pieces, axes, 0, 0)  9.99 us
    ppermute x2, starting transfers between devices, halves(): return (keep, lax.ppermute(give, 'yh', SWAP))  9.12 us
    ppermute x1, waiting for transfers between devices, body(): other = lax.ppermute(mine, 'yh', SWAP)  8.79 us
    ppermute x3, starting transfers between devices, weight_grad(): from_sib = lax.ppermute(there, 'co', SWAP)  8.45 us
  transfers between devices with their start and end apart: 19, of which 8 were waited for; matrix products, arithmetic and copies ran while one was open for 13% of the time, Pallas kernels for 3%

profile of v8, /device:TPU:1, one launch (start us, length us, event | category | flops | bytes accessed | tf_op | source)
XLA Modules:
  0.0 214.2 jit_solution(10156479992993791422)
XLA Ops:
  7.2 0.8 convert_element_type.34
  8.0 10.0 %all_to_all.30 = bf16[4,128,128]{2,1,0:T(8,128)(2,1)S(1)} all-to-all(bf16[4,128,128]{2,1,0:T(8,128)(2,1)S(1)} %broadcast_in_dim.94), channel_id=1, replica_groups=mesh['yl'=4,'co'=2,'gy'=8,'yh'=2,'xx'=4] {'yl'}, dimensions={0} | all-to-all | bytes 262144 | tf_op jit(solution)/shard_map/all_to_all | solution.py:20
  18.0 2.1 broadcast_in_dim.95
  20.1 12.3 %all-to-all-start.1 = ((bf16[32,128,128]{2,1,0:T(8,128)(2,1)}), bf16[32,128,128]{2,1,0:T(8,128)(2,1)S(1)}, u32[]{:S(2)}, u32[]{:S(2)}) async-start(bf16[32,128,128]{2,1,0:T(8,128)(2,1)} %broadcast_in_dim.95), calls=%async_computation.1 | async-start | bytes 2097152 | tf_op jit(solution)/shard_map/all_to_all | solution.py:20
  32.5 3.4 %collective-permute-start.1 = (bf16[224,1024]{1,0:T(8,128)(2,1)S(1)}, bf16[224,1024]{1,0:T(8,128)(2,1)S(1)}, u32[]{:S(2)}, u32[]{:S(2)}) collective-permute-start(bf16[224,1024]{1,0:T(8,128)(2,1)S(1)} %copy-done.21), channel_id=1, source_target_pairs={{0,64},{64,0},{1,65},{65,1},{2,66},{66,2},{3,67},{67,3},{4,68},{68... | collective-permute-start | bytes 1376264 | tf_op jit(solution)/shard_map/ppermute | solution.py:183
  35.9 1.9 collective-permute-start
  38.0 0.7 pad_maximum_fusion.2
  38.7 0.9 collective-permute-done
  40.1 17.7 %all-to-all-done.1.tok_got = bf16[32,128,128]{2,1,0:T(8,128)(2,1)S(1)} async-done(((bf16[32,128,128]{2,1,0:T(8,128)(2,1)}), bf16[32,128,128]{2,1,0:T(8,128)(2,1)S(1)}, u32[]{:S(2)}, u32[]{:S(2)}) %all-to-all-start.1) | async-done | bytes 1048608 | tf_op jit(solution)/shard_map/all_to_all | solution.py:20
  57.9 1.0 copy-done.10
  58.8 1.2 copy-done.11
  60.1 1.2 token_products.1
  61.3 4.9 %collective-permute-start.2 = (bf16[512,1024]{1,0:T(8,128)(2,1)S(1)}, bf16[512,1024]{1,0:T(8,128)(2,1)S(1)}, u32[]{:S(2)}, u32[]{:S(2)}) collective-permute-start(bf16[512,1024]{1,0:T(8,128)(2,1)S(1)} %get-tuple-element.23.tok), channel_id=1, source_target_pairs={{0,64},{64,0},{1,65},{65,1},{2,66},{66,2},{3,67},{67,3},{4,68},{68... | collective-permute-start | bytes 3145736 | tf_op jit(solution)/shard_map/ppermute | solution.py:214
  66.2 1.9 collective-permute-start.3
  68.2 4.2 %all-to-all-start.2 = ((bf16[4,112,1024]{2,1,0:T(8,128)(2,1)}), bf16[4,112,1024]{2,1,0:T(8,128)(2,1)}, u32[]{:S(2)}, u32[]{:S(2)}) async-start(bf16[4,112,1024]{2,1,0:T(8,128)(2,1)} %bitcast.59), calls=%async_computation.2 | async-start | bytes 1835008 | tf_op jit(solution)/shard_map/all_to_all | solution.py:20
  72.4 1.2 broadcast_select_fusion.1
  73.7 1.0 pad_maximum_fusion.down_w
  74.6 3.5 %all-gather.3.cloned.1.call-done = bf16[4224,128]{1,0:T(8,128)(2,1)} async-done(((bf16[528,128]{1,0:T(8,128)(2,1)}), bf16[4224,128]{1,0:T(8,128)(2,1)}) %all-gather.3.cloned.1.call-update) | async-done | bytes 1081360 | tf_op jit(solution)/shard_map/all_gather | solution.py:194
  78.2 1.2 copy-done.3
  79.4 1.2 copy-done.6
  80.6 1.2 copy-done.7
  81.8 1.5 cotangent_products.1
  83.3 1.0 copy-done.8
  84.3 0.8 copy-done.13
  85.7 3.7 %all-to-all-start.3 = ((bf16[4,112,640]{2,1,0:T(8,128)(2,1)}), bf16[4,112,640]{2,1,0:T(8,128)(2,1)S(1)}, u32[]{:S(2)}, u32[]{:S(2)}) async-start(bf16[4,112,640]{2,1,0:T(8,128)(2,1)} %bitcast.60), calls=%async_computation.3 | async-start | bytes 1146880 | tf_op jit(solution)/shard_map/all_to_all | solution.py:20
  89.5 1.4 split_sums.2
  90.8 7.0 %collective-permute-start.4 = (bf16[56,1024]{1,0:T(8,128)(2,1)S(1)}, bf16[56,1024]{1,0:T(8,128)(2,1)S(1)}, u32[]{:S(2)}, u32[]{:S(2)}) collective-permute-start(bf16[56,1024]{1,0:T(8,128)(2,1)S(1)} %get-tuple-element.27), channel_id=1, source_target_pairs={{0,4},{4,0},{1,5},{5,1},{2,6},{6,2},{3,7},{7,3},{8,12},{12,8},{9,1... | collective-permute-start | bytes 344072 | tf_op jit(solution)/shard_map/ppermute | solution.py:232
  97.9 1.3 fusion.31
  99.2 6.9 %collective-permute-start.6 = (f32[1]{0:T(128)}, f32[1]{0:T(128)}, u32[]{:S(2)}, u32[]{:S(2)}) collective-permute-start(f32[1]{0:T(128)} %bitcast.9), channel_id=1, source_target_pairs={{0,64},{64,0},{1,65},{65,1},{2,66},{66,2},{3,67},{67,3},{4,68},{68... | collective-permute-start | bytes 20 | tf_op jit(solution)/shard_map/ppermute | solution.py:257
  106.1 1.1 collective-permute-done.6
  109.8 2.1 collective-permute-start.5
  111.9 7.3 %collective-permute-done.5.back_got = bf16[56,640]{1,0:T(8,128)(2,1)S(1)} collective-permute-done((bf16[56,640]{1,0:T(8,128)(2,1)S(1)}, bf16[56,640]{1,0:T(8,128)(2,1)S(1)}, u32[]{:S(2)}, u32[]{:S(2)}) %collective-permute-start.5) | collective-permute-done | bytes 71712 | tf_op jit(solution)/shard_map/ppermute | solution.py:232
  119.6 1.9 collective-permute-start.7
  121.5 8.8 %collective-permute-done.7 = bf16[176,512]{1,0:T(8,128)(2,1)S(1)} collective-permute-done((bf16[176,512]{1,0:T(8,128)(2,1)S(1)}, bf16[176,512]{1,0:T(8,128)(2,1)S(1)}, u32[]{:S(2)}, u32[]{:S(2)}) %collective-permute-start.7) | collective-permute-done | bytes 180256 | tf_op jit(solution)/shard_map/ppermute | solution.py:273
  130.4 1.3 broadcast_in_dim.102
  131.7 4.6 %all-to-all-start.4 = ((bf16[4,2,176,512]{3,2,1,0:T(8,128)(2,1)}), bf16[4,2,176,512]{3,2,1,0:T(8,128)(2,1)S(1)}, u32[]{:S(2)}, u32[]{:S(2)}) async-start(bf16[4,2,176,512]{3,2,1,0:T(8,128)(2,1)} %broadcast_in_dim.102), calls=%async_computation.4 | async-start | bytes 2883584 | tf_op jit(solution)/shard_map/all_to_all | solution.py:20
  137.4 8.1 %collective-permute-start.12 = (bf16[512,1024]{1,0:T(8,128)(2,1)}, bf16[512,1024]{1,0:T(8,128)(2,1)}, u32[]{:S(2)}, u32[]{:S(2)}) collective-permute-start(bf16[512,1024]{1,0:T(8,128)(2,1)} %copy-done.8), channel_id=1, source_target_pairs={{0,64},{64,0},{1,65},{65,1},{2,66},{66,2},{3,67},{67,3},{4,68},{68... | collective-permute-start | bytes 3145736 | tf_op jit(solution)/shard_map/ppermute | solution.py:314
  145.6 1.3 slice_convert_fusion
  146.9 2.2 %all-to-all-done.4 = bf16[4,2,176,512]{3,2,1,0:T(8,128)(2,1)S(1)} async-done(((bf16[4,2,176,512]{3,2,1,0:T(8,128)(2,1)}), bf16[4,2,176,512]{3,2,1,0:T(8,128)(2,1)S(1)}, u32[]{:S(2)}, u32[]{:S(2)}) %all-to-all-start.4) | async-done | bytes 1441824 | tf_op jit(solution)/shard_map/all_to_all | solution.py:20
  149.1 1.2 copy-done.1
  150.3 1.2 copy-done.4
  151.6 1.5 token_gradients.1
  153.1 1.2 fusion.35
  154.6 0.6 slice_reduce_fusion
  155.2 16.2 %all-to-all-start.5 = ((bf16[32,144,128]{2,1,0:T(8,128)(2,1)}), bf16[32,144,128]{2,1,0:T(8,128)(2,1)S(1)}, u32[]{:S(2)}, u32[]{:S(2)}) async-start(bf16[32,144,128]{2,1,0:T(8,128)(2,1)} %copy-done.5), calls=%async_computation.5 | async-start | bytes 2359296 | tf_op jit(solution)/shard_map/all_to_all | solution.py:20
  171.4 1.6 constant_dynamic-slice_fusion.5
  173.1 4.0 %collective-permute-start.8 = (bf16[224,512]{1,0:T(8,128)(2,1)}, bf16[224,512]{1,0:T(8,128)(2,1)}, u32[]{:S(2)}, u32[]{:S(2)}) collective-permute-start(bf16[224,512]{1,0:T(8,128)(2,1)} %constant_dynamic-slice_fusion.5), channel_id=1, source_target_pairs={{0,64},{64,0},{1,65},{65,1},{2,66},{66,2},{3,67},{67,3},{4,68},{68... | collective-permute-start | bytes 688136 | tf_op jit(solution)/shard_map/ppermute | solution.py:335
  177.2 1.9 collective-permute-start.9
  179.1 1.7 constant_dynamic-slice_fusion.3
  180.7 2.4 %collective-permute-start.10 = (bf16[224,512]{1,0:T(8,128)(2,1)}, bf16[224,512]{1,0:T(8,128)(2,1)}, u32[]{:S(2)}, u32[]{:S(2)}) collective-permute-start(bf16[224,512]{1,0:T(8,128)(2,1)} %constant_dynamic-slice_fusion.3), channel_id=1, source_target_pairs={{0,64},{64,0},{1,65},{65,1},{2,66},{66,2},{3,67},{67,3},{4,68},{68... | collective-permute-start | bytes 688136 | tf_op jit(solution)/shard_map/ppermute | solution.py:335
  183.1 2.3 %fusion.8 = f32[224,1024]{1,0:T(8,128)} fusion(bf16[512,1024]{1,0:T(8,128)(2,1)S(1)} %get-tuple-element.23.tok, bf16[448,512]{1,0:T(8,128)(2,1)} %bitcast.64, s32[]{:T(128)S(6)} %select_n.111), kind=kOutput, calls=%fused_computation.25 | convolution fusion | flops 234881024 | bytes 2195460 | tf_op jit(solution)/shard_map/dot_general | solution.py:28
  185.4 1.3 fusion.6
  186.8 0.7 constant_dynamic-slice_fusion.2
  187.6 2.1 collective-permute-start.11
  190.1 2.7 %fusion.5 = f32[224,1024]{1,0:T(8,128)} fusion(f32[224,1024]{1,0:T(8,128)} %fusion.8, bf16[224,512]{1,0:T(8,128)(2,1)} %collective-permute-done.8, bf16[512,1024]{1,0:T(8,128)(2,1)S(1)} %collective-permute-done.2.tok_sib), kind=kOutput, calls=%fused_computation.12 | convolution fusion | flops 235339776 | bytes 3112960 | tf_op jit(solution)/shard_map/dot_general | solution.py:28
  192.8 2.3 %fusion.3 = f32[224,1024]{1,0:T(8,128)} fusion(f32[224,1024]{1,0:T(8,128)S(1)} %copy-done.15, bf16[224,512]{1,0:T(8,128)(2,1)} %collective-permute-done.10, bf16[512,1024]{1,0:T(8,128)(2,1)S(1)} %collective-permute-done.2.tok_sib), kind=kOutput, calls=%fused_computation.8 | convolution fusion | flops 235339776 | bytes 3112960 | tf_op jit(solution)/shard_map/dot_general | solution.py:28
  195.1 1.8 fusion.38
  197.0 1.4 fusion.1
  198.3 1.1 reshape.110
  201.8 0.6 fusion.30
  202.7 0.7 fusion.10
  203.5 1.3 fusion.4
  204.8 1.3 fusion.2
  206.0 1.3 fusion
  (110 shorter events, 6.8 us)
Async XLA Ops:
  18.0 14.5 %copy-start.21 = (bf16[224,1024]{1,0:T(8,128)(2,1)S(1)}, bf16[224,1024]{1,0:T(8,128)(2,1)}, u32[]{:S(2)}) copy-start(bf16[224,1024]{1,0:T(8,128)(2,1)} %param.9) | copy-start | bytes 1376260
  18.0 17.9 %copy-start.22 = (bf16[224,1024]{1,0:T(8,128)(2,1)S(1)}, bf16[224,1024]{1,0:T(8,128)(2,1)}, u32[]{:S(2)}) copy-start(bf16[224,1024]{1,0:T(8,128)(2,1)} %param.8) | copy-start | bytes 1376260
  18.0 19.9 %copy-start.28 = (bf16[128]{0:T(256)(128)(2,1)S(1)}, bf16[128]{0:T(256)(128)(2,1)}, u32[]{:S(2)}) copy-start(bf16[128]{0:T(256)(128)(2,1)} %param.11) | copy-start | bytes 772
  20.1 37.8 %all-to-all-start.1 = ((bf16[32,128,128]{2,1,0:T(8,128)(2,1)}), bf16[32,128,128]{2,1,0:T(8,128)(2,1)S(1)}, u32[]{:S(2)}, u32[]{:S(2)}) async-start(bf16[32,128,128]{2,1,0:T(8,128)(2,1)} %broadcast_in_dim.95), calls=%async_computation.1 | async-start | bytes 2097152 | tf_op jit(solution)/shard_map/all_to_all | solution.py:20
  32.4 45.7 %all-gather.3.cloned.1.call-start = ((), (), s32[]{:S(2)}) async-start(), calls=%async_computation.6 | async-start | bytes 1216512 | tf_op jit(solution)/shard_map/all_gather | solution.py:194
  32.5 6.2 %collective-permute-start.1 = (bf16[224,1024]{1,0:T(8,128)(2,1)S(1)}, bf16[224,1024]{1,0:T(8,128)(2,1)S(1)}, u32[]{:S(2)}, u32[]{:S(2)}) collective-permute-start(bf16[224,1024]{1,0:T(8,128)(2,1)S(1)} %copy-done.21), channel_id=1, source_target_pairs={{0,64},{64,0},{1,65},{65,1},{2,66},{66,2},{3,67},{67,3},{4,68},{68... | collective-permute-start | bytes 1376264 | tf_op jit(solution)/shard_map/ppermute | solution.py:183
  35.9 3.7 %collective-permute-start = (bf16[224,1024]{1,0:T(8,128)(2,1)S(1)}, bf16[224,1024]{1,0:T(8,128)(2,1)S(1)}, u32[]{:S(2)}, u32[]{:S(2)}) collective-permute-start(bf16[224,1024]{1,0:T(8,128)(2,1)S(1)} %copy-done.22), channel_id=1, source_target_pairs={{0,64},{64,0},{1,65},{65,1},{2,66},{66,2},{3,67},{67,3},{4,68},{68... | collective-permute-start | bytes 1376264 | tf_op jit(solution)/shard_map/ppermute | solution.py:183
  40.1 21.2 %copy-start.2 = (bf16[512,1024]{1,0:T(8,128)(2,1)}, bf16[512,1024]{1,0:T(8,128)(2,1)S(1)}, u32[]{:S(2)}) copy-start(bf16[512,1024]{1,0:T(8,128)(2,1)S(1)} %get-tuple-element.57.gate_w) | copy-start | bytes 3145732
  40.1 38.0 %copy-start = (bf16[512,1024]{1,0:T(8,128)(2,1)}, bf16[512,1024]{1,0:T(8,128)(2,1)S(1)}, u32[]{:S(2)}) copy-start(bf16[512,1024]{1,0:T(8,128)(2,1)S(1)} %get-tuple-element.56.up_w) | copy-start | bytes 3145732
  57.9 1.0 copy-start.10
  58.8 1.2 copy-start.11
  61.3 6.9 %copy-start.12 = (bf16[448,1024]{1,0:T(8,128)(2,1)}, bf16[448,1024]{1,0:T(8,128)(2,1)S(1)}, u32[]{:S(2)}) copy-start(bf16[448,1024]{1,0:T(8,128)(2,1)S(1)} %get-tuple-element.21) | copy-start | bytes 2752516
  61.3 16.9 %collective-permute-start.2 = (bf16[512,1024]{1,0:T(8,128)(2,1)S(1)}, bf16[512,1024]{1,0:T(8,128)(2,1)S(1)}, u32[]{:S(2)}, u32[]{:S(2)}) collective-permute-start(bf16[512,1024]{1,0:T(8,128)(2,1)S(1)} %get-tuple-element.23.tok), channel_id=1, source_target_pairs={{0,64},{64,0},{1,65},{65,1},{2,66},{66,2},{3,67},{67,3},{4,68},{68... | collective-permute-start | bytes 3145736 | tf_op jit(solution)/shard_map/ppermute | solution.py:214
  66.2 6.2 %collective-permute-start.3 = (bf16[224,1024]{1,0:T(8,128)(2,1)}, bf16[224,1024]{1,0:T(8,128)(2,1)}, u32[]{:S(2)}, u32[]{:S(2)}) collective-permute-start(bf16[224,1024]{1,0:T(8,128)(2,1)} %param.10), channel_id=1, source_target_pairs={{0,64},{64,0},{1,65},{65,1},{2,66},{66,2},{3,67},{67,3},{4,68},{68... | collective-permute-start | bytes 1376264 | tf_op jit(solution)/shard_map/ppermute | solution.py:183
  68.2 17.5 %all-to-all-start.2 = ((bf16[4,112,1024]{2,1,0:T(8,128)(2,1)}), bf16[4,112,1024]{2,1,0:T(8,128)(2,1)}, u32[]{:S(2)}, u32[]{:S(2)}) async-start(bf16[4,112,1024]{2,1,0:T(8,128)(2,1)} %bitcast.59), calls=%async_computation.2 | async-start | bytes 1835008 | tf_op jit(solution)/shard_map/all_to_all | solution.py:20
  78.2 1.2 copy-start.3
  79.4 1.2 copy-start.6
  80.6 1.2 copy-start.7
  83.3 1.0 copy-start.8
  84.3 0.8 copy-start.13
  85.1 0.6 copy-start.14
  85.7 23.9 %all-to-all-start.3 = ((bf16[4,112,640]{2,1,0:T(8,128)(2,1)}), bf16[4,112,640]{2,1,0:T(8,128)(2,1)S(1)}, u32[]{:S(2)}, u32[]{:S(2)}) async-start(bf16[4,112,640]{2,1,0:T(8,128)(2,1)} %bitcast.60), calls=%async_computation.3 | async-start | bytes 1146880 | tf_op jit(solution)/shard_map/all_to_all | solution.py:20
  90.8 21.0 %collective-permute-start.4 = (bf16[56,1024]{1,0:T(8,128)(2,1)S(1)}, bf16[56,1024]{1,0:T(8,128)(2,1)S(1)}, u32[]{:S(2)}, u32[]{:S(2)}) collective-permute-start(bf16[56,1024]{1,0:T(8,128)(2,1)S(1)} %get-tuple-element.27), channel_id=1, source_target_pairs={{0,4},{4,0},{1,5},{5,1},{2,6},{6,2},{3,7},{7,3},{8,12},{12,8},{9,1... | collective-permute-start | bytes 344072 | tf_op jit(solution)/shard_map/ppermute | solution.py:232
  99.2 8.0 %collective-permute-start.6 = (f32[1]{0:T(128)}, f32[1]{0:T(128)}, u32[]{:S(2)}, u32[]{:S(2)}) collective-permute-start(f32[1]{0:T(128)} %bitcast.9), channel_id=1, source_target_pairs={{0,64},{64,0},{1,65},{65,1},{2,66},{66,2},{3,67},{67,3},{4,68},{68... | collective-permute-start | bytes 20 | tf_op jit(solution)/shard_map/ppermute | solution.py:257
  109.8 9.4 %collective-permute-start.5 = (bf16[56,640]{1,0:T(8,128)(2,1)S(1)}, bf16[56,640]{1,0:T(8,128)(2,1)S(1)}, u32[]{:S(2)}, u32[]{:S(2)}) collective-permute-start(bf16[56,640]{1,0:T(8,128)(2,1)S(1)} %get-tuple-element.30), channel_id=1, source_target_pairs={{0,4},{4,0},{1,5},{5,1},{2,6},{6,2},{3,7},{7,3},{8,12},{12,8},{9,1... | collective-permute-start | bytes 215048 | tf_op jit(solution)/shard_map/ppermute | solution.py:232
  119.6 10.7 %collective-permute-start.7 = (bf16[176,512]{1,0:T(8,128)(2,1)S(1)}, bf16[176,512]{1,0:T(8,128)(2,1)S(1)}, u32[]{:S(2)}, u32[]{:S(2)}) collective-permute-start(bf16[176,512]{1,0:T(8,128)(2,1)S(1)} %hidden_units.1), channel_id=1, source_target_pairs={{0,4},{4,0},{1,5},{5,1},{2,6},{6,2},{3,7},{7,3},{8,12},{12,8},{9,1... | collective-permute-start | bytes 540680 | tf_op jit(solution)/shard_map/ppermute | solution.py:273
  131.7 5.2 %copy-start.31 = (s32[4,2]{0,1:T(2,128)S(1)}, s32[4,2]{0,1:T(2,128)}, u32[]{:S(2)}) copy-start(s32[4,2]{0,1:T(2,128)} %param.13) | copy-start | bytes 100
  131.7 17.5 %all-to-all-start.4 = ((bf16[4,2,176,512]{3,2,1,0:T(8,128)(2,1)}), bf16[4,2,176,512]{3,2,1,0:T(8,128)(2,1)S(1)}, u32[]{:S(2)}, u32[]{:S(2)}) async-start(bf16[4,2,176,512]{3,2,1,0:T(8,128)(2,1)} %broadcast_in_dim.102), calls=%async_computation.4 | async-start | bytes 2883584 | tf_op jit(solution)/shard_map/all_to_all | solution.py:20
  137.4 57.7 %collective-permute-start.12 = (bf16[512,1024]{1,0:T(8,128)(2,1)}, bf16[512,1024]{1,0:T(8,128)(2,1)}, u32[]{:S(2)}, u32[]{:S(2)}) collective-permute-start(bf16[512,1024]{1,0:T(8,128)(2,1)} %copy-done.8), channel_id=1, source_target_pairs={{0,64},{64,0},{1,65},{65,1},{2,66},{66,2},{3,67},{67,3},{4,68},{68... | collective-permute-start | bytes 3145736 | tf_op jit(solution)/shard_map/ppermute | solution.py:314
  149.1 1.2 copy-start.1
  150.3 1.2 copy-start.4
  153.1 1.5 copy-start.5
  155.2 21.8 %copy-start.24 = (bf16[8,448]{1,0:T(8,128)(2,1)S(1)}, bf16[8,448]{1,0:T(8,128)(2,1)}, u32[]{:S(2)}) copy-start(bf16[8,448]{1,0:T(8,128)(2,1)} %slice_reduce_fusion) | copy-start | bytes 21508
  155.2 45.2 %all-to-all-start.5 = ((bf16[32,144,128]{2,1,0:T(8,128)(2,1)}), bf16[32,144,128]{2,1,0:T(8,128)(2,1)S(1)}, u32[]{:S(2)}, u32[]{:S(2)}) async-start(bf16[32,144,128]{2,1,0:T(8,128)(2,1)} %copy-done.5), calls=%async_computation.5 | async-start | bytes 2359296 | tf_op jit(solution)/shard_map/all_to_all | solution.py:20
  173.1 12.3 %copy-start.19 = (bf16[8,56,512]{2,1,0:T(8,128)(2,1)S(1)}, bf16[8,56,512]{2,1,0:T(8,128)(2,1)}, u32[]{:S(2)}) copy-start(bf16[8,56,512]{2,1,0:T(8,128)(2,1)} %get-tuple-element.38) | copy-start | bytes 1376260
  173.1 17.0 %collective-permute-start.8 = (bf16[224,512]{1,0:T(8,128)(2,1)}, bf16[224,512]{1,0:T(8,128)(2,1)}, u32[]{:S(2)}, u32[]{:S(2)}) collective-permute-start(bf16[224,512]{1,0:T(8,128)(2,1)} %constant_dynamic-slice_fusion.5), channel_id=1, source_target_pairs={{0,64},{64,0},{1,65},{65,1},{2,66},{66,2},{3,67},{67,3},{4,68},{68... | collective-permute-start | bytes 688136 | tf_op jit(solution)/shard_map/ppermute | solution.py:335
  177.2 12.9 %collective-permute-start.9 = (bf16[8,224]{1,0:T(8,128)(2,1)S(1)}, bf16[8,224]{1,0:T(8,128)(2,1)S(1)}, u32[]{:S(2)}, u32[]{:S(2)}) collective-permute-start(bf16[8,224]{1,0:T(8,128)(2,1)S(1)} %constant_dynamic-slice_fusion.4), channel_id=1, source_target_pairs={{0,64},{64,0},{1,65},{65,1},{2,66},{66,2},{3,67},{67,3},{4,68},{68... | collective-permute-start | bytes 10760 | tf_op jit(solution)/shard_map/ppermute | solution.py:322
  180.7 12.1 %collective-permute-start.10 = (bf16[224,512]{1,0:T(8,128)(2,1)}, bf16[224,512]{1,0:T(8,128)(2,1)}, u32[]{:S(2)}, u32[]{:S(2)}) collective-permute-start(bf16[224,512]{1,0:T(8,128)(2,1)} %constant_dynamic-slice_fusion.3), channel_id=1, source_target_pairs={{0,64},{64,0},{1,65},{65,1},{2,66},{66,2},{3,67},{67,3},{4,68},{68... | collective-permute-start | bytes 688136 | tf_op jit(solution)/shard_map/ppermute | solution.py:335
  185.4 1.4 copy-start.20
  187.6 7.6 %collective-permute-start.11 = (bf16[224,512]{1,0:T(8,128)(2,1)}, bf16[224,512]{1,0:T(8,128)(2,1)}, u32[]{:S(2)}, u32[]{:S(2)}) collective-permute-start(bf16[224,512]{1,0:T(8,128)(2,1)} %get-tuple-element.47), channel_id=1, source_target_pairs={{0,64},{64,0},{1,65},{65,1},{2,66},{66,2},{3,67},{67,3},{4,68},{68... | collective-permute-start | bytes 688136 | tf_op jit(solution)/shard_map/ppermute | solution.py:335
  190.1 2.7 %copy-start.15 = (f32[224,1024]{1,0:T(8,128)S(1)}, f32[224,1024]{1,0:T(8,128)}, u32[]{:S(2)}) copy-start(f32[224,1024]{1,0:T(8,128)} %fusion.6) | copy-start | bytes 2752516
  195.1 1.8 copy-start.9
  198.3 2.6 %copy-start.26 = (s32[4]{0:T(128)S(1)}, s32[4]{0:T(128)}, u32[]{:S(2)}) copy-start(s32[4]{0:T(128)} %get-tuple-element.54) | copy-start | bytes 52
  198.3 2.6 %copy-start.27 = (s32[4]{0:T(128)S(1)}, s32[4]{0:T(128)}, u32[]{:S(2)}) copy-start(s32[4]{0:T(128)} %get-tuple-element.55) | copy-start | bytes 52
  198.3 3.5 %copy-start.29 = (bf16[128]{0:T(256)(128)(2,1)S(1)}, bf16[128]{0:T(256)(128)(2,1)}, u32[]{:S(2)}) copy-start(bf16[128]{0:T(256)(128)(2,1)} %param.11) | copy-start | bytes 772
  198.3 4.4 %copy-start.23 = (f32[128,128]{1,0:T(8,128)S(1)}, f32[128,128]{1,0:T(8,128)}, u32[]{:S(2)}) copy-start(f32[128,128]{1,0:T(8,128)} %param.12) | copy-start | bytes 196612
  198.3 4.4 %copy-start.32 = (pred[128]{0:T(512)(128)(4,1)S(1)}, pred[128]{0:T(512)(128)(4,1)}, u32[]{:S(2)}) copy-start(pred[128]{0:T(512)(128)(4,1)} %iota_compare_fusion.2) | copy-start | bytes 388
  198.3 5.2 %copy-start.17 = (f32[224,1024]{1,0:T(8,128)S(1)}, f32[224,1024]{1,0:T(8,128)}, u32[]{:S(2)}) copy-start(f32[224,1024]{1,0:T(8,128)} %fusion.5) | copy-start | bytes 2752516
  199.8 5.0 %copy-start.16 = (f32[224,1024]{1,0:T(8,128)S(1)}, f32[224,1024]{1,0:T(8,128)}, u32[]{:S(2)}) copy-start(f32[224,1024]{1,0:T(8,128)} %fusion.3) | copy-start | bytes 2752516
  200.9 5.2 %copy-start.30 = (f32[8]{0:T(128)}, f32[8]{0:T(128)S(1)}, u32[]{:S(2)}) copy-start(f32[8]{0:T(128)S(1)} %mul.101) | copy-start | bytes 100
  203.5 2.5 %copy-start.18 = (f32[224,1024]{1,0:T(8,128)S(1)}, f32[224,1024]{1,0:T(8,128)}, u32[]{:S(2)}) copy-start(f32[224,1024]{1,0:T(8,128)} %fusion.1) | copy-start | bytes 2752516
  203.5 2.5 %copy-start.25 = (f32[1,1024]{1,0:T(1,128)S(1)}, f32[1,1024]{1,0:T(1,128)}, u32[]{:S(2)}) copy-start(f32[1,1024]{1,0:T(1,128)} %slice_convert_fusion) | copy-start | bytes 12292
Sparse Core Ops, SparseCore 0:
  38.8 39.3 all-gather.2

commit v9 on v8

--- a/solution.py
+++ b/solution.py
@@ -30,7 +30,7 @@
     )
 
 
-def token_products(tok_got, gate_w, up_w, parts, tok):
+def token_products(tok_got, gate_w, up_w, parts, tok, ends):
     n_plane, rows, cols = tok_got.shape
     half, width = tok.shape
     n_gy, n_yl = width // cols, half // rows
@@ -38,11 +38,13 @@
     for y in range(n_yl):
         for z in range(n_gy):
             tok[y * rows : (y + 1) * rows, z * cols : (z + 1) * cols] = tok_got[y * n_gy + z]
+    last = [tok[(y + 1) * rows - 16 : (y + 1) * rows].astype(f32)[15:] for y in range(n_yl)]
+    ends[...] = jnp.concatenate(last + [jnp.zeros((16 - n_yl, width), f32)], axis=0).astype(bf16)
     parts[:, :half] = dot(gate_w[:chip_units], tok[...], 1, 1).astype(bf16)
     parts[:, half:] = dot(up_w[:chip_units], tok[...], 1, 1).astype(bf16)
 
 
-def cotangent_products(core, low_got, tok, tok_sib, gate_w, up_w, down_w, parts, low, head, wide):
+def cotangent_products(core, low_got, ends, ends_sib, gate_w, up_w, down_w, parts, low, head, wide):
     n_gy, _, cols = low_got.shape
     half, width = low.shape
     n_yl = half // SEQ_LEN
@@ -51,14 +53,10 @@
         at = slice(z * cols, (z + 1) * cols)
         low[:, at] = low_got[z, :half]
         head[:, at] = low_got[z, half:]
-    ends = [
-        [ref[(y + 1) * SEQ_LEN - 16 : (y + 1) * SEQ_LEN].astype(f32)[15:] for y in range(n_yl)]
-        for ref in (tok, tok_sib)
-    ]
-    here, there = (jnp.concatenate(rows, axis=0) for rows in ends)
-    ends = [jnp.where(core[0] == 0, here, there), jnp.where(core[0] == 0, there, here)]
+    here, there = (ref[...].astype(f32)[:n_yl] for ref in (ends, ends_sib))
+    last = [jnp.where(core[0] == 0, here, there), jnp.where(core[0] == 0, there, here)]
     wide[:16] = head[...]
-    wide[16:32] = jnp.concatenate(ends + [jnp.zeros((16 - 2 * n_yl, width), f32)], axis=0).astype(bf16)
+    wide[16:32] = jnp.concatenate(last + [jnp.zeros((16 - 2 * n_yl, width), f32)], axis=0).astype(bf16)
     wide[32:] = jnp.zeros((96, width), bf16)
     parts[:, :half] = dot(down_w[...], low[...], 1, 1).astype(bf16)
     v = dot(down_w[...], wide[...], 1, 1)
@@ -194,24 +192,32 @@
     low_got = lax.all_gather(jnp.concatenate([low_got, head_rows], axis=0), "gy")
     tok_got = to_all(tok_block, PLANE, n_plane)
 
+    own_term = jnp.sum(tokens[rows - 1].astype(f32) * reward_head.astype(f32))
+    sib_term = lax.ppermute(own_term[None], "co", SWAP)[0]
+    spot = jnp.arange(128)[None, :] - 16 - lax.axis_index("yl")
+    first_term, second_term = core_order(own_term, sib_term)
+    tok_terms = jnp.where(spot == 0, first_term, jnp.where(spot == n_yl, second_term, 0.0))
+    gate_w, up_w, down_w, tok_terms = lax.optimization_barrier((gate_w, up_w, down_w, tok_terms))
+
     own = 2 * units // n_gz
     whole, scalar = pl.BlockSpec(memory_space=pltpu.VMEM), pl.BlockSpec(memory_space=pltpu.SMEM)
-    grant = pltpu.CompilerParams(vmem_limit_bytes=40 * 2**20)
-    parts, tok_half = pl.pallas_call(
+    grant = pltpu.CompilerParams(vmem_limit_bytes=16 * 2**20)
+    parts, tok_half, ends = pl.pallas_call(
         token_products,
         out_shape=(
             jax.ShapeDtypeStruct((2 * units, 2 * half), bf16),
             jax.ShapeDtypeStruct((half, width), bf16),
+            jax.ShapeDtypeStruct((16, width), bf16),
         ),
         in_specs=[whole] * 3,
-        out_specs=(whole,) * 2,
+        out_specs=(whole,) * 3,
         compiler_params=grant,
         cost_estimate=pl.CostEstimate(
             flops=8 * units * width * half, bytes_accessed=8 * 2**20, transcendentals=0
         ),
         name="token_products",
     )(tok_got, gate_w, up_w)
-    tok_sib = lax.ppermute(tok_half, "co", SWAP)
+    ends_sib = lax.ppermute(ends, "co", SWAP)
 
     n_xx = lax.axis_size("xx")
     first = exchange(parts.reshape(n_xx, 2 * own, 2 * half), "xx")
@@ -246,18 +252,13 @@
             flops=4 * units * width * (half + 384), bytes_accessed=5 * 2**20, transcendentals=0
         ),
         name="cotangent_products",
-    )(core.astype(jnp.int32)[None], low_got, tok_half, tok_sib, gate_w, up_w, down_w)
+    )(core.astype(jnp.int32)[None], low_got, ends, ends_sib, gate_w, up_w, down_w)
     head_vec = head_vec[:1]
     first, back_parts = lax.optimization_barrier((first, back_parts))
     second = exchange(back_parts.reshape(n_xx, 2 * own, half + 128), "xx")
     sums, sums_got = halves(first, False)
     back, back_got = halves(second, True)
 
-    own_term = jnp.sum(tokens[rows - 1].astype(f32) * reward_head.astype(f32))
-    sib_term = lax.ppermute(own_term[None], "co", SWAP)[0]
-    spot = jnp.arange(128)[None, :] - 16 - lax.axis_index("yl")
-    first_term, second_term = core_order(own_term, sib_term)
-    tok_terms = jnp.where(spot == 0, first_term, jnp.where(spot == n_yl, second_term, 0.0))
     place = (lax.axis_index(("xx", "yh")) * own).astype(jnp.int32)[None]
     mine = pl.pallas_call(
         functools.partial(hidden_units, 2 * units),
@@ -311,6 +312,7 @@
     grad_tokens = lm_grad + token_sum[:rows] + jnp.where(row == rows - 1, head_term[None, :], 0.0)
 
     loss_scale = 1.0 / jnp.sqrt(f32(rows * 2 * n_yl))
+    tok_sib = lax.ppermute(tok_half, "co", SWAP)
     low_sib = lax.ppermute(low_half, "co", SWAP)
 
     def core_parts(value, axis):

time: 217 us -> 204 us (0.940)
  waiting for transfers between devices: 42.1 us -> 29.4 us
  starting transfers between devices: 89.9 us -> 92.4 us
  matrix products: 15.5 us -> 13.1 us
    all_to_all x5, waiting for transfers between devices: 20.5 us -> 8.02 us  [exchange(): return lax.all_to_all(pieces, axes, 0, 0)]
    all_gather x1, waiting for transfers between devices: 3.51 us -> 13.4 us  [body(): lax.all_gather(jnp.concatenate([low_got, head_rows], axis=0), 'gy')]
    all_to_all x5, starting transfers between devices: 41.2 us -> 31.3 us  [exchange(): return lax.all_to_all(pieces, axes, 0, 0)]
    ppermute x1, starting transfers between devices: 4.95 us -> 11.3 us  [body(): tok_sib = lax.ppermute(tok_half, 'co', SWAP)]
    ppermute x1, starting transfers between devices: 8.15 us -> 1.92 us  [body(): low_sib = lax.ppermute(low_half, 'co', SWAP)]
    ppermute x1, waiting for transfers between devices: 8.79 us -> 3.49 us  [body(): other = lax.ppermute(mine, 'yh', SWAP)]
    ppermute x1, starting transfers between devices: 1.92 us -> 6.95 us  [body(): other = lax.ppermute(mine, 'yh', SWAP)]
    ppermute x1, starting transfers between devices: 6.89 us -> 1.91 us  [body(): sib_term = lax.ppermute(own_term[None], 'co', SWAP)[0]]
  transfers between devices with their start and end apart: 19 -> 20, of which waited for: 8 -> 5; matrix products, arithmetic and copies ran while one was open for 13% -> 14% of each run, Pallas kernels for 3% -> 3%
where the time goes in v9:
time: 204 us; the launch traced here: 202 us
  starting transfers between devices  92.4 us (45%)
  waiting for transfers between devices  29.4 us (14%)
  local copies, waits for them, and re-layouts  23 us (11%)
  between operations  17.1 us (8%)
  matrix products  13.1 us (6%)
  blocking collectives  9.99 us (5%)
  other arithmetic  9.77 us (5%)
  Pallas kernels  7.41 us (4%)
    all_to_all x5, starting transfers between devices, exchange(): return lax.all_to_all(pieces, axes, 0, 0)  31.3 us
    all_gather x1, waiting for transfers between devices, body(): lax.all_gather(jnp.concatenate([low_got, head_rows], axis=0), 'gy')  13.4 us
    dot_general x9, matrix products, dot(): lax.dot_general(left, right, (((left_dim,), (right_dim,)), ((), ())), pre...  13.1 us
    ppermute x2, starting transfers between devices, halves(): return (keep, lax.ppermute(give, 'yh', SWAP))  12.6 us
    ppermute x3, starting transfers between devices, weight_grad(): from_sib = lax.ppermute(there, 'co', SWAP)  11.7 us
    ppermute x1, starting transfers between devices, body(): tok_sib = lax.ppermute(tok_half, 'co', SWAP)  11.3 us
    all_to_all x1, blocking collectives, exchange(): return lax.all_to_all(pieces, axes, 0, 0)  9.99 us
    all_to_all x5, waiting for transfers between devices, exchange(): return lax.all_to_all(pieces, axes, 0, 0)  8.02 us
  transfers between devices with their start and end apart: 20, of which 5 were waited for; matrix products, arithmetic and copies ran while one was open for 14% of the time, Pallas kernels for 3%

profile of v9, /device:TPU:1, one launch (start us, length us, event | category | flops | bytes accessed | tf_op | source)
XLA Modules:
  0.0 202.2 jit_solution(8096256985368139577)
XLA Ops:
  7.2 0.8 convert_element_type.34
  8.0 10.0 %all_to_all.30 = bf16[4,128,128]{2,1,0:T(8,128)(2,1)S(1)} all-to-all(bf16[4,128,128]{2,1,0:T(8,128)(2,1)S(1)} %broadcast_in_dim.94), channel_id=1, replica_groups=mesh['yl'=4,'co'=2,'gy'=8,'yh'=2,'xx'=4] {'yl'}, dimensions={0} | all-to-all | bytes 262144 | tf_op jit(solution)/shard_map/all_to_all | solution.py:20
  18.0 2.1 %broadcast_in_dim.95 = bf16[32,128,128]{2,1,0:T(8,128)(2,1)} broadcast(bf16[128,128]{1,0:T(8,128)(2,1)} %param.7), dimensions={1,2} | broadcast | bytes 1081344 | tf_op jit(solution)/shard_map/broadcast_in_dim | solution.py:24
  20.1 12.5 %all-to-all-start.1 = ((bf16[32,128,128]{2,1,0:T(8,128)(2,1)}), bf16[32,128,128]{2,1,0:T(8,128)(2,1)}, u32[]{:S(2)}, u32[]{:S(2)}) async-start(bf16[32,128,128]{2,1,0:T(8,128)(2,1)} %broadcast_in_dim.95), calls=%async_computation.1 | async-start | bytes 2097152 | tf_op jit(solution)/shard_map/all_to_all | solution.py:20
  32.6 3.4 %collective-permute-start.2 = (bf16[224,1024]{1,0:T(8,128)(2,1)S(1)}, bf16[224,1024]{1,0:T(8,128)(2,1)S(1)}, u32[]{:S(2)}, u32[]{:S(2)}) collective-permute-start(bf16[224,1024]{1,0:T(8,128)(2,1)S(1)} %copy-done.16), channel_id=1, source_target_pairs={{0,64},{64,0},{1,65},{65,1},{2,66},{66,2},{3,67},{67,3},{4,68},{68... | collective-permute-start | bytes 1376264 | tf_op jit(solution)/shard_map/ppermute | solution.py:181
  36.1 1.9 collective-permute-start.1
  38.0 2.4 %collective-permute-start = (bf16[224,1024]{1,0:T(8,128)(2,1)S(1)}, bf16[224,1024]{1,0:T(8,128)(2,1)S(1)}, u32[]{:S(2)}, u32[]{:S(2)}) collective-permute-start(bf16[224,1024]{1,0:T(8,128)(2,1)S(1)} %copy-done.18), channel_id=1, source_target_pairs={{0,64},{64,0},{1,65},{65,1},{2,66},{66,2},{3,67},{67,3},{4,68},{68... | collective-permute-start | bytes 1376264 | tf_op jit(solution)/shard_map/ppermute | solution.py:181
  40.5 1.3 fusion.31
  41.8 1.9 collective-permute-start.3
  43.8 1.3 collective-permute-done.3
  47.5 0.7 pad_maximum_fusion.2
  48.4 1.1 broadcast_select_fusion.3
  49.9 8.0 %all-to-all-done.1.tok_got = bf16[32,128,128]{2,1,0:T(8,128)(2,1)} async-done(((bf16[32,128,128]{2,1,0:T(8,128)(2,1)}), bf16[32,128,128]{2,1,0:T(8,128)(2,1)}, u32[]{:S(2)}, u32[]{:S(2)}) %all-to-all-start.1) | async-done | bytes 1048608 | tf_op jit(solution)/shard_map/all_to_all | solution.py:20
  57.9 2.4 %token_products.1 = (bf16[448,1024]{1,0:T(8,128)(2,1)S(1)}, bf16[512,1024]{1,0:T(8,128)(2,1)S(1)}, bf16[16,1024]{1,0:T(8,128)(2,1)S(1)}) custom-call(bf16[32,128,128]{2,1,0:T(8,128)(2,1)} %all-to-all-done.1.tok_got, bf16[512,1024]{1,0:T(8,128)(2,1)S(1)} %get-tuple-element.26.gate_w, bf16[512,1024]{1,0:T(8,128)(2,1)S(1)} %get-tuple-element.27.up_w), custom_call_target="tpu_custom_call" | custom-call | flops 939524096 | bytes 8388608 | tf_op jit(solution)/shard_map/token_products/pallas_call | solution.py:205
  60.4 1.0 copy-done.1
  61.3 0.9 copy-done.6
  62.2 4.2 %all-to-all-start.2 = ((bf16[4,112,1024]{2,1,0:T(8,128)(2,1)}), bf16[4,112,1024]{2,1,0:T(8,128)(2,1)}, u32[]{:S(2)}, u32[]{:S(2)}) async-start(bf16[4,112,1024]{2,1,0:T(8,128)(2,1)} %bitcast.58), calls=%async_computation.2 | async-start | bytes 1835008 | tf_op jit(solution)/shard_map/all_to_all | solution.py:20
  66.5 5.0 %collective-permute-start.4 = (bf16[16,1024]{1,0:T(8,128)(2,1)S(1)}, bf16[16,1024]{1,0:T(8,128)(2,1)S(1)}, u32[]{:S(2)}, u32[]{:S(2)}) collective-permute-start(bf16[16,1024]{1,0:T(8,128)(2,1)S(1)} %get-tuple-element.30.ends), channel_id=1, source_target_pairs={{0,64},{64,0},{1,65},{65,1},{2,66},{66,2},{3,67},{67,3},{4,68},{68... | collective-permute-start | bytes 98312 | tf_op jit(solution)/shard_map/ppermute | solution.py:220
  71.5 13.4 %all-gather.3.cloned.1.call-done = bf16[4224,128]{1,0:T(8,128)(2,1)} async-done(((bf16[528,128]{1,0:T(8,128)(2,1)}), bf16[4224,128]{1,0:T(8,128)(2,1)}) %all-gather.3.cloned.1.call-update) | async-done | bytes 1081360 | tf_op jit(solution)/shard_map/all_gather | solution.py:192
  84.9 1.2 copy-done.3
  86.1 1.5 cotangent_products.1
  87.6 1.0 copy-done.4
  88.6 0.8 copy-done.7
  89.5 4.2 %all-to-all-start.3 = ((bf16[4,112,640]{2,1,0:T(8,128)(2,1)}), bf16[4,112,640]{2,1,0:T(8,128)(2,1)S(1)}, u32[]{:S(2)}, u32[]{:S(2)}) async-start(bf16[4,112,640]{2,1,0:T(8,128)(2,1)} %bitcast.59), calls=%async_computation.3 | async-start | bytes 1146880 | tf_op jit(solution)/shard_map/all_to_all | solution.py:20
  93.7 1.4 split_sums.2
  95.1 6.8 %collective-permute-start.5 = (bf16[56,1024]{1,0:T(8,128)(2,1)S(1)}, bf16[56,1024]{1,0:T(8,128)(2,1)S(1)}, u32[]{:S(2)}, u32[]{:S(2)}) collective-permute-start(bf16[56,1024]{1,0:T(8,128)(2,1)S(1)} %get-tuple-element.35), channel_id=1, source_target_pairs={{0,4},{4,0},{1,5},{5,1},{2,6},{6,2},{3,7},{7,3},{8,12},{12,8},{9,1... | collective-permute-start | bytes 344072 | tf_op jit(solution)/shard_map/ppermute | solution.py:238
  102.1 5.8 %collective-permute-start.6 = (bf16[56,640]{1,0:T(8,128)(2,1)S(1)}, bf16[56,640]{1,0:T(8,128)(2,1)S(1)}, u32[]{:S(2)}, u32[]{:S(2)}) collective-permute-start(bf16[56,640]{1,0:T(8,128)(2,1)S(1)} %get-tuple-element.38), channel_id=1, source_target_pairs={{0,4},{4,0},{1,5},{5,1},{2,6},{6,2},{3,7},{7,3},{8,12},{12,8},{9,1... | collective-permute-start | bytes 215048 | tf_op jit(solution)/shard_map/ppermute | solution.py:238
  107.9 3.2 %collective-permute-done.6.back_got = bf16[56,640]{1,0:T(8,128)(2,1)S(1)} collective-permute-done((bf16[56,640]{1,0:T(8,128)(2,1)S(1)}, bf16[56,640]{1,0:T(8,128)(2,1)S(1)}, u32[]{:S(2)}, u32[]{:S(2)}) %collective-permute-start.6) | collective-permute-done | bytes 71712 | tf_op jit(solution)/shard_map/ppermute | solution.py:238
  111.5 6.9 %collective-permute-start.7 = (bf16[176,512]{1,0:T(8,128)(2,1)S(1)}, bf16[176,512]{1,0:T(8,128)(2,1)S(1)}, u32[]{:S(2)}, u32[]{:S(2)}) collective-permute-start(bf16[176,512]{1,0:T(8,128)(2,1)S(1)} %hidden_units.1), channel_id=1, source_target_pairs={{0,4},{4,0},{1,5},{5,1},{2,6},{6,2},{3,7},{7,3},{8,12},{12,8},{9,1... | collective-permute-start | bytes 540680 | tf_op jit(solution)/shard_map/ppermute | solution.py:274
  118.4 3.5 %collective-permute-done.7 = bf16[176,512]{1,0:T(8,128)(2,1)S(1)} collective-permute-done((bf16[176,512]{1,0:T(8,128)(2,1)S(1)}, bf16[176,512]{1,0:T(8,128)(2,1)S(1)}, u32[]{:S(2)}, u32[]{:S(2)}) %collective-permute-start.7) | collective-permute-done | bytes 180256 | tf_op jit(solution)/shard_map/ppermute | solution.py:274
  122.0 1.3 broadcast_in_dim.102
  123.3 5.6 %all-to-all-start.4 = ((bf16[4,2,176,512]{3,2,1,0:T(8,128)(2,1)}), bf16[4,2,176,512]{3,2,1,0:T(8,128)(2,1)S(1)}, u32[]{:S(2)}, u32[]{:S(2)}) async-start(bf16[4,2,176,512]{3,2,1,0:T(8,128)(2,1)} %broadcast_in_dim.102), calls=%async_computation.4 | async-start | bytes 2883584 | tf_op jit(solution)/shard_map/all_to_all | solution.py:20
  128.9 11.3 %collective-permute-start.9 = (bf16[512,1024]{1,0:T(8,128)(2,1)}, bf16[512,1024]{1,0:T(8,128)(2,1)}, u32[]{:S(2)}, u32[]{:S(2)}) collective-permute-start(bf16[512,1024]{1,0:T(8,128)(2,1)} %copy-done.1), channel_id=1, source_target_pairs={{0,64},{64,0},{1,65},{65,1},{2,66},{66,2},{3,67},{67,3},{4,68},{68... | collective-permute-start | bytes 3145736 | tf_op jit(solution)/shard_map/ppermute | solution.py:315
  141.4 0.9 slice.90
  142.3 1.9 collective-permute-start.13
  144.2 1.3 slice_convert_fusion
  145.5 0.9 slice.91
  146.4 1.5 token_gradients.1
  147.9 1.0 copy-done
  149.0 1.1 fusion.35
  150.7 4.8 %all-to-all-start.5 = ((bf16[32,144,128]{2,1,0:T(8,128)(2,1)}), bf16[32,144,128]{2,1,0:T(8,128)(2,1)S(1)}, u32[]{:S(2)}, u32[]{:S(2)}) async-start(bf16[32,144,128]{2,1,0:T(8,128)(2,1)} %copy-done), calls=%async_computation.5 | async-start | bytes 2359296 | tf_op jit(solution)/shard_map/all_to_all | solution.py:20
  155.5 0.7 constant_dynamic-slice_fusion.5
  156.3 7.2 %collective-permute-start.8 = (bf16[224,512]{1,0:T(8,128)(2,1)}, bf16[224,512]{1,0:T(8,128)(2,1)}, u32[]{:S(2)}, u32[]{:S(2)}) collective-permute-start(bf16[224,512]{1,0:T(8,128)(2,1)} %constant_dynamic-slice_fusion.5), channel_id=1, source_target_pairs={{0,64},{64,0},{1,65},{65,1},{2,66},{66,2},{3,67},{67,3},{4,68},{68... | collective-permute-start | bytes 688136 | tf_op jit(solution)/shard_map/ppermute | solution.py:337
  163.6 1.9 collective-permute-start.10
  165.5 0.7 constant_dynamic-slice_fusion.3
  166.2 2.4 %collective-permute-start.11 = (bf16[224,512]{1,0:T(8,128)(2,1)}, bf16[224,512]{1,0:T(8,128)(2,1)}, u32[]{:S(2)}, u32[]{:S(2)}) collective-permute-start(bf16[224,512]{1,0:T(8,128)(2,1)} %constant_dynamic-slice_fusion.3), channel_id=1, source_target_pairs={{0,64},{64,0},{1,65},{65,1},{2,66},{66,2},{3,67},{67,3},{4,68},{68... | collective-permute-start | bytes 688136 | tf_op jit(solution)/shard_map/ppermute | solution.py:337
  168.6 1.3 fusion.8
  171.0 0.7 constant_dynamic-slice_fusion.2
  171.7 2.1 %collective-permute-start.12 = (bf16[224,512]{1,0:T(8,128)(2,1)}, bf16[224,512]{1,0:T(8,128)(2,1)}, u32[]{:S(2)}, u32[]{:S(2)}) collective-permute-start(bf16[224,512]{1,0:T(8,128)(2,1)} %get-tuple-element.57), channel_id=1, source_target_pairs={{0,64},{64,0},{1,65},{65,1},{2,66},{66,2},{3,67},{67,3},{4,68},{68... | collective-permute-start | bytes 688136 | tf_op jit(solution)/shard_map/ppermute | solution.py:337
  173.8 0.7 reshape.109
  174.6 1.8 slice.93
  176.4 1.1 copy.28
  177.6 2.7 %fusion.5 = f32[224,1024]{1,0:T(8,128)} fusion(f32[224,1024]{1,0:T(8,128)S(1)} %copy-done.9, bf16[224,512]{1,0:T(8,128)(2,1)} %collective-permute-done.8, bf16[512,1024]{1,0:T(8,128)(2,1)} %collective-permute-done.9), kind=kOutput, calls=%fused_computation.12 | convolution fusion | flops 235339776 | bytes 3112960 | tf_op jit(solution)/shard_map/dot_general | solution.py:28
  180.3 1.8 fusion.3
  182.1 1.8 fusion.38
  183.9 1.3 fusion.1
  185.3 1.1 reshape.110
  186.4 0.9 slice.94
  187.3 1.1 copy.29
  189.8 0.6 fusion.30
  190.8 0.7 fusion.10
  191.6 1.3 fusion.4
  192.8 1.3 fusion.2
  194.1 1.3 fusion
  (104 shorter events, 6.2 us)
Async XLA Ops:
  18.0 14.6 %copy-start.16 = (bf16[224,1024]{1,0:T(8,128)(2,1)S(1)}, bf16[224,1024]{1,0:T(8,128)(2,1)}, u32[]{:S(2)}) copy-start(bf16[224,1024]{1,0:T(8,128)(2,1)} %param.10) | copy-start | bytes 1376260
  18.0 18.1 %copy-start.17 = (bf16[224,1024]{1,0:T(8,128)(2,1)S(1)}, bf16[224,1024]{1,0:T(8,128)(2,1)}, u32[]{:S(2)}) copy-start(bf16[224,1024]{1,0:T(8,128)(2,1)} %param.9) | copy-start | bytes 1376260
  18.0 20.0 %copy-start.18 = (bf16[224,1024]{1,0:T(8,128)(2,1)S(1)}, bf16[224,1024]{1,0:T(8,128)(2,1)}, u32[]{:S(2)}) copy-start(bf16[224,1024]{1,0:T(8,128)(2,1)} %param.8) | copy-start | bytes 1376260
  18.0 22.4 %copy-start.24 = (bf16[128]{0:T(256)(128)(2,1)S(1)}, bf16[128]{0:T(256)(128)(2,1)}, u32[]{:S(2)}) copy-start(bf16[128]{0:T(256)(128)(2,1)} %param.11) | copy-start | bytes 772
  20.1 37.8 %all-to-all-start.1 = ((bf16[32,128,128]{2,1,0:T(8,128)(2,1)}), bf16[32,128,128]{2,1,0:T(8,128)(2,1)}, u32[]{:S(2)}, u32[]{:S(2)}) async-start(bf16[32,128,128]{2,1,0:T(8,128)(2,1)} %broadcast_in_dim.95), calls=%async_computation.1 | async-start | bytes 2097152 | tf_op jit(solution)/shard_map/all_to_all | solution.py:20
  32.6 52.3 %all-gather.3.cloned.1.call-start = ((), (), s32[]{:S(2)}) async-start(), calls=%async_computation.6 | async-start | bytes 1216512 | tf_op jit(solution)/shard_map/all_gather | solution.py:192
  32.6 15.6 %collective-permute-start.2 = (bf16[224,1024]{1,0:T(8,128)(2,1)S(1)}, bf16[224,1024]{1,0:T(8,128)(2,1)S(1)}, u32[]{:S(2)}, u32[]{:S(2)}) collective-permute-start(bf16[224,1024]{1,0:T(8,128)(2,1)S(1)} %copy-done.16), channel_id=1, source_target_pairs={{0,64},{64,0},{1,65},{65,1},{2,66},{66,2},{3,67},{67,3},{4,68},{68... | collective-permute-start | bytes 1376264 | tf_op jit(solution)/shard_map/ppermute | solution.py:181
  36.1 12.3 %collective-permute-start.1 = (bf16[224,1024]{1,0:T(8,128)(2,1)S(1)}, bf16[224,1024]{1,0:T(8,128)(2,1)}, u32[]{:S(2)}, u32[]{:S(2)}) collective-permute-start(bf16[224,1024]{1,0:T(8,128)(2,1)S(1)} %copy-done.17), channel_id=1, source_target_pairs={{0,64},{64,0},{1,65},{65,1},{2,66},{66,2},{3,67},{67,3},{4,68},{68... | collective-permute-start | bytes 1376264 | tf_op jit(solution)/shard_map/ppermute | solution.py:181
  38.0 11.4 %collective-permute-start = (bf16[224,1024]{1,0:T(8,128)(2,1)S(1)}, bf16[224,1024]{1,0:T(8,128)(2,1)S(1)}, u32[]{:S(2)}, u32[]{:S(2)}) collective-permute-start(bf16[224,1024]{1,0:T(8,128)(2,1)S(1)} %copy-done.18), channel_id=1, source_target_pairs={{0,64},{64,0},{1,65},{65,1},{2,66},{66,2},{3,67},{67,3},{4,68},{68... | collective-permute-start | bytes 1376264 | tf_op jit(solution)/shard_map/ppermute | solution.py:181
  41.8 3.3 %collective-permute-start.3 = (f32[1]{0:T(128)}, f32[1]{0:T(128)}, u32[]{:S(2)}, u32[]{:S(2)}) collective-permute-start(f32[1]{0:T(128)} %bitcast.5), channel_id=1, source_target_pairs={{0,64},{64,0},{1,65},{65,1},{2,66},{66,2},{3,67},{67,3},{4,68},{68... | collective-permute-start | bytes 20 | tf_op jit(solution)/shard_map/ppermute | solution.py:196
  60.3 1.0 copy-start.1
  61.3 0.9 copy-start.6
  62.2 27.2 %all-to-all-start.2 = ((bf16[4,112,1024]{2,1,0:T(8,128)(2,1)}), bf16[4,112,1024]{2,1,0:T(8,128)(2,1)}, u32[]{:S(2)}, u32[]{:S(2)}) async-start(bf16[4,112,1024]{2,1,0:T(8,128)(2,1)} %bitcast.58), calls=%async_computation.2 | async-start | bytes 1835008 | tf_op jit(solution)/shard_map/all_to_all | solution.py:20
  66.5 18.4 %collective-permute-start.4 = (bf16[16,1024]{1,0:T(8,128)(2,1)S(1)}, bf16[16,1024]{1,0:T(8,128)(2,1)S(1)}, u32[]{:S(2)}, u32[]{:S(2)}) collective-permute-start(bf16[16,1024]{1,0:T(8,128)(2,1)S(1)} %get-tuple-element.30.ends), channel_id=1, source_target_pairs={{0,64},{64,0},{1,65},{65,1},{2,66},{66,2},{3,67},{67,3},{4,68},{68... | collective-permute-start | bytes 98312 | tf_op jit(solution)/shard_map/ppermute | solution.py:220
  84.9 1.2 copy-start.3
  87.6 1.0 copy-start.4
  88.6 0.8 copy-start.7
  89.5 5.6 %copy-start.8 = (bf16[16,1024]{1,0:T(8,128)(2,1)}, bf16[16,1024]{1,0:T(8,128)(2,1)S(1)}, u32[]{:S(2)}) copy-start(bf16[16,1024]{1,0:T(8,128)(2,1)S(1)} %get-tuple-element.44) | copy-start | bytes 98308
  89.5 12.5 %all-to-all-start.3 = ((bf16[4,112,640]{2,1,0:T(8,128)(2,1)}), bf16[4,112,640]{2,1,0:T(8,128)(2,1)S(1)}, u32[]{:S(2)}, u32[]{:S(2)}) async-start(bf16[4,112,640]{2,1,0:T(8,128)(2,1)} %bitcast.59), calls=%async_computation.3 | async-start | bytes 1146880 | tf_op jit(solution)/shard_map/all_to_all | solution.py:20
  95.1 12.8 %collective-permute-start.5 = (bf16[56,1024]{1,0:T(8,128)(2,1)S(1)}, bf16[56,1024]{1,0:T(8,128)(2,1)S(1)}, u32[]{:S(2)}, u32[]{:S(2)}) collective-permute-start(bf16[56,1024]{1,0:T(8,128)(2,1)S(1)} %get-tuple-element.35), channel_id=1, source_target_pairs={{0,4},{4,0},{1,5},{5,1},{2,6},{6,2},{3,7},{7,3},{8,12},{12,8},{9,1... | collective-permute-start | bytes 344072 | tf_op jit(solution)/shard_map/ppermute | solution.py:238
  102.1 9.0 %collective-permute-start.6 = (bf16[56,640]{1,0:T(8,128)(2,1)S(1)}, bf16[56,640]{1,0:T(8,128)(2,1)S(1)}, u32[]{:S(2)}, u32[]{:S(2)}) collective-permute-start(bf16[56,640]{1,0:T(8,128)(2,1)S(1)} %get-tuple-element.38), channel_id=1, source_target_pairs={{0,4},{4,0},{1,5},{5,1},{2,6},{6,2},{3,7},{7,3},{8,12},{12,8},{9,1... | collective-permute-start | bytes 215048 | tf_op jit(solution)/shard_map/ppermute | solution.py:238
  111.5 10.5 %collective-permute-start.7 = (bf16[176,512]{1,0:T(8,128)(2,1)S(1)}, bf16[176,512]{1,0:T(8,128)(2,1)S(1)}, u32[]{:S(2)}, u32[]{:S(2)}) collective-permute-start(bf16[176,512]{1,0:T(8,128)(2,1)S(1)} %hidden_units.1), channel_id=1, source_target_pairs={{0,4},{4,0},{1,5},{5,1},{2,6},{6,2},{3,7},{7,3},{8,12},{12,8},{9,1... | collective-permute-start | bytes 540680 | tf_op jit(solution)/shard_map/ppermute | solution.py:274
  123.3 17.5 %copy-start.27 = (s32[4,2]{0,1:T(2,128)S(1)}, s32[4,2]{0,1:T(2,128)}, u32[]{:S(2)}) copy-start(s32[4,2]{0,1:T(2,128)} %param.13) | copy-start | bytes 100
  123.3 23.1 %all-to-all-start.4 = ((bf16[4,2,176,512]{3,2,1,0:T(8,128)(2,1)}), bf16[4,2,176,512]{3,2,1,0:T(8,128)(2,1)S(1)}, u32[]{:S(2)}, u32[]{:S(2)}) async-start(bf16[4,2,176,512]{3,2,1,0:T(8,128)(2,1)} %broadcast_in_dim.102), calls=%async_computation.4 | async-start | bytes 2883584 | tf_op jit(solution)/shard_map/all_to_all | solution.py:20
  128.9 16.7 %collective-permute-start.9 = (bf16[512,1024]{1,0:T(8,128)(2,1)}, bf16[512,1024]{1,0:T(8,128)(2,1)}, u32[]{:S(2)}, u32[]{:S(2)}) collective-permute-start(bf16[512,1024]{1,0:T(8,128)(2,1)} %copy-done.1), channel_id=1, source_target_pairs={{0,64},{64,0},{1,65},{65,1},{2,66},{66,2},{3,67},{67,3},{4,68},{68... | collective-permute-start | bytes 3145736 | tf_op jit(solution)/shard_map/ppermute | solution.py:315
  142.3 39.8 %collective-permute-start.13 = (bf16[512,1024]{1,0:T(8,128)(2,1)}, bf16[512,1024]{1,0:T(8,128)(2,1)}, u32[]{:S(2)}, u32[]{:S(2)}) collective-permute-start(bf16[512,1024]{1,0:T(8,128)(2,1)} %copy-done.4), channel_id=1, source_target_pairs={{0,64},{64,0},{1,65},{65,1},{2,66},{66,2},{3,67},{67,3},{4,68},{68... | collective-permute-start | bytes 3145736 | tf_op jit(solution)/shard_map/ppermute | solution.py:316
  147.9 1.0 copy-start
  150.7 4.8 %copy-start.14 = (bf16[8,56,512]{2,1,0:T(8,128)(2,1)S(1)}, bf16[8,56,512]{2,1,0:T(8,128)(2,1)}, u32[]{:S(2)}) copy-start(bf16[8,56,512]{2,1,0:T(8,128)(2,1)} %get-tuple-element.49) | copy-start | bytes 1376260
  150.7 12.8 %copy-start.20 = (bf16[8,448]{1,0:T(8,128)(2,1)S(1)}, bf16[8,448]{1,0:T(8,128)(2,1)}, u32[]{:S(2)}) copy-start(bf16[8,448]{1,0:T(8,128)(2,1)} %slice_reduce_fusion) | copy-start | bytes 21508
  150.7 14.8 %copy-start.12 = (bf16[8,56,512]{2,1,0:T(8,128)(2,1)S(1)}, bf16[8,56,512]{2,1,0:T(8,128)(2,1)}, u32[]{:S(2)}) copy-start(bf16[8,56,512]{2,1,0:T(8,128)(2,1)} %get-tuple-element.48) | copy-start | bytes 1376260
  150.7 17.9 %copy-start.2 = (bf16[512,1024]{1,0:T(8,128)(2,1)S(1)}, bf16[512,1024]{1,0:T(8,128)(2,1)}, u32[]{:S(2)}) copy-start(bf16[512,1024]{1,0:T(8,128)(2,1)} %copy-done.1) | copy-start | bytes 3145732
  150.7 37.7 %all-to-all-start.5 = ((bf16[32,144,128]{2,1,0:T(8,128)(2,1)}), bf16[32,144,128]{2,1,0:T(8,128)(2,1)S(1)}, u32[]{:S(2)}, u32[]{:S(2)}) async-start(bf16[32,144,128]{2,1,0:T(8,128)(2,1)} %copy-done), calls=%async_computation.5 | async-start | bytes 2359296 | tf_op jit(solution)/shard_map/all_to_all | solution.py:20
  156.2 13.7 %copy-start.13 = (bf16[8,56,512]{2,1,0:T(8,128)(2,1)S(1)}, bf16[8,56,512]{2,1,0:T(8,128)(2,1)}, u32[]{:S(2)}) copy-start(bf16[8,56,512]{2,1,0:T(8,128)(2,1)} %get-tuple-element.48) | copy-start | bytes 1376260
  156.3 21.3 %collective-permute-start.8 = (bf16[224,512]{1,0:T(8,128)(2,1)}, bf16[224,512]{1,0:T(8,128)(2,1)}, u32[]{:S(2)}, u32[]{:S(2)}) collective-permute-start(bf16[224,512]{1,0:T(8,128)(2,1)} %constant_dynamic-slice_fusion.5), channel_id=1, source_target_pairs={{0,64},{64,0},{1,65},{65,1},{2,66},{66,2},{3,67},{67,3},{4,68},{68... | collective-permute-start | bytes 688136 | tf_op jit(solution)/shard_map/ppermute | solution.py:337
  163.6 13.9 %collective-permute-start.10 = (bf16[8,224]{1,0:T(8,128)(2,1)S(1)}, bf16[8,224]{1,0:T(8,128)(2,1)S(1)}, u32[]{:S(2)}, u32[]{:S(2)}) collective-permute-start(bf16[8,224]{1,0:T(8,128)(2,1)S(1)} %constant_dynamic-slice_fusion.4), channel_id=1, source_target_pairs={{0,64},{64,0},{1,65},{65,1},{2,66},{66,2},{3,67},{67,3},{4,68},{68... | collective-permute-start | bytes 10760 | tf_op jit(solution)/shard_map/ppermute | solution.py:324
  166.2 14.0 %collective-permute-start.11 = (bf16[224,512]{1,0:T(8,128)(2,1)}, bf16[224,512]{1,0:T(8,128)(2,1)}, u32[]{:S(2)}, u32[]{:S(2)}) collective-permute-start(bf16[224,512]{1,0:T(8,128)(2,1)} %constant_dynamic-slice_fusion.3), channel_id=1, source_target_pairs={{0,64},{64,0},{1,65},{65,1},{2,66},{66,2},{3,67},{67,3},{4,68},{68... | collective-permute-start | bytes 688136 | tf_op jit(solution)/shard_map/ppermute | solution.py:337
  170.0 1.0 copy-start.15
  170.4 7.2 %copy-start.9 = (f32[224,1024]{1,0:T(8,128)S(1)}, f32[224,1024]{1,0:T(8,128)}, u32[]{:S(2)}) copy-start(f32[224,1024]{1,0:T(8,128)} %fusion.8) | copy-start | bytes 2752516
  171.7 10.3 %collective-permute-start.12 = (bf16[224,512]{1,0:T(8,128)(2,1)}, bf16[224,512]{1,0:T(8,128)(2,1)}, u32[]{:S(2)}, u32[]{:S(2)}) collective-permute-start(bf16[224,512]{1,0:T(8,128)(2,1)} %get-tuple-element.57), channel_id=1, source_target_pairs={{0,64},{64,0},{1,65},{65,1},{2,66},{66,2},{3,67},{67,3},{4,68},{68... | collective-permute-start | bytes 688136 | tf_op jit(solution)/shard_map/ppermute | solution.py:337
  182.0 1.9 copy-start.5
  185.3 3.6 %copy-start.22 = (s32[4]{0:T(128)S(1)}, s32[4]{0:T(128)}, u32[]{:S(2)}) copy-start(s32[4]{0:T(128)} %get-tuple-element.64) | copy-start | bytes 52
  185.3 3.6 %copy-start.23 = (s32[4]{0:T(128)S(1)}, s32[4]{0:T(128)}, u32[]{:S(2)}) copy-start(s32[4]{0:T(128)} %get-tuple-element.65) | copy-start | bytes 52
  185.3 4.5 %copy-start.25 = (bf16[128]{0:T(256)(128)(2,1)S(1)}, bf16[128]{0:T(256)(128)(2,1)}, u32[]{:S(2)}) copy-start(bf16[128]{0:T(256)(128)(2,1)} %param.11) | copy-start | bytes 772
  185.3 5.5 %copy-start.19 = (f32[128,128]{1,0:T(8,128)S(1)}, f32[128,128]{1,0:T(8,128)}, u32[]{:S(2)}) copy-start(f32[128,128]{1,0:T(8,128)} %param.12) | copy-start | bytes 196612
  185.3 5.5 %copy-start.28 = (pred[128]{0:T(512)(128)(4,1)S(1)}, pred[128]{0:T(512)(128)(4,1)}, u32[]{:S(2)}) copy-start(pred[128]{0:T(512)(128)(4,1)} %iota_compare_fusion.2) | copy-start | bytes 388
  185.3 6.3 %copy-start.10 = (f32[224,1024]{1,0:T(8,128)S(1)}, f32[224,1024]{1,0:T(8,128)}, u32[]{:S(2)}) copy-start(f32[224,1024]{1,0:T(8,128)} %fusion.5) | copy-start | bytes 2752516
  188.9 5.2 %copy-start.26 = (f32[8]{0:T(128)}, f32[8]{0:T(128)S(1)}, u32[]{:S(2)}) copy-start(f32[8]{0:T(128)S(1)} %mul.101) | copy-start | bytes 100
  191.5 2.5 %copy-start.11 = (f32[224,1024]{1,0:T(8,128)S(1)}, f32[224,1024]{1,0:T(8,128)}, u32[]{:S(2)}) copy-start(f32[224,1024]{1,0:T(8,128)} %fusion.1) | copy-start | bytes 2752516
  191.5 2.5 %copy-start.21 = (f32[1,1024]{1,0:T(1,128)S(1)}, f32[1,1024]{1,0:T(1,128)}, u32[]{:S(2)}) copy-start(f32[1,1024]{1,0:T(1,128)} %slice_convert_fusion) | copy-start | bytes 12292
Sparse Core Ops, SparseCore 0:
  48.3 36.5 all-gather.2

commit v10 on v9

--- a/solution.py
+++ b/solution.py
@@ -187,9 +187,10 @@
 
     half = n_yl * rows
     low_got = to_all(lm_grad.astype(bf16), "yl", n_yl).reshape(half, cols)
+    head_rows = jnp.broadcast_to(reward_head[None, :], (16, cols))
+    low_got = jnp.concatenate([low_got, head_rows], axis=0)
     low_got, tok_block = lax.optimization_barrier((low_got, tokens))
-    head_rows = jnp.broadcast_to(reward_head[None, :], (16, cols))
-    low_got = lax.all_gather(jnp.concatenate([low_got, head_rows], axis=0), "gy")
+    low_got = lax.all_gather(low_got, "gy")
     tok_got = to_all(tok_block, PLANE, n_plane)
 
     own_term = jnp.sum(tokens[rows - 1].astype(f32) * reward_head.astype(f32))
@@ -325,10 +326,8 @@
     gate_u8 = jnp.concatenate([unit_here[:n_yl], unit_swap[:n_yl]], axis=0)
     up_u8 = jnp.concatenate([unit_here[n_yl:], unit_swap[n_yl:]], axis=0)
 
-    def last_rows(value):
-        return value.reshape(n_yl, rows, width)[:, rows - 1]
-
-    last_tok = jnp.concatenate([last_rows(tok_half), last_rows(tok_sib)], axis=0).astype(f32)
+    last_tok = jnp.concatenate([ends[:n_yl], ends_sib[:n_yl]], axis=0).astype(f32)
+    is_last = jnp.arange(half)[:, None] == jnp.arange(n_yl)[None, :] * rows + rows - 1
     last_tok = (last_tok * coefs[:, None]).astype(bf16)
     head_term8 = (coefs[:, None] * head_vec.astype(f32)).astype(bf16)
 
@@ -339,8 +338,8 @@
             (dot(here, own_right, 1, 0) + dot(from_sib, sib_right, 1, 0)) * loss_scale
         )
         if last_left is None:
-            ends = [v.reshape(units, n_yl, rows)[:, :, rows - 1] for v in (here, from_sib)]
-            last_left = jnp.concatenate(ends, axis=1).T
+            picked = [dot(is_last.astype(bf16), v, 0, 1) for v in (here, from_sib)]
+            last_left = jnp.concatenate(picked, axis=0).astype(bf16)
         return total + dot(last_left, last_right, 0, 0) * loss_scale
 
     grad_gate = weight_grad(gate_g, tok_half, tok_sib, gate_u8, last_tok)

time: 204 us -> 203 us (level)
  the two profiles are of different devices: /device:TPU:1 before, /device:TPU:2 now
where the time goes in v10:
time: 203 us; the launch traced here: 201 us
  starting transfers between devices  75.4 us (37%)
  waiting for transfers between devices  55.2 us (27%)
  between operations  17.2 us (8%)
  local copies, waits for them, and re-layouts  13.9 us (7%)
  matrix products  11.3 us (6%)
  blocking collectives  10.7 us (5%)
  other arithmetic  10.3 us (5%)
  Pallas kernels  7.41 us (4%)
    all_to_all x5, starting transfers between devices, exchange(): return lax.all_to_all(pieces, axes, 0, 0)  32.7 us
    all_to_all x5, waiting for transfers between devices, exchange(): return lax.all_to_all(pieces, axes, 0, 0)  25.5 us
    all_gather x1, waiting for transfers between devices, body(): low_got = lax.all_gather(low_got, 'gy')  17.3 us
    ppermute x2, starting transfers between devices, halves(): return (keep, lax.ppermute(give, 'yh', SWAP))  12.8 us
    dot_general x11, matrix products, dot(): lax.dot_general(left, right, (((left_dim,), (right_dim,)), ((), ())), pre...  11.3 us
    all_to_all x1, blocking collectives, exchange(): return lax.all_to_all(pieces, axes, 0, 0)  10.7 us
    ppermute x1, waiting for transfers between devices, body(): other = lax.ppermute(mine, 'yh', SWAP)  6.91 us
    ppermute x1, starting transfers between devices, body(): other = lax.ppermute(mine, 'yh', SWAP)  6.35 us
  transfers between devices with their start and end apart: 20, of which 7 were waited for; matrix products, arithmetic and copies ran while one was open for 8% of the time, Pallas kernels for 3%

profile of v10, /device:TPU:2, one launch (start us, length us, event | category | flops | bytes accessed | tf_op | source)
XLA Modules:
  0.0 201.5 jit_solution(6077766664204824509)
XLA Ops:
  7.2 0.8 convert_element_type.37
  8.0 10.7 %all_to_all.30 = bf16[4,128,128]{2,1,0:T(8,128)(2,1)S(1)} all-to-all(bf16[4,128,128]{2,1,0:T(8,128)(2,1)S(1)} %broadcast_in_dim.96), channel_id=1, replica_groups=mesh['yl'=4,'co'=2,'gy'=8,'yh'=2,'xx'=4] {'yl'}, dimensions={0} | all-to-all | bytes 262144 | tf_op jit(solution)/shard_map/all_to_all | solution.py:20
  18.8 0.7 broadcast_in_dim.97
  19.4 0.7 pad_maximum_fusion.2
  20.1 2.1 %broadcast_in_dim.98 = bf16[32,128,128]{2,1,0:T(8,128)(2,1)} broadcast(bf16[128,128]{1,0:T(8,128)(2,1)} %param.7), dimensions={1,2} | broadcast | bytes 1081344 | tf_op jit(solution)/shard_map/broadcast_in_dim | solution.py:24
  22.2 11.7 %all-to-all-start.1 = ((bf16[32,128,128]{2,1,0:T(8,128)(2,1)}), bf16[32,128,128]{2,1,0:T(8,128)(2,1)}, u32[]{:S(2)}, u32[]{:S(2)}) async-start(bf16[32,128,128]{2,1,0:T(8,128)(2,1)} %broadcast_in_dim.98), calls=%async_computation.1 | async-start | bytes 2097152 | tf_op jit(solution)/shard_map/all_to_all | solution.py:20
  34.0 1.9 collective-permute-start.2
  35.9 2.4 %collective-permute-start.1 = (bf16[224,1024]{1,0:T(8,128)(2,1)S(1)}, bf16[224,1024]{1,0:T(8,128)(2,1)}, u32[]{:S(2)}, u32[]{:S(2)}) collective-permute-start(bf16[224,1024]{1,0:T(8,128)(2,1)S(1)} %copy-done.16), channel_id=1, source_target_pairs={{0,64},{64,0},{1,65},{65,1},{2,66},{66,2},{3,67},{67,3},{4,68},{68... | collective-permute-start | bytes 1376264 | tf_op jit(solution)/shard_map/ppermute | solution.py:181
  38.4 1.9 collective-permute-start
  40.3 1.3 fusion.40
  41.6 2.4 %collective-permute-start.3 = (f32[1]{0:T(128)}, f32[1]{0:T(128)}, u32[]{:S(2)}, u32[]{:S(2)}) collective-permute-start(f32[1]{0:T(128)} %bitcast.5), channel_id=1, source_target_pairs={{0,64},{64,0},{1,65},{65,1},{2,66},{66,2},{3,67},{67,3},{4,68},{68... | collective-permute-start | bytes 20 | tf_op jit(solution)/shard_map/ppermute | solution.py:197
  44.1 0.8 collective-permute-done.3
  47.6 1.1 broadcast_select_fusion.3
  49.2 11.5 %all-to-all-done.1.tok_got = bf16[32,128,128]{2,1,0:T(8,128)(2,1)} async-done(((bf16[32,128,128]{2,1,0:T(8,128)(2,1)}), bf16[32,128,128]{2,1,0:T(8,128)(2,1)}, u32[]{:S(2)}, u32[]{:S(2)}) %all-to-all-start.1) | async-done | bytes 1048608 | tf_op jit(solution)/shard_map/all_to_all | solution.py:20
  60.8 2.4 %token_products.1 = (bf16[448,1024]{1,0:T(8,128)(2,1)S(1)}, bf16[512,1024]{1,0:T(8,128)(2,1)S(1)}, bf16[16,1024]{1,0:T(8,128)(2,1)S(1)}) custom-call(bf16[32,128,128]{2,1,0:T(8,128)(2,1)} %all-to-all-done.1.tok_got, bf16[512,1024]{1,0:T(8,128)(2,1)S(1)} %get-tuple-element.26.gate_w, bf16[512,1024]{1,0:T(8,128)(2,1)S(1)} %get-tuple-element.27.up_w), custom_call_target="tpu_custom_call" | custom-call | flops 939524096 | bytes 8388608 | tf_op jit(solution)/shard_map/token_products/pallas_call | solution.py:206
  63.2 1.0 copy-done.1
  64.2 0.9 copy-done.6
  65.1 4.8 %all-to-all-start.2 = ((bf16[4,112,1024]{2,1,0:T(8,128)(2,1)}), bf16[4,112,1024]{2,1,0:T(8,128)(2,1)}, u32[]{:S(2)}, u32[]{:S(2)}) async-start(bf16[4,112,1024]{2,1,0:T(8,128)(2,1)} %bitcast.47), calls=%async_computation.2 | async-start | bytes 1835008 | tf_op jit(solution)/shard_map/all_to_all | solution.py:20
  69.9 1.9 collective-permute-start.4
  71.8 17.3 %all-gather.3.cloned.1.call-done = bf16[4224,128]{1,0:T(8,128)(2,1)} async-done(((bf16[528,128]{1,0:T(8,128)(2,1)}), bf16[4224,128]{1,0:T(8,128)(2,1)}) %all-gather.3.cloned.1.call-update) | async-done | bytes 1081360 | tf_op jit(solution)/shard_map/all_gather | solution.py:193
  89.1 1.2 copy-done.3
  90.3 1.5 cotangent_products.1
  91.9 1.0 copy-done.4
  92.9 0.8 copy-done.7
  93.7 4.8 %all-to-all-start.3 = ((bf16[4,112,640]{2,1,0:T(8,128)(2,1)}), bf16[4,112,640]{2,1,0:T(8,128)(2,1)S(1)}, u32[]{:S(2)}, u32[]{:S(2)}) async-start(bf16[4,112,640]{2,1,0:T(8,128)(2,1)} %bitcast.48), calls=%async_computation.3 | async-start | bytes 1146880 | tf_op jit(solution)/shard_map/all_to_all | solution.py:20
  98.5 1.4 split_sums.2
  99.9 7.4 %collective-permute-start.5 = (bf16[56,1024]{1,0:T(8,128)(2,1)S(1)}, bf16[56,1024]{1,0:T(8,128)(2,1)S(1)}, u32[]{:S(2)}, u32[]{:S(2)}) collective-permute-start(bf16[56,1024]{1,0:T(8,128)(2,1)S(1)} %get-tuple-element.35), channel_id=1, source_target_pairs={{0,4},{4,0},{1,5},{5,1},{2,6},{6,2},{3,7},{7,3},{8,12},{12,8},{9,1... | collective-permute-start | bytes 344072 | tf_op jit(solution)/shard_map/ppermute | solution.py:239
  107.4 5.5 %collective-permute-start.6 = (bf16[56,640]{1,0:T(8,128)(2,1)S(1)}, bf16[56,640]{1,0:T(8,128)(2,1)S(1)}, u32[]{:S(2)}, u32[]{:S(2)}) collective-permute-start(bf16[56,640]{1,0:T(8,128)(2,1)S(1)} %get-tuple-element.38), channel_id=1, source_target_pairs={{0,4},{4,0},{1,5},{5,1},{2,6},{6,2},{3,7},{7,3},{8,12},{12,8},{9,1... | collective-permute-start | bytes 215048 | tf_op jit(solution)/shard_map/ppermute | solution.py:239
  112.9 4.6 %collective-permute-done.6.back_got = bf16[56,640]{1,0:T(8,128)(2,1)S(1)} collective-permute-done((bf16[56,640]{1,0:T(8,128)(2,1)S(1)}, bf16[56,640]{1,0:T(8,128)(2,1)S(1)}, u32[]{:S(2)}, u32[]{:S(2)}) %collective-permute-start.6) | collective-permute-done | bytes 71712 | tf_op jit(solution)/shard_map/ppermute | solution.py:239
  118.0 6.3 %collective-permute-start.7 = (bf16[176,512]{1,0:T(8,128)(2,1)S(1)}, bf16[176,512]{1,0:T(8,128)(2,1)S(1)}, u32[]{:S(2)}, u32[]{:S(2)}) collective-permute-start(bf16[176,512]{1,0:T(8,128)(2,1)S(1)} %hidden_units.1), channel_id=1, source_target_pairs={{0,4},{4,0},{1,5},{5,1},{2,6},{6,2},{3,7},{7,3},{8,12},{12,8},{9,1... | collective-permute-start | bytes 540680 | tf_op jit(solution)/shard_map/ppermute | solution.py:275
  124.3 6.9 %collective-permute-done.7 = bf16[176,512]{1,0:T(8,128)(2,1)S(1)} collective-permute-done((bf16[176,512]{1,0:T(8,128)(2,1)S(1)}, bf16[176,512]{1,0:T(8,128)(2,1)S(1)}, u32[]{:S(2)}, u32[]{:S(2)}) %collective-permute-start.7) | collective-permute-done | bytes 180256 | tf_op jit(solution)/shard_map/ppermute | solution.py:275
  131.3 1.3 broadcast_in_dim.104
  132.6 5.3 %all-to-all-start.4 = ((bf16[4,2,176,512]{3,2,1,0:T(8,128)(2,1)}), bf16[4,2,176,512]{3,2,1,0:T(8,128)(2,1)S(1)}, u32[]{:S(2)}, u32[]{:S(2)}) async-start(bf16[4,2,176,512]{3,2,1,0:T(8,128)(2,1)} %broadcast_in_dim.104), calls=%async_computation.4 | async-start | bytes 2883584 | tf_op jit(solution)/shard_map/all_to_all | solution.py:20
  137.9 0.6 iota_compare_fusion.3
  138.5 0.5 multiply_add_fusion
  139.0 0.6 slice_bitcast_fusion.2
  139.6 0.7 slice.69
  140.3 1.9 collective-permute-start.9
  142.3 2.4 %collective-permute-start.13 = (bf16[512,1024]{1,0:T(8,128)(2,1)}, bf16[512,1024]{1,0:T(8,128)(2,1)}, u32[]{:S(2)}, u32[]{:S(2)}) collective-permute-start(bf16[512,1024]{1,0:T(8,128)(2,1)} %copy-done.4), channel_id=1, source_target_pairs={{0,64},{64,0},{1,65},{65,1},{2,66},{66,2},{3,67},{67,3},{4,68},{68... | collective-permute-start | bytes 3145736 | tf_op jit(solution)/shard_map/ppermute | solution.py:317
  144.7 0.7 slice.82
  145.4 1.3 slice_convert_fusion
  146.7 2.8 %all-to-all-done.4 = bf16[4,2,176,512]{3,2,1,0:T(8,128)(2,1)S(1)} async-done(((bf16[4,2,176,512]{3,2,1,0:T(8,128)(2,1)}), bf16[4,2,176,512]{3,2,1,0:T(8,128)(2,1)S(1)}, u32[]{:S(2)}, u32[]{:S(2)}) %all-to-all-start.4) | async-done | bytes 1441824 | tf_op jit(solution)/shard_map/all_to_all | solution.py:20
  149.5 1.5 token_gradients.1
  151.0 1.0 copy-done
  152.0 1.1 fusion.44
  153.2 0.6 slice_reduce_fusion
  153.8 6.0 %all-to-all-start.5 = ((bf16[32,144,128]{2,1,0:T(8,128)(2,1)}), bf16[32,144,128]{2,1,0:T(8,128)(2,1)S(1)}, u32[]{:S(2)}, u32[]{:S(2)}) async-start(bf16[32,144,128]{2,1,0:T(8,128)(2,1)} %copy-done), calls=%async_computation.5 | async-start | bytes 2359296 | tf_op jit(solution)/shard_map/all_to_all | solution.py:20
  159.9 0.4 fusion.9
  160.3 1.9 collective-permute-start.8
  162.3 2.4 %collective-permute-start.10 = (bf16[8,224]{1,0:T(8,128)(2,1)S(1)}, bf16[8,224]{1,0:T(8,128)(2,1)S(1)}, u32[]{:S(2)}, u32[]{:S(2)}) collective-permute-start(bf16[8,224]{1,0:T(8,128)(2,1)S(1)} %constant_dynamic-slice_fusion.3), channel_id=1, source_target_pairs={{0,64},{64,0},{1,65},{65,1},{2,66},{66,2},{3,67},{67,3},{4,68},{68... | collective-permute-start | bytes 10760 | tf_op jit(solution)/shard_map/ppermute | solution.py:325
  164.8 1.9 collective-permute-start.11
  166.9 0.4 fusion.7
  167.5 2.4 %collective-permute-start.12 = (bf16[224,512]{1,0:T(8,128)(2,1)S(1)}, bf16[224,512]{1,0:T(8,128)(2,1)S(1)}, u32[]{:S(2)}, u32[]{:S(2)}) collective-permute-start(bf16[224,512]{1,0:T(8,128)(2,1)S(1)} %constant_dynamic-slice_fusion.1), channel_id=1, source_target_pairs={{0,64},{64,0},{1,65},{65,1},{2,66},{66,2},{3,67},{67,3},{4,68},{68... | collective-permute-start | bytes 688136 | tf_op jit(solution)/shard_map/ppermute | solution.py:336
  169.9 1.6 fusion.5
  171.6 1.6 fusion.3
  173.2 1.7 fusion.47
  175.0 1.3 fusion.1
  176.5 11.2 %all-to-all-done.5 = bf16[32,144,128]{2,1,0:T(8,128)(2,1)S(1)} async-done(((bf16[32,144,128]{2,1,0:T(8,128)(2,1)}), bf16[32,144,128]{2,1,0:T(8,128)(2,1)S(1)}, u32[]{:S(2)}, u32[]{:S(2)}) %all-to-all-start.5) | async-done | bytes 1179680 | tf_op jit(solution)/shard_map/all_to_all | solution.py:20
  188.5 0.6 broadcast_multiply_fusion
  189.1 0.6 fusion.39
  190.1 0.7 fusion.17
  190.9 1.3 fusion.4
  192.1 1.3 fusion.2
  193.4 1.3 fusion
  (99 shorter events, 3.3 us)
Async XLA Ops:
  20.1 13.9 %copy-start.15 = (bf16[224,1024]{1,0:T(8,128)(2,1)S(1)}, bf16[224,1024]{1,0:T(8,128)(2,1)}, u32[]{:S(2)}) copy-start(bf16[224,1024]{1,0:T(8,128)(2,1)} %param.10) | copy-start | bytes 1376260
  20.1 15.8 %copy-start.16 = (bf16[224,1024]{1,0:T(8,128)(2,1)S(1)}, bf16[224,1024]{1,0:T(8,128)(2,1)}, u32[]{:S(2)}) copy-start(bf16[224,1024]{1,0:T(8,128)(2,1)} %param.9) | copy-start | bytes 1376260
  20.1 18.2 %copy-start.17 = (bf16[224,1024]{1,0:T(8,128)(2,1)S(1)}, bf16[224,1024]{1,0:T(8,128)(2,1)}, u32[]{:S(2)}) copy-start(bf16[224,1024]{1,0:T(8,128)(2,1)} %param.8) | copy-start | bytes 1376260
  20.1 20.2 %copy-start.24 = (bf16[128]{0:T(256)(128)(2,1)S(1)}, bf16[128]{0:T(256)(128)(2,1)}, u32[]{:S(2)}) copy-start(bf16[128]{0:T(256)(128)(2,1)} %param.11) | copy-start | bytes 772
  22.2 38.5 %all-to-all-start.1 = ((bf16[32,128,128]{2,1,0:T(8,128)(2,1)}), bf16[32,128,128]{2,1,0:T(8,128)(2,1)}, u32[]{:S(2)}, u32[]{:S(2)}) async-start(bf16[32,128,128]{2,1,0:T(8,128)(2,1)} %broadcast_in_dim.98), calls=%async_computation.1 | async-start | bytes 2097152 | tf_op jit(solution)/shard_map/all_to_all | solution.py:20
  33.9 55.1 %all-gather.3.cloned.1.call-start = ((), (), s32[]{:S(2)}) async-start(), calls=%async_computation.6 | async-start | bytes 1216512 | tf_op jit(solution)/shard_map/all_gather | solution.py:193
  34.0 13.5 %collective-permute-start.2 = (bf16[224,1024]{1,0:T(8,128)(2,1)S(1)}, bf16[224,1024]{1,0:T(8,128)(2,1)S(1)}, u32[]{:S(2)}, u32[]{:S(2)}) collective-permute-start(bf16[224,1024]{1,0:T(8,128)(2,1)S(1)} %copy-done.15), channel_id=1, source_target_pairs={{0,64},{64,0},{1,65},{65,1},{2,66},{66,2},{3,67},{67,3},{4,68},{68... | collective-permute-start | bytes 1376264 | tf_op jit(solution)/shard_map/ppermute | solution.py:181
  35.9 11.7 %collective-permute-start.1 = (bf16[224,1024]{1,0:T(8,128)(2,1)S(1)}, bf16[224,1024]{1,0:T(8,128)(2,1)}, u32[]{:S(2)}, u32[]{:S(2)}) collective-permute-start(bf16[224,1024]{1,0:T(8,128)(2,1)S(1)} %copy-done.16), channel_id=1, source_target_pairs={{0,64},{64,0},{1,65},{65,1},{2,66},{66,2},{3,67},{67,3},{4,68},{68... | collective-permute-start | bytes 1376264 | tf_op jit(solution)/shard_map/ppermute | solution.py:181
  38.4 10.4 %collective-permute-start = (bf16[224,1024]{1,0:T(8,128)(2,1)S(1)}, bf16[224,1024]{1,0:T(8,128)(2,1)S(1)}, u32[]{:S(2)}, u32[]{:S(2)}) collective-permute-start(bf16[224,1024]{1,0:T(8,128)(2,1)S(1)} %copy-done.17), channel_id=1, source_target_pairs={{0,64},{64,0},{1,65},{65,1},{2,66},{66,2},{3,67},{67,3},{4,68},{68... | collective-permute-start | bytes 1376264 | tf_op jit(solution)/shard_map/ppermute | solution.py:181
  41.6 3.3 %collective-permute-start.3 = (f32[1]{0:T(128)}, f32[1]{0:T(128)}, u32[]{:S(2)}, u32[]{:S(2)}) collective-permute-start(f32[1]{0:T(128)} %bitcast.5), channel_id=1, source_target_pairs={{0,64},{64,0},{1,65},{65,1},{2,66},{66,2},{3,67},{67,3},{4,68},{68... | collective-permute-start | bytes 20 | tf_op jit(solution)/shard_map/ppermute | solution.py:197
  63.2 1.0 copy-start.1
  64.2 0.9 copy-start.6
  65.1 26.8 %copy-start.8 = (bf16[16,1024]{1,0:T(8,128)(2,1)}, bf16[16,1024]{1,0:T(8,128)(2,1)S(1)}, u32[]{:S(2)}) copy-start(bf16[16,1024]{1,0:T(8,128)(2,1)S(1)} %get-tuple-element.30.ends) | copy-start | bytes 98308
  65.1 28.6 %all-to-all-start.2 = ((bf16[4,112,1024]{2,1,0:T(8,128)(2,1)}), bf16[4,112,1024]{2,1,0:T(8,128)(2,1)}, u32[]{:S(2)}, u32[]{:S(2)}) async-start(bf16[4,112,1024]{2,1,0:T(8,128)(2,1)} %bitcast.47), calls=%async_computation.2 | async-start | bytes 1835008 | tf_op jit(solution)/shard_map/all_to_all | solution.py:20
  69.9 19.2 %collective-permute-start.4 = (bf16[16,1024]{1,0:T(8,128)(2,1)S(1)}, bf16[16,1024]{1,0:T(8,128)(2,1)S(1)}, u32[]{:S(2)}, u32[]{:S(2)}) collective-permute-start(bf16[16,1024]{1,0:T(8,128)(2,1)S(1)} %get-tuple-element.30.ends), channel_id=1, source_target_pairs={{0,64},{64,0},{1,65},{65,1},{2,66},{66,2},{3,67},{67,3},{4,68},{68... | collective-permute-start | bytes 98312 | tf_op jit(solution)/shard_map/ppermute | solution.py:221
  89.1 2.8 %copy-start.9 = (bf16[16,1024]{1,0:T(8,128)(2,1)}, bf16[16,1024]{1,0:T(8,128)(2,1)S(1)}, u32[]{:S(2)}) copy-start(bf16[16,1024]{1,0:T(8,128)(2,1)S(1)} %collective-permute-done.4.ends_sib) | copy-start | bytes 98308
  89.1 1.2 copy-start.3
  91.9 1.0 copy-start.4
  92.9 0.8 copy-start.7
  93.7 6.2 %copy-start.10 = (bf16[16,1024]{1,0:T(8,128)(2,1)}, bf16[16,1024]{1,0:T(8,128)(2,1)S(1)}, u32[]{:S(2)}) copy-start(bf16[16,1024]{1,0:T(8,128)(2,1)S(1)} %get-tuple-element.44) | copy-start | bytes 98308
  93.7 13.6 %all-to-all-start.3 = ((bf16[4,112,640]{2,1,0:T(8,128)(2,1)}), bf16[4,112,640]{2,1,0:T(8,128)(2,1)S(1)}, u32[]{:S(2)}, u32[]{:S(2)}) async-start(bf16[4,112,640]{2,1,0:T(8,128)(2,1)} %bitcast.48), calls=%async_computation.3 | async-start | bytes 1146880 | tf_op jit(solution)/shard_map/all_to_all | solution.py:20
  99.9 13.1 %collective-permute-start.5 = (bf16[56,1024]{1,0:T(8,128)(2,1)S(1)}, bf16[56,1024]{1,0:T(8,128)(2,1)S(1)}, u32[]{:S(2)}, u32[]{:S(2)}) collective-permute-start(bf16[56,1024]{1,0:T(8,128)(2,1)S(1)} %get-tuple-element.35), channel_id=1, source_target_pairs={{0,4},{4,0},{1,5},{5,1},{2,6},{6,2},{3,7},{7,3},{8,12},{12,8},{9,1... | collective-permute-start | bytes 344072 | tf_op jit(solution)/shard_map/ppermute | solution.py:239
  107.4 10.1 %collective-permute-start.6 = (bf16[56,640]{1,0:T(8,128)(2,1)S(1)}, bf16[56,640]{1,0:T(8,128)(2,1)S(1)}, u32[]{:S(2)}, u32[]{:S(2)}) collective-permute-start(bf16[56,640]{1,0:T(8,128)(2,1)S(1)} %get-tuple-element.38), channel_id=1, source_target_pairs={{0,4},{4,0},{1,5},{5,1},{2,6},{6,2},{3,7},{7,3},{8,12},{12,8},{9,1... | collective-permute-start | bytes 215048 | tf_op jit(solution)/shard_map/ppermute | solution.py:239
  118.0 13.3 %collective-permute-start.7 = (bf16[176,512]{1,0:T(8,128)(2,1)S(1)}, bf16[176,512]{1,0:T(8,128)(2,1)S(1)}, u32[]{:S(2)}, u32[]{:S(2)}) collective-permute-start(bf16[176,512]{1,0:T(8,128)(2,1)S(1)} %hidden_units.1), channel_id=1, source_target_pairs={{0,4},{4,0},{1,5},{5,1},{2,6},{6,2},{3,7},{7,3},{8,12},{12,8},{9,1... | collective-permute-start | bytes 540680 | tf_op jit(solution)/shard_map/ppermute | solution.py:275
  132.6 6.4 %copy-start.27 = (s32[4,2]{0,1:T(2,128)S(1)}, s32[4,2]{0,1:T(2,128)}, u32[]{:S(2)}) copy-start(s32[4,2]{0,1:T(2,128)} %param.13) | copy-start | bytes 100
  132.6 16.9 %all-to-all-start.4 = ((bf16[4,2,176,512]{3,2,1,0:T(8,128)(2,1)}), bf16[4,2,176,512]{3,2,1,0:T(8,128)(2,1)S(1)}, u32[]{:S(2)}, u32[]{:S(2)}) async-start(bf16[4,2,176,512]{3,2,1,0:T(8,128)(2,1)} %broadcast_in_dim.104), calls=%async_computation.4 | async-start | bytes 2883584 | tf_op jit(solution)/shard_map/all_to_all | solution.py:20
  140.3 29.5 %collective-permute-start.9 = (bf16[512,1024]{1,0:T(8,128)(2,1)}, bf16[512,1024]{1,0:T(8,128)(2,1)}, u32[]{:S(2)}, u32[]{:S(2)}) collective-permute-start(bf16[512,1024]{1,0:T(8,128)(2,1)} %copy-done.1), channel_id=1, source_target_pairs={{0,64},{64,0},{1,65},{65,1},{2,66},{66,2},{3,67},{67,3},{4,68},{68... | collective-permute-start | bytes 3145736 | tf_op jit(solution)/shard_map/ppermute | solution.py:316
  142.3 30.9 %collective-permute-start.13 = (bf16[512,1024]{1,0:T(8,128)(2,1)}, bf16[512,1024]{1,0:T(8,128)(2,1)}, u32[]{:S(2)}, u32[]{:S(2)}) collective-permute-start(bf16[512,1024]{1,0:T(8,128)(2,1)} %copy-done.4), channel_id=1, source_target_pairs={{0,64},{64,0},{1,65},{65,1},{2,66},{66,2},{3,67},{67,3},{4,68},{68... | collective-permute-start | bytes 3145736 | tf_op jit(solution)/shard_map/ppermute | solution.py:317
  151.0 1.0 copy-start
  153.2 6.7 %copy-start.2 = (bf16[512,1024]{1,0:T(8,128)(2,1)S(1)}, bf16[512,1024]{1,0:T(8,128)(2,1)}, u32[]{:S(2)}) copy-start(bf16[512,1024]{1,0:T(8,128)(2,1)} %copy-done.1) | copy-start | bytes 3145732
  153.8 6.1 %copy-start.14 = (bf16[8,56,512]{2,1,0:T(8,128)(2,1)S(1)}, bf16[8,56,512]{2,1,0:T(8,128)(2,1)}, u32[]{:S(2)}) copy-start(bf16[8,56,512]{2,1,0:T(8,128)(2,1)} %get-tuple-element.49) | copy-start | bytes 1376260
  153.8 34.0 %all-to-all-start.5 = ((bf16[32,144,128]{2,1,0:T(8,128)(2,1)}), bf16[32,144,128]{2,1,0:T(8,128)(2,1)S(1)}, u32[]{:S(2)}, u32[]{:S(2)}) async-start(bf16[32,144,128]{2,1,0:T(8,128)(2,1)} %copy-done), calls=%async_computation.5 | async-start | bytes 2359296 | tf_op jit(solution)/shard_map/all_to_all | solution.py:20
  159.8 2.4 %copy-start.19 = (bf16[8,448]{1,0:T(8,128)(2,1)S(1)}, bf16[8,448]{1,0:T(8,128)(2,1)}, u32[]{:S(2)}) copy-start(bf16[8,448]{1,0:T(8,128)(2,1)} %slice_reduce_fusion) | copy-start | bytes 21508
  159.8 4.9 %copy-start.13 = (bf16[8,56,512]{2,1,0:T(8,128)(2,1)S(1)}, bf16[8,56,512]{2,1,0:T(8,128)(2,1)}, u32[]{:S(2)}) copy-start(bf16[8,56,512]{2,1,0:T(8,128)(2,1)} %get-tuple-element.48) | copy-start | bytes 1376260
  159.8 6.9 %copy-start.12 = (bf16[8,56,512]{2,1,0:T(8,128)(2,1)S(1)}, bf16[8,56,512]{2,1,0:T(8,128)(2,1)}, u32[]{:S(2)}) copy-start(bf16[8,56,512]{2,1,0:T(8,128)(2,1)} %get-tuple-element.47) | copy-start | bytes 1376260
  159.8 6.9 %copy-start.23 = (s32[4]{0:T(128)S(1)}, s32[4]{0:T(128)}, u32[]{:S(2)}) copy-start(s32[4]{0:T(128)} %multiply_add_fusion) | copy-start | bytes 52
  160.3 9.6 %collective-permute-start.8 = (bf16[224,512]{1,0:T(8,128)(2,1)S(1)}, bf16[224,512]{1,0:T(8,128)(2,1)S(1)}, u32[]{:S(2)}, u32[]{:S(2)}) collective-permute-start(bf16[224,512]{1,0:T(8,128)(2,1)S(1)} %constant_dynamic-slice_fusion.4), channel_id=1, source_target_pairs={{0,64},{64,0},{1,65},{65,1},{2,66},{66,2},{3,67},{67,3},{4,68},{68... | collective-permute-start | bytes 688136 | tf_op jit(solution)/shard_map/ppermute | solution.py:336
  162.3 5.1 %collective-permute-start.10 = (bf16[8,224]{1,0:T(8,128)(2,1)S(1)}, bf16[8,224]{1,0:T(8,128)(2,1)S(1)}, u32[]{:S(2)}, u32[]{:S(2)}) collective-permute-start(bf16[8,224]{1,0:T(8,128)(2,1)S(1)} %constant_dynamic-slice_fusion.3), channel_id=1, source_target_pairs={{0,64},{64,0},{1,65},{65,1},{2,66},{66,2},{3,67},{67,3},{4,68},{68... | collective-permute-start | bytes 10760 | tf_op jit(solution)/shard_map/ppermute | solution.py:325
  164.8 6.8 %collective-permute-start.11 = (bf16[224,512]{1,0:T(8,128)(2,1)S(1)}, bf16[224,512]{1,0:T(8,128)(2,1)S(1)}, u32[]{:S(2)}, u32[]{:S(2)}) collective-permute-start(bf16[224,512]{1,0:T(8,128)(2,1)S(1)} %constant_dynamic-slice_fusion.2), channel_id=1, source_target_pairs={{0,64},{64,0},{1,65},{65,1},{2,66},{66,2},{3,67},{67,3},{4,68},{68... | collective-permute-start | bytes 688136 | tf_op jit(solution)/shard_map/ppermute | solution.py:336
  167.5 5.8 %collective-permute-start.12 = (bf16[224,512]{1,0:T(8,128)(2,1)S(1)}, bf16[224,512]{1,0:T(8,128)(2,1)S(1)}, u32[]{:S(2)}, u32[]{:S(2)}) collective-permute-start(bf16[224,512]{1,0:T(8,128)(2,1)S(1)} %constant_dynamic-slice_fusion.1), channel_id=1, source_target_pairs={{0,64},{64,0},{1,65},{65,1},{2,66},{66,2},{3,67},{67,3},{4,68},{68... | collective-permute-start | bytes 688136 | tf_op jit(solution)/shard_map/ppermute | solution.py:336
  173.2 1.8 copy-start.5
  176.3 11.9 %copy-start.21 = (s32[4]{0:T(128)S(1)}, s32[4]{0:T(128)}, u32[]{:S(2)}) copy-start(s32[4]{0:T(128)} %get-tuple-element.62) | copy-start | bytes 52
  176.3 11.9 %copy-start.22 = (s32[4]{0:T(128)S(1)}, s32[4]{0:T(128)}, u32[]{:S(2)}) copy-start(s32[4]{0:T(128)} %get-tuple-element.63) | copy-start | bytes 52
  176.3 12.8 %copy-start.25 = (bf16[128]{0:T(256)(128)(2,1)S(1)}, bf16[128]{0:T(256)(128)(2,1)}, u32[]{:S(2)}) copy-start(bf16[128]{0:T(256)(128)(2,1)} %param.11) | copy-start | bytes 772
  176.3 13.7 %copy-start.18 = (f32[128,128]{1,0:T(8,128)S(1)}, f32[128,128]{1,0:T(8,128)}, u32[]{:S(2)}) copy-start(f32[128,128]{1,0:T(8,128)} %param.12) | copy-start | bytes 196612
  176.3 13.7 %copy-start.28 = (pred[128]{0:T(512)(128)(4,1)S(1)}, pred[128]{0:T(512)(128)(4,1)}, u32[]{:S(2)}) copy-start(pred[128]{0:T(512)(128)(4,1)} %iota_compare_fusion.3) | copy-start | bytes 388
  188.2 5.2 %copy-start.26 = (f32[8]{0:T(128)}, f32[8]{0:T(128)S(1)}, u32[]{:S(2)}) copy-start(f32[8]{0:T(128)S(1)} %mul.111) | copy-start | bytes 100
  190.9 2.5 %copy-start.11 = (f32[224,1024]{1,0:T(8,128)S(1)}, f32[224,1024]{1,0:T(8,128)}, u32[]{:S(2)}) copy-start(f32[224,1024]{1,0:T(8,128)} %fusion.1) | copy-start | bytes 2752516
  190.9 2.5 %copy-start.20 = (f32[1,1024]{1,0:T(1,128)S(1)}, f32[1,1024]{1,0:T(1,128)}, u32[]{:S(2)}) copy-start(f32[1,1024]{1,0:T(1,128)} %slice_convert_fusion) | copy-start | bytes 12292
Sparse Core Ops, SparseCore 0:
  47.6 41.4 all-gather.2

commit v11 on v10

--- a/solution.py
+++ b/solution.py
@@ -193,12 +193,7 @@
     low_got = lax.all_gather(low_got, "gy")
     tok_got = to_all(tok_block, PLANE, n_plane)
 
-    own_term = jnp.sum(tokens[rows - 1].astype(f32) * reward_head.astype(f32))
-    sib_term = lax.ppermute(own_term[None], "co", SWAP)[0]
-    spot = jnp.arange(128)[None, :] - 16 - lax.axis_index("yl")
-    first_term, second_term = core_order(own_term, sib_term)
-    tok_terms = jnp.where(spot == 0, first_term, jnp.where(spot == n_yl, second_term, 0.0))
-    gate_w, up_w, down_w, tok_terms = lax.optimization_barrier((gate_w, up_w, down_w, tok_terms))
+    gate_w, up_w, down_w = lax.optimization_barrier((gate_w, up_w, down_w))
 
     own = 2 * units // n_gz
     whole, scalar = pl.BlockSpec(memory_space=pltpu.VMEM), pl.BlockSpec(memory_space=pltpu.SMEM)
@@ -260,6 +255,10 @@
     sums, sums_got = halves(first, False)
     back, back_got = halves(second, True)
 
+    last_rows = jnp.concatenate(core_order(ends[:n_yl], ends_sib[:n_yl]), axis=0).astype(f32)
+    counted = (lax.axis_index("yl") == 0) & (lax.axis_index("gy") == 0)
+    tok_terms = jnp.where(counted, jnp.sum(last_rows * head_vec.astype(f32), axis=1), 0.0)
+    tok_terms = jnp.pad(tok_terms[None, :], ((0, 0), (16, 112 - 2 * n_yl)))
     place = (lax.axis_index(("xx", "yh")) * own).astype(jnp.int32)[None]
     mine = pl.pallas_call(
         functools.partial(hidden_units, 2 * units),

time: 203 us -> 195 us (0.961)
  the two profiles are of different devices: /device:TPU:2 before, /device:TPU:4 now
where the time goes in v11:
time: 195 us; the launch traced here: 194 us
  starting transfers between devices  70.1 us (36%)
  waiting for transfers between devices  59.6 us (31%)
  between operations  14.6 us (7%)
  local copies, waits for them, and re-layouts  13.7 us (7%)
  matrix products  11.3 us (6%)
  blocking collectives  10.7 us (5%)
  Pallas kernels  7.42 us (4%)
  other arithmetic  6.8 us (3%)
    all_to_all x5, waiting for transfers between devices, exchange(): return lax.all_to_all(pieces, axes, 0, 0)  34.2 us
    all_to_all x5, starting transfers between devices, exchange(): return lax.all_to_all(pieces, axes, 0, 0)  34 us
    dot_general x11, matrix products, dot(): lax.dot_general(left, right, (((left_dim,), (right_dim,)), ((), ())), pre...  11.3 us
    all_gather x1, waiting for transfers between devices, body(): low_got = lax.all_gather(low_got, 'gy')  11.2 us
    all_to_all x1, blocking collectives, exchange(): return lax.all_to_all(pieces, axes, 0, 0)  10.7 us
    ppermute x2, starting transfers between devices, halves(): return (keep, lax.ppermute(give, 'yh', SWAP))  9.74 us
    ppermute x2, waiting for transfers between devices, halves(): return (keep, lax.ppermute(give, 'yh', SWAP))  6.53 us
    unnamed x50, local copies, waits for them, and re-layouts  6.48 us
  transfers between devices with their start and end apart: 19, of which 8 were waited for; matrix products, arithmetic and copies ran while one was open for 7% of the time, Pallas kernels for 4%

profile of v11, /device:TPU:4, one launch (start us, length us, event | category | flops | bytes accessed | tf_op | source)
XLA Modules:
  0.0 194.3 jit_solution(16433494108167351093)
XLA Ops:
  7.2 0.8 convert_element_type.36
  8.0 10.7 %all_to_all.30 = bf16[4,128,128]{2,1,0:T(8,128)(2,1)S(1)} all-to-all(bf16[4,128,128]{2,1,0:T(8,128)(2,1)S(1)} %broadcast_in_dim.83), channel_id=1, replica_groups=mesh['yl'=4,'co'=2,'gy'=8,'yh'=2,'xx'=4] {'yl'}, dimensions={0} | all-to-all | bytes 262144 | tf_op jit(solution)/shard_map/all_to_all | solution.py:20
  18.8 0.7 broadcast_in_dim.84
  19.4 0.7 pad_maximum_fusion.2
  20.1 2.1 %broadcast_in_dim.85 = bf16[32,128,128]{2,1,0:T(8,128)(2,1)} broadcast(bf16[128,128]{1,0:T(8,128)(2,1)} %param.7), dimensions={1,2} | broadcast | bytes 1081344 | tf_op jit(solution)/shard_map/broadcast_in_dim | solution.py:24
  22.2 11.7 %all-to-all-start.1 = ((bf16[32,128,128]{2,1,0:T(8,128)(2,1)}), bf16[32,128,128]{2,1,0:T(8,128)(2,1)}, u32[]{:S(2)}, u32[]{:S(2)}) async-start(bf16[32,128,128]{2,1,0:T(8,128)(2,1)} %broadcast_in_dim.85), calls=%async_computation.1 | async-start | bytes 2097152 | tf_op jit(solution)/shard_map/all_to_all | solution.py:20
  34.0 1.9 collective-permute-start.2
  35.9 2.4 %collective-permute-start.1 = (bf16[224,1024]{1,0:T(8,128)(2,1)S(1)}, bf16[224,1024]{1,0:T(8,128)(2,1)S(1)}, u32[]{:S(2)}, u32[]{:S(2)}) collective-permute-start(bf16[224,1024]{1,0:T(8,128)(2,1)S(1)} %copy-done.13), channel_id=1, source_target_pairs={{0,64},{64,0},{1,65},{65,1},{2,66},{66,2},{3,67},{67,3},{4,68},{68... | collective-permute-start | bytes 1376264 | tf_op jit(solution)/shard_map/ppermute | solution.py:181
  38.3 1.9 collective-permute-start
  40.6 1.4 collective-permute-done
  42.1 0.4 maximum_maximum_fusion.1
  42.5 18.3 %all-to-all-done.1.tok_got = bf16[32,128,128]{2,1,0:T(8,128)(2,1)} async-done(((bf16[32,128,128]{2,1,0:T(8,128)(2,1)}), bf16[32,128,128]{2,1,0:T(8,128)(2,1)}, u32[]{:S(2)}, u32[]{:S(2)}) %all-to-all-start.1) | async-done | bytes 1048608 | tf_op jit(solution)/shard_map/all_to_all | solution.py:20
  60.8 2.4 %token_products.1 = (bf16[448,1024]{1,0:T(8,128)(2,1)S(1)}, bf16[512,1024]{1,0:T(8,128)(2,1)S(1)}, bf16[16,1024]{1,0:T(8,128)(2,1)S(1)}) custom-call(bf16[32,128,128]{2,1,0:T(8,128)(2,1)} %all-to-all-done.1.tok_got, bf16[512,1024]{1,0:T(8,128)(2,1)S(1)} %get-tuple-element.25.gate_w, bf16[512,1024]{1,0:T(8,128)(2,1)S(1)} %get-tuple-element.26.up_w), custom_call_target="tpu_custom_call" | custom-call | flops 939524096 | bytes 8388608 | tf_op jit(solution)/shard_map/token_products/pallas_call | solution.py:201
  63.3 1.0 copy-done.1
  64.3 0.9 copy-done.6
  65.2 4.8 %all-to-all-start.2 = ((bf16[4,112,1024]{2,1,0:T(8,128)(2,1)}), bf16[4,112,1024]{2,1,0:T(8,128)(2,1)}, u32[]{:S(2)}, u32[]{:S(2)}) async-start(bf16[4,112,1024]{2,1,0:T(8,128)(2,1)} %bitcast.44), calls=%async_computation.2 | async-start | bytes 1835008 | tf_op jit(solution)/shard_map/all_to_all | solution.py:20
  70.0 1.9 collective-permute-start.3
  71.9 11.2 %all-gather.3.cloned.1.call-done = bf16[4224,128]{1,0:T(8,128)(2,1)} async-done(((bf16[528,128]{1,0:T(8,128)(2,1)}), bf16[4224,128]{1,0:T(8,128)(2,1)}) %all-gather.3.cloned.1.call-update) | async-done | bytes 1081360 | tf_op jit(solution)/shard_map/all_gather | solution.py:193
  83.1 1.2 copy-done.3
  84.4 1.5 cotangent_products.1
  85.9 1.0 copy-done.4
  86.9 0.8 copy-done.7
  87.7 4.8 %all-to-all-start.3 = ((bf16[4,112,640]{2,1,0:T(8,128)(2,1)}), bf16[4,112,640]{2,1,0:T(8,128)(2,1)S(1)}, u32[]{:S(2)}, u32[]{:S(2)}) async-start(bf16[4,112,640]{2,1,0:T(8,128)(2,1)} %bitcast.45), calls=%async_computation.3 | async-start | bytes 1146880 | tf_op jit(solution)/shard_map/all_to_all | solution.py:20
  92.6 0.4 copy-done.16
  93.1 1.4 split_sums.2
  94.4 6.2 %collective-permute-start.4 = (bf16[56,1024]{1,0:T(8,128)(2,1)S(1)}, bf16[56,1024]{1,0:T(8,128)(2,1)S(1)}, u32[]{:S(2)}, u32[]{:S(2)}) collective-permute-start(bf16[56,1024]{1,0:T(8,128)(2,1)S(1)} %get-tuple-element.34), channel_id=1, source_target_pairs={{0,4},{4,0},{1,5},{5,1},{2,6},{6,2},{3,7},{7,3},{8,12},{12,8},{9,1... | collective-permute-start | bytes 344072 | tf_op jit(solution)/shard_map/ppermute | solution.py:234
  100.9 3.5 %collective-permute-start.5 = (bf16[56,640]{1,0:T(8,128)(2,1)S(1)}, bf16[56,640]{1,0:T(8,128)(2,1)S(1)}, u32[]{:S(2)}, u32[]{:S(2)}) collective-permute-start(bf16[56,640]{1,0:T(8,128)(2,1)S(1)} %get-tuple-element.37), channel_id=1, source_target_pairs={{0,4},{4,0},{1,5},{5,1},{2,6},{6,2},{3,7},{7,3},{8,12},{12,8},{9,1... | collective-permute-start | bytes 215048 | tf_op jit(solution)/shard_map/ppermute | solution.py:234
  104.5 3.3 %collective-permute-done.4.got = bf16[56,1024]{1,0:T(8,128)(2,1)S(1)} collective-permute-done((bf16[56,1024]{1,0:T(8,128)(2,1)S(1)}, bf16[56,1024]{1,0:T(8,128)(2,1)S(1)}, u32[]{:S(2)}, u32[]{:S(2)}) %collective-permute-start.4) | collective-permute-done | bytes 114720 | tf_op jit(solution)/shard_map/ppermute | solution.py:234
  107.8 3.2 %collective-permute-done.5.back_got = bf16[56,640]{1,0:T(8,128)(2,1)S(1)} collective-permute-done((bf16[56,640]{1,0:T(8,128)(2,1)S(1)}, bf16[56,640]{1,0:T(8,128)(2,1)S(1)}, u32[]{:S(2)}, u32[]{:S(2)}) %collective-permute-start.5) | collective-permute-done | bytes 71712 | tf_op jit(solution)/shard_map/ppermute | solution.py:234
  111.0 0.4 hidden_units.1
  111.4 5.2 %collective-permute-start.6 = (bf16[176,512]{1,0:T(8,128)(2,1)S(1)}, bf16[176,512]{1,0:T(8,128)(2,1)S(1)}, u32[]{:S(2)}, u32[]{:S(2)}) collective-permute-start(bf16[176,512]{1,0:T(8,128)(2,1)S(1)} %hidden_units.1), channel_id=1, source_target_pairs={{0,4},{4,0},{1,5},{5,1},{2,6},{6,2},{3,7},{7,3},{8,12},{12,8},{9,1... | collective-permute-start | bytes 540680 | tf_op jit(solution)/shard_map/ppermute | solution.py:274
  116.6 6.2 %collective-permute-done.6 = bf16[176,512]{1,0:T(8,128)(2,1)S(1)} collective-permute-done((bf16[176,512]{1,0:T(8,128)(2,1)S(1)}, bf16[176,512]{1,0:T(8,128)(2,1)S(1)}, u32[]{:S(2)}, u32[]{:S(2)}) %collective-permute-start.6) | collective-permute-done | bytes 180256 | tf_op jit(solution)/shard_map/ppermute | solution.py:274
  122.9 1.3 broadcast_in_dim.88
  124.2 5.1 %all-to-all-start.4 = ((bf16[4,2,176,512]{3,2,1,0:T(8,128)(2,1)}), bf16[4,2,176,512]{3,2,1,0:T(8,128)(2,1)S(1)}, u32[]{:S(2)}, u32[]{:S(2)}) async-start(bf16[4,2,176,512]{3,2,1,0:T(8,128)(2,1)} %broadcast_in_dim.88), calls=%async_computation.4 | async-start | bytes 2883584 | tf_op jit(solution)/shard_map/all_to_all | solution.py:20
  129.3 0.6 iota_compare_fusion.3
  129.8 0.5 multiply_add_fusion
  130.3 1.3 slice_bitcast_fusion.2
  131.6 1.9 collective-permute-start.8
  133.6 2.4 %collective-permute-start.12 = (bf16[512,1024]{1,0:T(8,128)(2,1)}, bf16[512,1024]{1,0:T(8,128)(2,1)}, u32[]{:S(2)}, u32[]{:S(2)}) collective-permute-start(bf16[512,1024]{1,0:T(8,128)(2,1)} %copy-done.4), channel_id=1, source_target_pairs={{0,64},{64,0},{1,65},{65,1},{2,66},{66,2},{3,67},{67,3},{4,68},{68... | collective-permute-start | bytes 3145736 | tf_op jit(solution)/shard_map/ppermute | solution.py:316
  136.0 4.8 %all-to-all-done.4 = bf16[4,2,176,512]{3,2,1,0:T(8,128)(2,1)S(1)} async-done(((bf16[4,2,176,512]{3,2,1,0:T(8,128)(2,1)}), bf16[4,2,176,512]{3,2,1,0:T(8,128)(2,1)S(1)}, u32[]{:S(2)}, u32[]{:S(2)}) %all-to-all-start.4) | async-done | bytes 1441824 | tf_op jit(solution)/shard_map/all_to_all | solution.py:20
  140.7 1.5 token_gradients.1
  142.3 1.0 copy-done
  143.3 1.1 fusion.44
  144.4 0.6 slice_reduce_fusion
  145.0 7.6 %all-to-all-start.5 = ((bf16[32,144,128]{2,1,0:T(8,128)(2,1)}), bf16[32,144,128]{2,1,0:T(8,128)(2,1)S(1)}, u32[]{:S(2)}, u32[]{:S(2)}) async-start(bf16[32,144,128]{2,1,0:T(8,128)(2,1)} %copy-done), calls=%async_computation.5 | async-start | bytes 2359296 | tf_op jit(solution)/shard_map/all_to_all | solution.py:20
  152.8 0.4 fusion.9
  153.2 1.9 collective-permute-start.7
  155.2 2.4 %collective-permute-start.9 = (bf16[8,224]{1,0:T(8,128)(2,1)S(1)}, bf16[8,224]{1,0:T(8,128)(2,1)S(1)}, u32[]{:S(2)}, u32[]{:S(2)}) collective-permute-start(bf16[8,224]{1,0:T(8,128)(2,1)S(1)} %constant_dynamic-slice_fusion.3), channel_id=1, source_target_pairs={{0,64},{64,0},{1,65},{65,1},{2,66},{66,2},{3,67},{67,3},{4,68},{68... | collective-permute-start | bytes 10760 | tf_op jit(solution)/shard_map/ppermute | solution.py:324
  157.7 1.9 collective-permute-start.10
  159.8 0.4 fusion.7
  160.4 2.4 %collective-permute-start.11 = (bf16[224,512]{1,0:T(8,128)(2,1)S(1)}, bf16[224,512]{1,0:T(8,128)(2,1)S(1)}, u32[]{:S(2)}, u32[]{:S(2)}) collective-permute-start(bf16[224,512]{1,0:T(8,128)(2,1)S(1)} %constant_dynamic-slice_fusion.1), channel_id=1, source_target_pairs={{0,64},{64,0},{1,65},{65,1},{2,66},{66,2},{3,67},{67,3},{4,68},{68... | collective-permute-start | bytes 688136 | tf_op jit(solution)/shard_map/ppermute | solution.py:335
  162.8 1.6 fusion.5
  164.4 1.6 fusion.3
  166.1 1.7 fusion.47
  167.8 1.3 fusion.1
  169.4 11.1 %all-to-all-done.5 = bf16[32,144,128]{2,1,0:T(8,128)(2,1)S(1)} async-done(((bf16[32,144,128]{2,1,0:T(8,128)(2,1)}), bf16[32,144,128]{2,1,0:T(8,128)(2,1)S(1)}, u32[]{:S(2)}, u32[]{:S(2)}) %all-to-all-start.5) | async-done | bytes 1179680 | tf_op jit(solution)/shard_map/all_to_all | solution.py:20
  181.0 0.2 fusion.32
  181.3 0.6 broadcast_multiply_fusion
  181.9 0.6 fusion.40
  182.6 0.2 select_reduce_fusion.1
  182.8 0.7 fusion.17
  183.6 1.3 fusion.4
  184.9 1.3 fusion.2
  186.2 1.3 fusion
  (89 shorter events, 2.4 us)
Async XLA Ops:
  20.1 13.9 %copy-start.12 = (bf16[224,1024]{1,0:T(8,128)(2,1)S(1)}, bf16[224,1024]{1,0:T(8,128)(2,1)}, u32[]{:S(2)}) copy-start(bf16[224,1024]{1,0:T(8,128)(2,1)} %param.10) | copy-start | bytes 1376260
  20.1 15.8 %copy-start.13 = (bf16[224,1024]{1,0:T(8,128)(2,1)S(1)}, bf16[224,1024]{1,0:T(8,128)(2,1)}, u32[]{:S(2)}) copy-start(bf16[224,1024]{1,0:T(8,128)(2,1)} %param.9) | copy-start | bytes 1376260
  20.1 18.2 %copy-start.14 = (bf16[224,1024]{1,0:T(8,128)(2,1)S(1)}, bf16[224,1024]{1,0:T(8,128)(2,1)}, u32[]{:S(2)}) copy-start(bf16[224,1024]{1,0:T(8,128)(2,1)} %param.8) | copy-start | bytes 1376260
  22.2 38.6 %all-to-all-start.1 = ((bf16[32,128,128]{2,1,0:T(8,128)(2,1)}), bf16[32,128,128]{2,1,0:T(8,128)(2,1)}, u32[]{:S(2)}, u32[]{:S(2)}) async-start(bf16[32,128,128]{2,1,0:T(8,128)(2,1)} %broadcast_in_dim.85), calls=%async_computation.1 | async-start | bytes 2097152 | tf_op jit(solution)/shard_map/all_to_all | solution.py:20
  33.9 49.2 %all-gather.3.cloned.1.call-start = ((), (), s32[]{:S(2)}) async-start(), calls=%async_computation.6 | async-start | bytes 1216512 | tf_op jit(solution)/shard_map/all_gather | solution.py:193
  34.0 6.4 %collective-permute-start.2 = (bf16[224,1024]{1,0:T(8,128)(2,1)S(1)}, bf16[224,1024]{1,0:T(8,128)(2,1)S(1)}, u32[]{:S(2)}, u32[]{:S(2)}) collective-permute-start(bf16[224,1024]{1,0:T(8,128)(2,1)S(1)} %copy-done.12), channel_id=1, source_target_pairs={{0,64},{64,0},{1,65},{65,1},{2,66},{66,2},{3,67},{67,3},{4,68},{68... | collective-permute-start | bytes 1376264 | tf_op jit(solution)/shard_map/ppermute | solution.py:181
  35.9 4.6 %collective-permute-start.1 = (bf16[224,1024]{1,0:T(8,128)(2,1)S(1)}, bf16[224,1024]{1,0:T(8,128)(2,1)S(1)}, u32[]{:S(2)}, u32[]{:S(2)}) collective-permute-start(bf16[224,1024]{1,0:T(8,128)(2,1)S(1)} %copy-done.13), channel_id=1, source_target_pairs={{0,64},{64,0},{1,65},{65,1},{2,66},{66,2},{3,67},{67,3},{4,68},{68... | collective-permute-start | bytes 1376264 | tf_op jit(solution)/shard_map/ppermute | solution.py:181
  38.3 3.7 %collective-permute-start = (bf16[224,1024]{1,0:T(8,128)(2,1)S(1)}, bf16[224,1024]{1,0:T(8,128)(2,1)S(1)}, u32[]{:S(2)}, u32[]{:S(2)}) collective-permute-start(bf16[224,1024]{1,0:T(8,128)(2,1)S(1)} %copy-done.14), channel_id=1, source_target_pairs={{0,64},{64,0},{1,65},{65,1},{2,66},{66,2},{3,67},{67,3},{4,68},{68... | collective-permute-start | bytes 1376264 | tf_op jit(solution)/shard_map/ppermute | solution.py:181
  63.3 1.0 copy-start.1
  64.3 0.9 copy-start.6
  65.2 22.5 %all-to-all-start.2 = ((bf16[4,112,1024]{2,1,0:T(8,128)(2,1)}), bf16[4,112,1024]{2,1,0:T(8,128)(2,1)}, u32[]{:S(2)}, u32[]{:S(2)}) async-start(bf16[4,112,1024]{2,1,0:T(8,128)(2,1)} %bitcast.44), calls=%async_computation.2 | async-start | bytes 1835008 | tf_op jit(solution)/shard_map/all_to_all | solution.py:20
  70.0 13.2 %collective-permute-start.3 = (bf16[16,1024]{1,0:T(8,128)(2,1)S(1)}, bf16[16,1024]{1,0:T(8,128)(2,1)S(1)}, u32[]{:S(2)}, u32[]{:S(2)}) collective-permute-start(bf16[16,1024]{1,0:T(8,128)(2,1)S(1)} %get-tuple-element.29.ends), channel_id=1, source_target_pairs={{0,64},{64,0},{1,65},{65,1},{2,66},{66,2},{3,67},{67,3},{4,68},{68... | collective-permute-start | bytes 98312 | tf_op jit(solution)/shard_map/ppermute | solution.py:216
  83.1 1.2 copy-start.3
  85.9 1.0 copy-start.4
  86.9 0.8 copy-start.7
  87.7 13.0 %all-to-all-start.3 = ((bf16[4,112,640]{2,1,0:T(8,128)(2,1)}), bf16[4,112,640]{2,1,0:T(8,128)(2,1)S(1)}, u32[]{:S(2)}, u32[]{:S(2)}) async-start(bf16[4,112,640]{2,1,0:T(8,128)(2,1)} %bitcast.45), calls=%async_computation.3 | async-start | bytes 1146880 | tf_op jit(solution)/shard_map/all_to_all | solution.py:20
  92.5 0.6 copy-start.16
  94.4 13.3 %collective-permute-start.4 = (bf16[56,1024]{1,0:T(8,128)(2,1)S(1)}, bf16[56,1024]{1,0:T(8,128)(2,1)S(1)}, u32[]{:S(2)}, u32[]{:S(2)}) collective-permute-start(bf16[56,1024]{1,0:T(8,128)(2,1)S(1)} %get-tuple-element.34), channel_id=1, source_target_pairs={{0,4},{4,0},{1,5},{5,1},{2,6},{6,2},{3,7},{7,3},{8,12},{12,8},{9,1... | collective-permute-start | bytes 344072 | tf_op jit(solution)/shard_map/ppermute | solution.py:234
  100.9 10.1 %collective-permute-start.5 = (bf16[56,640]{1,0:T(8,128)(2,1)S(1)}, bf16[56,640]{1,0:T(8,128)(2,1)S(1)}, u32[]{:S(2)}, u32[]{:S(2)}) collective-permute-start(bf16[56,640]{1,0:T(8,128)(2,1)S(1)} %get-tuple-element.37), channel_id=1, source_target_pairs={{0,4},{4,0},{1,5},{5,1},{2,6},{6,2},{3,7},{7,3},{8,12},{12,8},{9,1... | collective-permute-start | bytes 215048 | tf_op jit(solution)/shard_map/ppermute | solution.py:234
  111.4 11.4 %collective-permute-start.6 = (bf16[176,512]{1,0:T(8,128)(2,1)S(1)}, bf16[176,512]{1,0:T(8,128)(2,1)S(1)}, u32[]{:S(2)}, u32[]{:S(2)}) collective-permute-start(bf16[176,512]{1,0:T(8,128)(2,1)S(1)} %hidden_units.1), channel_id=1, source_target_pairs={{0,4},{4,0},{1,5},{5,1},{2,6},{6,2},{3,7},{7,3},{8,12},{12,8},{9,1... | collective-permute-start | bytes 540680 | tf_op jit(solution)/shard_map/ppermute | solution.py:274
  124.2 16.6 %all-to-all-start.4 = ((bf16[4,2,176,512]{3,2,1,0:T(8,128)(2,1)}), bf16[4,2,176,512]{3,2,1,0:T(8,128)(2,1)S(1)}, u32[]{:S(2)}, u32[]{:S(2)}) async-start(bf16[4,2,176,512]{3,2,1,0:T(8,128)(2,1)} %broadcast_in_dim.88), calls=%async_computation.4 | async-start | bytes 2883584 | tf_op jit(solution)/shard_map/all_to_all | solution.py:20
  131.6 31.1 %collective-permute-start.8 = (bf16[512,1024]{1,0:T(8,128)(2,1)}, bf16[512,1024]{1,0:T(8,128)(2,1)}, u32[]{:S(2)}, u32[]{:S(2)}) collective-permute-start(bf16[512,1024]{1,0:T(8,128)(2,1)} %copy-done.1), channel_id=1, source_target_pairs={{0,64},{64,0},{1,65},{65,1},{2,66},{66,2},{3,67},{67,3},{4,68},{68... | collective-permute-start | bytes 3145736 | tf_op jit(solution)/shard_map/ppermute | solution.py:315
  133.6 32.5 %collective-permute-start.12 = (bf16[512,1024]{1,0:T(8,128)(2,1)}, bf16[512,1024]{1,0:T(8,128)(2,1)}, u32[]{:S(2)}, u32[]{:S(2)}) collective-permute-start(bf16[512,1024]{1,0:T(8,128)(2,1)} %copy-done.4), channel_id=1, source_target_pairs={{0,64},{64,0},{1,65},{65,1},{2,66},{66,2},{3,67},{67,3},{4,68},{68... | collective-permute-start | bytes 3145736 | tf_op jit(solution)/shard_map/ppermute | solution.py:316
  142.3 1.0 copy-start
  144.4 8.3 %copy-start.2 = (bf16[512,1024]{1,0:T(8,128)(2,1)S(1)}, bf16[512,1024]{1,0:T(8,128)(2,1)}, u32[]{:S(2)}) copy-start(bf16[512,1024]{1,0:T(8,128)(2,1)} %copy-done.1) | copy-start | bytes 3145732
  145.0 7.7 %copy-start.11 = (bf16[8,56,512]{2,1,0:T(8,128)(2,1)S(1)}, bf16[8,56,512]{2,1,0:T(8,128)(2,1)}, u32[]{:S(2)}) copy-start(bf16[8,56,512]{2,1,0:T(8,128)(2,1)} %get-tuple-element.47) | copy-start | bytes 1376260
  145.0 35.5 %all-to-all-start.5 = ((bf16[32,144,128]{2,1,0:T(8,128)(2,1)}), bf16[32,144,128]{2,1,0:T(8,128)(2,1)S(1)}, u32[]{:S(2)}, u32[]{:S(2)}) async-start(bf16[32,144,128]{2,1,0:T(8,128)(2,1)} %copy-done), calls=%async_computation.5 | async-start | bytes 2359296 | tf_op jit(solution)/shard_map/all_to_all | solution.py:20
  152.7 2.4 %copy-start.18 = (bf16[8,448]{1,0:T(8,128)(2,1)S(1)}, bf16[8,448]{1,0:T(8,128)(2,1)}, u32[]{:S(2)}) copy-start(bf16[8,448]{1,0:T(8,128)(2,1)} %slice_reduce_fusion) | copy-start | bytes 21508
  152.7 4.9 %copy-start.10 = (bf16[8,56,512]{2,1,0:T(8,128)(2,1)S(1)}, bf16[8,56,512]{2,1,0:T(8,128)(2,1)}, u32[]{:S(2)}) copy-start(bf16[8,56,512]{2,1,0:T(8,128)(2,1)} %get-tuple-element.46) | copy-start | bytes 1376260
  152.7 6.9 %copy-start.9 = (bf16[8,56,512]{2,1,0:T(8,128)(2,1)S(1)}, bf16[8,56,512]{2,1,0:T(8,128)(2,1)}, u32[]{:S(2)}) copy-start(bf16[8,56,512]{2,1,0:T(8,128)(2,1)} %get-tuple-element.45) | copy-start | bytes 1376260
  152.7 6.9 %copy-start.21 = (s32[4]{0:T(128)S(1)}, s32[4]{0:T(128)}, u32[]{:S(2)}) copy-start(s32[4]{0:T(128)} %multiply_add_fusion) | copy-start | bytes 52
  153.2 9.6 %collective-permute-start.7 = (bf16[224,512]{1,0:T(8,128)(2,1)S(1)}, bf16[224,512]{1,0:T(8,128)(2,1)S(1)}, u32[]{:S(2)}, u32[]{:S(2)}) collective-permute-start(bf16[224,512]{1,0:T(8,128)(2,1)S(1)} %constant_dynamic-slice_fusion.4), channel_id=1, source_target_pairs={{0,64},{64,0},{1,65},{65,1},{2,66},{66,2},{3,67},{67,3},{4,68},{68... | collective-permute-start | bytes 688136 | tf_op jit(solution)/shard_map/ppermute | solution.py:335
  155.2 5.1 %collective-permute-start.9 = (bf16[8,224]{1,0:T(8,128)(2,1)S(1)}, bf16[8,224]{1,0:T(8,128)(2,1)S(1)}, u32[]{:S(2)}, u32[]{:S(2)}) collective-permute-start(bf16[8,224]{1,0:T(8,128)(2,1)S(1)} %constant_dynamic-slice_fusion.3), channel_id=1, source_target_pairs={{0,64},{64,0},{1,65},{65,1},{2,66},{66,2},{3,67},{67,3},{4,68},{68... | collective-permute-start | bytes 10760 | tf_op jit(solution)/shard_map/ppermute | solution.py:324
  157.7 6.8 %collective-permute-start.10 = (bf16[224,512]{1,0:T(8,128)(2,1)S(1)}, bf16[224,512]{1,0:T(8,128)(2,1)S(1)}, u32[]{:S(2)}, u32[]{:S(2)}) collective-permute-start(bf16[224,512]{1,0:T(8,128)(2,1)S(1)} %constant_dynamic-slice_fusion.2), channel_id=1, source_target_pairs={{0,64},{64,0},{1,65},{65,1},{2,66},{66,2},{3,67},{67,3},{4,68},{68... | collective-permute-start | bytes 688136 | tf_op jit(solution)/shard_map/ppermute | solution.py:335
  160.4 5.7 %collective-permute-start.11 = (bf16[224,512]{1,0:T(8,128)(2,1)S(1)}, bf16[224,512]{1,0:T(8,128)(2,1)S(1)}, u32[]{:S(2)}, u32[]{:S(2)}) collective-permute-start(bf16[224,512]{1,0:T(8,128)(2,1)S(1)} %constant_dynamic-slice_fusion.1), channel_id=1, source_target_pairs={{0,64},{64,0},{1,65},{65,1},{2,66},{66,2},{3,67},{67,3},{4,68},{68... | collective-permute-start | bytes 688136 | tf_op jit(solution)/shard_map/ppermute | solution.py:335
  166.1 1.8 copy-start.5
  169.2 11.8 %copy-start.19 = (s32[4]{0:T(128)S(1)}, s32[4]{0:T(128)}, u32[]{:S(2)}) copy-start(s32[4]{0:T(128)} %get-tuple-element.64) | copy-start | bytes 52
  169.2 11.8 %copy-start.20 = (s32[4]{0:T(128)S(1)}, s32[4]{0:T(128)}, u32[]{:S(2)}) copy-start(s32[4]{0:T(128)} %get-tuple-element.65) | copy-start | bytes 52
  169.2 12.7 %copy-start.22 = (bf16[128]{0:T(256)(128)(2,1)S(1)}, bf16[128]{0:T(256)(128)(2,1)}, u32[]{:S(2)}) copy-start(bf16[128]{0:T(256)(128)(2,1)} %param.11) | copy-start | bytes 772
  169.2 13.6 %copy-start.15 = (f32[128,128]{1,0:T(8,128)S(1)}, f32[128,128]{1,0:T(8,128)}, u32[]{:S(2)}) copy-start(f32[128,128]{1,0:T(8,128)} %param.12) | copy-start | bytes 196612
  169.2 13.6 %copy-start.24 = (pred[128]{0:T(512)(128)(4,1)S(1)}, pred[128]{0:T(512)(128)(4,1)}, u32[]{:S(2)}) copy-start(pred[128]{0:T(512)(128)(4,1)} %iota_compare_fusion.3) | copy-start | bytes 388
  181.0 5.2 %copy-start.23 = (f32[8]{0:T(128)}, f32[8]{0:T(128)S(1)}, u32[]{:S(2)}) copy-start(f32[8]{0:T(128)S(1)} %mul.117) | copy-start | bytes 100
  183.6 2.5 %copy-start.8 = (f32[224,1024]{1,0:T(8,128)S(1)}, f32[224,1024]{1,0:T(8,128)}, u32[]{:S(2)}) copy-start(f32[224,1024]{1,0:T(8,128)} %fusion.1) | copy-start | bytes 2752516
  183.6 2.5 %copy-start.17 = (f32[1,1024]{1,0:T(1,128)S(1)}, f32[1,1024]{1,0:T(1,128)}, u32[]{:S(2)}) copy-start(f32[1,1024]{1,0:T(1,128)} %copy-done.16) | copy-start | bytes 12292
Sparse Core Ops, SparseCore 0:
  40.5 42.5 all-gather.2

commit v12 on v11

--- a/solution.py
+++ b/solution.py
@@ -189,9 +189,10 @@
     low_got = to_all(lm_grad.astype(bf16), "yl", n_yl).reshape(half, cols)
     head_rows = jnp.broadcast_to(reward_head[None, :], (16, cols))
     low_got = jnp.concatenate([low_got, head_rows], axis=0)
-    low_got, tok_block = lax.optimization_barrier((low_got, tokens))
+    tok_sent = jnp.broadcast_to(tokens[None], (n_plane, rows, cols))
+    low_got, tok_sent = lax.optimization_barrier((low_got, tok_sent))
     low_got = lax.all_gather(low_got, "gy")
-    tok_got = to_all(tok_block, PLANE, n_plane)
+    tok_got = exchange(tok_sent, PLANE)
 
     gate_w, up_w, down_w = lax.optimization_barrier((gate_w, up_w, down_w))
 

time: 195 us -> 195 us (level)
    broadcast_in_dim x0 -> x1, local copies, waits for them, and re-layouts: none -> 2.08 us  [body(): tok_sent = jnp.broadcast_to(tokens[None], (n_plane, rows, cols))]
    broadcast_in_dim x3 -> x2, local copies, waits for them, and re-layouts: 3.37 us -> 1.29 us  [to_all(): return exchange(jnp.broadcast_to(value[None], (count,) + value.shape), axes)]
where the time goes in v12:
time: 195 us; the launch traced here: 194 us
  starting transfers between devices  70.1 us (36%)
  waiting for transfers between devices  59.6 us (31%)
  between operations  14.6 us (7%)
  local copies, waits for them, and re-layouts  13.7 us (7%)
  matrix products  11.3 us (6%)
  blocking collectives  10.7 us (5%)
  Pallas kernels  7.42 us (4%)
  other arithmetic  6.8 us (3%)
    all_to_all x5, waiting for transfers between devices, exchange(): return lax.all_to_all(pieces, axes, 0, 0)  34.2 us
    all_to_all x5, starting transfers between devices, exchange(): return lax.all_to_all(pieces, axes, 0, 0)  34 us
    dot_general x11, matrix products, dot(): lax.dot_general(left, right, (((left_dim,), (right_dim,)), ((), ())), pre...  11.3 us
    all_gather x1, waiting for transfers between devices, body(): low_got = lax.all_gather(low_got, 'gy')  11.2 us
    all_to_all x1, blocking collectives, exchange(): return lax.all_to_all(pieces, axes, 0, 0)  10.7 us
    ppermute x2, starting transfers between devices, halves(): return (keep, lax.ppermute(give, 'yh', SWAP))  9.74 us
    ppermute x2, waiting for transfers between devices, halves(): return (keep, lax.ppermute(give, 'yh', SWAP))  6.53 us
    unnamed x50, local copies, waits for them, and re-layouts  6.48 us
  transfers between devices with their start and end apart: 19, of which 8 were waited for; matrix products, arithmetic and copies ran while one was open for 7% of the time, Pallas kernels for 4%

profile of v12, /device:TPU:4, one launch (start us, length us, event | category | flops | bytes accessed | tf_op | source)
XLA Modules:
  0.0 194.3 jit_solution(16433494108167351093)
XLA Ops:
  7.2 0.8 convert_element_type.36
  8.0 10.7 %all_to_all.30 = bf16[4,128,128]{2,1,0:T(8,128)(2,1)S(1)} all-to-all(bf16[4,128,128]{2,1,0:T(8,128)(2,1)S(1)} %broadcast_in_dim.83), channel_id=1, replica_groups=mesh['yl'=4,'co'=2,'gy'=8,'yh'=2,'xx'=4] {'yl'}, dimensions={0} | all-to-all | bytes 262144 | tf_op jit(solution)/shard_map/all_to_all | solution.py:20
  18.8 0.7 broadcast_in_dim.84
  19.4 0.7 pad_maximum_fusion.2
  20.1 2.1 %broadcast_in_dim.85 = bf16[32,128,128]{2,1,0:T(8,128)(2,1)} broadcast(bf16[128,128]{1,0:T(8,128)(2,1)} %param.7), dimensions={1,2} | broadcast | bytes 1081344 | tf_op jit(solution)/shard_map/broadcast_in_dim | solution.py:192
  22.2 11.7 %all-to-all-start.1 = ((bf16[32,128,128]{2,1,0:T(8,128)(2,1)}), bf16[32,128,128]{2,1,0:T(8,128)(2,1)}, u32[]{:S(2)}, u32[]{:S(2)}) async-start(bf16[32,128,128]{2,1,0:T(8,128)(2,1)} %broadcast_in_dim.85), calls=%async_computation.1 | async-start | bytes 2097152 | tf_op jit(solution)/shard_map/all_to_all | solution.py:20
  34.0 1.9 collective-permute-start.2
  35.9 2.4 %collective-permute-start.1 = (bf16[224,1024]{1,0:T(8,128)(2,1)S(1)}, bf16[224,1024]{1,0:T(8,128)(2,1)S(1)}, u32[]{:S(2)}, u32[]{:S(2)}) collective-permute-start(bf16[224,1024]{1,0:T(8,128)(2,1)S(1)} %copy-done.13), channel_id=1, source_target_pairs={{0,64},{64,0},{1,65},{65,1},{2,66},{66,2},{3,67},{67,3},{4,68},{68... | collective-permute-start | bytes 1376264 | tf_op jit(solution)/shard_map/ppermute | solution.py:181
  38.3 1.9 collective-permute-start
  40.6 1.4 collective-permute-done
  42.1 0.4 maximum_maximum_fusion.1
  42.5 18.3 %all-to-all-done.1.tok_got = bf16[32,128,128]{2,1,0:T(8,128)(2,1)} async-done(((bf16[32,128,128]{2,1,0:T(8,128)(2,1)}), bf16[32,128,128]{2,1,0:T(8,128)(2,1)}, u32[]{:S(2)}, u32[]{:S(2)}) %all-to-all-start.1) | async-done | bytes 1048608 | tf_op jit(solution)/shard_map/all_to_all | solution.py:20
  60.8 2.4 %token_products.1 = (bf16[448,1024]{1,0:T(8,128)(2,1)S(1)}, bf16[512,1024]{1,0:T(8,128)(2,1)S(1)}, bf16[16,1024]{1,0:T(8,128)(2,1)S(1)}) custom-call(bf16[32,128,128]{2,1,0:T(8,128)(2,1)} %all-to-all-done.1.tok_got, bf16[512,1024]{1,0:T(8,128)(2,1)S(1)} %get-tuple-element.25.gate_w, bf16[512,1024]{1,0:T(8,128)(2,1)S(1)} %get-tuple-element.26.up_w), custom_call_target="tpu_custom_call" | custom-call | flops 939524096 | bytes 8388608 | tf_op jit(solution)/shard_map/token_products/pallas_call | solution.py:202
  63.3 1.0 copy-done.1
  64.3 0.9 copy-done.6
  65.2 4.8 %all-to-all-start.2 = ((bf16[4,112,1024]{2,1,0:T(8,128)(2,1)}), bf16[4,112,1024]{2,1,0:T(8,128)(2,1)}, u32[]{:S(2)}, u32[]{:S(2)}) async-start(bf16[4,112,1024]{2,1,0:T(8,128)(2,1)} %bitcast.44), calls=%async_computation.2 | async-start | bytes 1835008 | tf_op jit(solution)/shard_map/all_to_all | solution.py:20
  70.0 1.9 collective-permute-start.3
  71.9 11.2 %all-gather.3.cloned.1.call-done = bf16[4224,128]{1,0:T(8,128)(2,1)} async-done(((bf16[528,128]{1,0:T(8,128)(2,1)}), bf16[4224,128]{1,0:T(8,128)(2,1)}) %all-gather.3.cloned.1.call-update) | async-done | bytes 1081360 | tf_op jit(solution)/shard_map/all_gather | solution.py:194
  83.1 1.2 copy-done.3
  84.4 1.5 cotangent_products.1
  85.9 1.0 copy-done.4
  86.9 0.8 copy-done.7
  87.7 4.8 %all-to-all-start.3 = ((bf16[4,112,640]{2,1,0:T(8,128)(2,1)}), bf16[4,112,640]{2,1,0:T(8,128)(2,1)S(1)}, u32[]{:S(2)}, u32[]{:S(2)}) async-start(bf16[4,112,640]{2,1,0:T(8,128)(2,1)} %bitcast.45), calls=%async_computation.3 | async-start | bytes 1146880 | tf_op jit(solution)/shard_map/all_to_all | solution.py:20
  92.6 0.4 copy-done.16
  93.1 1.4 split_sums.2
  94.4 6.2 %collective-permute-start.4 = (bf16[56,1024]{1,0:T(8,128)(2,1)S(1)}, bf16[56,1024]{1,0:T(8,128)(2,1)S(1)}, u32[]{:S(2)}, u32[]{:S(2)}) collective-permute-start(bf16[56,1024]{1,0:T(8,128)(2,1)S(1)} %get-tuple-element.34), channel_id=1, source_target_pairs={{0,4},{4,0},{1,5},{5,1},{2,6},{6,2},{3,7},{7,3},{8,12},{12,8},{9,1... | collective-permute-start | bytes 344072 | tf_op jit(solution)/shard_map/ppermute | solution.py:235
  100.9 3.5 %collective-permute-start.5 = (bf16[56,640]{1,0:T(8,128)(2,1)S(1)}, bf16[56,640]{1,0:T(8,128)(2,1)S(1)}, u32[]{:S(2)}, u32[]{:S(2)}) collective-permute-start(bf16[56,640]{1,0:T(8,128)(2,1)S(1)} %get-tuple-element.37), channel_id=1, source_target_pairs={{0,4},{4,0},{1,5},{5,1},{2,6},{6,2},{3,7},{7,3},{8,12},{12,8},{9,1... | collective-permute-start | bytes 215048 | tf_op jit(solution)/shard_map/ppermute | solution.py:235
  104.5 3.3 %collective-permute-done.4.got = bf16[56,1024]{1,0:T(8,128)(2,1)S(1)} collective-permute-done((bf16[56,1024]{1,0:T(8,128)(2,1)S(1)}, bf16[56,1024]{1,0:T(8,128)(2,1)S(1)}, u32[]{:S(2)}, u32[]{:S(2)}) %collective-permute-start.4) | collective-permute-done | bytes 114720 | tf_op jit(solution)/shard_map/ppermute | solution.py:235
  107.8 3.2 %collective-permute-done.5.back_got = bf16[56,640]{1,0:T(8,128)(2,1)S(1)} collective-permute-done((bf16[56,640]{1,0:T(8,128)(2,1)S(1)}, bf16[56,640]{1,0:T(8,128)(2,1)S(1)}, u32[]{:S(2)}, u32[]{:S(2)}) %collective-permute-start.5) | collective-permute-done | bytes 71712 | tf_op jit(solution)/shard_map/ppermute | solution.py:235
  111.0 0.4 hidden_units.1
  111.4 5.2 %collective-permute-start.6 = (bf16[176,512]{1,0:T(8,128)(2,1)S(1)}, bf16[176,512]{1,0:T(8,128)(2,1)S(1)}, u32[]{:S(2)}, u32[]{:S(2)}) collective-permute-start(bf16[176,512]{1,0:T(8,128)(2,1)S(1)} %hidden_units.1), channel_id=1, source_target_pairs={{0,4},{4,0},{1,5},{5,1},{2,6},{6,2},{3,7},{7,3},{8,12},{12,8},{9,1... | collective-permute-start | bytes 540680 | tf_op jit(solution)/shard_map/ppermute | solution.py:275
  116.6 6.2 %collective-permute-done.6 = bf16[176,512]{1,0:T(8,128)(2,1)S(1)} collective-permute-done((bf16[176,512]{1,0:T(8,128)(2,1)S(1)}, bf16[176,512]{1,0:T(8,128)(2,1)S(1)}, u32[]{:S(2)}, u32[]{:S(2)}) %collective-permute-start.6) | collective-permute-done | bytes 180256 | tf_op jit(solution)/shard_map/ppermute | solution.py:275
  122.9 1.3 broadcast_in_dim.88
  124.2 5.1 %all-to-all-start.4 = ((bf16[4,2,176,512]{3,2,1,0:T(8,128)(2,1)}), bf16[4,2,176,512]{3,2,1,0:T(8,128)(2,1)S(1)}, u32[]{:S(2)}, u32[]{:S(2)}) async-start(bf16[4,2,176,512]{3,2,1,0:T(8,128)(2,1)} %broadcast_in_dim.88), calls=%async_computation.4 | async-start | bytes 2883584 | tf_op jit(solution)/shard_map/all_to_all | solution.py:20
  129.3 0.6 iota_compare_fusion.3
  129.8 0.5 multiply_add_fusion
  130.3 1.3 slice_bitcast_fusion.2
  131.6 1.9 collective-permute-start.8
  133.6 2.4 %collective-permute-start.12 = (bf16[512,1024]{1,0:T(8,128)(2,1)}, bf16[512,1024]{1,0:T(8,128)(2,1)}, u32[]{:S(2)}, u32[]{:S(2)}) collective-permute-start(bf16[512,1024]{1,0:T(8,128)(2,1)} %copy-done.4), channel_id=1, source_target_pairs={{0,64},{64,0},{1,65},{65,1},{2,66},{66,2},{3,67},{67,3},{4,68},{68... | collective-permute-start | bytes 3145736 | tf_op jit(solution)/shard_map/ppermute | solution.py:317
  136.0 4.8 %all-to-all-done.4 = bf16[4,2,176,512]{3,2,1,0:T(8,128)(2,1)S(1)} async-done(((bf16[4,2,176,512]{3,2,1,0:T(8,128)(2,1)}), bf16[4,2,176,512]{3,2,1,0:T(8,128)(2,1)S(1)}, u32[]{:S(2)}, u32[]{:S(2)}) %all-to-all-start.4) | async-done | bytes 1441824 | tf_op jit(solution)/shard_map/all_to_all | solution.py:20
  140.7 1.5 token_gradients.1
  142.3 1.0 copy-done
  143.3 1.1 fusion.44
  144.4 0.6 slice_reduce_fusion
  145.0 7.6 %all-to-all-start.5 = ((bf16[32,144,128]{2,1,0:T(8,128)(2,1)}), bf16[32,144,128]{2,1,0:T(8,128)(2,1)S(1)}, u32[]{:S(2)}, u32[]{:S(2)}) async-start(bf16[32,144,128]{2,1,0:T(8,128)(2,1)} %copy-done), calls=%async_computation.5 | async-start | bytes 2359296 | tf_op jit(solution)/shard_map/all_to_all | solution.py:20
  152.8 0.4 fusion.9
  153.2 1.9 collective-permute-start.7
  155.2 2.4 %collective-permute-start.9 = (bf16[8,224]{1,0:T(8,128)(2,1)S(1)}, bf16[8,224]{1,0:T(8,128)(2,1)S(1)}, u32[]{:S(2)}, u32[]{:S(2)}) collective-permute-start(bf16[8,224]{1,0:T(8,128)(2,1)S(1)} %constant_dynamic-slice_fusion.3), channel_id=1, source_target_pairs={{0,64},{64,0},{1,65},{65,1},{2,66},{66,2},{3,67},{67,3},{4,68},{68... | collective-permute-start | bytes 10760 | tf_op jit(solution)/shard_map/ppermute | solution.py:325
  157.7 1.9 collective-permute-start.10
  159.8 0.4 fusion.7
  160.4 2.4 %collective-permute-start.11 = (bf16[224,512]{1,0:T(8,128)(2,1)S(1)}, bf16[224,512]{1,0:T(8,128)(2,1)S(1)}, u32[]{:S(2)}, u32[]{:S(2)}) collective-permute-start(bf16[224,512]{1,0:T(8,128)(2,1)S(1)} %constant_dynamic-slice_fusion.1), channel_id=1, source_target_pairs={{0,64},{64,0},{1,65},{65,1},{2,66},{66,2},{3,67},{67,3},{4,68},{68... | collective-permute-start | bytes 688136 | tf_op jit(solution)/shard_map/ppermute | solution.py:336
  162.8 1.6 fusion.5
  164.4 1.6 fusion.3
  166.1 1.7 fusion.47
  167.8 1.3 fusion.1
  169.4 11.1 %all-to-all-done.5 = bf16[32,144,128]{2,1,0:T(8,128)(2,1)S(1)} async-done(((bf16[32,144,128]{2,1,0:T(8,128)(2,1)}), bf16[32,144,128]{2,1,0:T(8,128)(2,1)S(1)}, u32[]{:S(2)}, u32[]{:S(2)}) %all-to-all-start.5) | async-done | bytes 1179680 | tf_op jit(solution)/shard_map/all_to_all | solution.py:20
  181.0 0.2 fusion.32
  181.3 0.6 broadcast_multiply_fusion
  181.9 0.6 fusion.40
  182.6 0.2 select_reduce_fusion.1
  182.8 0.7 fusion.17
  183.6 1.3 fusion.4
  184.9 1.3 fusion.2
  186.2 1.3 fusion
  (89 shorter events, 2.4 us)
Async XLA Ops:
  20.1 13.9 %copy-start.12 = (bf16[224,1024]{1,0:T(8,128)(2,1)S(1)}, bf16[224,1024]{1,0:T(8,128)(2,1)}, u32[]{:S(2)}) copy-start(bf16[224,1024]{1,0:T(8,128)(2,1)} %param.10) | copy-start | bytes 1376260
  20.1 15.8 %copy-start.13 = (bf16[224,1024]{1,0:T(8,128)(2,1)S(1)}, bf16[224,1024]{1,0:T(8,128)(2,1)}, u32[]{:S(2)}) copy-start(bf16[224,1024]{1,0:T(8,128)(2,1)} %param.9) | copy-start | bytes 1376260
  20.1 18.2 %copy-start.14 = (bf16[224,1024]{1,0:T(8,128)(2,1)S(1)}, bf16[224,1024]{1,0:T(8,128)(2,1)}, u32[]{:S(2)}) copy-start(bf16[224,1024]{1,0:T(8,128)(2,1)} %param.8) | copy-start | bytes 1376260
  22.2 38.6 %all-to-all-start.1 = ((bf16[32,128,128]{2,1,0:T(8,128)(2,1)}), bf16[32,128,128]{2,1,0:T(8,128)(2,1)}, u32[]{:S(2)}, u32[]{:S(2)}) async-start(bf16[32,128,128]{2,1,0:T(8,128)(2,1)} %broadcast_in_dim.85), calls=%async_computation.1 | async-start | bytes 2097152 | tf_op jit(solution)/shard_map/all_to_all | solution.py:20
  33.9 49.2 %all-gather.3.cloned.1.call-start = ((), (), s32[]{:S(2)}) async-start(), calls=%async_computation.6 | async-start | bytes 1216512 | tf_op jit(solution)/shard_map/all_gather | solution.py:194
  34.0 6.4 %collective-permute-start.2 = (bf16[224,1024]{1,0:T(8,128)(2,1)S(1)}, bf16[224,1024]{1,0:T(8,128)(2,1)S(1)}, u32[]{:S(2)}, u32[]{:S(2)}) collective-permute-start(bf16[224,1024]{1,0:T(8,128)(2,1)S(1)} %copy-done.12), channel_id=1, source_target_pairs={{0,64},{64,0},{1,65},{65,1},{2,66},{66,2},{3,67},{67,3},{4,68},{68... | collective-permute-start | bytes 1376264 | tf_op jit(solution)/shard_map/ppermute | solution.py:181
  35.9 4.6 %collective-permute-start.1 = (bf16[224,1024]{1,0:T(8,128)(2,1)S(1)}, bf16[224,1024]{1,0:T(8,128)(2,1)S(1)}, u32[]{:S(2)}, u32[]{:S(2)}) collective-permute-start(bf16[224,1024]{1,0:T(8,128)(2,1)S(1)} %copy-done.13), channel_id=1, source_target_pairs={{0,64},{64,0},{1,65},{65,1},{2,66},{66,2},{3,67},{67,3},{4,68},{68... | collective-permute-start | bytes 1376264 | tf_op jit(solution)/shard_map/ppermute | solution.py:181
  38.3 3.7 %collective-permute-start = (bf16[224,1024]{1,0:T(8,128)(2,1)S(1)}, bf16[224,1024]{1,0:T(8,128)(2,1)S(1)}, u32[]{:S(2)}, u32[]{:S(2)}) collective-permute-start(bf16[224,1024]{1,0:T(8,128)(2,1)S(1)} %copy-done.14), channel_id=1, source_target_pairs={{0,64},{64,0},{1,65},{65,1},{2,66},{66,2},{3,67},{67,3},{4,68},{68... | collective-permute-start | bytes 1376264 | tf_op jit(solution)/shard_map/ppermute | solution.py:181
  63.3 1.0 copy-start.1
  64.3 0.9 copy-start.6
  65.2 22.5 %all-to-all-start.2 = ((bf16[4,112,1024]{2,1,0:T(8,128)(2,1)}), bf16[4,112,1024]{2,1,0:T(8,128)(2,1)}, u32[]{:S(2)}, u32[]{:S(2)}) async-start(bf16[4,112,1024]{2,1,0:T(8,128)(2,1)} %bitcast.44), calls=%async_computation.2 | async-start | bytes 1835008 | tf_op jit(solution)/shard_map/all_to_all | solution.py:20
  70.0 13.2 %collective-permute-start.3 = (bf16[16,1024]{1,0:T(8,128)(2,1)S(1)}, bf16[16,1024]{1,0:T(8,128)(2,1)S(1)}, u32[]{:S(2)}, u32[]{:S(2)}) collective-permute-start(bf16[16,1024]{1,0:T(8,128)(2,1)S(1)} %get-tuple-element.29.ends), channel_id=1, source_target_pairs={{0,64},{64,0},{1,65},{65,1},{2,66},{66,2},{3,67},{67,3},{4,68},{68... | collective-permute-start | bytes 98312 | tf_op jit(solution)/shard_map/ppermute | solution.py:217
  83.1 1.2 copy-start.3
  85.9 1.0 copy-start.4
  86.9 0.8 copy-start.7
  87.7 13.0 %all-to-all-start.3 = ((bf16[4,112,640]{2,1,0:T(8,128)(2,1)}), bf16[4,112,640]{2,1,0:T(8,128)(2,1)S(1)}, u32[]{:S(2)}, u32[]{:S(2)}) async-start(bf16[4,112,640]{2,1,0:T(8,128)(2,1)} %bitcast.45), calls=%async_computation.3 | async-start | bytes 1146880 | tf_op jit(solution)/shard_map/all_to_all | solution.py:20
  92.5 0.6 copy-start.16
  94.4 13.3 %collective-permute-start.4 = (bf16[56,1024]{1,0:T(8,128)(2,1)S(1)}, bf16[56,1024]{1,0:T(8,128)(2,1)S(1)}, u32[]{:S(2)}, u32[]{:S(2)}) collective-permute-start(bf16[56,1024]{1,0:T(8,128)(2,1)S(1)} %get-tuple-element.34), channel_id=1, source_target_pairs={{0,4},{4,0},{1,5},{5,1},{2,6},{6,2},{3,7},{7,3},{8,12},{12,8},{9,1... | collective-permute-start | bytes 344072 | tf_op jit(solution)/shard_map/ppermute | solution.py:235
  100.9 10.1 %collective-permute-start.5 = (bf16[56,640]{1,0:T(8,128)(2,1)S(1)}, bf16[56,640]{1,0:T(8,128)(2,1)S(1)}, u32[]{:S(2)}, u32[]{:S(2)}) collective-permute-start(bf16[56,640]{1,0:T(8,128)(2,1)S(1)} %get-tuple-element.37), channel_id=1, source_target_pairs={{0,4},{4,0},{1,5},{5,1},{2,6},{6,2},{3,7},{7,3},{8,12},{12,8},{9,1... | collective-permute-start | bytes 215048 | tf_op jit(solution)/shard_map/ppermute | solution.py:235
  111.4 11.4 %collective-permute-start.6 = (bf16[176,512]{1,0:T(8,128)(2,1)S(1)}, bf16[176,512]{1,0:T(8,128)(2,1)S(1)}, u32[]{:S(2)}, u32[]{:S(2)}) collective-permute-start(bf16[176,512]{1,0:T(8,128)(2,1)S(1)} %hidden_units.1), channel_id=1, source_target_pairs={{0,4},{4,0},{1,5},{5,1},{2,6},{6,2},{3,7},{7,3},{8,12},{12,8},{9,1... | collective-permute-start | bytes 540680 | tf_op jit(solution)/shard_map/ppermute | solution.py:275
  124.2 16.6 %all-to-all-start.4 = ((bf16[4,2,176,512]{3,2,1,0:T(8,128)(2,1)}), bf16[4,2,176,512]{3,2,1,0:T(8,128)(2,1)S(1)}, u32[]{:S(2)}, u32[]{:S(2)}) async-start(bf16[4,2,176,512]{3,2,1,0:T(8,128)(2,1)} %broadcast_in_dim.88), calls=%async_computation.4 | async-start | bytes 2883584 | tf_op jit(solution)/shard_map/all_to_all | solution.py:20
  131.6 31.1 %collective-permute-start.8 = (bf16[512,1024]{1,0:T(8,128)(2,1)}, bf16[512,1024]{1,0:T(8,128)(2,1)}, u32[]{:S(2)}, u32[]{:S(2)}) collective-permute-start(bf16[512,1024]{1,0:T(8,128)(2,1)} %copy-done.1), channel_id=1, source_target_pairs={{0,64},{64,0},{1,65},{65,1},{2,66},{66,2},{3,67},{67,3},{4,68},{68... | collective-permute-start | bytes 3145736 | tf_op jit(solution)/shard_map/ppermute | solution.py:316
  133.6 32.5 %collective-permute-start.12 = (bf16[512,1024]{1,0:T(8,128)(2,1)}, bf16[512,1024]{1,0:T(8,128)(2,1)}, u32[]{:S(2)}, u32[]{:S(2)}) collective-permute-start(bf16[512,1024]{1,0:T(8,128)(2,1)} %copy-done.4), channel_id=1, source_target_pairs={{0,64},{64,0},{1,65},{65,1},{2,66},{66,2},{3,67},{67,3},{4,68},{68... | collective-permute-start | bytes 3145736 | tf_op jit(solution)/shard_map/ppermute | solution.py:317
  142.3 1.0 copy-start
  144.4 8.3 %copy-start.2 = (bf16[512,1024]{1,0:T(8,128)(2,1)S(1)}, bf16[512,1024]{1,0:T(8,128)(2,1)}, u32[]{:S(2)}) copy-start(bf16[512,1024]{1,0:T(8,128)(2,1)} %copy-done.1) | copy-start | bytes 3145732
  145.0 7.7 %copy-start.11 = (bf16[8,56,512]{2,1,0:T(8,128)(2,1)S(1)}, bf16[8,56,512]{2,1,0:T(8,128)(2,1)}, u32[]{:S(2)}) copy-start(bf16[8,56,512]{2,1,0:T(8,128)(2,1)} %get-tuple-element.47) | copy-start | bytes 1376260
  145.0 35.5 %all-to-all-start.5 = ((bf16[32,144,128]{2,1,0:T(8,128)(2,1)}), bf16[32,144,128]{2,1,0:T(8,128)(2,1)S(1)}, u32[]{:S(2)}, u32[]{:S(2)}) async-start(bf16[32,144,128]{2,1,0:T(8,128)(2,1)} %copy-done), calls=%async_computation.5 | async-start | bytes 2359296 | tf_op jit(solution)/shard_map/all_to_all | solution.py:20
  152.7 2.4 %copy-start.18 = (bf16[8,448]{1,0:T(8,128)(2,1)S(1)}, bf16[8,448]{1,0:T(8,128)(2,1)}, u32[]{:S(2)}) copy-start(bf16[8,448]{1,0:T(8,128)(2,1)} %slice_reduce_fusion) | copy-start | bytes 21508
  152.7 4.9 %copy-start.10 = (bf16[8,56,512]{2,1,0:T(8,128)(2,1)S(1)}, bf16[8,56,512]{2,1,0:T(8,128)(2,1)}, u32[]{:S(2)}) copy-start(bf16[8,56,512]{2,1,0:T(8,128)(2,1)} %get-tuple-element.46) | copy-start | bytes 1376260
  152.7 6.9 %copy-start.9 = (bf16[8,56,512]{2,1,0:T(8,128)(2,1)S(1)}, bf16[8,56,512]{2,1,0:T(8,128)(2,1)}, u32[]{:S(2)}) copy-start(bf16[8,56,512]{2,1,0:T(8,128)(2,1)} %get-tuple-element.45) | copy-start | bytes 1376260
  152.7 6.9 %copy-start.21 = (s32[4]{0:T(128)S(1)}, s32[4]{0:T(128)}, u32[]{:S(2)}) copy-start(s32[4]{0:T(128)} %multiply_add_fusion) | copy-start | bytes 52
  153.2 9.6 %collective-permute-start.7 = (bf16[224,512]{1,0:T(8,128)(2,1)S(1)}, bf16[224,512]{1,0:T(8,128)(2,1)S(1)}, u32[]{:S(2)}, u32[]{:S(2)}) collective-permute-start(bf16[224,512]{1,0:T(8,128)(2,1)S(1)} %constant_dynamic-slice_fusion.4), channel_id=1, source_target_pairs={{0,64},{64,0},{1,65},{65,1},{2,66},{66,2},{3,67},{67,3},{4,68},{68... | collective-permute-start | bytes 688136 | tf_op jit(solution)/shard_map/ppermute | solution.py:336
  155.2 5.1 %collective-permute-start.9 = (bf16[8,224]{1,0:T(8,128)(2,1)S(1)}, bf16[8,224]{1,0:T(8,128)(2,1)S(1)}, u32[]{:S(2)}, u32[]{:S(2)}) collective-permute-start(bf16[8,224]{1,0:T(8,128)(2,1)S(1)} %constant_dynamic-slice_fusion.3), channel_id=1, source_target_pairs={{0,64},{64,0},{1,65},{65,1},{2,66},{66,2},{3,67},{67,3},{4,68},{68... | collective-permute-start | bytes 10760 | tf_op jit(solution)/shard_map/ppermute | solution.py:325
  157.7 6.8 %collective-permute-start.10 = (bf16[224,512]{1,0:T(8,128)(2,1)S(1)}, bf16[224,512]{1,0:T(8,128)(2,1)S(1)}, u32[]{:S(2)}, u32[]{:S(2)}) collective-permute-start(bf16[224,512]{1,0:T(8,128)(2,1)S(1)} %constant_dynamic-slice_fusion.2), channel_id=1, source_target_pairs={{0,64},{64,0},{1,65},{65,1},{2,66},{66,2},{3,67},{67,3},{4,68},{68... | collective-permute-start | bytes 688136 | tf_op jit(solution)/shard_map/ppermute | solution.py:336
  160.4 5.7 %collective-permute-start.11 = (bf16[224,512]{1,0:T(8,128)(2,1)S(1)}, bf16[224,512]{1,0:T(8,128)(2,1)S(1)}, u32[]{:S(2)}, u32[]{:S(2)}) collective-permute-start(bf16[224,512]{1,0:T(8,128)(2,1)S(1)} %constant_dynamic-slice_fusion.1), channel_id=1, source_target_pairs={{0,64},{64,0},{1,65},{65,1},{2,66},{66,2},{3,67},{67,3},{4,68},{68... | collective-permute-start | bytes 688136 | tf_op jit(solution)/shard_map/ppermute | solution.py:336
  166.1 1.8 copy-start.5
  169.2 11.8 %copy-start.19 = (s32[4]{0:T(128)S(1)}, s32[4]{0:T(128)}, u32[]{:S(2)}) copy-start(s32[4]{0:T(128)} %get-tuple-element.64) | copy-start | bytes 52
  169.2 11.8 %copy-start.20 = (s32[4]{0:T(128)S(1)}, s32[4]{0:T(128)}, u32[]{:S(2)}) copy-start(s32[4]{0:T(128)} %get-tuple-element.65) | copy-start | bytes 52
  169.2 12.7 %copy-start.22 = (bf16[128]{0:T(256)(128)(2,1)S(1)}, bf16[128]{0:T(256)(128)(2,1)}, u32[]{:S(2)}) copy-start(bf16[128]{0:T(256)(128)(2,1)} %param.11) | copy-start | bytes 772
  169.2 13.6 %copy-start.15 = (f32[128,128]{1,0:T(8,128)S(1)}, f32[128,128]{1,0:T(8,128)}, u32[]{:S(2)}) copy-start(f32[128,128]{1,0:T(8,128)} %param.12) | copy-start | bytes 196612
  169.2 13.6 %copy-start.24 = (pred[128]{0:T(512)(128)(4,1)S(1)}, pred[128]{0:T(512)(128)(4,1)}, u32[]{:S(2)}) copy-start(pred[128]{0:T(512)(128)(4,1)} %iota_compare_fusion.3) | copy-start | bytes 388
  181.0 5.2 %copy-start.23 = (f32[8]{0:T(128)}, f32[8]{0:T(128)S(1)}, u32[]{:S(2)}) copy-start(f32[8]{0:T(128)S(1)} %mul.117) | copy-start | bytes 100
  183.6 2.5 %copy-start.8 = (f32[224,1024]{1,0:T(8,128)S(1)}, f32[224,1024]{1,0:T(8,128)}, u32[]{:S(2)}) copy-start(f32[224,1024]{1,0:T(8,128)} %fusion.1) | copy-start | bytes 2752516
  183.6 2.5 %copy-start.17 = (f32[1,1024]{1,0:T(1,128)S(1)}, f32[1,1024]{1,0:T(1,128)}, u32[]{:S(2)}) copy-start(f32[1,1024]{1,0:T(1,128)} %copy-done.16) | copy-start | bytes 12292
Sparse Core Ops, SparseCore 0:
  40.5 42.5 all-gather.2

commit v13 on v12

--- a/solution.py
+++ b/solution.py
@@ -85,11 +85,11 @@
         give[:, -128:] = jnp.where(lane == 1, ends + lost, ends).astype(bf16)
 
 
-def hidden_units(chip_units, place, keep, got, back_keep, back_got, tok_terms, mine):
+def hidden_units(chip_units, place, keep, got, back_keep, tok_terms, mine):
     own, half = keep.shape[0], keep.shape[1] // 2
     n_seq = half // SEQ_LEN
-    sums = keep[...] + got[...].astype(f32)
-    back = back_keep[...] + back_got[...].astype(f32)
+    sums = keep[...] + got[:, : 2 * half].astype(f32)
+    back = back_keep[...] + got[:, 2 * half :].astype(f32)
     gate_sum, up_sum, hidden_grad = sums[:, :half], sums[:, half:], back[:, :half]
     more = back[:, half:]
     head_down = more[:, 0:1] + more[:, 1:2]
@@ -232,7 +232,7 @@
             cost_estimate=pl.CostEstimate(flops=8 * own * lanes, bytes_accessed=22 * own * lanes, transcendentals=0),
             name="split_sums",
         )(y_half, got)
-        return keep, lax.ppermute(give, "yh", SWAP)
+        return keep, give
 
     back_parts, low_half, head_vec = pl.pallas_call(
         cotangent_products,
@@ -255,6 +255,7 @@
     second = exchange(back_parts.reshape(n_xx, 2 * own, half + 128), "xx")
     sums, sums_got = halves(first, False)
     back, back_got = halves(second, True)
+    both_got = lax.ppermute(jnp.concatenate([sums_got, back_got], axis=1), "yh", SWAP)
 
     last_rows = jnp.concatenate(core_order(ends[:n_yl], ends_sib[:n_yl]), axis=0).astype(f32)
     counted = (lax.axis_index("yl") == 0) & (lax.axis_index("gy") == 0)
@@ -264,14 +265,14 @@
     mine = pl.pallas_call(
         functools.partial(hidden_units, 2 * units),
         out_shape=jax.ShapeDtypeStruct((3 * own + 8, half), bf16),
-        in_specs=[scalar] + [whole] * 5,
+        in_specs=[scalar] + [whole] * 4,
         out_specs=whole,
         compiler_params=grant,
         cost_estimate=pl.CostEstimate(
             flops=40 * own * half, bytes_accessed=12 * own * half, transcendentals=own * half
         ),
         name="hidden_units",
-    )(place, sums, sums_got, back, back_got, tok_terms)
+    )(place, sums, both_got, back, tok_terms)
     other = lax.ppermute(mine, "yh", SWAP)
     pair = jnp.stack([jnp.where(y_half == 0, mine, other), jnp.where(y_half == 0, other, mine)])
     everyone = to_all(pair, "xx", n_xx).reshape(n_gz, 3 * own + 8, half)

time: 195 us -> 196 us (level)
  the two profiles are of different devices: /device:TPU:4 before, /device:TPU:60 now
where the time goes in v13:
time: 196 us; the launch traced here: 195 us
  starting transfers between devices  66.5 us (34%)
  waiting for transfers between devices  65.8 us (34%)
  between operations  14.6 us (7%)
  local copies, waits for them, and re-layouts  13.7 us (7%)
  matrix products  11.3 us (6%)
  blocking collectives  9.28 us (5%)
  Pallas kernels  7.4 us (4%)
  other arithmetic  6.76 us (3%)
    all_to_all x5, starting transfers between devices, exchange(): return lax.all_to_all(pieces, axes, 0, 0)  36.9 us
    all_to_all x5, waiting for transfers between devices, exchange(): return lax.all_to_all(pieces, axes, 0, 0)  36.2 us
    dot_general x11, matrix products, dot(): lax.dot_general(left, right, (((left_dim,), (right_dim,)), ((), ())), pre...  11.3 us
    all_gather x1, waiting for transfers between devices, body(): low_got = lax.all_gather(low_got, 'gy')  10.4 us
    all_to_all x1, blocking collectives, exchange(): return lax.all_to_all(pieces, axes, 0, 0)  9.28 us
    ppermute x1, waiting for transfers between devices, body(): lax.ppermute(jnp.concatenate([sums_got, back_got], axis=1), 'yh', SWAP)  8.9 us
    ppermute x1, waiting for transfers between devices, body(): other = lax.ppermute(mine, 'yh', SWAP)  8.81 us
    unnamed x50, local copies, waits for them, and re-layouts  6.46 us
  transfers between devices with their start and end apart: 18, of which 8 were waited for; matrix products, arithmetic and copies ran while one was open for 7% of the time, Pallas kernels for 3%

profile of v13, /device:TPU:60, one launch (start us, length us, event | category | flops | bytes accessed | tf_op | source)
XLA Modules:
  0.0 195.3 jit_solution(10248692322634044311)
XLA Ops:
  7.2 0.8 convert_element_type.36
  8.0 9.3 %all_to_all.30 = bf16[4,128,128]{2,1,0:T(8,128)(2,1)S(1)} all-to-all(bf16[4,128,128]{2,1,0:T(8,128)(2,1)S(1)} %broadcast_in_dim.83), channel_id=1, replica_groups=mesh['yl'=4,'co'=2,'gy'=8,'yh'=2,'xx'=4] {'yl'}, dimensions={0} | all-to-all | bytes 262144 | tf_op jit(solution)/shard_map/all_to_all | solution.py:20
  17.3 0.7 broadcast_in_dim.84
  18.0 0.7 pad_maximum_fusion.3
  18.6 2.1 %broadcast_in_dim.85 = bf16[32,128,128]{2,1,0:T(8,128)(2,1)} broadcast(bf16[128,128]{1,0:T(8,128)(2,1)} %param.7), dimensions={1,2} | broadcast | bytes 1081344 | tf_op jit(solution)/shard_map/broadcast_in_dim | solution.py:192
  20.7 13.8 %all-to-all-start.1 = ((bf16[32,128,128]{2,1,0:T(8,128)(2,1)}), bf16[32,128,128]{2,1,0:T(8,128)(2,1)}, u32[]{:S(2)}, u32[]{:S(2)}) async-start(bf16[32,128,128]{2,1,0:T(8,128)(2,1)} %broadcast_in_dim.85), calls=%async_computation.1 | async-start | bytes 2097152 | tf_op jit(solution)/shard_map/all_to_all | solution.py:20
  34.6 1.9 collective-permute-start.2
  36.6 2.4 %collective-permute-start.1 = (bf16[224,1024]{1,0:T(8,128)(2,1)S(1)}, bf16[224,1024]{1,0:T(8,128)(2,1)S(1)}, u32[]{:S(2)}, u32[]{:S(2)}) collective-permute-start(bf16[224,1024]{1,0:T(8,128)(2,1)S(1)} %copy-done.13), channel_id=1, source_target_pairs={{0,64},{64,0},{1,65},{65,1},{2,66},{66,2},{3,67},{67,3},{4,68},{68... | collective-permute-start | bytes 1376264 | tf_op jit(solution)/shard_map/ppermute | solution.py:181
  39.0 1.9 collective-permute-start
  41.3 1.4 collective-permute-done
  42.8 0.4 maximum_maximum_fusion.1
  43.2 18.4 %all-to-all-done.1.tok_got = bf16[32,128,128]{2,1,0:T(8,128)(2,1)} async-done(((bf16[32,128,128]{2,1,0:T(8,128)(2,1)}), bf16[32,128,128]{2,1,0:T(8,128)(2,1)}, u32[]{:S(2)}, u32[]{:S(2)}) %all-to-all-start.1) | async-done | bytes 1048608 | tf_op jit(solution)/shard_map/all_to_all | solution.py:20
  61.5 2.4 %token_products.1 = (bf16[448,1024]{1,0:T(8,128)(2,1)S(1)}, bf16[512,1024]{1,0:T(8,128)(2,1)S(1)}, bf16[16,1024]{1,0:T(8,128)(2,1)S(1)}) custom-call(bf16[32,128,128]{2,1,0:T(8,128)(2,1)} %all-to-all-done.1.tok_got, bf16[512,1024]{1,0:T(8,128)(2,1)S(1)} %get-tuple-element.25.gate_w, bf16[512,1024]{1,0:T(8,128)(2,1)S(1)} %get-tuple-element.26.up_w), custom_call_target="tpu_custom_call" | custom-call | flops 939524096 | bytes 8388608 | tf_op jit(solution)/shard_map/token_products/pallas_call | solution.py:202
  64.0 1.0 copy-done.1
  64.9 0.9 copy-done.6
  65.9 4.8 %all-to-all-start.2 = ((bf16[4,112,1024]{2,1,0:T(8,128)(2,1)}), bf16[4,112,1024]{2,1,0:T(8,128)(2,1)}, u32[]{:S(2)}, u32[]{:S(2)}) async-start(bf16[4,112,1024]{2,1,0:T(8,128)(2,1)} %bitcast.44), calls=%async_computation.2 | async-start | bytes 1835008 | tf_op jit(solution)/shard_map/all_to_all | solution.py:20
  70.7 1.9 collective-permute-start.3
  72.6 10.4 %all-gather.3.cloned.1.call-done = bf16[4224,128]{1,0:T(8,128)(2,1)} async-done(((bf16[528,128]{1,0:T(8,128)(2,1)}), bf16[4224,128]{1,0:T(8,128)(2,1)}) %all-gather.3.cloned.1.call-update) | async-done | bytes 1081360 | tf_op jit(solution)/shard_map/all_gather | solution.py:194
  83.0 1.2 copy-done.3
  84.3 1.5 cotangent_products.1
  85.8 1.0 copy-done.4
  86.8 0.8 copy-done.7
  87.6 4.8 %all-to-all-start.3 = ((bf16[4,112,640]{2,1,0:T(8,128)(2,1)}), bf16[4,112,640]{2,1,0:T(8,128)(2,1)S(1)}, u32[]{:S(2)}, u32[]{:S(2)}) async-start(bf16[4,112,640]{2,1,0:T(8,128)(2,1)} %bitcast.45), calls=%async_computation.3 | async-start | bytes 1146880 | tf_op jit(solution)/shard_map/all_to_all | solution.py:20
  92.5 0.4 copy-done.16
  93.0 1.4 split_sums.2
  94.3 3.4 %all-to-all-done.3.got = bf16[4,112,640]{2,1,0:T(8,128)(2,1)S(1)} async-done(((bf16[4,112,640]{2,1,0:T(8,128)(2,1)}), bf16[4,112,640]{2,1,0:T(8,128)(2,1)S(1)}, u32[]{:S(2)}, u32[]{:S(2)}) %all-to-all-start.3) | async-done | bytes 573472 | tf_op jit(solution)/shard_map/all_to_all | solution.py:20
  98.0 4.1 %collective-permute-start.4 = (bf16[56,1664]{1,0:T(8,128)(2,1)S(1)}, bf16[56,1664]{1,0:T(8,128)(2,1)S(1)}, u32[]{:S(2)}, u32[]{:S(2)}) collective-permute-start(bf16[56,1664]{1,0:T(8,128)(2,1)S(1)} %pad_maximum_fusion.2), channel_id=1, source_target_pairs={{0,4},{4,0},{1,5},{5,1},{2,6},{6,2},{3,7},{7,3},{8,12},{12,8},{9,1... | collective-permute-start | bytes 559112 | tf_op jit(solution)/shard_map/ppermute | solution.py:258
  102.1 8.9 %collective-permute-done.4.got = bf16[56,1664]{1,0:T(8,128)(2,1)S(1)} collective-permute-done((bf16[56,1664]{1,0:T(8,128)(2,1)S(1)}, bf16[56,1664]{1,0:T(8,128)(2,1)S(1)}, u32[]{:S(2)}, u32[]{:S(2)}) %collective-permute-start.4) | collective-permute-done | bytes 186400 | tf_op jit(solution)/shard_map/ppermute | solution.py:258
  111.0 0.4 hidden_units.1
  111.4 4.4 %collective-permute-start.5 = (bf16[176,512]{1,0:T(8,128)(2,1)S(1)}, bf16[176,512]{1,0:T(8,128)(2,1)S(1)}, u32[]{:S(2)}, u32[]{:S(2)}) collective-permute-start(bf16[176,512]{1,0:T(8,128)(2,1)S(1)} %hidden_units.1), channel_id=1, source_target_pairs={{0,4},{4,0},{1,5},{5,1},{2,6},{6,2},{3,7},{7,3},{8,12},{12,8},{9,1... | collective-permute-start | bytes 540680 | tf_op jit(solution)/shard_map/ppermute | solution.py:276
  115.8 8.8 %collective-permute-done.5 = bf16[176,512]{1,0:T(8,128)(2,1)S(1)} collective-permute-done((bf16[176,512]{1,0:T(8,128)(2,1)S(1)}, bf16[176,512]{1,0:T(8,128)(2,1)S(1)}, u32[]{:S(2)}, u32[]{:S(2)}) %collective-permute-start.5) | collective-permute-done | bytes 180256 | tf_op jit(solution)/shard_map/ppermute | solution.py:276
  124.7 1.3 broadcast_in_dim.88
  126.0 6.5 %all-to-all-start.4 = ((bf16[4,2,176,512]{3,2,1,0:T(8,128)(2,1)}), bf16[4,2,176,512]{3,2,1,0:T(8,128)(2,1)S(1)}, u32[]{:S(2)}, u32[]{:S(2)}) async-start(bf16[4,2,176,512]{3,2,1,0:T(8,128)(2,1)} %broadcast_in_dim.88), calls=%async_computation.4 | async-start | bytes 2883584 | tf_op jit(solution)/shard_map/all_to_all | solution.py:20
  132.5 0.5 iota_compare_fusion.3
  133.0 0.5 multiply_add_fusion
  133.5 1.3 slice_bitcast_fusion.2
  134.9 1.9 collective-permute-start.7
  136.8 2.4 %collective-permute-start.11 = (bf16[512,1024]{1,0:T(8,128)(2,1)}, bf16[512,1024]{1,0:T(8,128)(2,1)}, u32[]{:S(2)}, u32[]{:S(2)}) collective-permute-start(bf16[512,1024]{1,0:T(8,128)(2,1)} %copy-done.4), channel_id=1, source_target_pairs={{0,64},{64,0},{1,65},{65,1},{2,66},{66,2},{3,67},{67,3},{4,68},{68... | collective-permute-start | bytes 3145736 | tf_op jit(solution)/shard_map/ppermute | solution.py:318
  139.2 3.3 %all-to-all-done.4 = bf16[4,2,176,512]{3,2,1,0:T(8,128)(2,1)S(1)} async-done(((bf16[4,2,176,512]{3,2,1,0:T(8,128)(2,1)}), bf16[4,2,176,512]{3,2,1,0:T(8,128)(2,1)S(1)}, u32[]{:S(2)}, u32[]{:S(2)}) %all-to-all-start.4) | async-done | bytes 1441824 | tf_op jit(solution)/shard_map/all_to_all | solution.py:20
  142.5 1.5 token_gradients.1
  144.0 1.0 copy-done
  145.1 1.1 fusion.44
  146.2 0.6 slice_reduce_fusion
  146.8 6.9 %all-to-all-start.5 = ((bf16[32,144,128]{2,1,0:T(8,128)(2,1)}), bf16[32,144,128]{2,1,0:T(8,128)(2,1)S(1)}, u32[]{:S(2)}, u32[]{:S(2)}) async-start(bf16[32,144,128]{2,1,0:T(8,128)(2,1)} %copy-done), calls=%async_computation.5 | async-start | bytes 2359296 | tf_op jit(solution)/shard_map/all_to_all | solution.py:20
  153.8 0.4 fusion.9
  154.2 1.9 collective-permute-start.6
  156.3 2.4 %collective-permute-start.8 = (bf16[8,224]{1,0:T(8,128)(2,1)S(1)}, bf16[8,224]{1,0:T(8,128)(2,1)S(1)}, u32[]{:S(2)}, u32[]{:S(2)}) collective-permute-start(bf16[8,224]{1,0:T(8,128)(2,1)S(1)} %constant_dynamic-slice_fusion.3), channel_id=1, source_target_pairs={{0,64},{64,0},{1,65},{65,1},{2,66},{66,2},{3,67},{67,3},{4,68},{68... | collective-permute-start | bytes 10760 | tf_op jit(solution)/shard_map/ppermute | solution.py:326
  158.7 1.9 collective-permute-start.9
  160.7 0.2 convolution_convert_fusion.1
  160.8 0.4 fusion.7
  161.4 2.4 %collective-permute-start.10 = (bf16[224,512]{1,0:T(8,128)(2,1)S(1)}, bf16[224,512]{1,0:T(8,128)(2,1)S(1)}, u32[]{:S(2)}, u32[]{:S(2)}) collective-permute-start(bf16[224,512]{1,0:T(8,128)(2,1)S(1)} %constant_dynamic-slice_fusion.1), channel_id=1, source_target_pairs={{0,64},{64,0},{1,65},{65,1},{2,66},{66,2},{3,67},{67,3},{4,68},{68... | collective-permute-start | bytes 688136 | tf_op jit(solution)/shard_map/ppermute | solution.py:337
  163.8 1.6 fusion.5
  165.5 1.6 fusion.3
  167.2 1.7 fusion.47
  168.9 1.3 fusion.1
  170.4 11.1 %all-to-all-done.5 = bf16[32,144,128]{2,1,0:T(8,128)(2,1)S(1)} async-done(((bf16[32,144,128]{2,1,0:T(8,128)(2,1)}), bf16[32,144,128]{2,1,0:T(8,128)(2,1)S(1)}, u32[]{:S(2)}, u32[]{:S(2)}) %all-to-all-start.5) | async-done | bytes 1179680 | tf_op jit(solution)/shard_map/all_to_all | solution.py:20
  182.0 0.2 fusion.32
  182.3 0.6 broadcast_multiply_fusion
  182.9 0.6 fusion.40
  183.7 0.2 select_reduce_fusion.1
  183.9 0.7 fusion.17
  184.7 1.3 fusion.4
  185.9 1.3 fusion.2
  187.2 1.3 fusion
  (88 shorter events, 2.2 us)
Async XLA Ops:
  18.6 16.0 %copy-start.12 = (bf16[224,1024]{1,0:T(8,128)(2,1)S(1)}, bf16[224,1024]{1,0:T(8,128)(2,1)}, u32[]{:S(2)}) copy-start(bf16[224,1024]{1,0:T(8,128)(2,1)} %param.10) | copy-start | bytes 1376260
  18.6 17.9 %copy-start.13 = (bf16[224,1024]{1,0:T(8,128)(2,1)S(1)}, bf16[224,1024]{1,0:T(8,128)(2,1)}, u32[]{:S(2)}) copy-start(bf16[224,1024]{1,0:T(8,128)(2,1)} %param.9) | copy-start | bytes 1376260
  18.6 20.3 %copy-start.14 = (bf16[224,1024]{1,0:T(8,128)(2,1)S(1)}, bf16[224,1024]{1,0:T(8,128)(2,1)}, u32[]{:S(2)}) copy-start(bf16[224,1024]{1,0:T(8,128)(2,1)} %param.8) | copy-start | bytes 1376260
  20.7 40.8 %all-to-all-start.1 = ((bf16[32,128,128]{2,1,0:T(8,128)(2,1)}), bf16[32,128,128]{2,1,0:T(8,128)(2,1)}, u32[]{:S(2)}, u32[]{:S(2)}) async-start(bf16[32,128,128]{2,1,0:T(8,128)(2,1)} %broadcast_in_dim.85), calls=%async_computation.1 | async-start | bytes 2097152 | tf_op jit(solution)/shard_map/all_to_all | solution.py:20
  34.6 48.5 %all-gather.3.cloned.1.call-start = ((), (), s32[]{:S(2)}) async-start(), calls=%async_computation.6 | async-start | bytes 1216512 | tf_op jit(solution)/shard_map/all_gather | solution.py:194
  34.6 6.4 %collective-permute-start.2 = (bf16[224,1024]{1,0:T(8,128)(2,1)S(1)}, bf16[224,1024]{1,0:T(8,128)(2,1)S(1)}, u32[]{:S(2)}, u32[]{:S(2)}) collective-permute-start(bf16[224,1024]{1,0:T(8,128)(2,1)S(1)} %copy-done.12), channel_id=1, source_target_pairs={{0,64},{64,0},{1,65},{65,1},{2,66},{66,2},{3,67},{67,3},{4,68},{68... | collective-permute-start | bytes 1376264 | tf_op jit(solution)/shard_map/ppermute | solution.py:181
  36.6 4.6 %collective-permute-start.1 = (bf16[224,1024]{1,0:T(8,128)(2,1)S(1)}, bf16[224,1024]{1,0:T(8,128)(2,1)S(1)}, u32[]{:S(2)}, u32[]{:S(2)}) collective-permute-start(bf16[224,1024]{1,0:T(8,128)(2,1)S(1)} %copy-done.13), channel_id=1, source_target_pairs={{0,64},{64,0},{1,65},{65,1},{2,66},{66,2},{3,67},{67,3},{4,68},{68... | collective-permute-start | bytes 1376264 | tf_op jit(solution)/shard_map/ppermute | solution.py:181
  39.0 3.7 %collective-permute-start = (bf16[224,1024]{1,0:T(8,128)(2,1)S(1)}, bf16[224,1024]{1,0:T(8,128)(2,1)S(1)}, u32[]{:S(2)}, u32[]{:S(2)}) collective-permute-start(bf16[224,1024]{1,0:T(8,128)(2,1)S(1)} %copy-done.14), channel_id=1, source_target_pairs={{0,64},{64,0},{1,65},{65,1},{2,66},{66,2},{3,67},{67,3},{4,68},{68... | collective-permute-start | bytes 1376264 | tf_op jit(solution)/shard_map/ppermute | solution.py:181
  64.0 1.0 copy-start.1
  64.9 0.9 copy-start.6
  65.9 21.7 %all-to-all-start.2 = ((bf16[4,112,1024]{2,1,0:T(8,128)(2,1)}), bf16[4,112,1024]{2,1,0:T(8,128)(2,1)}, u32[]{:S(2)}, u32[]{:S(2)}) async-start(bf16[4,112,1024]{2,1,0:T(8,128)(2,1)} %bitcast.44), calls=%async_computation.2 | async-start | bytes 1835008 | tf_op jit(solution)/shard_map/all_to_all | solution.py:20
  70.7 12.4 %collective-permute-start.3 = (bf16[16,1024]{1,0:T(8,128)(2,1)S(1)}, bf16[16,1024]{1,0:T(8,128)(2,1)S(1)}, u32[]{:S(2)}, u32[]{:S(2)}) collective-permute-start(bf16[16,1024]{1,0:T(8,128)(2,1)S(1)} %get-tuple-element.29.ends), channel_id=1, source_target_pairs={{0,64},{64,0},{1,65},{65,1},{2,66},{66,2},{3,67},{67,3},{4,68},{68... | collective-permute-start | bytes 98312 | tf_op jit(solution)/shard_map/ppermute | solution.py:217
  83.0 1.2 copy-start.3
  85.8 1.0 copy-start.4
  86.8 0.8 copy-start.7
  87.6 10.2 %all-to-all-start.3 = ((bf16[4,112,640]{2,1,0:T(8,128)(2,1)}), bf16[4,112,640]{2,1,0:T(8,128)(2,1)S(1)}, u32[]{:S(2)}, u32[]{:S(2)}) async-start(bf16[4,112,640]{2,1,0:T(8,128)(2,1)} %bitcast.45), calls=%async_computation.3 | async-start | bytes 1146880 | tf_op jit(solution)/shard_map/all_to_all | solution.py:20
  92.4 0.6 copy-start.16
  98.0 13.1 %collective-permute-start.4 = (bf16[56,1664]{1,0:T(8,128)(2,1)S(1)}, bf16[56,1664]{1,0:T(8,128)(2,1)S(1)}, u32[]{:S(2)}, u32[]{:S(2)}) collective-permute-start(bf16[56,1664]{1,0:T(8,128)(2,1)S(1)} %pad_maximum_fusion.2), channel_id=1, source_target_pairs={{0,4},{4,0},{1,5},{5,1},{2,6},{6,2},{3,7},{7,3},{8,12},{12,8},{9,1... | collective-permute-start | bytes 559112 | tf_op jit(solution)/shard_map/ppermute | solution.py:258
  111.4 13.2 %collective-permute-start.5 = (bf16[176,512]{1,0:T(8,128)(2,1)S(1)}, bf16[176,512]{1,0:T(8,128)(2,1)S(1)}, u32[]{:S(2)}, u32[]{:S(2)}) collective-permute-start(bf16[176,512]{1,0:T(8,128)(2,1)S(1)} %hidden_units.1), channel_id=1, source_target_pairs={{0,4},{4,0},{1,5},{5,1},{2,6},{6,2},{3,7},{7,3},{8,12},{12,8},{9,1... | collective-permute-start | bytes 540680 | tf_op jit(solution)/shard_map/ppermute | solution.py:276
  126.0 16.5 %all-to-all-start.4 = ((bf16[4,2,176,512]{3,2,1,0:T(8,128)(2,1)}), bf16[4,2,176,512]{3,2,1,0:T(8,128)(2,1)S(1)}, u32[]{:S(2)}, u32[]{:S(2)}) async-start(bf16[4,2,176,512]{3,2,1,0:T(8,128)(2,1)} %broadcast_in_dim.88), calls=%async_computation.4 | async-start | bytes 2883584 | tf_op jit(solution)/shard_map/all_to_all | solution.py:20
  134.9 29.0 %collective-permute-start.7 = (bf16[512,1024]{1,0:T(8,128)(2,1)}, bf16[512,1024]{1,0:T(8,128)(2,1)}, u32[]{:S(2)}, u32[]{:S(2)}) collective-permute-start(bf16[512,1024]{1,0:T(8,128)(2,1)} %copy-done.1), channel_id=1, source_target_pairs={{0,64},{64,0},{1,65},{65,1},{2,66},{66,2},{3,67},{67,3},{4,68},{68... | collective-permute-start | bytes 3145736 | tf_op jit(solution)/shard_map/ppermute | solution.py:317
  136.8 30.4 %collective-permute-start.11 = (bf16[512,1024]{1,0:T(8,128)(2,1)}, bf16[512,1024]{1,0:T(8,128)(2,1)}, u32[]{:S(2)}, u32[]{:S(2)}) collective-permute-start(bf16[512,1024]{1,0:T(8,128)(2,1)} %copy-done.4), channel_id=1, source_target_pairs={{0,64},{64,0},{1,65},{65,1},{2,66},{66,2},{3,67},{67,3},{4,68},{68... | collective-permute-start | bytes 3145736 | tf_op jit(solution)/shard_map/ppermute | solution.py:318
  144.0 1.0 copy-start
  146.2 7.6 %copy-start.2 = (bf16[512,1024]{1,0:T(8,128)(2,1)S(1)}, bf16[512,1024]{1,0:T(8,128)(2,1)}, u32[]{:S(2)}) copy-start(bf16[512,1024]{1,0:T(8,128)(2,1)} %copy-done.1) | copy-start | bytes 3145732
  146.8 7.0 %copy-start.11 = (bf16[8,56,512]{2,1,0:T(8,128)(2,1)S(1)}, bf16[8,56,512]{2,1,0:T(8,128)(2,1)}, u32[]{:S(2)}) copy-start(bf16[8,56,512]{2,1,0:T(8,128)(2,1)} %get-tuple-element.47) | copy-start | bytes 1376260
  146.8 34.7 %all-to-all-start.5 = ((bf16[32,144,128]{2,1,0:T(8,128)(2,1)}), bf16[32,144,128]{2,1,0:T(8,128)(2,1)S(1)}, u32[]{:S(2)}, u32[]{:S(2)}) async-start(bf16[32,144,128]{2,1,0:T(8,128)(2,1)} %copy-done), calls=%async_computation.5 | async-start | bytes 2359296 | tf_op jit(solution)/shard_map/all_to_all | solution.py:20
  153.7 2.4 %copy-start.18 = (bf16[8,448]{1,0:T(8,128)(2,1)S(1)}, bf16[8,448]{1,0:T(8,128)(2,1)}, u32[]{:S(2)}) copy-start(bf16[8,448]{1,0:T(8,128)(2,1)} %slice_reduce_fusion) | copy-start | bytes 21508
  153.7 4.9 %copy-start.10 = (bf16[8,56,512]{2,1,0:T(8,128)(2,1)S(1)}, bf16[8,56,512]{2,1,0:T(8,128)(2,1)}, u32[]{:S(2)}) copy-start(bf16[8,56,512]{2,1,0:T(8,128)(2,1)} %get-tuple-element.46) | copy-start | bytes 1376260
  153.8 6.9 %copy-start.9 = (bf16[8,56,512]{2,1,0:T(8,128)(2,1)S(1)}, bf16[8,56,512]{2,1,0:T(8,128)(2,1)}, u32[]{:S(2)}) copy-start(bf16[8,56,512]{2,1,0:T(8,128)(2,1)} %get-tuple-element.45) | copy-start | bytes 1376260
  153.8 6.9 %copy-start.21 = (s32[4]{0:T(128)S(1)}, s32[4]{0:T(128)}, u32[]{:S(2)}) copy-start(s32[4]{0:T(128)} %multiply_add_fusion) | copy-start | bytes 52
  154.2 9.6 %collective-permute-start.6 = (bf16[224,512]{1,0:T(8,128)(2,1)S(1)}, bf16[224,512]{1,0:T(8,128)(2,1)S(1)}, u32[]{:S(2)}, u32[]{:S(2)}) collective-permute-start(bf16[224,512]{1,0:T(8,128)(2,1)S(1)} %constant_dynamic-slice_fusion.4), channel_id=1, source_target_pairs={{0,64},{64,0},{1,65},{65,1},{2,66},{66,2},{3,67},{67,3},{4,68},{68... | collective-permute-start | bytes 688136 | tf_op jit(solution)/shard_map/ppermute | solution.py:337
  156.3 5.1 %collective-permute-start.8 = (bf16[8,224]{1,0:T(8,128)(2,1)S(1)}, bf16[8,224]{1,0:T(8,128)(2,1)S(1)}, u32[]{:S(2)}, u32[]{:S(2)}) collective-permute-start(bf16[8,224]{1,0:T(8,128)(2,1)S(1)} %constant_dynamic-slice_fusion.3), channel_id=1, source_target_pairs={{0,64},{64,0},{1,65},{65,1},{2,66},{66,2},{3,67},{67,3},{4,68},{68... | collective-permute-start | bytes 10760 | tf_op jit(solution)/shard_map/ppermute | solution.py:326
  158.7 6.8 %collective-permute-start.9 = (bf16[224,512]{1,0:T(8,128)(2,1)S(1)}, bf16[224,512]{1,0:T(8,128)(2,1)S(1)}, u32[]{:S(2)}, u32[]{:S(2)}) collective-permute-start(bf16[224,512]{1,0:T(8,128)(2,1)S(1)} %constant_dynamic-slice_fusion.2), channel_id=1, source_target_pairs={{0,64},{64,0},{1,65},{65,1},{2,66},{66,2},{3,67},{67,3},{4,68},{68... | collective-permute-start | bytes 688136 | tf_op jit(solution)/shard_map/ppermute | solution.py:337
  161.4 5.8 %collective-permute-start.10 = (bf16[224,512]{1,0:T(8,128)(2,1)S(1)}, bf16[224,512]{1,0:T(8,128)(2,1)S(1)}, u32[]{:S(2)}, u32[]{:S(2)}) collective-permute-start(bf16[224,512]{1,0:T(8,128)(2,1)S(1)} %constant_dynamic-slice_fusion.1), channel_id=1, source_target_pairs={{0,64},{64,0},{1,65},{65,1},{2,66},{66,2},{3,67},{67,3},{4,68},{68... | collective-permute-start | bytes 688136 | tf_op jit(solution)/shard_map/ppermute | solution.py:337
  167.1 1.8 copy-start.5
  170.2 11.8 %copy-start.19 = (s32[4]{0:T(128)S(1)}, s32[4]{0:T(128)}, u32[]{:S(2)}) copy-start(s32[4]{0:T(128)} %get-tuple-element.64) | copy-start | bytes 52
  170.2 11.8 %copy-start.20 = (s32[4]{0:T(128)S(1)}, s32[4]{0:T(128)}, u32[]{:S(2)}) copy-start(s32[4]{0:T(128)} %get-tuple-element.65) | copy-start | bytes 52
  170.2 12.7 %copy-start.22 = (bf16[128]{0:T(256)(128)(2,1)S(1)}, bf16[128]{0:T(256)(128)(2,1)}, u32[]{:S(2)}) copy-start(bf16[128]{0:T(256)(128)(2,1)} %param.11) | copy-start | bytes 772
  170.2 13.6 %copy-start.15 = (f32[128,128]{1,0:T(8,128)S(1)}, f32[128,128]{1,0:T(8,128)}, u32[]{:S(2)}) copy-start(f32[128,128]{1,0:T(8,128)} %param.12) | copy-start | bytes 196612
  170.3 13.6 %copy-start.24 = (pred[128]{0:T(512)(128)(4,1)S(1)}, pred[128]{0:T(512)(128)(4,1)}, u32[]{:S(2)}) copy-start(pred[128]{0:T(512)(128)(4,1)} %iota_compare_fusion.3) | copy-start | bytes 388
  182.0 5.2 %copy-start.23 = (f32[8]{0:T(128)}, f32[8]{0:T(128)S(1)}, u32[]{:S(2)}) copy-start(f32[8]{0:T(128)S(1)} %mul.117) | copy-start | bytes 100
  184.7 2.5 %copy-start.8 = (f32[224,1024]{1,0:T(8,128)S(1)}, f32[224,1024]{1,0:T(8,128)}, u32[]{:S(2)}) copy-start(f32[224,1024]{1,0:T(8,128)} %fusion.1) | copy-start | bytes 2752516
  184.7 2.5 %copy-start.17 = (f32[1,1024]{1,0:T(1,128)S(1)}, f32[1,1024]{1,0:T(1,128)}, u32[]{:S(2)}) copy-start(f32[1,1024]{1,0:T(1,128)} %copy-done.16) | copy-start | bytes 12292
Sparse Core Ops, SparseCore 0:
  41.2 41.8 all-gather.2
